TPU v7x, 256 devices: a whole 4x4x8 slice. The times are simulated.
256 devices in a mesh: tile: 64 (over y, z, core), section: 4 (over x).
Axes of the slice: x: 4, y: 4, z: 8, core: 2. Of those that a mesh axis runs over, the one named last changes fastest.
Arguments:
- features: bfloat16 [131072, 128], P(('tile', 'section')), may hold values from -6 to 6
- kernel_map: int32 [27, 131072], P(None, ('tile', 'section')), may hold values from 0 to 4096, as said below
- send_lists: int32 [64, 4, 64, 32], P('tile', 'section'), may hold values from 0 to 2048, as said below
- fine_to_coarse: int32 [131072], P('tile'), may hold values from 0 to 8191, as said below
- conv_weight: bfloat16 [27, 128, 128], replicated, may hold values from -0.125 to 0.125
- down_weight: bfloat16 [8, 128, 256], replicated, may hold values from -0.375 to 0.375
- coarse_grad: bfloat16 [65536, 256], P(('tile', 'section')), may hold values from -0.046875 to 0.046875
Outputs:
- coarse_out: bfloat16 [65536, 256], P(('tile', 'section'))
- conv_grad: float32 [27, 128, 128], replicated
- down_grad: float32 [8, 128, 256], replicated
Inputs may be any that keep to these rules, and one draw needn't show every extreme that they name: Tile t sits at grid place (t % 8, (t % 32) // 8, t // 32); two different tiles are neighbours when each of their three places differs by at most 1. For sending device (p, s) and receiving tile t, the first c entries of send_lists[p, s, t] are rows of tile p (below 2048) and the rest equal 2048; c is 0 unless p is a neighbour of t, and at most 32; every device (t, s) has some neighbour sender p of its section that fills all 32. `kernel_map`: an entry below 2048 is a row of the device's own tile; an entry 2048 + p * 32 + h names a row that send_lists fills for this device from tile p; 4096 marks a missing neighbour. Entry [13, r] is row r itself. Every filled row of send_lists is named by some entry of its receiver. `fine_to_coarse`: each entry is 8 * j + o with j a coarse row of the tile (below 1024) and o an octant below 8; the entries of one tile are distinct, every coarse row of a tile has 1 to 3 fine rows, and octant 7 of the tile's last coarse row is present in every tile.
All inputs are finite; a program needn't handle non-finite values.
Results may differ from a plain program's by a relative error of at most 0.01.
Values may be sent and summed in bfloat16 or wider, within the bound.
No kernel may reach another device: no remote copies, remote signals or barrier semaphores. Data moves between devices by JAX's collectives and lax.ppermute only.
A program may use at most 64 MiB of HBM per device.

v0:
```python
import jax
import jax.numpy as jnp
from jax import lax
from jax.sharding import PartitionSpec as P


def shards(features, kernel_map, send_lists, fine_to_coarse, conv_weight, down_weight, coarse_grad):
    rows_dev, channels = features.shape
    tile_count = lax.axis_size("tile")
    section_count = lax.axis_size("section")
    slot_count = send_lists.shape[-1]
    offset_count = kernel_map.shape[0]
    octants = down_weight.shape[0]
    out_channels = down_weight.shape[2]
    coarse_rows = coarse_grad.shape[0]
    coarse_tile = coarse_rows * section_count
    section_id = lax.axis_index("section")
    group_size = 9
    tile_feats = lax.all_gather(features, "section", axis=0, tiled=True)
    zero_row = jnp.zeros((1, channels), jnp.bfloat16)
    padded = jnp.concatenate([tile_feats, zero_row], axis=0)
    outgoing = padded[send_lists.reshape(tile_count, slot_count)]
    incoming = lax.all_to_all(outgoing, "tile", split_axis=0, concat_axis=0, tiled=True)
    lookup = jnp.concatenate(
        [tile_feats, incoming.reshape(tile_count * slot_count, channels), zero_row], axis=0
    )

    def gathered(group_id):
        picks = kernel_map[group_id * group_size : (group_id + 1) * group_size].T
        return lookup[picks].reshape(rows_dev, group_size * channels)

    group_total = offset_count // group_size
    pre_act = jnp.zeros((rows_dev, channels), jnp.float32)
    for group_id in range(group_total):
        weights = conv_weight[group_id * group_size : (group_id + 1) * group_size].reshape(
            group_size * channels, channels
        )
        pre_act = pre_act + jnp.dot(gathered(group_id), weights, preferred_element_type=jnp.float32)
    hidden = jax.nn.silu(pre_act).astype(jnp.bfloat16)
    own_map = lax.dynamic_slice_in_dim(fine_to_coarse, section_id * rows_dev, rows_dev)
    own_parent = own_map // octants
    own_octant = own_map % octants
    octant_hit = own_octant[:, None] == jnp.arange(octants, dtype=jnp.int32)[None, :]
    down_flat = down_weight.reshape(octants * channels, out_channels)
    tile_grad = lax.all_gather(coarse_grad, "section", axis=0, tiled=True)
    parent_grad = tile_grad[own_parent]
    stacked = jnp.transpose(down_weight, (1, 0, 2)).reshape(channels, octants * out_channels)
    every_octant = jnp.dot(hidden, stacked, preferred_element_type=jnp.float32)
    every_octant = every_octant.reshape(rows_dev, octants, out_channels)
    own_term = jnp.sum(jnp.where(octant_hit[:, :, None], every_octant, 0.0), axis=1)
    partial_value = jnp.zeros((coarse_tile, out_channels), jnp.float32).at[own_parent].add(own_term)
    coarse_out = lax.psum_scatter(
        partial_value.astype(jnp.bfloat16), "section", scatter_dimension=0, tiled=True
    )
    expanded = jnp.where(octant_hit[:, :, None], hidden[:, None, :], jnp.zeros((), jnp.bfloat16))
    expanded = expanded.reshape(rows_dev, octants * channels)
    down_grad = lax.dot_general(
        expanded, parent_grad, (((0,), (0,)), ((), ())), preferred_element_type=jnp.float32
    )
    back_all = lax.dot_general(
        parent_grad, down_flat, (((1,), (1,)), ((), ())), preferred_element_type=jnp.float32
    )
    back_all = back_all.reshape(rows_dev, octants, channels)
    hidden_grad = jnp.sum(jnp.where(octant_hit[:, :, None], back_all, 0.0), axis=1)
    gate_vals = jax.nn.sigmoid(pre_act)
    pre_grad = (hidden_grad * gate_vals * (1.0 + pre_act * (1.0 - gate_vals))).astype(jnp.bfloat16)
    conv_parts = []
    for group_id in range(group_total):
        product = lax.dot_general(
            gathered(group_id),
            pre_grad,
            (((0,), (0,)), ((), ())),
            preferred_element_type=jnp.float32,
        )
        conv_parts.append(product.reshape(group_size, channels, channels))
    conv_grad = jnp.concatenate(conv_parts, axis=0)
    conv_grad, down_grad = lax.psum(
        (conv_grad, down_grad.reshape(octants, channels, out_channels)), ("tile", "section")
    )
    return (coarse_out, conv_grad, down_grad)


def solution(mesh):
    placed = (
        P(("tile", "section"), None),
        P(None, ("tile", "section")),
        P("tile", "section", None, None),
        P("tile"),
        P(),
        P(),
        P(("tile", "section"), None),
    )
    return jax.shard_map(
        shards,
        mesh=mesh,
        in_specs=placed,
        out_specs=(P(("tile", "section"), None), P(), P()),
        check_vma=False,
    )
```

profile of v0, /device:TPU:1, one launch (start us, length us, event | category | flops | bytes accessed | tf_op | source)
XLA Modules:
  0.0 407.4 jit_solution(1967785928713537779)
XLA Ops:
  8.0 12.5 %all_gather.6 = bf16[2048,128]{1,0:T(8,128)(2,1)S(1)} all-gather(bf16[512,128]{1,0:T(8,128)(2,1)} %param.7), channel_id=1, replica_groups=mesh['tile'=64,'section'=4] {'section'}, dimensions={0}, use_global_device_ids=true | all-gather | bytes 655360 | tf_op jit(solution)/shard_map/all_gather | solution.py:19
  21.5 8.1 %gather_fusion = bf16[2048,128]{1,0:T(8,128)(2,1)} fusion(bf16[2049,128]{1,0:T(8,128)(2,1)S(1)} %concatenate.9, s32[2048]{0:T(1024)S(1)} %broadcast_clamp_fusion), kind=kCustom, calls=%fused_computation | custom fusion | bytes 1056768 | tf_op jit(solution)/shard_map/gather | solution.py:22
  29.5 14.0 %all-to-all-start = ((bf16[64,32,128]{2,1,0:T(8,128)(2,1)}), bf16[64,32,128]{2,1,0:T(8,128)(2,1)S(1)}, u32[]{:S(2)}, u32[]{:S(2)}) async-start(bf16[64,32,128]{2,1,0:T(8,128)(2,1)} %bitcast.1), calls=%async_computation | async-start | bytes 1048576 | tf_op jit(solution)/shard_map/all_to_all | solution.py:23
  44.7 1.0 copy.23
  46.5 11.8 %all_gather.7 = bf16[1024,256]{1,0:T(8,128)(2,1)S(1)} all-gather(bf16[256,256]{1,0:T(8,128)(2,1)S(1)} %copy-done.13), channel_id=1, replica_groups=mesh['tile'=64,'section'=4] {'section'}, dimensions={0}, use_global_device_ids=true | all-gather | bytes 655360 | tf_op jit(solution)/shard_map/all_gather | solution.py:45
  58.3 1.9 gather_fusion.4
  60.3 1.5 select_reduce_fusion.1
  61.8 5.8 %maximum_maximum_fusion = bf16[4097,128]{1,0:T(8,128)(2,1)S(1)} fusion(bf16[2048,128]{1,0:T(8,128)(2,1)S(1)} %bitcast.70, bf16[2048,128]{1,0:T(8,128)(2,1)S(1)} %all_gather.6, bf16[4097]{0:T(1024)(128)(2,1)S(1)} %pad.6.clone), kind=kLoop, calls=%fused_computation.20 | loop fusion | flops 3146496 | bytes 2105602 | tf_op jit(solution)/shard_map/concatenate | solution.py:24
  67.7 8.8 %gather_fusion.2 = bf16[4608,128]{1,0:T(8,128)(2,1)S(1)} fusion(bf16[4097,128]{1,0:T(8,128)(2,1)S(1)} %maximum_maximum_fusion, s32[5120]{0:T(1024)S(1)} %pad_clamp_fusion.1), kind=kCustom, calls=%fused_computation.2 | custom fusion | bytes 2377728 | tf_op jit(solution)/shard_map/gather | solution.py:30
  76.5 1.6 reshape.122
  78.1 2.2 reshape.103
  80.3 8.8 %gather_fusion.1 = bf16[4608,128]{1,0:T(8,128)(2,1)S(1)} fusion(bf16[4097,128]{1,0:T(8,128)(2,1)S(1)} %maximum_maximum_fusion, s32[5120]{0:T(1024)S(1)} %pad_clamp_fusion.2), kind=kCustom, calls=%fused_computation.1 | custom fusion | bytes 2377728 | tf_op jit(solution)/shard_map/gather | solution.py:30
  89.1 1.6 reshape.114
  90.7 8.8 %gather_fusion.3 = bf16[4608,128]{1,0:T(8,128)(2,1)S(1)} fusion(bf16[4097,128]{1,0:T(8,128)(2,1)S(1)} %maximum_maximum_fusion, s32[5120]{0:T(1024)S(1)} %pad_clamp_fusion), kind=kCustom, calls=%fused_computation.3 | custom fusion | bytes 2377728 | tf_op jit(solution)/shard_map/gather | solution.py:30
  99.5 1.6 reshape.130
  101.0 1.4 copy.25
  102.4 2.2 fusion.6
  104.8 1.6 fusion.18
  106.4 2.3 multiply_convert_fusion
  110.3 4.3 %scatter_custom_fusion = f32[1024,256]{1,0:T(8,128)} fusion(s32[512]{0:T(512)S(1)} %get-tuple-element.11, f32[512,256]{1,0:T(8,128)S(1)} %select_reduce_fusion, f32[]{:T(128)} %constant.19.clone.1), kind=kCustom, calls=%fused_computation.25 | custom fusion | flops 131072 | bytes 1048580 | tf_op jit(solution)/shard_map/scatter-add | solution.py:51
  114.6 2.2 convert_element_type.10
  116.9 2.2 fusion.33
  119.1 1.5 broadcast_select_fusion
  120.6 1.4 reshape.102
  122.0 1.4 reshape.104
  123.5 1.4 copy.24
  125.5 1.6 copy.27
  128.7 1.3 pad_maximum_fusion
  130.0 1.4 fusion.21
  131.4 10.6 %reduce-scatter.2.cloned.1.call-done = bf16[256,256]{1,0:T(8,128)(2,1)} async-done(((bf16[1024,256]{1,0:T(8,128)(2,1)}), bf16[256,256]{1,0:T(8,128)(2,1)}) %reduce-scatter.2.cloned.1.call-update) | async-done | bytes 131088 | tf_op jit(solution)/shard_map/reduce_scatter | solution.py:52
  142.0 254.0 %all-reduce.4.cloned.1.call-done = (f32[27,128,128]{2,1,0:T(8,128)}, f32[8,128,256]{2,1,0:T(8,128)}) async-done(((f32[27,128,128]{2,1,0:T(8,128)}, f32[8,128,256]{2,1,0:T(8,128)}), (f32[27,128,128]{2,1,0:T(8,128)}, f32[8,128,256]{2,1,0:T(8,128)})) %all-reduce.4.cloned.1.call-update) | async-done | bytes 2818064 | tf_op jit(solution)/shard_map/psum | solution.py:77
  396.0 3.0 copy.48
  (61 shorter events, 7.8 us)
Async XLA Ops:
  21.5 22.1 %copy-start.12 = (s32[27,512]{1,0:T(8,128)S(1)}, s32[27,512]{1,0:T(8,128)}, u32[]{:S(2)}) copy-start(s32[27,512]{1,0:T(8,128)} %param.8) | copy-start | bytes 165892
  29.5 32.3 %all-to-all-start = ((bf16[64,32,128]{2,1,0:T(8,128)(2,1)}), bf16[64,32,128]{2,1,0:T(8,128)(2,1)S(1)}, u32[]{:S(2)}, u32[]{:S(2)}) async-start(bf16[64,32,128]{2,1,0:T(8,128)(2,1)} %bitcast.1), calls=%async_computation | async-start | bytes 1048576 | tf_op jit(solution)/shard_map/all_to_all | solution.py:23
  43.5 1.2 copy-start.10
  43.5 98.5 %reduce-scatter.2.cloned.1.call-start = ((), (), s32[]{:S(2)}) async-start(), calls=%async_computation.2 | async-start | bytes 655360 | tf_op jit(solution)/shard_map/reduce_scatter | solution.py:52
  44.0 2.5 copy-start.13
  60.3 1.6 copy-start.8
  99.5 1.6 copy-start
  102.4 2.3 copy-start.4
  104.8 1.7 copy-start.5
  106.4 3.0 copy-start.11
  108.7 0.7 copy-start.14
  114.6 2.3 copy-start.1
  116.8 279.2 %all-reduce.4.cloned.1.call-start = ((), (), s32[]{:S(2)}) async-start(), calls=%async_computation.3 | async-start | bytes 5636096 | tf_op jit(solution)/shard_map/psum | solution.py:77
  116.9 2.3 copy-start.15
  125.5 1.6 copy-start.2
  125.5 1.6 copy-start.6
  127.6 1.1 copy-start.3
  128.7 1.3 copy-start.9
  396.0 3.0 copy-start.7
Sparse Core Ops, SparseCore 0:
  117.0 24.9 reduce-scatter.1
Sparse Core Ops, SparseCore 1:
  131.5 264.4 all-reduce.3
where the time goes:
time: 409 us; the launch traced here: 407 us
  waiting for transfers between devices  265 us (65%)
  local copies, waits for them, and re-layouts  58.8 us (14%)
  blocking collectives  24.4 us (6%)
  other arithmetic  16.7 us (4%)
  between operations  15.8 us (4%)
  starting transfers between devices  14 us (3%)
  matrix products  13.1 us (3%)
    psum x1, waiting for transfers between devices, shards(): lax.psum((conv_grad, down_grad.reshape(octants, channels, out_channels)),...  254 us
    gather x6, local copies, waits for them, and re-layouts, gathered(): return lookup[picks].reshape(rows_dev, group_size * channels)  31.1 us
    all_to_all x1, starting transfers between devices, shards(): lax.all_to_all(outgoing, 'tile', split_axis=0, concat_axis=0, tiled=True)  14 us
    all_gather x1, blocking collectives, shards(): tile_feats = lax.all_gather(features, 'section', axis=0, tiled=True)  12.5 us
    all_gather x1, blocking collectives, shards(): tile_grad = lax.all_gather(coarse_grad, 'section', axis=0, tiled=True)  11.8 us
    reduce_scatter x1, waiting for transfers between devices, shards(): lax.psum_scatter(partial_value.astype(jnp.bfloat16), 'section', scatter_d...  10.6 us
  transfers between devices with their start and end apart: 3, of which 2 were waited for; matrix products, arithmetic and copies ran while one was open for 5% of the time, Pallas kernels for 0%

commit v1 on v0

--- a/solution.py
+++ b/solution.py
@@ -1,26 +1,129 @@
 import jax
 import jax.numpy as jnp
 from jax import lax
-from jax.sharding import PartitionSpec as P
+from jax.sharding import Mesh, PartitionSpec as P
+
+RING_Y, DEPTH_Z, CORES, RING_X = 4, 8, 2, 4
+AXES = ("y", "z", "core", "x")
+TILE = ("y", "z", "core")
+
+
+def device_index(place):
+    tile = (place[0] * DEPTH_Z + place[1]) * CORES + place[2]
+    return tile * RING_X + place[3]
+
+
+def partner_pairs(partner):
+    pairs = []
+    for y in range(RING_Y):
+        for z in range(DEPTH_Z):
+            for core in range(CORES):
+                for x in range(RING_X):
+                    place = (y, z, core, x)
+                    pairs.append((device_index(place), device_index(partner(*place))))
+    return pairs
+
+
+def send(value, partner):
+    return lax.ppermute(value, AXES, partner_pairs(partner))
+
+
+def across_core(y, z, core, x):
+    return (y, z, 1 - core, x)
+
+
+def first_ring(step):
+    return lambda y, z, core, x: (y, z, core, x ^ step) if core == 0 else (y ^ step, z, core, x)
+
+
+def second_ring(step):
+    return lambda y, z, core, x: (y ^ step, z, core, x) if core == 0 else (y, z, core, x ^ step)
+
+
+def along_z(step):
+    return lambda y, z, core, x: (y, z ^ step, core, x)
+
+
+def narrow(value):
+    return value.astype(jnp.bfloat16)
+
+
+def wide(value):
+    return value.astype(jnp.float32)
+
+
+def pick(parts, digit):
+    return lax.dynamic_index_in_dim(parts, digit, 0, keepdims=False)
+
+
+def scatter_pair(parts, digit, partner):
+    other = send(pick(parts, 1 - digit), partner)
+    return narrow(wide(pick(parts, digit)) + wide(other))
+
+
+def scatter_ring(parts, digit, ring):
+    received = [send(pick(parts, digit ^ step), ring(step)) for step in (1, 2, 3)]
+    total = wide(pick(parts, digit))
+    for part in received:
+        total = total + wide(part)
+    return narrow(total)
+
+
+def swap(first, second, flip):
+    return jnp.where(flip, second, first), jnp.where(flip, first, second)
+
+
+def gather_pair(part, digit, partner):
+    other = send(part, partner)
+    return jnp.stack(swap(part, other, digit == 1))
+
+
+def gather_ring(part, digit, ring):
+    parts = [part] + [send(part, ring(step)) for step in (1, 2, 3)]
+    low, high = digit % 2 == 1, digit // 2 == 1
+    first, second = swap(parts[0], parts[1], low)
+    third, fourth = swap(parts[2], parts[3], low)
+    first, third = swap(first, third, high)
+    second, fourth = swap(second, fourth, high)
+    return jnp.stack([first, second, third, fourth])
+
+
+def sum_over_devices(partial_sums):
+    y, z, core, x = (lax.axis_index(name) for name in AXES)
+    ring_one = jnp.where(core == 0, x, y)
+    ring_two = jnp.where(core == 0, y, x)
+    rows = partial_sums.shape[0] // (CORES * RING_X * RING_Y * 2)
+    lanes = partial_sums.shape[1]
+    parts = narrow(partial_sums).reshape(CORES, RING_X * RING_Y * 2 * rows, lanes)
+    part = scatter_pair(parts, core, across_core)
+    part = scatter_ring(part.reshape(RING_X, RING_Y * 2 * rows, lanes), ring_one, first_ring)
+    part = scatter_ring(part.reshape(RING_Y, 2 * rows, lanes), ring_two, second_ring)
+    part = scatter_pair(part.reshape(2, rows, lanes), z % 2, along_z(1))
+    others = [send(part, along_z(step)) for step in (2, 4, 6)]
+    part = narrow((wide(part) + wide(others[0])) + (wide(others[1]) + wide(others[2])))
+    part = gather_pair(part, z % 2, along_z(1)).reshape(2 * rows, lanes)
+    part = gather_ring(part, ring_two, second_ring).reshape(RING_Y * 2 * rows, lanes)
+    part = gather_ring(part, ring_one, first_ring).reshape(RING_X * RING_Y * 2 * rows, lanes)
+    return wide(gather_pair(part, core, across_core)).reshape(partial_sums.shape)
 
 
 def shards(features, kernel_map, send_lists, fine_to_coarse, conv_weight, down_weight, coarse_grad):
     rows_dev, channels = features.shape
-    tile_count = lax.axis_size("tile")
-    section_count = lax.axis_size("section")
+    tile_count = lax.axis_size(TILE)
+    section_count = RING_X
     slot_count = send_lists.shape[-1]
     offset_count = kernel_map.shape[0]
     octants = down_weight.shape[0]
     out_channels = down_weight.shape[2]
     coarse_rows = coarse_grad.shape[0]
     coarse_tile = coarse_rows * section_count
-    section_id = lax.axis_index("section")
+    section_id = lax.axis_index("x")
     group_size = 9
-    tile_feats = lax.all_gather(features, "section", axis=0, tiled=True)
+    tile_feats = lax.all_gather(features, "x", axis=0, tiled=True)
     zero_row = jnp.zeros((1, channels), jnp.bfloat16)
     padded = jnp.concatenate([tile_feats, zero_row], axis=0)
     outgoing = padded[send_lists.reshape(tile_count, slot_count)]
-    incoming = lax.all_to_all(outgoing, "tile", split_axis=0, concat_axis=0, tiled=True)
+    incoming = lax.all_to_all(outgoing, TILE, split_axis=0, concat_axis=0, tiled=True)
     lookup = jnp.concatenate(
         [tile_feats, incoming.reshape(tile_count * slot_count, channels), zero_row], axis=0
     )
@@ -42,7 +145,7 @@
     own_octant = own_map % octants
     octant_hit = own_octant[:, None] == jnp.arange(octants, dtype=jnp.int32)[None, :]
     down_flat = down_weight.reshape(octants * channels, out_channels)
-    tile_grad = lax.all_gather(coarse_grad, "section", axis=0, tiled=True)
+    tile_grad = lax.all_gather(coarse_grad, "x", axis=0, tiled=True)
     parent_grad = tile_grad[own_parent]
     stacked = jnp.transpose(down_weight, (1, 0, 2)).reshape(channels, octants * out_channels)
     every_octant = jnp.dot(hidden, stacked, preferred_element_type=jnp.float32)
@@ -50,7 +153,7 @@
     own_term = jnp.sum(jnp.where(octant_hit[:, :, None], every_octant, 0.0), axis=1)
     partial_value = jnp.zeros((coarse_tile, out_channels), jnp.float32).at[own_parent].add(own_term)
     coarse_out = lax.psum_scatter(
-        partial_value.astype(jnp.bfloat16), "section", scatter_dimension=0, tiled=True
+        partial_value.astype(jnp.bfloat16), "x", scatter_dimension=0, tiled=True
     )
     expanded = jnp.where(octant_hit[:, :, None], hidden[:, None, :], jnp.zeros((), jnp.bfloat16))
     expanded = expanded.reshape(rows_dev, octants * channels)
@@ -74,26 +177,34 @@
         )
         conv_parts.append(product.reshape(group_size, channels, channels))
     conv_grad = jnp.concatenate(conv_parts, axis=0)
-    conv_grad, down_grad = lax.psum(
-        (conv_grad, down_grad.reshape(octants, channels, out_channels)), ("tile", "section")
-    )
+    conv_flat = conv_grad.reshape(offset_count * channels, channels)
+    down_flat = jnp.concatenate([down_grad[:, :channels], down_grad[:, channels:]], axis=0)
+    used = conv_flat.shape[0] + down_flat.shape[0]
+    filler = jnp.zeros((-used % 512, channels), jnp.float32)
+    sums = sum_over_devices(jnp.concatenate([conv_flat, down_flat, filler], axis=0))
+    conv_grad = sums[: conv_flat.shape[0]].reshape(offset_count, channels, channels)
+    down_sums = sums[conv_flat.shape[0] : used]
+    half = octants * channels
+    down_grad = jnp.concatenate([down_sums[:half], down_sums[half:]], axis=1)
+    down_grad = down_grad.reshape(octants, channels, out_channels)
     return (coarse_out, conv_grad, down_grad)
 
 
 def solution(mesh):
+    fine_mesh = Mesh(mesh.devices.reshape(RING_Y, DEPTH_Z, CORES, RING_X), AXES)
     placed = (
-        P(("tile", "section"), None),
-        P(None, ("tile", "section")),
-        P("tile", "section", None, None),
-        P("tile"),
+        P(AXES, None),
+        P(None, AXES),
+        P(TILE, "x", None, None),
+        P(TILE),
         P(),
         P(),
-        P(("tile", "section"), None),
+        P(AXES, None),
     )
     return jax.shard_map(
         shards,
-        mesh=mesh,
+        mesh=fine_mesh,
         in_specs=placed,
-        out_specs=(P(("tile", "section"), None), P(), P()),
+        out_specs=(P(AXES, None), P(), P()),
         check_vma=False,
     )

time: 409 us -> 225 us (0.55)
  waiting for transfers between devices: 265 us -> 42.6 us
  starting transfers between devices: 14 us -> 48.8 us
  other arithmetic: 16.7 us -> 24.8 us
  matrix products: 13.1 us -> 8.51 us
    psum x1 -> x0, waiting for transfers between devices: 254 us -> none  [shards(): lax.psum((conv_grad, down_grad.reshape(octants, channels, out_channels)),...]
    ppermute x0 -> x19, starting transfers between devices: none -> 34.6 us  [send(): return lax.ppermute(value, AXES, partner_pairs(partner))]
    ppermute x0 -> x19, waiting for transfers between devices: none -> 30.7 us  [send(): return lax.ppermute(value, AXES, partner_pairs(partner))]
    concatenate x0 -> x2, other arithmetic: none -> 10 us  [the longest x1 9 us: shards(): jnp.concatenate([conv_flat, down_flat, filler], axis=0)]
    unnamed x35 -> x23, local copies, waits for them, and re-layouts: 6.41 us -> 2.2 us
  transfers between devices with their start and end apart: 3 -> 21, of which waited for: 2 -> 16; matrix products, arithmetic and copies ran while one was open for 5% -> 7% of each run, Pallas kernels for 0% -> 0%
where the time goes in v1:
time: 225 us; the launch traced here: 221 us
  local copies, waits for them, and re-layouts  56.7 us (25%)
  starting transfers between devices  48.8 us (22%)
  waiting for transfers between devices  42.6 us (19%)
  blocking collectives  24.8 us (11%)
  other arithmetic  24.8 us (11%)
  between operations  14.8 us (7%)
  matrix products  8.51 us (4%)
    ppermute x19, starting transfers between devices, send(): return lax.ppermute(value, AXES, partner_pairs(partner))  34.6 us
    gather x6, local copies, waits for them, and re-layouts, gathered(): return lookup[picks].reshape(rows_dev, group_size * channels)  32.4 us
    ppermute x19, waiting for transfers between devices, send(): return lax.ppermute(value, AXES, partner_pairs(partner))  30.7 us
    all_to_all x1, starting transfers between devices, shards(): lax.all_to_all(outgoing, TILE, split_axis=0, concat_axis=0, tiled=True)  14.1 us
    all_gather x1, blocking collectives, shards(): tile_feats = lax.all_gather(features, 'x', axis=0, tiled=True)  12.5 us
    all_gather x1, blocking collectives, shards(): tile_grad = lax.all_gather(coarse_grad, 'x', axis=0, tiled=True)  12.2 us
    reduce_scatter x1, waiting for transfers between devices, shards(): lax.psum_scatter(partial_value.astype(jnp.bfloat16), 'x', scatter_dimensi...  11.9 us
    concatenate x1, other arithmetic, shards(): jnp.concatenate([conv_flat, down_flat, filler], axis=0)  9 us
  transfers between devices with their start and end apart: 21, of which 16 were waited for; matrix products, arithmetic and copies ran while one was open for 7% of the time, Pallas kernels for 0%

profile of v1, /device:TPU:1, one launch (start us, length us, event | category | flops | bytes accessed | tf_op | source)
XLA Modules:
  0.0 221.0 jit_solution(3623064087047193606)
XLA Ops:
  7.2 12.5 %all_gather.6 = bf16[2048,128]{1,0:T(8,128)(2,1)S(1)} all-gather(bf16[512,128]{1,0:T(8,128)(2,1)} %param.7), channel_id=1, replica_groups=mesh['y'=4,'z'=8,'core'=2,'x'=4] {'x'}, dimensions={0}, use_global_device_ids=true | all-gather | bytes 655360 | tf_op jit(solution)/shard_map/all_gather | solution.py:122
  20.7 8.1 %gather_fusion = bf16[2048,128]{1,0:T(8,128)(2,1)} fusion(bf16[2049,128]{1,0:T(8,128)(2,1)S(1)} %concatenate.17, s32[2048]{0:T(1024)S(1)} %broadcast_clamp_fusion), kind=kCustom, calls=%fused_computation | custom fusion | bytes 1056768 | tf_op jit(solution)/shard_map/gather | solution.py:125
  28.7 14.1 %all-to-all-start = ((bf16[64,32,128]{2,1,0:T(8,128)(2,1)}), bf16[64,32,128]{2,1,0:T(8,128)(2,1)S(1)}, u32[]{:S(2)}, u32[]{:S(2)}) async-start(bf16[64,32,128]{2,1,0:T(8,128)(2,1)} %bitcast.1), calls=%async_computation | async-start | bytes 1048576 | tf_op jit(solution)/shard_map/all_to_all | solution.py:126
  44.8 12.2 %all_gather.7 = bf16[1024,256]{1,0:T(8,128)(2,1)S(1)} all-gather(bf16[256,256]{1,0:T(8,128)(2,1)S(1)} %copy-done.8), channel_id=1, replica_groups=mesh['y'=4,'z'=8,'core'=2,'x'=4] {'x'}, dimensions={0}, use_global_device_ids=true | all-gather | bytes 655360 | tf_op jit(solution)/shard_map/all_gather | solution.py:148
  57.1 1.9 gather_fusion.4
  61.3 5.8 %maximum_maximum_fusion.1 = bf16[4097,128]{1,0:T(8,128)(2,1)S(1)} fusion(bf16[2048,128]{1,0:T(8,128)(2,1)S(1)} %bitcast.146, bf16[2048,128]{1,0:T(8,128)(2,1)S(1)} %all_gather.6, bf16[4097]{0:T(1024)(128)(2,1)S(1)} %pad.24.clone), kind=kLoop, calls=%fused_computation.28 | loop fusion | flops 3146496 | bytes 2105602 | tf_op jit(solution)/shard_map/concatenate | solution.py:127
  67.1 8.8 %gather_fusion.3 = bf16[4608,128]{1,0:T(8,128)(2,1)S(1)} fusion(bf16[4097,128]{1,0:T(8,128)(2,1)S(1)} %maximum_maximum_fusion.1, s32[5120]{0:T(1024)S(1)} %pad_clamp_fusion), kind=kCustom, calls=%fused_computation.3 | custom fusion | bytes 2377728 | tf_op jit(solution)/shard_map/gather | solution.py:133
  79.0 8.8 %gather_fusion.2 = bf16[4608,128]{1,0:T(8,128)(2,1)S(1)} fusion(bf16[4097,128]{1,0:T(8,128)(2,1)S(1)} %maximum_maximum_fusion.1, s32[5120]{0:T(1024)S(1)} %pad_clamp_fusion.1), kind=kCustom, calls=%fused_computation.2 | custom fusion | bytes 2377728 | tf_op jit(solution)/shard_map/gather | solution.py:133
  89.3 2.2 reshape.144
  91.5 10.0 %gather_fusion.1 = bf16[4608,128]{1,0:T(8,128)(2,1)S(1)} fusion(bf16[4097,128]{1,0:T(8,128)(2,1)S(1)} %maximum_maximum_fusion.1, s32[5120]{0:T(1024)} %pad_clamp_fusion.2), kind=kCustom, calls=%fused_computation.1 | custom fusion | bytes 2377728 | tf_op jit(solution)/shard_map/gather | solution.py:133
  105.2 2.5 %copy.25 = bf16[1152,512]{1,0:T(8,128)(2,1)} copy(bf16[1152,512]{0,1:T(8,128)(2,1)} %bitcast.139) | data formatting | bytes 2359296 | tf_op jit(solution)/shard_map/dot_general | solution.py:172
  107.8 2.2 %fusion.7 = f32[512,128]{1,0:T(8,128)S(1)} fusion(bf16[512,9,128]{2,1,0:T(8,128)(2,1)} %reshape.169, bf16[27,128,128]{2,1,0:T(8,128)(2,1)S(1)} %copy-done.10), kind=kOutput, calls=%fused_computation.23 | convolution fusion | flops 150994944 | bytes 1736704 | tf_op jit(solution)/shard_map/dot_general | solution.py:141
  118.0 9.0 %maximum_maximum_fusion = bf16[5632,128]{1,0:T(8,128)(2,1)S(1)} fusion(bf16[1024,128]{1,0:T(8,128)(2,1)S(1)} %get-tuple-element.15, bf16[1024,128]{1,0:T(8,128)(2,1)S(1)} %get-tuple-element.14, bf16[3456,128]{1,0:T(8,128)(2,1)S(1)} %bitcast.142, bf16[5632]{0:T(1024)(128)(2,1)S(1)} %pad.18.clone), kind=kLoop, calls=%fused_computation.8 | loop fusion | flops 5767168 | bytes 2862080 | tf_op jit(solution)/shard_map/concatenate | solution.py:184
  127.1 1.9 collective-permute-start
  128.9 1.8 collective-permute-done
  132.3 2.6 %collective-permute-start.2 = (bf16[704,128]{1,0:T(8,128)(2,1)S(1)}, bf16[704,128]{1,0:T(8,128)(2,1)S(1)}, u32[]{:S(2)}, u32[]{:S(2)}) collective-permute-start(bf16[704,128]{1,0:T(8,128)(2,1)S(1)} %get-tuple-element.13), channel_id=1, source_target_pairs={{0,2},{1,3},{2,0},{3,1},{4,132},{5,133},{6,134},{7,135},{8,10},{9,... | collective-permute-start | bytes 540680 | tf_op jit(solution)/shard_map/ppermute | solution.py:28
  135.7 4.3 %collective-permute-done.2 = bf16[704,128]{1,0:T(8,128)(2,1)S(1)} collective-permute-done((bf16[704,128]{1,0:T(8,128)(2,1)S(1)}, bf16[704,128]{1,0:T(8,128)(2,1)S(1)}, u32[]{:S(2)}, u32[]{:S(2)}) %collective-permute-start.2) | collective-permute-done | bytes 180256 | tf_op jit(solution)/shard_map/ppermute | solution.py:28
  140.0 1.9 collective-permute-done.3
  142.1 1.8 collective-permute-start.4
  143.9 2.4 %collective-permute-start.5 = (bf16[176,128]{1,0:T(8,128)(2,1)S(1)}, bf16[176,128]{1,0:T(8,128)(2,1)S(1)}, u32[]{:S(2)}, u32[]{:S(2)}) collective-permute-start(bf16[176,128]{1,0:T(8,128)(2,1)S(1)} %get-tuple-element.24), channel_id=1, source_target_pairs={{0,128},{1,129},{2,130},{3,131},{4,6},{5,7},{6,4},{7,5},{8,136},{9... | collective-permute-start | bytes 135176 | tf_op jit(solution)/shard_map/ppermute | solution.py:28
  146.4 1.9 collective-permute-done.5
  148.3 2.3 %collective-permute-done.6 = bf16[176,128]{1,0:T(8,128)(2,1)S(1)} collective-permute-done((bf16[176,128]{1,0:T(8,128)(2,1)S(1)}, bf16[176,128]{1,0:T(8,128)(2,1)S(1)}, u32[]{:S(2)}, u32[]{:S(2)}) %collective-permute-start.6) | collective-permute-done | bytes 45088 | tf_op jit(solution)/shard_map/ppermute | solution.py:28
  153.4 3.4 %collective-permute-start.10 = (bf16[88,128]{1,0:T(8,128)(2,1)S(1)}, bf16[88,128]{1,0:T(8,128)(2,1)S(1)}, u32[]{:S(2)}, u32[]{:S(2)}) collective-permute-start(bf16[88,128]{1,0:T(8,128)(2,1)S(1)} %fusion.39), channel_id=1, source_target_pairs={{0,48},{1,49},{2,50},{3,51},{4,52},{5,53},{6,54},{7,55},{8,56},{9,... | collective-permute-start | bytes 67592 | tf_op jit(solution)/shard_map/ppermute | solution.py:28
  156.9 2.0 collective-permute-start.8
  160.7 5.1 %collective-permute-done.9 = bf16[88,128]{1,0:T(8,128)(2,1)S(1)} collective-permute-done((bf16[88,128]{1,0:T(8,128)(2,1)S(1)}, bf16[88,128]{1,0:T(8,128)(2,1)S(1)}, u32[]{:S(2)}, u32[]{:S(2)}) %collective-permute-start.9) | collective-permute-done | bytes 22560 | tf_op jit(solution)/shard_map/ppermute | solution.py:28
  166.5 2.1 collective-permute-done.11
  169.4 2.6 %collective-permute-start.14 = (bf16[176,128]{1,0:T(8,128)(2,1)S(1)}, bf16[176,128]{1,0:T(8,128)(2,1)S(1)}, u32[]{:S(2)}, u32[]{:S(2)}) collective-permute-start(bf16[176,128]{1,0:T(8,128)(2,1)S(1)} %bitcast.158), channel_id=1, source_target_pairs={{0,64},{1,65},{2,66},{3,67},{4,5},{5,4},{6,7},{7,6},{8,72},{9,73},... | collective-permute-start | bytes 135176 | tf_op jit(solution)/shard_map/ppermute | solution.py:28
  175.2 2.1 collective-permute-start.17
  177.3 5.4 %collective-permute-done.15 = bf16[704,128]{1,0:T(8,128)(2,1)S(1)} collective-permute-done((bf16[704,128]{1,0:T(8,128)(2,1)S(1)}, bf16[704,128]{1,0:T(8,128)(2,1)S(1)}, u32[]{:S(2)}, u32[]{:S(2)}) %collective-permute-start.15) | collective-permute-done | bytes 180256 | tf_op jit(solution)/shard_map/ppermute | solution.py:28
  183.3 9.9 %collective-permute-start.18 = (bf16[2816,128]{1,0:T(8,128)(2,1)S(1)}, bf16[2816,128]{1,0:T(8,128)(2,1)S(1)}, u32[]{:S(2)}, u32[]{:S(2)}) collective-permute-start(bf16[2816,128]{1,0:T(8,128)(2,1)S(1)} %bitcast.145), channel_id=1, source_target_pairs={{0,4},{1,5},{2,6},{3,7},{4,0},{5,1},{6,2},{7,3},{8,12},{9,13},{10,... | collective-permute-start | bytes 2162696 | tf_op jit(solution)/shard_map/ppermute | solution.py:28
  194.4 3.7 %scatter_custom_fusion = f32[1024,256]{1,0:T(8,128)S(1)} fusion(s32[512]{0:T(512)} %copy-done.9, f32[512,256]{1,0:T(8,128)S(1)} %select_reduce_fusion, f32[]{:T(128)} %constant.125.clone.1), kind=kCustom, calls=%fused_computation.37 | custom fusion | flops 131072 | bytes 1049088 | tf_op jit(solution)/shard_map/scatter-add | solution.py:154
  202.0 11.9 %reduce-scatter.2.cloned.1.call-done = bf16[256,256]{1,0:T(8,128)(2,1)} async-done(((bf16[1024,256]{1,0:T(8,128)(2,1)}), bf16[256,256]{1,0:T(8,128)(2,1)}) %reduce-scatter.2.cloned.1.call-update) | async-done | bytes 131088 | tf_op jit(solution)/shard_map/reduce_scatter | solution.py:155
  (109 shorter events, 38.8 us)
Async XLA Ops:
  20.6 22.2 %copy-start.7 = (s32[27,512]{1,0:T(8,128)S(1)}, s32[27,512]{1,0:T(8,128)}, u32[]{:S(2)}) copy-start(s32[27,512]{1,0:T(8,128)} %param.8) | copy-start | bytes 165892
  28.7 16.1 %copy-start.8 = (bf16[256,256]{1,0:T(8,128)(2,1)S(1)}, bf16[256,256]{1,0:T(8,128)(2,1)}, u32[]{:S(2)}) copy-start(bf16[256,256]{1,0:T(8,128)(2,1)} %param.13) | copy-start | bytes 393220
  28.7 32.6 %all-to-all-start = ((bf16[64,32,128]{2,1,0:T(8,128)(2,1)}), bf16[64,32,128]{2,1,0:T(8,128)(2,1)S(1)}, u32[]{:S(2)}, u32[]{:S(2)}) async-start(bf16[64,32,128]{2,1,0:T(8,128)(2,1)} %bitcast.1), calls=%async_computation | async-start | bytes 1048576 | tf_op jit(solution)/shard_map/all_to_all | solution.py:126
  42.8 171.1 %reduce-scatter.2.cloned.1.call-start = ((), (), s32[]{:S(2)}) async-start(), calls=%async_computation.2 | async-start | bytes 655360 | tf_op jit(solution)/shard_map/reduce_scatter | solution.py:155
  44.8 14.2 %copy-start.9 = (s32[512]{0:T(512)}, s32[512]{0:T(512)S(1)}, u32[]{:S(2)}) copy-start(s32[512]{0:T(512)S(1)} %get-tuple-element.31) | copy-start | bytes 6148
  44.8 14.9 %copy-start.5 = (bf16[8,128,256]{2,1,0:T(8,128)(2,1)S(1)}, bf16[8,128,256]{2,1,0:T(8,128)(2,1)}, u32[]{:S(2)}) copy-start(bf16[8,128,256]{2,1,0:T(8,128)(2,1)} %param.12) | copy-start | bytes 1572868
  59.0 2.3 %copy-start.3 = (bf16[512,256]{1,0:T(8,128)(2,1)}, bf16[512,256]{1,0:T(8,128)(2,1)S(1)}, u32[]{:S(2)}) copy-start(bf16[512,256]{1,0:T(8,128)(2,1)S(1)} %gather_fusion.4) | copy-start | bytes 786436
  105.2 2.5 %copy-start.10 = (bf16[27,128,128]{2,1,0:T(8,128)(2,1)S(1)}, bf16[27,128,128]{2,1,0:T(8,128)(2,1)}, u32[]{:S(2)}) copy-start(bf16[27,128,128]{2,1,0:T(8,128)(2,1)} %param.11) | copy-start | bytes 2654212
  107.8 2.2 %copy-start.2 = (bf16[512,9,128]{2,1,0:T(8,128)(2,1)S(1)}, bf16[512,9,128]{2,1,0:T(8,128)(2,1)}, u32[]{:S(2)}) copy-start(bf16[512,9,128]{2,1,0:T(8,128)(2,1)} %reshape.177) | copy-start | bytes 3538948
  110.0 1.6 copy-start.1
  113.1 1.3 copy-start
  115.9 1.4 copy-start.4
  127.1 3.7 %collective-permute-start = (bf16[2816,128]{1,0:T(8,128)(2,1)S(1)}, bf16[2816,128]{1,0:T(8,128)(2,1)S(1)}, u32[]{:S(2)}, u32[]{:S(2)}) collective-permute-start(bf16[2816,128]{1,0:T(8,128)(2,1)S(1)} %dynamic-slice_bitcast_fusion), channel_id=1, source_target_pairs={{0,4},{1,5},{2,6},{3,7},{4,0},{5,1},{6,2},{7,3},{8,12},{9,13},{10,... | collective-permute-start | bytes 2162696 | tf_op jit(solution)/shard_map/ppermute | solution.py:28
  131.0 4.7 %collective-permute-start.1 = (bf16[704,128]{1,0:T(8,128)(2,1)S(1)}, bf16[704,128]{1,0:T(8,128)(2,1)S(1)}, u32[]{:S(2)}, u32[]{:S(2)}) collective-permute-start(bf16[704,128]{1,0:T(8,128)(2,1)S(1)} %get-tuple-element.11), channel_id=1, source_target_pairs={{0,1},{1,0},{2,3},{3,2},{4,68},{5,69},{6,70},{7,71},{8,9},{9,8},{1... | collective-permute-start | bytes 540680 | tf_op jit(solution)/shard_map/ppermute | solution.py:28
  132.3 7.7 %collective-permute-start.2 = (bf16[704,128]{1,0:T(8,128)(2,1)S(1)}, bf16[704,128]{1,0:T(8,128)(2,1)S(1)}, u32[]{:S(2)}, u32[]{:S(2)}) collective-permute-start(bf16[704,128]{1,0:T(8,128)(2,1)S(1)} %get-tuple-element.13), channel_id=1, source_target_pairs={{0,2},{1,3},{2,0},{3,1},{4,132},{5,133},{6,134},{7,135},{8,10},{9,... | collective-permute-start | bytes 540680 | tf_op jit(solution)/shard_map/ppermute | solution.py:28
  134.9 7.0 %collective-permute-start.3 = (bf16[704,128]{1,0:T(8,128)(2,1)S(1)}, bf16[704,128]{1,0:T(8,128)(2,1)S(1)}, u32[]{:S(2)}, u32[]{:S(2)}) collective-permute-start(bf16[704,128]{1,0:T(8,128)(2,1)S(1)} %get-tuple-element.12), channel_id=1, source_target_pairs={{0,3},{1,2},{2,1},{3,0},{4,196},{5,197},{6,198},{7,199},{8,11},{9,... | collective-permute-start | bytes 540680 | tf_op jit(solution)/shard_map/ppermute | solution.py:28
  142.1 4.3 %collective-permute-start.4 = (bf16[176,128]{1,0:T(8,128)(2,1)S(1)}, bf16[176,128]{1,0:T(8,128)(2,1)S(1)}, u32[]{:S(2)}, u32[]{:S(2)}) collective-permute-start(bf16[176,128]{1,0:T(8,128)(2,1)S(1)} %get-tuple-element.22), channel_id=1, source_target_pairs={{0,64},{1,65},{2,66},{3,67},{4,5},{5,4},{6,7},{7,6},{8,72},{9,73},... | collective-permute-start | bytes 135176 | tf_op jit(solution)/shard_map/ppermute | solution.py:28
  143.9 4.4 %collective-permute-start.5 = (bf16[176,128]{1,0:T(8,128)(2,1)S(1)}, bf16[176,128]{1,0:T(8,128)(2,1)S(1)}, u32[]{:S(2)}, u32[]{:S(2)}) collective-permute-start(bf16[176,128]{1,0:T(8,128)(2,1)S(1)} %get-tuple-element.24), channel_id=1, source_target_pairs={{0,128},{1,129},{2,130},{3,131},{4,6},{5,7},{6,4},{7,5},{8,136},{9... | collective-permute-start | bytes 135176 | tf_op jit(solution)/shard_map/ppermute | solution.py:28
  146.3 4.4 %collective-permute-start.6 = (bf16[176,128]{1,0:T(8,128)(2,1)S(1)}, bf16[176,128]{1,0:T(8,128)(2,1)S(1)}, u32[]{:S(2)}, u32[]{:S(2)}) collective-permute-start(bf16[176,128]{1,0:T(8,128)(2,1)S(1)} %get-tuple-element.23), channel_id=1, source_target_pairs={{0,192},{1,193},{2,194},{3,195},{4,7},{5,6},{6,5},{7,4},{8,200},{9... | collective-permute-start | bytes 135176 | tf_op jit(solution)/shard_map/ppermute | solution.py:28
  150.7 2.7 %collective-permute-start.7 = (bf16[88,128]{1,0:T(8,128)(2,1)S(1)}, bf16[88,128]{1,0:T(8,128)(2,1)S(1)}, u32[]{:S(2)}, u32[]{:S(2)}) collective-permute-start(bf16[88,128]{1,0:T(8,128)(2,1)S(1)} %dynamic-slice_bitcast_fusion.7), channel_id=1, source_target_pairs={{0,8},{1,9},{2,10},{3,11},{4,12},{5,13},{6,14},{7,15},{8,0},{9,1},... | collective-permute-start | bytes 67592 | tf_op jit(solution)/shard_map/ppermute | solution.py:28
  153.4 6.0 %collective-permute-start.10 = (bf16[88,128]{1,0:T(8,128)(2,1)S(1)}, bf16[88,128]{1,0:T(8,128)(2,1)S(1)}, u32[]{:S(2)}, u32[]{:S(2)}) collective-permute-start(bf16[88,128]{1,0:T(8,128)(2,1)S(1)} %fusion.39), channel_id=1, source_target_pairs={{0,48},{1,49},{2,50},{3,51},{4,52},{5,53},{6,54},{7,55},{8,56},{9,... | collective-permute-start | bytes 67592 | tf_op jit(solution)/shard_map/ppermute | solution.py:28
  156.9 3.8 %collective-permute-start.8 = (bf16[88,128]{1,0:T(8,128)(2,1)S(1)}, bf16[88,128]{1,0:T(8,128)(2,1)S(1)}, u32[]{:S(2)}, u32[]{:S(2)}) collective-permute-start(bf16[88,128]{1,0:T(8,128)(2,1)S(1)} %fusion.39), channel_id=1, source_target_pairs={{0,16},{1,17},{2,18},{3,19},{4,20},{5,21},{6,22},{7,23},{8,24},{9,... | collective-permute-start | bytes 67592 | tf_op jit(solution)/shard_map/ppermute | solution.py:28
  158.9 6.9 %collective-permute-start.9 = (bf16[88,128]{1,0:T(8,128)(2,1)S(1)}, bf16[88,128]{1,0:T(8,128)(2,1)S(1)}, u32[]{:S(2)}, u32[]{:S(2)}) collective-permute-start(bf16[88,128]{1,0:T(8,128)(2,1)S(1)} %fusion.39), channel_id=1, source_target_pairs={{0,32},{1,33},{2,34},{3,35},{4,36},{5,37},{6,38},{7,39},{8,40},{9,... | collective-permute-start | bytes 67592 | tf_op jit(solution)/shard_map/ppermute | solution.py:28
  165.8 2.8 %collective-permute-start.11 = (bf16[88,128]{1,0:T(8,128)(2,1)S(1)}, bf16[88,128]{1,0:T(8,128)(2,1)S(1)}, u32[]{:S(2)}, u32[]{:S(2)}) collective-permute-start(bf16[88,128]{1,0:T(8,128)(2,1)S(1)} %add_convert_fusion), channel_id=1, source_target_pairs={{0,8},{1,9},{2,10},{3,11},{4,12},{5,13},{6,14},{7,15},{8,0},{9,1},... | collective-permute-start | bytes 67592 | tf_op jit(solution)/shard_map/ppermute | solution.py:28
  168.6 4.2 %collective-permute-start.12 = (bf16[176,128]{1,0:T(8,128)(2,1)S(1)}, bf16[176,128]{1,0:T(8,128)(2,1)S(1)}, u32[]{:S(2)}, u32[]{:S(2)}) collective-permute-start(bf16[176,128]{1,0:T(8,128)(2,1)S(1)} %bitcast.156), channel_id=1, source_target_pairs={{0,192},{1,193},{2,194},{3,195},{4,7},{5,6},{6,5},{7,4},{8,200},{9... | collective-permute-start | bytes 135176 | tf_op jit(solution)/shard_map/ppermute | solution.py:28
  168.7 4.6 %collective-permute-start.13 = (bf16[176,128]{1,0:T(8,128)(2,1)S(1)}, bf16[176,128]{1,0:T(8,128)(2,1)S(1)}, u32[]{:S(2)}, u32[]{:S(2)}) collective-permute-start(bf16[176,128]{1,0:T(8,128)(2,1)S(1)} %bitcast.157), channel_id=1, source_target_pairs={{0,128},{1,129},{2,130},{3,131},{4,6},{5,7},{6,4},{7,5},{8,136},{9... | collective-permute-start | bytes 135176 | tf_op jit(solution)/shard_map/ppermute | solution.py:28
  169.4 4.5 %collective-permute-start.14 = (bf16[176,128]{1,0:T(8,128)(2,1)S(1)}, bf16[176,128]{1,0:T(8,128)(2,1)S(1)}, u32[]{:S(2)}, u32[]{:S(2)}) collective-permute-start(bf16[176,128]{1,0:T(8,128)(2,1)S(1)} %bitcast.158), channel_id=1, source_target_pairs={{0,64},{1,65},{2,66},{3,67},{4,5},{5,4},{6,7},{7,6},{8,72},{9,73},... | collective-permute-start | bytes 135176 | tf_op jit(solution)/shard_map/ppermute | solution.py:28
  173.9 8.7 %collective-permute-start.15 = (bf16[704,128]{1,0:T(8,128)(2,1)S(1)}, bf16[704,128]{1,0:T(8,128)(2,1)S(1)}, u32[]{:S(2)}, u32[]{:S(2)}) collective-permute-start(bf16[704,128]{1,0:T(8,128)(2,1)S(1)} %bitcast.149), channel_id=1, source_target_pairs={{0,3},{1,2},{2,1},{3,0},{4,196},{5,197},{6,198},{7,199},{8,11},{9,... | collective-permute-start | bytes 540680 | tf_op jit(solution)/shard_map/ppermute | solution.py:28
  175.1 7.6 %collective-permute-start.16 = (bf16[704,128]{1,0:T(8,128)(2,1)S(1)}, bf16[704,128]{1,0:T(8,128)(2,1)S(1)}, u32[]{:S(2)}, u32[]{:S(2)}) collective-permute-start(bf16[704,128]{1,0:T(8,128)(2,1)S(1)} %bitcast.150), channel_id=1, source_target_pairs={{0,2},{1,3},{2,0},{3,1},{4,132},{5,133},{6,134},{7,135},{8,10},{9,... | collective-permute-start | bytes 540680 | tf_op jit(solution)/shard_map/ppermute | solution.py:28
  175.2 7.9 %collective-permute-start.17 = (bf16[704,128]{1,0:T(8,128)(2,1)S(1)}, bf16[704,128]{1,0:T(8,128)(2,1)S(1)}, u32[]{:S(2)}, u32[]{:S(2)}) collective-permute-start(bf16[704,128]{1,0:T(8,128)(2,1)S(1)} %bitcast.151), channel_id=1, source_target_pairs={{0,1},{1,0},{2,3},{3,2},{4,68},{5,69},{6,70},{7,71},{8,9},{9,8},{1... | collective-permute-start | bytes 540680 | tf_op jit(solution)/shard_map/ppermute | solution.py:28
  177.3 15.9 %copy-start.6 = (bf16[8,128,256]{2,1,0:T(8,128)(2,1)S(1)}, bf16[8,128,256]{2,1,0:T(8,128)(2,1)}, u32[]{:S(2)}) copy-start(bf16[8,128,256]{2,1,0:T(8,128)(2,1)} %param.12) | copy-start | bytes 1572868
  183.3 15.7 %collective-permute-start.18 = (bf16[2816,128]{1,0:T(8,128)(2,1)S(1)}, bf16[2816,128]{1,0:T(8,128)(2,1)S(1)}, u32[]{:S(2)}, u32[]{:S(2)}) collective-permute-start(bf16[2816,128]{1,0:T(8,128)(2,1)S(1)} %bitcast.145), channel_id=1, source_target_pairs={{0,4},{1,5},{2,6},{3,7},{4,0},{5,1},{6,2},{7,3},{8,12},{9,13},{10,... | collective-permute-start | bytes 2162696 | tf_op jit(solution)/shard_map/ppermute | solution.py:28
Sparse Core Ops, SparseCore 0:
  199.1 14.7 reduce-scatter.1

commit v2 on v1

v2 whole, which is shorter than its diff:
```python
import jax
import jax.numpy as jnp
from jax import lax
from jax.experimental import pallas as pl
from jax.experimental.pallas import tpu as pltpu
from jax.sharding import Mesh, PartitionSpec as P

RING_Y, DEPTH_Z, CORES, RING_X = 4, 8, 2, 4
AXES = ("y", "z", "core", "x")
TILE = ("y", "z", "core")
UNROLL = 16


def device_index(place):
    tile = (place[0] * DEPTH_Z + place[1]) * CORES + place[2]
    return tile * RING_X + place[3]


def partner_pairs(partner):
    pairs = []
    for y in range(RING_Y):
        for z in range(DEPTH_Z):
            for core in range(CORES):
                for x in range(RING_X):
                    place = (y, z, core, x)
                    pairs.append((device_index(place), device_index(partner(*place))))
    return pairs


def send(value, partner):
    return lax.ppermute(value, AXES, partner_pairs(partner))


def across_core(y, z, core, x):
    return (y, z, 1 - core, x)


def first_ring(step):
    return lambda y, z, core, x: (y, z, core, x ^ step) if core == 0 else (y ^ step, z, core, x)


def second_ring(step):
    return lambda y, z, core, x: (y ^ step, z, core, x) if core == 0 else (y, z, core, x ^ step)


def along_z(step):
    return lambda y, z, core, x: (y, z ^ step, core, x)


def narrow(value):
    return value.astype(jnp.bfloat16)


def wide(value):
    return value.astype(jnp.float32)


def pick(parts, digit):
    return lax.dynamic_index_in_dim(parts, digit, 0, keepdims=False)


def scatter_pair(parts, digit, partner):
    other = send(pick(parts, 1 - digit), partner)
    return narrow(wide(pick(parts, digit)) + wide(other))


def scatter_ring(parts, digit, ring):
    received = [send(pick(parts, digit ^ step), ring(step)) for step in (1, 2, 3)]
    total = wide(pick(parts, digit))
    for part in received:
        total = total + wide(part)
    return narrow(total)


def swap(first, second, flip):
    return jnp.where(flip, second, first), jnp.where(flip, first, second)


def gather_pair(part, digit, partner):
    other = send(part, partner)
    return jnp.stack(swap(part, other, digit == 1))


def gather_ring(part, digit, ring):
    parts = [part] + [send(part, ring(step)) for step in (1, 2, 3)]
    low, high = digit % 2 == 1, digit // 2 == 1
    first, second = swap(parts[0], parts[1], low)
    third, fourth = swap(parts[2], parts[3], low)
    first, third = swap(first, third, high)
    second, fourth = swap(second, fourth, high)
    return jnp.stack([first, second, third, fourth])


def sum_over_devices(partial_sums, coarse):
    y, z, core, x = (lax.axis_index(name) for name in AXES)
    ring_one = jnp.where(core == 0, x, y)
    ring_two = jnp.where(core == 0, y, x)
    rows = partial_sums.shape[0] // (CORES * RING_X * RING_Y * 2)
    lanes = partial_sums.shape[1]
    parts = partial_sums.reshape(CORES, RING_X * RING_Y * 2 * rows, lanes)
    part = scatter_pair(parts, core, across_core)
    part = scatter_ring(part.reshape(RING_X, RING_Y * 2 * rows, lanes), ring_one, first_ring)
    part, coarse = lax.optimization_barrier((part, coarse))
    part = scatter_ring(part.reshape(RING_Y, 2 * rows, lanes), ring_two, second_ring)
    part = scatter_pair(part.reshape(2, rows, lanes), z % 2, along_z(1))
    others = [send(part, along_z(step)) for step in (2, 4, 6)]
    part = narrow((wide(part) + wide(others[0])) + (wide(others[1]) + wide(others[2])))
    part = gather_pair(part, z % 2, along_z(1)).reshape(2 * rows, lanes)
    part = gather_ring(part, ring_two, second_ring).reshape(RING_Y * 2 * rows, lanes)
    part = gather_ring(part, ring_one, first_ring).reshape(RING_X * RING_Y * 2 * rows, lanes)
    return wide(gather_pair(part, core, across_core)).reshape(partial_sums.shape), coarse


def ring_x(step):
    return lambda y, z, core, x: (y, z, core, x ^ step)


def share_over_x(value):
    return [value] + [send(value, ring_x(step)) for step in (1, 2, 3)]


def place_parts(target, parts, x):
    rows = parts[0].shape[0]
    for step, part in enumerate(parts):
        start = pl.multiple_of((x ^ step) * rows, rows)
        target[pl.ds(start, rows), :] = part[...].astype(target.dtype)


def copy_rows(table, target, picks, count):
    def block(block_id, carry):
        base = pl.multiple_of(block_id * UNROLL, UNROLL)
        rows = [table[pl.ds(picks(base + j), 1), :] for j in range(UNROLL)]
        for j, row in enumerate(rows):
            target[pl.ds(base + j, 1), :] = row
        return carry

    lax.fori_loop(0, count // UNROLL, block, 0)


def pick_halo(lists, part0, part1, part2, part3, out, table, stage):
    tile_rows = 4 * part0.shape[0]
    slots = lists.shape[1]
    place_parts(table, (part0, part1, part2, part3), lax.axis_index("x"))
    table[pl.ds(tile_rows, 8), :] = jnp.zeros((8, table.shape[1]), jnp.float32)
    copy_rows(table, stage, lambda at: lists[at // slots, at % slots], stage.shape[0])
    out[...] = stage[...].astype(jnp.bfloat16)


def matmul(left, right, left_dim=1, right_dim=0):
    return lax.dot_general(
        left, right, (((left_dim,), (right_dim,)), ((), ())), preferred_element_type=jnp.float32
    )


def step_kernel(
    kernel_map, part0, part1, part2, part3, incoming, conv_weight, down_weight,
    grad0, grad1, grad2, grad3, link_column, link_row,
    coarse, sums, table, stage, gathered, pre_act, tile_grad,
):
    x = lax.axis_index("x")
    offsets, rows = kernel_map.shape
    channels = part0.shape[1]
    octants, _, out_channels = down_weight.shape
    tile_rows = 4 * rows
    coarse_tile = tile_grad.shape[0]
    place_parts(table, (part0, part1, part2, part3), x)
    table[pl.ds(tile_rows, incoming.shape[0]), :] = incoming[...].astype(jnp.float32)
    table[pl.ds(tile_rows + incoming.shape[0], 8), :] = jnp.zeros((8, channels), jnp.float32)
    place_parts(tile_grad, (grad0, grad1, grad2, grad3), x)
    pre_act[...] = jnp.zeros_like(pre_act)

    def forward(offset, carry):
        copy_rows(table, stage, lambda at: kernel_map[offset, at], rows)
        block = stage[...].astype(jnp.bfloat16)
        gathered[offset] = block
        pre_act[...] += matmul(block, conv_weight[offset])
        return carry

    lax.fori_loop(0, offsets, forward, 0)

    act = pre_act[...]
    gate = 1.0 / (1.0 + jnp.exp(-act))
    hidden = (act * gate).astype(jnp.bfloat16)
    link = link_column[...]
    octant = link % octants
    at_parent = (link // octants) == lax.broadcasted_iota(jnp.int32, (rows, coarse_tile), 1)
    parent_grad = matmul(at_parent.astype(jnp.bfloat16), tile_grad[...]).astype(jnp.bfloat16)
    own_term = jnp.zeros((rows, out_channels), jnp.float32)
    hidden_grad = jnp.zeros((rows, channels), jnp.float32)
    conv_rows = offsets * channels
    for o in range(octants):
        hit = octant == o
        weight = down_weight[o]
        only = jnp.where(hit, hidden, jnp.zeros_like(hidden))
        own_term += matmul(only, weight)
        product = matmul(only, parent_grad, 0, 0).astype(jnp.bfloat16)
        sums[pl.ds(conv_rows + o * channels, channels), :] = product[:, :channels]
        sums[pl.ds(conv_rows + (octants + o) * channels, channels), :] = product[:, channels:]
        hidden_grad += jnp.where(hit, matmul(parent_grad, weight, 1, 1), 0.0)
    pre_grad = (hidden_grad * gate * (1.0 + act * (1.0 - gate))).astype(jnp.bfloat16)

    from_row = (link_row[...] // octants) == lax.broadcasted_iota(jnp.int32, (coarse_tile, rows), 0)
    from_row = from_row.astype(jnp.bfloat16)
    high = own_term.astype(jnp.bfloat16)
    low = (own_term - high.astype(jnp.float32)).astype(jnp.bfloat16)
    coarse[...] = (matmul(from_row, high) + matmul(from_row, low)).astype(jnp.bfloat16)

    def backward(offset, carry):
        start = pl.multiple_of(offset * channels, channels)
        product = matmul(gathered[offset], pre_grad, 0, 0)
        sums[pl.ds(start, channels), :] = product.astype(jnp.bfloat16)
        return carry

    lax.fori_loop(0, offsets, backward, 0)
    used = conv_rows + 2 * octants * channels
    sums[pl.ds(used, sums.shape[0] - used), :] = jnp.zeros((sums.shape[0] - used, channels), jnp.bfloat16)


def shards(features, kernel_map, send_lists, fine_to_coarse, conv_weight, down_weight, coarse_grad):
    rows, channels = features.shape
    tiles, slots = send_lists.shape[2:]
    offsets = kernel_map.shape[0]
    octants, _, out_channels = down_weight.shape
    tile_rows = RING_X * rows
    coarse_rows = coarse_grad.shape[0]
    coarse_tile = RING_X * coarse_rows
    x = lax.axis_index("x")
    smem, vmem = pl.BlockSpec(memory_space=pltpu.SMEM), pl.BlockSpec(memory_space=pltpu.VMEM)
    parts = share_over_x(features)
    outgoing = pl.pallas_call(
        pick_halo,
        out_shape=jax.ShapeDtypeStruct((tiles * slots, channels), jnp.bfloat16),
        in_specs=[smem] + [vmem] * 4,
        out_specs=vmem,
        scratch_shapes=[
            pltpu.VMEM((tile_rows + 8, channels), jnp.float32),
            pltpu.VMEM((tiles * slots, channels), jnp.float32),
        ],
        compiler_params=pltpu.CompilerParams(vmem_limit_bytes=16 << 20),
        name="pick_halo",
    )(send_lists.reshape(tiles, slots), *parts)
    later_grad, outgoing = lax.optimization_barrier((coarse_grad, outgoing))
    incoming = lax.all_to_all(
        outgoing.reshape(tiles, slots, channels), TILE, split_axis=0, concat_axis=0, tiled=True
    )
    grads = share_over_x(later_grad)
    link = lax.dynamic_slice_in_dim(fine_to_coarse, x * rows, rows)
    used = offsets * channels + 2 * octants * channels
    total = used + (-used % 512)
    coarse, sums = pl.pallas_call(
        step_kernel,
        out_shape=(
            jax.ShapeDtypeStruct((coarse_tile, out_channels), jnp.bfloat16),
            jax.ShapeDtypeStruct((total, channels), jnp.bfloat16),
        ),
        in_specs=[smem] + [vmem] * 13,
        out_specs=(vmem, vmem),
        scratch_shapes=[
            pltpu.VMEM((tile_rows + tiles * slots + 8, channels), jnp.float32),
            pltpu.VMEM((rows, channels), jnp.float32),
            pltpu.VMEM((offsets, rows, channels), jnp.bfloat16),
            pltpu.VMEM((rows, channels), jnp.float32),
            pltpu.VMEM((coarse_tile, out_channels), jnp.bfloat16),
        ],
        compiler_params=pltpu.CompilerParams(vmem_limit_bytes=40 << 20),
        name="step",
    )(
        kernel_map, *parts, incoming.reshape(tiles * slots, channels), conv_weight, down_weight,
        *grads, link.reshape(rows, 1), link.reshape(1, rows),
    )
    sums, coarse = sum_over_devices(sums, coarse)
    coarse = coarse.reshape(RING_X, coarse_rows, out_channels)
    shares = [wide(pick(coarse, x))]
    shares += [wide(send(pick(coarse, x ^ step), ring_x(step))) for step in (1, 2, 3)]
    coarse_out = narrow((shares[0] + shares[1]) + (shares[2] + shares[3]))
    conv_grad = sums[: offsets * channels].reshape(offsets, channels, channels)
    down_sums = sums[offsets * channels : used]
    half = octants * channels
    down_grad = jnp.concatenate([down_sums[:half], down_sums[half:]], axis=1)
    down_grad = down_grad.reshape(octants, channels, out_channels)
    return (coarse_out, conv_grad, down_grad)


def solution(mesh):
    fine_mesh = Mesh(mesh.devices.reshape(RING_Y, DEPTH_Z, CORES, RING_X), AXES)
    placed = (
        P(AXES, None),
        P(None, AXES),
        P(TILE, "x", None, None),
        P(TILE),
        P(),
        P(),
        P(AXES, None),
    )
    return jax.shard_map(
        shards,
        mesh=fine_mesh,
        in_specs=placed,
        out_specs=(P(AXES, None), P(), P()),
        check_vma=False,
    )
```

time: 225 us -> 196 us (0.87); the launches traced: 221 us -> 196 us
  Pallas kernels: 0 us -> 71.3 us
  local copies, waits for them, and re-layouts: 56.7 us -> 13.4 us
  blocking collectives: 24.8 us -> 0 us
  other arithmetic: 24.8 us -> 2.9 us
  between operations: 14.8 us -> 0.84 us
  starting transfers between devices: 48.8 us -> 58.8 us
  matrix products: 8.51 us -> 0 us
  waiting for transfers between devices: 42.6 us -> 48.5 us
    pallas_call x0 -> x2, Pallas kernels: none -> 71.3 us  [the longest x1 54.1 us: shards(): pl.pallas_call(step_kernel, out_shape=(jax.ShapeDtypeStruct((coarse_tile,...]
    gather x8 -> x0, local copies, waits for them, and re-layouts: 42.4 us -> none  [the longest x6 32.4 us: gathered(): return lookup[picks].reshape(rows_dev, group_size * channels)]
    all_gather x2 -> x0, blocking collectives: 24.8 us -> none  [the longest x1 12.5 us: shards(): tile_feats = lax.all_gather(features, 'x', axis=0, tiled=True)]
    concatenate x3 -> x0, other arithmetic: 15 us -> none  [the longest x1 9 us: shards(): jnp.concatenate([conv_flat, down_flat, filler], axis=0)]
    reduce_scatter x1 -> x0, waiting for transfers between devices: 11.9 us -> none  [shards(): lax.psum_scatter(partial_value.astype(jnp.bfloat16), 'x', scatter_dimensi...]
    ppermute x19 -> x28, waiting for transfers between devices: 30.7 us -> 40.9 us  [send(): return lax.ppermute(value, AXES, partner_pairs(partner))]
    ppermute x19 -> x28, starting transfers between devices: 34.6 us -> 43.8 us  [send(): return lax.ppermute(value, AXES, partner_pairs(partner))]
    unnamed x23 -> x35, local copies, waits for them, and re-layouts: 2.2 us -> 10.9 us
  transfers between devices with their start and end apart: 21 -> 29, of which waited for: 16 -> 23; matrix products, arithmetic and copies ran while one was open for 7% -> 1% of each run, Pallas kernels for 0% -> 0%
where the time goes in v2:
time: 196 us
  Pallas kernels  71.3 us (36%)
  starting transfers between devices  58.8 us (30%)
  waiting for transfers between devices  48.5 us (25%)
  local copies, waits for them, and re-layouts  13.4 us (7%)
  other arithmetic  2.9 us (1%)
    pallas_call x1, Pallas kernels, shards(): pl.pallas_call(step_kernel, out_shape=(jax.ShapeDtypeStruct((coarse_tile,...  54.1 us
    ppermute x28, starting transfers between devices, send(): return lax.ppermute(value, AXES, partner_pairs(partner))  43.8 us
    ppermute x28, waiting for transfers between devices, send(): return lax.ppermute(value, AXES, partner_pairs(partner))  40.9 us
    pallas_call x1, Pallas kernels, shards(): pl.pallas_call(pick_halo, out_shape=jax.ShapeDtypeStruct((tiles * slots,...  17.3 us
    all_to_all x1, starting transfers between devices, shards(): lax.all_to_all(outgoing.reshape(tiles, slots, channels), TILE, split_axis...  15 us
    unnamed x35, local copies, waits for them, and re-layouts  10.9 us
    all_to_all x1, waiting for transfers between devices, shards(): lax.all_to_all(outgoing.reshape(tiles, slots, channels), TILE, split_axis...  7.59 us
  transfers between devices with their start and end apart: 29, of which 23 were waited for; matrix products, arithmetic and copies ran while one was open for 1% of the time, Pallas kernels for 0%

profile of v2, /device:TPU:1, one launch (start us, length us, event | category | flops | bytes accessed | tf_op | source)
XLA Modules:
  0.0 195.8 jit_solution(14896396788535657399)
XLA Ops:
  0.6 3.4 %collective-permute-start.2 = (bf16[512,128]{1,0:T(8,128)(2,1)}, bf16[512,128]{1,0:T(8,128)(2,1)S(1)}, u32[]{:S(2)}, u32[]{:S(2)}) collective-permute-start(bf16[512,128]{1,0:T(8,128)(2,1)} %part0.3), channel_id=1, source_target_pairs={{0,3},{1,2},{2,1},{3,0},{4,7},{5,6},{6,5},{7,4},{8,11},{9,10},{10,... | collective-permute-start | bytes 393224 | tf_op jit(solution)/shard_map/ppermute | solution.py:31
  5.5 3.0 %collective-permute-done.2.part3 = bf16[512,128]{1,0:T(8,128)(2,1)S(1)} collective-permute-done((bf16[512,128]{1,0:T(8,128)(2,1)}, bf16[512,128]{1,0:T(8,128)(2,1)S(1)}, u32[]{:S(2)}, u32[]{:S(2)}) %collective-permute-start.2) | collective-permute-done | bytes 131104 | tf_op jit(solution)/shard_map/ppermute | solution.py:31
  10.6 17.3 %pick_halo.1 = bf16[2048,128]{1,0:T(8,128)(2,1)} custom-call(s32[64,32]{1,0:T(8,128)S(1)} %bitcast.94, bf16[512,128]{1,0:T(8,128)(2,1)S(1)} %copy-done.1, bf16[512,128]{1,0:T(8,128)(2,1)S(1)} %collective-permute-done.part1, bf16[512,128]{1,0:T(8,128)(2,1)S(1)} %collective-permute-done.1.part2, bf16[512,128]{1,0:T(8,128)(2,1)S(1)} %collective-permute-done.2.part3), custom_call_target="tpu_custom_call" | custom-call | tf_op jit(solution)/shard_map/pick_halo/pallas_call | solution.py:230
  27.9 15.0 %all-to-all-start = ((bf16[64,32,128]{2,1,0:T(8,128)(2,1)}), bf16[64,32,128]{2,1,0:T(8,128)(2,1)S(1)}, u32[]{:S(2)}, u32[]{:S(2)}) async-start(bf16[64,32,128]{2,1,0:T(8,128)(2,1)} %bitcast.1), calls=%async_computation | async-start | bytes 1048576 | tf_op jit(solution)/shard_map/all_to_all | solution.py:243
  43.0 1.8 collective-permute-start.5
  47.2 1.7 collective-permute-done.5.grad3
  52.7 7.6 %all-to-all-done = bf16[64,32,128]{2,1,0:T(8,128)(2,1)S(1)} async-done(((bf16[64,32,128]{2,1,0:T(8,128)(2,1)}), bf16[64,32,128]{2,1,0:T(8,128)(2,1)S(1)}, u32[]{:S(2)}, u32[]{:S(2)}) %all-to-all-start) | async-done | bytes 524320 | tf_op jit(solution)/shard_map/all_to_all | solution.py:243
  66.7 54.1 %step.1 = (bf16[1024,256]{1,0:T(8,128)(2,1)S(1)}, bf16[5632,128]{1,0:T(8,128)(2,1)S(1)}) custom-call(s32[27,512]{1,0:T(8,128)S(1)} %copy-done.16, bf16[512,128]{1,0:T(8,128)(2,1)S(1)} %copy-done.2, bf16[512,128]{1,0:T(8,128)(2,1)S(1)} %copy-done.4, bf16[512,128]{1,0:T(8,128)(2,1)S(1)} %collective-permute-done.1.part2, ...), custom_call_target="tpu_custom_call" | custom-call | tf_op jit(solution)/shard_map/step/pallas_call | solution.py:250
  122.0 1.9 collective-permute-done.6
  124.2 1.3 collective-permute-start.7
  125.5 1.9 collective-permute-start.9
  128.9 2.9 %collective-permute-done.9 = bf16[704,128]{1,0:T(8,128)(2,1)S(1)} collective-permute-done((bf16[704,128]{1,0:T(8,128)(2,1)S(1)}, bf16[704,128]{1,0:T(8,128)(2,1)S(1)}, u32[]{:S(2)}, u32[]{:S(2)}) %collective-permute-start.9) | collective-permute-done | bytes 180256 | tf_op jit(solution)/shard_map/ppermute | solution.py:31
  131.8 1.8 collective-permute-done.8
  133.9 1.8 collective-permute-start.15
  135.7 1.3 collective-permute-start.14
  138.0 2.1 %collective-permute-done.14 = bf16[176,128]{1,0:T(8,128)(2,1)S(1)} collective-permute-done((bf16[176,128]{1,0:T(8,128)(2,1)S(1)}, bf16[176,128]{1,0:T(8,128)(2,1)S(1)}, u32[]{:S(2)}, u32[]{:S(2)}) %collective-permute-start.14) | collective-permute-done | bytes 45088 | tf_op jit(solution)/shard_map/ppermute | solution.py:31
  140.6 2.6 %collective-permute-done.16 = bf16[88,128]{1,0:T(8,128)(2,1)S(1)} collective-permute-done((bf16[88,128]{1,0:T(8,128)(2,1)S(1)}, bf16[88,128]{1,0:T(8,128)(2,1)S(1)}, u32[]{:S(2)}, u32[]{:S(2)}) %collective-permute-start.16) | collective-permute-done | bytes 22560 | tf_op jit(solution)/shard_map/ppermute | solution.py:31
  144.3 3.5 %collective-permute-start.18 = (bf16[88,128]{1,0:T(8,128)(2,1)S(1)}, bf16[88,128]{1,0:T(8,128)(2,1)S(1)}, u32[]{:S(2)}, u32[]{:S(2)}) collective-permute-start(bf16[88,128]{1,0:T(8,128)(2,1)S(1)} %fusion.9), channel_id=1, source_target_pairs={{0,32},{1,33},{2,34},{3,35},{4,36},{5,37},{6,38},{7,39},{8,40},{9,... | collective-permute-start | bytes 67592 | tf_op jit(solution)/shard_map/ppermute | solution.py:31
  147.8 1.2 collective-permute-start.17
  149.0 1.9 collective-permute-done.18
  152.1 2.0 %collective-permute-done.20 = bf16[88,128]{1,0:T(8,128)(2,1)S(1)} collective-permute-done((bf16[88,128]{1,0:T(8,128)(2,1)S(1)}, bf16[88,128]{1,0:T(8,128)(2,1)S(1)}, u32[]{:S(2)}, u32[]{:S(2)}) %collective-permute-start.20) | collective-permute-done | bytes 22560 | tf_op jit(solution)/shard_map/ppermute | solution.py:31
  155.1 1.2 collective-permute-start.22
  156.3 1.8 collective-permute-start.21
  158.1 1.4 collective-permute-done.22
  160.6 3.5 %collective-permute-start.25 = (bf16[704,128]{1,0:T(8,128)(2,1)S(1)}, bf16[704,128]{1,0:T(8,128)(2,1)S(1)}, u32[]{:S(2)}, u32[]{:S(2)}) collective-permute-start(bf16[704,128]{1,0:T(8,128)(2,1)S(1)} %bitcast.103), channel_id=1, source_target_pairs={{0,2},{1,3},{2,0},{3,1},{4,132},{5,133},{6,134},{7,135},{8,10},{9,... | collective-permute-start | bytes 540680 | tf_op jit(solution)/shard_map/ppermute | solution.py:31
  165.2 4.8 %collective-permute-done.25 = bf16[704,128]{1,0:T(8,128)(2,1)S(1)} collective-permute-done((bf16[704,128]{1,0:T(8,128)(2,1)S(1)}, bf16[704,128]{1,0:T(8,128)(2,1)S(1)}, u32[]{:S(2)}, u32[]{:S(2)}) %collective-permute-start.25) | collective-permute-done | bytes 180256 | tf_op jit(solution)/shard_map/ppermute | solution.py:31
  169.9 2.1 %collective-permute-done.24 = bf16[704,128]{1,0:T(8,128)(2,1)S(1)} collective-permute-done((bf16[704,128]{1,0:T(8,128)(2,1)S(1)}, bf16[704,128]{1,0:T(8,128)(2,1)S(1)}, u32[]{:S(2)}, u32[]{:S(2)}) %collective-permute-start.24) | collective-permute-done | bytes 180256 | tf_op jit(solution)/shard_map/ppermute | solution.py:31
  172.2 10.5 %collective-permute-start.27 = (bf16[2816,128]{1,0:T(8,128)(2,1)S(1)}, bf16[2816,128]{1,0:T(8,128)(2,1)S(1)}, u32[]{:S(2)}, u32[]{:S(2)}) collective-permute-start(bf16[2816,128]{1,0:T(8,128)(2,1)S(1)} %bitcast.99), channel_id=1, source_target_pairs={{0,4},{1,5},{2,6},{3,7},{4,0},{5,1},{6,2},{7,3},{8,12},{9,13},{10,... | collective-permute-start | bytes 2162696 | tf_op jit(solution)/shard_map/ppermute | solution.py:31
  184.0 2.1 %collective-permute-start.11 = (bf16[256,256]{1,0:T(8,128)(2,1)S(1)}, bf16[256,256]{1,0:T(8,128)(2,1)S(1)}, u32[]{:S(2)}, u32[]{:S(2)}) collective-permute-start(bf16[256,256]{1,0:T(8,128)(2,1)S(1)} %get-tuple-element.28), channel_id=1, source_target_pairs={{0,2},{1,3},{2,0},{3,1},{4,6},{5,7},{6,4},{7,5},{8,10},{9,11},{10,... | collective-permute-start | bytes 393224 | tf_op jit(solution)/shard_map/ppermute | solution.py:31
  186.1 1.8 collective-permute-done.10
  187.9 4.1 %collective-permute-done.12 = bf16[256,256]{1,0:T(8,128)(2,1)S(1)} collective-permute-done((bf16[256,256]{1,0:T(8,128)(2,1)S(1)}, bf16[256,256]{1,0:T(8,128)(2,1)S(1)}, u32[]{:S(2)}, u32[]{:S(2)}) %collective-permute-start.12) | collective-permute-done | bytes 131104 | tf_op jit(solution)/shard_map/ppermute | solution.py:31
  193.4 1.3 slice.15
  (88 shorter events, 30.4 us)
Async XLA Ops:
  0.6 59.7 %copy-start = (bf16[27,128,128]{2,1,0:T(8,128)(2,1)S(1)}, bf16[27,128,128]{2,1,0:T(8,128)(2,1)}, u32[]{:S(2)}) copy-start(bf16[27,128,128]{2,1,0:T(8,128)(2,1)} %conv_weight.1) | copy-start | bytes 2654212
  0.6 7.9 %collective-permute-start.2 = (bf16[512,128]{1,0:T(8,128)(2,1)}, bf16[512,128]{1,0:T(8,128)(2,1)S(1)}, u32[]{:S(2)}, u32[]{:S(2)}) collective-permute-start(bf16[512,128]{1,0:T(8,128)(2,1)} %part0.3), channel_id=1, source_target_pairs={{0,3},{1,2},{2,1},{3,0},{4,7},{5,6},{6,5},{7,4},{8,11},{9,10},{10,... | collective-permute-start | bytes 393224 | tf_op jit(solution)/shard_map/ppermute | solution.py:31
  4.0 5.6 %collective-permute-start.1 = (bf16[512,128]{1,0:T(8,128)(2,1)}, bf16[512,128]{1,0:T(8,128)(2,1)S(1)}, u32[]{:S(2)}, u32[]{:S(2)}) collective-permute-start(bf16[512,128]{1,0:T(8,128)(2,1)} %part0.3), channel_id=1, source_target_pairs={{0,2},{1,3},{2,0},{3,1},{4,6},{5,7},{6,4},{7,5},{8,10},{9,11},{10,... | collective-permute-start | bytes 393224 | tf_op jit(solution)/shard_map/ppermute | solution.py:31
  4.6 5.1 %collective-permute-start = (bf16[512,128]{1,0:T(8,128)(2,1)}, bf16[512,128]{1,0:T(8,128)(2,1)S(1)}, u32[]{:S(2)}, u32[]{:S(2)}) collective-permute-start(bf16[512,128]{1,0:T(8,128)(2,1)} %part0.3), channel_id=1, source_target_pairs={{0,1},{1,0},{2,3},{3,2},{4,5},{5,4},{6,7},{7,6},{8,9},{9,8},{10,11... | collective-permute-start | bytes 393224 | tf_op jit(solution)/shard_map/ppermute | solution.py:31
  10.6 32.3 %copy-start.8 = (bf16[256,256]{1,0:T(8,128)(2,1)S(1)}, bf16[256,256]{1,0:T(8,128)(2,1)}, u32[]{:S(2)}) copy-start(bf16[256,256]{1,0:T(8,128)(2,1)} %grad0) | copy-start | bytes 393220
  10.6 49.7 %copy-start.2 = (bf16[512,128]{1,0:T(8,128)(2,1)S(1)}, bf16[512,128]{1,0:T(8,128)(2,1)}, u32[]{:S(2)}) copy-start(bf16[512,128]{1,0:T(8,128)(2,1)} %part0.3) | copy-start | bytes 393220
  27.9 32.4 %all-to-all-start = ((bf16[64,32,128]{2,1,0:T(8,128)(2,1)}), bf16[64,32,128]{2,1,0:T(8,128)(2,1)S(1)}, u32[]{:S(2)}, u32[]{:S(2)}) async-start(bf16[64,32,128]{2,1,0:T(8,128)(2,1)} %bitcast.1), calls=%async_computation | async-start | bytes 1048576 | tf_op jit(solution)/shard_map/all_to_all | solution.py:243
  43.0 5.9 %collective-permute-start.5 = (bf16[256,256]{1,0:T(8,128)(2,1)S(1)}, bf16[256,256]{1,0:T(8,128)(2,1)S(1)}, u32[]{:S(2)}, u32[]{:S(2)}) collective-permute-start(bf16[256,256]{1,0:T(8,128)(2,1)S(1)} %copy-done.8), channel_id=1, source_target_pairs={{0,3},{1,2},{2,1},{3,0},{4,7},{5,6},{6,5},{7,4},{8,11},{9,10},{10,... | collective-permute-start | bytes 393224 | tf_op jit(solution)/shard_map/ppermute | solution.py:31
  44.8 5.9 %collective-permute-start.4 = (bf16[256,256]{1,0:T(8,128)(2,1)S(1)}, bf16[256,256]{1,0:T(8,128)(2,1)S(1)}, u32[]{:S(2)}, u32[]{:S(2)}) collective-permute-start(bf16[256,256]{1,0:T(8,128)(2,1)S(1)} %copy-done.8), channel_id=1, source_target_pairs={{0,2},{1,3},{2,0},{3,1},{4,6},{5,7},{6,4},{7,5},{8,10},{9,11},{10,... | collective-permute-start | bytes 393224 | tf_op jit(solution)/shard_map/ppermute | solution.py:31
  45.3 6.7 %collective-permute-start.3 = (bf16[256,256]{1,0:T(8,128)(2,1)S(1)}, bf16[256,256]{1,0:T(8,128)(2,1)S(1)}, u32[]{:S(2)}, u32[]{:S(2)}) collective-permute-start(bf16[256,256]{1,0:T(8,128)(2,1)S(1)} %copy-done.8), channel_id=1, source_target_pairs={{0,1},{1,0},{2,3},{3,2},{4,5},{5,4},{6,7},{7,6},{8,9},{9,8},{10,11... | collective-permute-start | bytes 393224 | tf_op jit(solution)/shard_map/ppermute | solution.py:31
  121.6 2.3 %collective-permute-start.6 = (bf16[2816,128]{1,0:T(8,128)(2,1)S(1)}, bf16[2816,128]{1,0:T(8,128)(2,1)S(1)}, u32[]{:S(2)}, u32[]{:S(2)}) collective-permute-start(bf16[2816,128]{1,0:T(8,128)(2,1)S(1)} %dynamic-slice_bitcast_fusion), channel_id=1, source_target_pairs={{0,4},{1,5},{2,6},{3,7},{4,0},{5,1},{6,2},{7,3},{8,12},{9,13},{10,... | collective-permute-start | bytes 2162696 | tf_op jit(solution)/shard_map/ppermute | solution.py:31
  124.2 4.7 %collective-permute-start.7 = (bf16[704,128]{1,0:T(8,128)(2,1)S(1)}, bf16[704,128]{1,0:T(8,128)(2,1)S(1)}, u32[]{:S(2)}, u32[]{:S(2)}) collective-permute-start(bf16[704,128]{1,0:T(8,128)(2,1)S(1)} %get-tuple-element.23), channel_id=1, source_target_pairs={{0,1},{1,0},{2,3},{3,2},{4,68},{5,69},{6,70},{7,71},{8,9},{9,8},{1... | collective-permute-start | bytes 540680 | tf_op jit(solution)/shard_map/ppermute | solution.py:31
  125.5 6.3 %collective-permute-start.9 = (bf16[704,128]{1,0:T(8,128)(2,1)S(1)}, bf16[704,128]{1,0:T(8,128)(2,1)S(1)}, u32[]{:S(2)}, u32[]{:S(2)}) collective-permute-start(bf16[704,128]{1,0:T(8,128)(2,1)S(1)} %get-tuple-element.24), channel_id=1, source_target_pairs={{0,3},{1,2},{2,1},{3,0},{4,196},{5,197},{6,198},{7,199},{8,11},{9,... | collective-permute-start | bytes 540680 | tf_op jit(solution)/shard_map/ppermute | solution.py:31
  127.4 6.1 %collective-permute-start.8 = (bf16[704,128]{1,0:T(8,128)(2,1)S(1)}, bf16[704,128]{1,0:T(8,128)(2,1)S(1)}, u32[]{:S(2)}, u32[]{:S(2)}) collective-permute-start(bf16[704,128]{1,0:T(8,128)(2,1)S(1)} %get-tuple-element.25), channel_id=1, source_target_pairs={{0,2},{1,3},{2,0},{3,1},{4,132},{5,133},{6,134},{7,135},{8,10},{9,... | collective-permute-start | bytes 540680 | tf_op jit(solution)/shard_map/ppermute | solution.py:31
  133.7 3.3 %collective-permute-start.13 = (bf16[176,128]{1,0:T(8,128)(2,1)S(1)}, bf16[176,128]{1,0:T(8,128)(2,1)S(1)}, u32[]{:S(2)}, u32[]{:S(2)}) collective-permute-start(bf16[176,128]{1,0:T(8,128)(2,1)S(1)} %get-tuple-element.33), channel_id=1, source_target_pairs={{0,64},{1,65},{2,66},{3,67},{4,5},{5,4},{6,7},{7,6},{8,72},{9,73},... | collective-permute-start | bytes 135176 | tf_op jit(solution)/shard_map/ppermute | solution.py:31
  133.9 4.1 %collective-permute-start.15 = (bf16[176,128]{1,0:T(8,128)(2,1)S(1)}, bf16[176,128]{1,0:T(8,128)(2,1)S(1)}, u32[]{:S(2)}, u32[]{:S(2)}) collective-permute-start(bf16[176,128]{1,0:T(8,128)(2,1)S(1)} %get-tuple-element.34), channel_id=1, source_target_pairs={{0,192},{1,193},{2,194},{3,195},{4,7},{5,6},{6,5},{7,4},{8,200},{9... | collective-permute-start | bytes 135176 | tf_op jit(solution)/shard_map/ppermute | solution.py:31
  135.7 4.4 %collective-permute-start.14 = (bf16[176,128]{1,0:T(8,128)(2,1)S(1)}, bf16[176,128]{1,0:T(8,128)(2,1)S(1)}, u32[]{:S(2)}, u32[]{:S(2)}) collective-permute-start(bf16[176,128]{1,0:T(8,128)(2,1)S(1)} %get-tuple-element.35), channel_id=1, source_target_pairs={{0,128},{1,129},{2,130},{3,131},{4,6},{5,7},{6,4},{7,5},{8,136},{9... | collective-permute-start | bytes 135176 | tf_op jit(solution)/shard_map/ppermute | solution.py:31
  140.2 3.0 %collective-permute-start.16 = (bf16[88,128]{1,0:T(8,128)(2,1)S(1)}, bf16[88,128]{1,0:T(8,128)(2,1)S(1)}, u32[]{:S(2)}, u32[]{:S(2)}) collective-permute-start(bf16[88,128]{1,0:T(8,128)(2,1)S(1)} %dynamic-slice_bitcast_fusion.10), channel_id=1, source_target_pairs={{0,8},{1,9},{2,10},{3,11},{4,12},{5,13},{6,14},{7,15},{8,0},{9,1},... | collective-permute-start | bytes 67592 | tf_op jit(solution)/shard_map/ppermute | solution.py:31
  143.2 5.7 %collective-permute-start.19 = (bf16[88,128]{1,0:T(8,128)(2,1)S(1)}, bf16[88,128]{1,0:T(8,128)(2,1)S(1)}, u32[]{:S(2)}, u32[]{:S(2)}) collective-permute-start(bf16[88,128]{1,0:T(8,128)(2,1)S(1)} %fusion.9), channel_id=1, source_target_pairs={{0,48},{1,49},{2,50},{3,51},{4,52},{5,53},{6,54},{7,55},{8,56},{9,... | collective-permute-start | bytes 67592 | tf_op jit(solution)/shard_map/ppermute | solution.py:31
  144.3 6.6 %collective-permute-start.18 = (bf16[88,128]{1,0:T(8,128)(2,1)S(1)}, bf16[88,128]{1,0:T(8,128)(2,1)S(1)}, u32[]{:S(2)}, u32[]{:S(2)}) collective-permute-start(bf16[88,128]{1,0:T(8,128)(2,1)S(1)} %fusion.9), channel_id=1, source_target_pairs={{0,32},{1,33},{2,34},{3,35},{4,36},{5,37},{6,38},{7,39},{8,40},{9,... | collective-permute-start | bytes 67592 | tf_op jit(solution)/shard_map/ppermute | solution.py:31
  147.8 3.6 %collective-permute-start.17 = (bf16[88,128]{1,0:T(8,128)(2,1)S(1)}, bf16[88,128]{1,0:T(8,128)(2,1)S(1)}, u32[]{:S(2)}, u32[]{:S(2)}) collective-permute-start(bf16[88,128]{1,0:T(8,128)(2,1)S(1)} %fusion.9), channel_id=1, source_target_pairs={{0,16},{1,17},{2,18},{3,19},{4,20},{5,21},{6,22},{7,23},{8,24},{9,... | collective-permute-start | bytes 67592 | tf_op jit(solution)/shard_map/ppermute | solution.py:31
  151.4 2.7 %collective-permute-start.20 = (bf16[88,128]{1,0:T(8,128)(2,1)S(1)}, bf16[88,128]{1,0:T(8,128)(2,1)S(1)}, u32[]{:S(2)}, u32[]{:S(2)}) collective-permute-start(bf16[88,128]{1,0:T(8,128)(2,1)S(1)} %add_convert_fusion), channel_id=1, source_target_pairs={{0,8},{1,9},{2,10},{3,11},{4,12},{5,13},{6,14},{7,15},{8,0},{9,1},... | collective-permute-start | bytes 67592 | tf_op jit(solution)/shard_map/ppermute | solution.py:31
  154.1 3.9 %collective-permute-start.23 = (bf16[176,128]{1,0:T(8,128)(2,1)S(1)}, bf16[176,128]{1,0:T(8,128)(2,1)S(1)}, u32[]{:S(2)}, u32[]{:S(2)}) collective-permute-start(bf16[176,128]{1,0:T(8,128)(2,1)S(1)} %bitcast.109), channel_id=1, source_target_pairs={{0,64},{1,65},{2,66},{3,67},{4,5},{5,4},{6,7},{7,6},{8,72},{9,73},... | collective-permute-start | bytes 135176 | tf_op jit(solution)/shard_map/ppermute | solution.py:31
  155.1 4.4 %collective-permute-start.22 = (bf16[176,128]{1,0:T(8,128)(2,1)S(1)}, bf16[176,128]{1,0:T(8,128)(2,1)S(1)}, u32[]{:S(2)}, u32[]{:S(2)}) collective-permute-start(bf16[176,128]{1,0:T(8,128)(2,1)S(1)} %bitcast.110), channel_id=1, source_target_pairs={{0,128},{1,129},{2,130},{3,131},{4,6},{5,7},{6,4},{7,5},{8,136},{9... | collective-permute-start | bytes 135176 | tf_op jit(solution)/shard_map/ppermute | solution.py:31
  156.3 4.1 %collective-permute-start.21 = (bf16[176,128]{1,0:T(8,128)(2,1)S(1)}, bf16[176,128]{1,0:T(8,128)(2,1)S(1)}, u32[]{:S(2)}, u32[]{:S(2)}) collective-permute-start(bf16[176,128]{1,0:T(8,128)(2,1)S(1)} %bitcast.111), channel_id=1, source_target_pairs={{0,192},{1,193},{2,194},{3,195},{4,7},{5,6},{6,5},{7,4},{8,200},{9... | collective-permute-start | bytes 135176 | tf_op jit(solution)/shard_map/ppermute | solution.py:31
  160.4 4.7 %collective-permute-start.26 = (bf16[704,128]{1,0:T(8,128)(2,1)S(1)}, bf16[704,128]{1,0:T(8,128)(2,1)S(1)}, u32[]{:S(2)}, u32[]{:S(2)}) collective-permute-start(bf16[704,128]{1,0:T(8,128)(2,1)S(1)} %bitcast.102), channel_id=1, source_target_pairs={{0,1},{1,0},{2,3},{3,2},{4,68},{5,69},{6,70},{7,71},{8,9},{9,8},{1... | collective-permute-start | bytes 540680 | tf_op jit(solution)/shard_map/ppermute | solution.py:31
  160.6 9.4 %collective-permute-start.25 = (bf16[704,128]{1,0:T(8,128)(2,1)S(1)}, bf16[704,128]{1,0:T(8,128)(2,1)S(1)}, u32[]{:S(2)}, u32[]{:S(2)}) collective-permute-start(bf16[704,128]{1,0:T(8,128)(2,1)S(1)} %bitcast.103), channel_id=1, source_target_pairs={{0,2},{1,3},{2,0},{3,1},{4,132},{5,133},{6,134},{7,135},{8,10},{9,... | collective-permute-start | bytes 540680 | tf_op jit(solution)/shard_map/ppermute | solution.py:31
  164.1 8.0 %collective-permute-start.24 = (bf16[704,128]{1,0:T(8,128)(2,1)S(1)}, bf16[704,128]{1,0:T(8,128)(2,1)S(1)}, u32[]{:S(2)}, u32[]{:S(2)}) collective-permute-start(bf16[704,128]{1,0:T(8,128)(2,1)S(1)} %bitcast.104), channel_id=1, source_target_pairs={{0,3},{1,2},{2,1},{3,0},{4,196},{5,197},{6,198},{7,199},{8,11},{9,... | collective-permute-start | bytes 540680 | tf_op jit(solution)/shard_map/ppermute | solution.py:31
  172.2 20.6 %collective-permute-start.27 = (bf16[2816,128]{1,0:T(8,128)(2,1)S(1)}, bf16[2816,128]{1,0:T(8,128)(2,1)S(1)}, u32[]{:S(2)}, u32[]{:S(2)}) collective-permute-start(bf16[2816,128]{1,0:T(8,128)(2,1)S(1)} %bitcast.99), channel_id=1, source_target_pairs={{0,4},{1,5},{2,6},{3,7},{4,0},{5,1},{6,2},{7,3},{8,12},{9,13},{10,... | collective-permute-start | bytes 2162696 | tf_op jit(solution)/shard_map/ppermute | solution.py:31
  182.8 5.2 %collective-permute-start.10 = (bf16[256,256]{1,0:T(8,128)(2,1)S(1)}, bf16[256,256]{1,0:T(8,128)(2,1)S(1)}, u32[]{:S(2)}, u32[]{:S(2)}) collective-permute-start(bf16[256,256]{1,0:T(8,128)(2,1)S(1)} %get-tuple-element.26), channel_id=1, source_target_pairs={{0,1},{1,0},{2,3},{3,2},{4,5},{5,4},{6,7},{7,6},{8,9},{9,8},{10,11... | collective-permute-start | bytes 393224 | tf_op jit(solution)/shard_map/ppermute | solution.py:31
  182.9 9.2 %collective-permute-start.12 = (bf16[256,256]{1,0:T(8,128)(2,1)S(1)}, bf16[256,256]{1,0:T(8,128)(2,1)S(1)}, u32[]{:S(2)}, u32[]{:S(2)}) collective-permute-start(bf16[256,256]{1,0:T(8,128)(2,1)S(1)} %get-tuple-element.27), channel_id=1, source_target_pairs={{0,3},{1,2},{2,1},{3,0},{4,7},{5,6},{6,5},{7,4},{8,11},{9,10},{10,... | collective-permute-start | bytes 393224 | tf_op jit(solution)/shard_map/ppermute | solution.py:31
  184.0 8.1 %collective-permute-start.11 = (bf16[256,256]{1,0:T(8,128)(2,1)S(1)}, bf16[256,256]{1,0:T(8,128)(2,1)S(1)}, u32[]{:S(2)}, u32[]{:S(2)}) collective-permute-start(bf16[256,256]{1,0:T(8,128)(2,1)S(1)} %get-tuple-element.28), channel_id=1, source_target_pairs={{0,2},{1,3},{2,0},{3,1},{4,6},{5,7},{6,4},{7,5},{8,10},{9,11},{10,... | collective-permute-start | bytes 393224 | tf_op jit(solution)/shard_map/ppermute | solution.py:31
  (14 other events, 46.7 us)

commit v3 on v2

v3 whole, which is shorter than its diff:
```python
import jax
import jax.numpy as jnp
from jax import lax
from jax.experimental import pallas as pl
from jax.experimental.pallas import tpu as pltpu
from jax.sharding import Mesh, PartitionSpec as P

RING_Y, DEPTH_Z, CORES, RING_X = 4, 8, 2, 4
AXES = ("y", "z", "core", "x")
TILE = ("y", "z", "core")
UNROLL = 32


def device_index(place):
    tile = (place[0] * DEPTH_Z + place[1]) * CORES + place[2]
    return tile * RING_X + place[3]


def partner_pairs(partner):
    pairs = []
    for y in range(RING_Y):
        for z in range(DEPTH_Z):
            for core in range(CORES):
                for x in range(RING_X):
                    place = (y, z, core, x)
                    pairs.append((device_index(place), device_index(partner(*place))))
    return pairs


def send(value, partner):
    return lax.ppermute(value, AXES, partner_pairs(partner))


def across_core(y, z, core, x):
    return (y, z, 1 - core, x)


def first_ring(step):
    return lambda y, z, core, x: (y, z, core, x ^ step) if core == 0 else (y ^ step, z, core, x)


def second_ring(step):
    return lambda y, z, core, x: (y ^ step, z, core, x) if core == 0 else (y, z, core, x ^ step)


def along_z(step):
    return lambda y, z, core, x: (y, z ^ step, core, x)


def narrow(value):
    return value.astype(jnp.bfloat16)


def wide(value):
    return value.astype(jnp.float32)


def pick(parts, digit):
    return lax.dynamic_index_in_dim(parts, digit, 0, keepdims=False)


def scatter_pair(parts, digit, partner):
    other = send(pick(parts, 1 - digit), partner)
    return narrow(wide(pick(parts, digit)) + wide(other))


def scatter_ring(parts, digit, ring):
    received = [send(pick(parts, digit ^ step), ring(step)) for step in (1, 2, 3)]
    total = wide(pick(parts, digit))
    for part in received:
        total = total + wide(part)
    return narrow(total)


def swap(first, second, flip):
    return jnp.where(flip, second, first), jnp.where(flip, first, second)


def gather_pair(part, digit, partner):
    other = send(part, partner)
    return jnp.stack(swap(part, other, digit == 1))


def gather_ring(part, digit, ring):
    parts = [part] + [send(part, ring(step)) for step in (1, 2, 3)]
    low, high = digit % 2 == 1, digit // 2 == 1
    first, second = swap(parts[0], parts[1], low)
    third, fourth = swap(parts[2], parts[3], low)
    first, third = swap(first, third, high)
    second, fourth = swap(second, fourth, high)
    return jnp.stack([first, second, third, fourth])


def sum_over_devices(partial_sums, coarse):
    y, z, core, x = (lax.axis_index(name) for name in AXES)
    ring_one = jnp.where(core == 0, x, y)
    ring_two = jnp.where(core == 0, y, x)
    rows = partial_sums.shape[0] // (CORES * RING_X * RING_Y * 2)
    lanes = partial_sums.shape[1]
    parts = partial_sums.reshape(CORES, RING_X * RING_Y * 2 * rows, lanes)
    part = scatter_pair(parts, core, across_core)
    part = scatter_ring(part.reshape(RING_X, RING_Y * 2 * rows, lanes), ring_one, first_ring)
    part, coarse = lax.optimization_barrier((part, coarse))
    shares = coarse.reshape(RING_X, coarse.shape[0] // RING_X, coarse.shape[1])
    shares = lax.all_to_all(shares, "x", split_axis=0, concat_axis=0, tiled=True)
    coarse_out = narrow(jnp.sum(wide(shares), axis=0))
    part = scatter_ring(part.reshape(RING_Y, 2 * rows, lanes), ring_two, second_ring)
    part = scatter_pair(part.reshape(2, rows, lanes), z % 2, along_z(1))
    part, coarse_out = lax.optimization_barrier((part, coarse_out))
    others = [send(part, along_z(step)) for step in (2, 4, 6)]
    part = narrow((wide(part) + wide(others[0])) + (wide(others[1]) + wide(others[2])))
    part = gather_pair(part, z % 2, along_z(1)).reshape(2 * rows, lanes)
    part = gather_ring(part, ring_two, second_ring).reshape(RING_Y * 2 * rows, lanes)
    part = gather_ring(part, ring_one, first_ring).reshape(RING_X * RING_Y * 2 * rows, lanes)
    return wide(gather_pair(part, core, across_core)).reshape(partial_sums.shape), coarse_out


def ring_x(step):
    return lambda y, z, core, x: (y, z, core, x ^ step)


def share_over_x(value):
    return [value] + [send(value, ring_x(step)) for step in (1, 2, 3)]


def part_copies(parts, target, sems, first):
    x = lax.axis_index("x")
    rows = parts[0].shape[0]
    copies = []
    for step, part in enumerate(parts):
        place = target.at[pl.ds(pl.multiple_of((x ^ step) * rows, rows), rows)]
        copies.append(pltpu.make_async_copy(part, place, sems.at[first + step]))
    return copies


def copy_rows(table, target, picks, first, count):
    for start in range(0, count, UNROLL):
        places = range(start, min(start + UNROLL, count))
        rows = [table[pl.ds(picks[first + at], 1), :] for at in places]
        for at, row in zip(places, rows):
            target[at : at + 1, :] = row


def matmul(left, right, left_dim=1, right_dim=0):
    return lax.dot_general(
        left, right, (((left_dim,), (right_dim,)), ((), ())), preferred_element_type=jnp.float32
    )


def pick_halo(lists, part0, part1, part2, part3, out, tile_feats, table, stage, sems):
    tile_rows, channels = tile_feats.shape
    block = stage.shape[0]
    copies = part_copies((part0, part1, part2, part3), tile_feats, sems, 0)
    for copy in copies:
        copy.start()
    table[pl.ds(tile_rows, 8), :] = jnp.zeros((8, channels), jnp.float32)
    for copy in copies:
        copy.wait()
    table[pl.ds(0, tile_rows), :] = tile_feats[...].astype(jnp.float32)

    def body(block_id, carry):
        first = pl.multiple_of(block_id * block, block)
        copy_rows(table, stage, lists, first, block)
        out[pl.ds(first, block), :] = stage[...].astype(jnp.bfloat16)
        return carry

    lax.fori_loop(0, out.shape[0] // block, body, 0)


def step_kernel(
    kernel_map, part0, part1, part2, part3, incoming, conv_hbm, down_hbm,
    grad0, grad1, grad2, grad3, link_column, link_row,
    coarse, sums,
    tile_feats, halo_feats, table, stage, gathered, pre_act, conv_weight, down_weight, tile_grad, sems,
):
    rows, channels = part0.shape
    offsets = conv_weight.shape[0]
    octants, _, out_channels = down_weight.shape
    tile_rows, halo_rows = tile_feats.shape[0], halo_feats.shape[0]
    coarse_tile = tile_grad.shape[0]
    feats = part_copies((part0, part1, part2, part3), tile_feats, sems, 0)
    halo = pltpu.make_async_copy(incoming, halo_feats, sems.at[4])
    conv = pltpu.make_async_copy(conv_hbm, conv_weight, sems.at[5])
    down = pltpu.make_async_copy(down_hbm, down_weight, sems.at[6])
    grads = part_copies((grad0, grad1, grad2, grad3), tile_grad, sems, 7)
    for copy in feats + [halo, conv, down] + grads:
        copy.start()
    pre_act[...] = jnp.zeros_like(pre_act)
    table[pl.ds(tile_rows + halo_rows, 8), :] = jnp.zeros((8, channels), jnp.float32)
    for copy in feats:
        copy.wait()
    table[pl.ds(0, tile_rows), :] = tile_feats[...].astype(jnp.float32)
    middle = offsets // 2
    own = pl.multiple_of(lax.axis_index("x") * rows, rows)
    gathered[middle] = tile_feats[pl.ds(own, rows), :]
    halo.wait()
    table[pl.ds(tile_rows, halo_rows), :] = halo_feats[...].astype(jnp.float32)
    conv.wait()

    def forward(at, previous):
        offset = at + (at >= middle).astype(jnp.int32)
        pre_act[...] += matmul(gathered[previous], conv_weight[previous])
        copy_rows(table, stage, kernel_map, offset * rows, rows)
        gathered[offset] = stage[...].astype(jnp.bfloat16)
        return offset

    last = lax.fori_loop(0, offsets - 1, forward, jnp.int32(middle))
    pre_act[...] += matmul(gathered[last], conv_weight[last])

    act = pre_act[...]
    gate = 1.0 / (1.0 + jnp.exp(-act))
    hidden_wide = act * gate
    hidden = hidden_wide.astype(jnp.bfloat16)
    hidden_turned = hidden_wide.T.astype(jnp.bfloat16)
    link = link_column[...]
    octant = link % octants
    link_turned = link_row[...]
    octant_turned = link_turned % octants
    at_parent = (link // octants) == lax.broadcasted_iota(jnp.int32, (rows, coarse_tile), 1)
    for copy in [down] + grads:
        copy.wait()
    parent_grad = matmul(at_parent.astype(jnp.bfloat16), tile_grad[...]).astype(jnp.bfloat16)
    own_term = jnp.zeros((rows, out_channels), jnp.float32)
    hidden_grad = jnp.zeros((rows, channels), jnp.float32)
    conv_rows = offsets * channels
    for o in range(octants):
        hit = octant == o
        weight = down_weight[o]
        own_term += matmul(jnp.where(hit, hidden, jnp.zeros_like(hidden)), weight)
        hidden_grad += jnp.where(hit, matmul(parent_grad, weight, 1, 1), 0.0)
        only = jnp.where(octant_turned == o, hidden_turned, jnp.zeros_like(hidden_turned))
        product = matmul(only, parent_grad).astype(jnp.bfloat16)
        sums[pl.ds(conv_rows + o * channels, channels), :] = product[:, :channels]
        sums[pl.ds(conv_rows + (octants + o) * channels, channels), :] = product[:, channels:]
    pre_grad = hidden_grad * gate * (1.0 + act * (1.0 - gate))
    pre_grad_turned = pre_grad.T.astype(jnp.bfloat16)

    from_row = (link_turned // octants) == lax.broadcasted_iota(jnp.int32, (coarse_tile, rows), 0)
    from_row = from_row.astype(jnp.bfloat16)
    high = own_term.astype(jnp.bfloat16)
    low = (own_term - high.astype(jnp.float32)).astype(jnp.bfloat16)
    coarse[...] = (matmul(from_row, high) + matmul(from_row, low)).astype(jnp.bfloat16)

    def backward(offset, carry):
        start = pl.multiple_of(offset * channels, channels)
        turned = matmul(pre_grad_turned, gathered[offset])
        sums[pl.ds(start, channels), :] = turned.T.astype(jnp.bfloat16)
        return carry

    lax.fori_loop(0, offsets, backward, 0, unroll=3)
    used = conv_rows + 2 * octants * channels
    sums[pl.ds(used, sums.shape[0] - used), :] = jnp.zeros((sums.shape[0] - used, channels), jnp.bfloat16)


def shards(features, kernel_map, send_lists, fine_to_coarse, conv_weight, down_weight, coarse_grad):
    rows, channels = features.shape
    tiles, slots = send_lists.shape[2:]
    offsets = kernel_map.shape[0]
    octants, _, out_channels = down_weight.shape
    tile_rows, halo_rows = RING_X * rows, tiles * slots
    coarse_rows = coarse_grad.shape[0]
    coarse_tile = RING_X * coarse_rows
    smem, vmem = pl.BlockSpec(memory_space=pltpu.SMEM), pl.BlockSpec(memory_space=pltpu.VMEM)
    anywhere = pl.BlockSpec(memory_space=pl.ANY)
    parts = share_over_x(features)
    outgoing = pl.pallas_call(
        pick_halo,
        out_shape=jax.ShapeDtypeStruct((halo_rows, channels), jnp.bfloat16),
        in_specs=[smem] + [anywhere] * 4,
        out_specs=vmem,
        scratch_shapes=[
            pltpu.VMEM((tile_rows, channels), jnp.bfloat16),
            pltpu.VMEM((tile_rows + 8, channels), jnp.float32),
            pltpu.VMEM((128, channels), jnp.float32),
            pltpu.SemaphoreType.DMA((4,)),
        ],
        compiler_params=pltpu.CompilerParams(vmem_limit_bytes=16 << 20),
        name="pick_halo",
    )(send_lists.reshape(halo_rows), *parts)
    later_grad, outgoing = lax.optimization_barrier((coarse_grad, outgoing))
    incoming = lax.all_to_all(
        outgoing.reshape(tiles, slots, channels), TILE, split_axis=0, concat_axis=0, tiled=True
    )
    grads = share_over_x(later_grad)
    x = lax.axis_index("x")
    link = lax.dynamic_slice_in_dim(fine_to_coarse, x * rows, rows)
    used = offsets * channels + 2 * octants * channels
    total = used + (-used % 512)
    coarse, sums = pl.pallas_call(
        step_kernel,
        out_shape=(
            jax.ShapeDtypeStruct((coarse_tile, out_channels), jnp.bfloat16),
            jax.ShapeDtypeStruct((total, channels), jnp.bfloat16),
        ),
        in_specs=[smem] + [anywhere] * 11 + [vmem] * 2,
        out_specs=(vmem, vmem),
        scratch_shapes=[
            pltpu.VMEM((tile_rows, channels), jnp.bfloat16),
            pltpu.VMEM((halo_rows, channels), jnp.bfloat16),
            pltpu.VMEM((tile_rows + halo_rows + 8, channels), jnp.float32),
            pltpu.VMEM((rows, channels), jnp.float32),
            pltpu.VMEM((offsets, rows, channels), jnp.bfloat16),
            pltpu.VMEM((rows, channels), jnp.float32),
            pltpu.VMEM(conv_weight.shape, jnp.bfloat16),
            pltpu.VMEM(down_weight.shape, jnp.bfloat16),
            pltpu.VMEM((coarse_tile, out_channels), jnp.bfloat16),
            pltpu.SemaphoreType.DMA((11,)),
        ],
        compiler_params=pltpu.CompilerParams(vmem_limit_bytes=40 << 20),
        name="step",
    )(
        kernel_map.reshape(offsets * rows), *parts, incoming.reshape(halo_rows, channels),
        conv_weight, down_weight, *grads, link.reshape(rows, 1), link.reshape(1, rows),
    )
    sums, coarse_out = sum_over_devices(sums, coarse)
    conv_grad = sums[: offsets * channels].reshape(offsets, channels, channels)
    down_sums = sums[offsets * channels : used]
    half = octants * channels
    down_grad = jnp.concatenate([down_sums[:half], down_sums[half:]], axis=1)
    down_grad = down_grad.reshape(octants, channels, out_channels)
    return (coarse_out, conv_grad, down_grad)


def solution(mesh):
    fine_mesh = Mesh(mesh.devices.reshape(RING_Y, DEPTH_Z, CORES, RING_X), AXES)
    placed = (
        P(AXES, None),
        P(None, AXES),
        P(TILE, "x", None, None),
        P(TILE),
        P(),
        P(),
        P(AXES, None),
    )
    return jax.shard_map(
        shards,
        mesh=fine_mesh,
        in_specs=placed,
        out_specs=(P(AXES, None), P(), P()),
        check_vma=False,
    )
```

time: 196 us -> 146 us (0.74)
  Pallas kernels: 71.3 us -> 26.3 us
  waiting for transfers between devices: 48.5 us -> 45.3 us
  starting transfers between devices: 58.8 us -> 56.7 us
    pallas_call x1, Pallas kernels: 54.1 us -> 22.1 us  [shards(): pl.pallas_call(step_kernel, out_shape=(jax.ShapeDtypeStruct((coarse_tile,...]
    pallas_call x1, Pallas kernels: 17.3 us -> 4.18 us  [shards(): pl.pallas_call(pick_halo, out_shape=jax.ShapeDtypeStruct((halo_rows, chan...]
    ppermute x28 -> x25, waiting for transfers between devices: 40.9 us -> 33.3 us  [send(): return lax.ppermute(value, AXES, partner_pairs(partner))]
    ppermute x28 -> x25, starting transfers between devices: 43.8 us -> 38.2 us  [send(): return lax.ppermute(value, AXES, partner_pairs(partner))]
    all_to_all x0 -> x1, waiting for transfers between devices: none -> 4.48 us  [sum_over_devices(): lax.all_to_all(shares, 'x', split_axis=0, concat_axis=0, tiled=True)]
    all_to_all x0 -> x1, starting transfers between devices: none -> 3.47 us  [sum_over_devices(): lax.all_to_all(shares, 'x', split_axis=0, concat_axis=0, tiled=True)]
    unnamed x35 -> x33, local copies, waits for them, and re-layouts: 10.9 us -> 10.1 us
  transfers between devices with their start and end apart: 29 -> 27, of which waited for: 23 -> 21; matrix products, arithmetic and copies ran while one was open for 1% -> 2% of each run, Pallas kernels for 0% -> 0%
where the time goes in v3:
time: 146 us; the launch traced here: 145 us
  starting transfers between devices  56.7 us (39%)
  waiting for transfers between devices  45.3 us (31%)
  Pallas kernels  26.3 us (18%)
  local copies, waits for them, and re-layouts  13.2 us (9%)
  other arithmetic  2.93 us (2%)
    ppermute x25, starting transfers between devices, send(): return lax.ppermute(value, AXES, partner_pairs(partner))  38.2 us
    ppermute x25, waiting for transfers between devices, send(): return lax.ppermute(value, AXES, partner_pairs(partner))  33.3 us
    pallas_call x1, Pallas kernels, shards(): pl.pallas_call(step_kernel, out_shape=(jax.ShapeDtypeStruct((coarse_tile,...  22.1 us
    all_to_all x1, starting transfers between devices, shards(): lax.all_to_all(outgoing.reshape(tiles, slots, channels), TILE, split_axis...  15.1 us
    unnamed x33, local copies, waits for them, and re-layouts  10.1 us
    all_to_all x1, waiting for transfers between devices, shards(): lax.all_to_all(outgoing.reshape(tiles, slots, channels), TILE, split_axis...  7.59 us
    all_to_all x1, waiting for transfers between devices, sum_over_devices(): lax.all_to_all(shares, 'x', split_axis=0, concat_axis=0, tiled=True)  4.48 us
    pallas_call x1, Pallas kernels, shards(): pl.pallas_call(pick_halo, out_shape=jax.ShapeDtypeStruct((halo_rows, chan...  4.18 us
  transfers between devices with their start and end apart: 27, of which 21 were waited for; matrix products, arithmetic and copies ran while one was open for 2% of the time, Pallas kernels for 0%

profile of v3, /device:TPU:1, one launch (start us, length us, event | category | flops | bytes accessed | tf_op | source)
XLA Modules:
  0.0 145.4 jit_solution(446777016250033953)
XLA Ops:
  0.6 3.4 %collective-permute-start.2 = (bf16[512,128]{1,0:T(8,128)(2,1)}, bf16[512,128]{1,0:T(8,128)(2,1)S(1)}, u32[]{:S(2)}, u32[]{:S(2)}) collective-permute-start(bf16[512,128]{1,0:T(8,128)(2,1)} %part0.3), channel_id=1, source_target_pairs={{0,3},{1,2},{2,1},{3,0},{4,7},{5,6},{6,5},{7,4},{8,11},{9,10},{10,... | collective-permute-start | bytes 393224 | tf_op jit(solution)/shard_map/ppermute | solution.py:31
  5.6 3.0 %collective-permute-done.2.part3 = bf16[512,128]{1,0:T(8,128)(2,1)S(1)} collective-permute-done((bf16[512,128]{1,0:T(8,128)(2,1)}, bf16[512,128]{1,0:T(8,128)(2,1)S(1)}, u32[]{:S(2)}, u32[]{:S(2)}) %collective-permute-start.2) | collective-permute-done | bytes 131104 | tf_op jit(solution)/shard_map/ppermute | solution.py:31
  10.6 4.2 %pick_halo.1 = bf16[2048,128]{1,0:T(8,128)(2,1)} custom-call(s32[2048]{0:T(1024)S(1)} %reshape.67.lists, bf16[512,128]{1,0:T(8,128)(2,1)S(1)} %copy-done.2, bf16[512,128]{1,0:T(8,128)(2,1)S(1)} %collective-permute-done.part1, bf16[512,128]{1,0:T(8,128)(2,1)S(1)} %collective-permute-done.1.part2, bf16[512,128]{1,0:T(8,128)(2,1)S(1)} %collective-permute-done.2.part3), custom_call_target="tpu_custom_call" | custom-call | tf_op jit(solution)/shard_map/pick_halo/pallas_call | solution.py:266
  14.8 15.1 %all-to-all-start = ((bf16[64,32,128]{2,1,0:T(8,128)(2,1)}), bf16[64,32,128]{2,1,0:T(8,128)(2,1)S(1)}, u32[]{:S(2)}, u32[]{:S(2)}) async-start(bf16[64,32,128]{2,1,0:T(8,128)(2,1)} %bitcast), calls=%async_computation | async-start | bytes 1048576 | tf_op jit(solution)/shard_map/all_to_all | solution.py:281
  29.9 1.8 %collective-permute-start.5 = (bf16[256,256]{1,0:T(8,128)(2,1)S(1)}, bf16[256,256]{1,0:T(8,128)(2,1)S(1)}, u32[]{:S(2)}, u32[]{:S(2)}) collective-permute-start(bf16[256,256]{1,0:T(8,128)(2,1)S(1)} %copy-done.7), channel_id=1, source_target_pairs={{0,3},{1,2},{2,1},{3,0},{4,7},{5,6},{6,5},{7,4},{8,11},{9,10},{10,... | collective-permute-start | bytes 393224 | tf_op jit(solution)/shard_map/ppermute | solution.py:31
  39.6 7.6 %all-to-all-done = bf16[64,32,128]{2,1,0:T(8,128)(2,1)S(1)} async-done(((bf16[64,32,128]{2,1,0:T(8,128)(2,1)}), bf16[64,32,128]{2,1,0:T(8,128)(2,1)S(1)}, u32[]{:S(2)}, u32[]{:S(2)}) %all-to-all-start) | async-done | bytes 524320 | tf_op jit(solution)/shard_map/all_to_all | solution.py:281
  53.6 22.1 %step.1 = (bf16[1024,256]{1,0:T(8,128)(2,1)}, bf16[5632,128]{1,0:T(8,128)(2,1)S(1)}) custom-call(s32[13824]{0:T(1024)S(1)} %copy-done.6, bf16[512,128]{1,0:T(8,128)(2,1)S(1)} %copy-done.3, bf16[512,128]{1,0:T(8,128)(2,1)S(1)} %copy-done.5, bf16[512,128]{1,0:T(8,128)(2,1)S(1)} %collective-permute-done.1.part2, ...), custom_call_target="tpu_custom_call" | custom-call | tf_op jit(solution)/shard_map/step/pallas_call | solution.py:289
  76.1 1.9 %collective-permute-done.6 = bf16[2816,128]{1,0:T(8,128)(2,1)S(1)} collective-permute-done((bf16[2816,128]{1,0:T(8,128)(2,1)S(1)}, bf16[2816,128]{1,0:T(8,128)(2,1)S(1)}, u32[]{:S(2)}, u32[]{:S(2)}) %collective-permute-start.6) | collective-permute-done | bytes 720928 | tf_op jit(solution)/shard_map/ppermute | solution.py:31
  78.3 1.3 collective-permute-start.7
  79.6 1.9 %collective-permute-start.9 = (bf16[704,128]{1,0:T(8,128)(2,1)S(1)}, bf16[704,128]{1,0:T(8,128)(2,1)S(1)}, u32[]{:S(2)}, u32[]{:S(2)}) collective-permute-start(bf16[704,128]{1,0:T(8,128)(2,1)S(1)} %get-tuple-element.28), channel_id=1, source_target_pairs={{0,3},{1,2},{2,1},{3,0},{4,196},{5,197},{6,198},{7,199},{8,11},{9,... | collective-permute-start | bytes 540680 | tf_op jit(solution)/shard_map/ppermute | solution.py:31
  83.0 2.9 %collective-permute-done.9 = bf16[704,128]{1,0:T(8,128)(2,1)S(1)} collective-permute-done((bf16[704,128]{1,0:T(8,128)(2,1)S(1)}, bf16[704,128]{1,0:T(8,128)(2,1)S(1)}, u32[]{:S(2)}, u32[]{:S(2)}) %collective-permute-start.9) | collective-permute-done | bytes 180256 | tf_op jit(solution)/shard_map/ppermute | solution.py:31
  85.8 1.8 %collective-permute-done.8 = bf16[704,128]{1,0:T(8,128)(2,1)S(1)} collective-permute-done((bf16[704,128]{1,0:T(8,128)(2,1)S(1)}, bf16[704,128]{1,0:T(8,128)(2,1)S(1)}, u32[]{:S(2)}, u32[]{:S(2)}) %collective-permute-start.8) | collective-permute-done | bytes 180256 | tf_op jit(solution)/shard_map/ppermute | solution.py:31
  88.2 1.8 %collective-permute-start.12 = (bf16[176,128]{1,0:T(8,128)(2,1)S(1)}, bf16[176,128]{1,0:T(8,128)(2,1)S(1)}, u32[]{:S(2)}, u32[]{:S(2)}) collective-permute-start(bf16[176,128]{1,0:T(8,128)(2,1)S(1)} %get-tuple-element.35), channel_id=1, source_target_pairs={{0,192},{1,193},{2,194},{3,195},{4,7},{5,6},{6,5},{7,4},{8,200},{9... | collective-permute-start | bytes 135176 | tf_op jit(solution)/shard_map/ppermute | solution.py:31
  90.0 1.3 collective-permute-start.11
  91.3 3.5 %all-to-all-start.1 = ((bf16[4,256,256]{2,1,0:T(8,128)(2,1)}), bf16[4,256,256]{2,1,0:T(8,128)(2,1)S(1)}, u32[]{:S(2)}, u32[]{:S(2)}) async-start(bf16[4,256,256]{2,1,0:T(8,128)(2,1)} %bitcast.20), calls=%async_computation.1 | async-start | bytes 1048576 | tf_op jit(solution)/shard_map/all_to_all | solution.py:105
  95.3 2.3 %collective-permute-done.13 = bf16[88,128]{1,0:T(8,128)(2,1)S(1)} collective-permute-done((bf16[88,128]{1,0:T(8,128)(2,1)S(1)}, bf16[88,128]{1,0:T(8,128)(2,1)S(1)}, u32[]{:S(2)}, u32[]{:S(2)}) %collective-permute-start.13) | collective-permute-done | bytes 22560 | tf_op jit(solution)/shard_map/ppermute | solution.py:31
  97.6 4.5 %all-to-all-done.1 = bf16[4,256,256]{2,1,0:T(8,128)(2,1)S(1)} async-done(((bf16[4,256,256]{2,1,0:T(8,128)(2,1)}), bf16[4,256,256]{2,1,0:T(8,128)(2,1)S(1)}, u32[]{:S(2)}, u32[]{:S(2)}) %all-to-all-start.1) | async-done | bytes 524320 | tf_op jit(solution)/shard_map/all_to_all | solution.py:105
  103.3 3.8 %collective-permute-start.15 = (bf16[88,128]{1,0:T(8,128)(2,1)S(1)}, bf16[88,128]{1,0:T(8,128)(2,1)S(1)}, u32[]{:S(2)}, u32[]{:S(2)}) collective-permute-start(bf16[88,128]{1,0:T(8,128)(2,1)S(1)} %fusion.7), channel_id=1, source_target_pairs={{0,32},{1,33},{2,34},{3,35},{4,36},{5,37},{6,38},{7,39},{8,40},{9,... | collective-permute-start | bytes 67592 | tf_op jit(solution)/shard_map/ppermute | solution.py:31
  107.1 1.4 collective-permute-start.14
  108.5 1.4 collective-permute-done.15
  109.9 1.3 collective-permute-done.14
  111.3 3.0 %collective-permute-done.17 = bf16[88,128]{1,0:T(8,128)(2,1)S(1)} collective-permute-done((bf16[88,128]{1,0:T(8,128)(2,1)S(1)}, bf16[88,128]{1,0:T(8,128)(2,1)S(1)}, u32[]{:S(2)}, u32[]{:S(2)}) %collective-permute-start.17) | collective-permute-done | bytes 22560 | tf_op jit(solution)/shard_map/ppermute | solution.py:31
  114.7 1.8 %collective-permute-start.19 = (bf16[176,128]{1,0:T(8,128)(2,1)S(1)}, bf16[176,128]{1,0:T(8,128)(2,1)S(1)}, u32[]{:S(2)}, u32[]{:S(2)}) collective-permute-start(bf16[176,128]{1,0:T(8,128)(2,1)S(1)} %bitcast.99), channel_id=1, source_target_pairs={{0,128},{1,129},{2,130},{3,131},{4,6},{5,7},{6,4},{7,5},{8,136},{9... | collective-permute-start | bytes 135176 | tf_op jit(solution)/shard_map/ppermute | solution.py:31
  116.5 1.8 %collective-permute-start.18 = (bf16[176,128]{1,0:T(8,128)(2,1)S(1)}, bf16[176,128]{1,0:T(8,128)(2,1)S(1)}, u32[]{:S(2)}, u32[]{:S(2)}) collective-permute-start(bf16[176,128]{1,0:T(8,128)(2,1)S(1)} %bitcast.100), channel_id=1, source_target_pairs={{0,192},{1,193},{2,194},{3,195},{4,7},{5,6},{6,5},{7,4},{8,200},{9... | collective-permute-start | bytes 135176 | tf_op jit(solution)/shard_map/ppermute | solution.py:31
  119.1 1.5 %collective-permute-done.18 = bf16[176,128]{1,0:T(8,128)(2,1)S(1)} collective-permute-done((bf16[176,128]{1,0:T(8,128)(2,1)S(1)}, bf16[176,128]{1,0:T(8,128)(2,1)S(1)}, u32[]{:S(2)}, u32[]{:S(2)}) %collective-permute-start.18) | collective-permute-done | bytes 45088 | tf_op jit(solution)/shard_map/ppermute | solution.py:31
  120.8 2.9 %collective-permute-start.22 = (bf16[704,128]{1,0:T(8,128)(2,1)S(1)}, bf16[704,128]{1,0:T(8,128)(2,1)S(1)}, u32[]{:S(2)}, u32[]{:S(2)}) collective-permute-start(bf16[704,128]{1,0:T(8,128)(2,1)S(1)} %bitcast.92), channel_id=1, source_target_pairs={{0,2},{1,3},{2,0},{3,1},{4,132},{5,133},{6,134},{7,135},{8,10},{9,... | collective-permute-start | bytes 540680 | tf_op jit(solution)/shard_map/ppermute | solution.py:31
  124.7 1.2 collective-permute-done.23
  125.8 3.4 %collective-permute-done.22 = bf16[704,128]{1,0:T(8,128)(2,1)S(1)} collective-permute-done((bf16[704,128]{1,0:T(8,128)(2,1)S(1)}, bf16[704,128]{1,0:T(8,128)(2,1)S(1)}, u32[]{:S(2)}, u32[]{:S(2)}) %collective-permute-start.22) | collective-permute-done | bytes 180256 | tf_op jit(solution)/shard_map/ppermute | solution.py:31
  129.2 2.3 %collective-permute-done.21 = bf16[704,128]{1,0:T(8,128)(2,1)S(1)} collective-permute-done((bf16[704,128]{1,0:T(8,128)(2,1)S(1)}, bf16[704,128]{1,0:T(8,128)(2,1)S(1)}, u32[]{:S(2)}, u32[]{:S(2)}) %collective-permute-start.21) | collective-permute-done | bytes 180256 | tf_op jit(solution)/shard_map/ppermute | solution.py:31
  131.7 8.9 %collective-permute-start.24 = (bf16[2816,128]{1,0:T(8,128)(2,1)S(1)}, bf16[2816,128]{1,0:T(8,128)(2,1)S(1)}, u32[]{:S(2)}, u32[]{:S(2)}) collective-permute-start(bf16[2816,128]{1,0:T(8,128)(2,1)S(1)} %bitcast.88), channel_id=1, source_target_pairs={{0,4},{1,5},{2,6},{3,7},{4,0},{5,1},{6,2},{7,3},{8,12},{9,13},{10,... | collective-permute-start | bytes 2162696 | tf_op jit(solution)/shard_map/ppermute | solution.py:31
  140.6 1.8 %collective-permute-done.24 = bf16[2816,128]{1,0:T(8,128)(2,1)S(1)} collective-permute-done((bf16[2816,128]{1,0:T(8,128)(2,1)S(1)}, bf16[2816,128]{1,0:T(8,128)(2,1)S(1)}, u32[]{:S(2)}, u32[]{:S(2)}) %collective-permute-start.24) | collective-permute-done | bytes 720928 | tf_op jit(solution)/shard_map/ppermute | solution.py:31
  143.0 1.3 slice.15
  (83 shorter events, 26.7 us)
Async XLA Ops:
  0.6 46.6 %copy-start = (bf16[27,128,128]{2,1,0:T(8,128)(2,1)S(1)}, bf16[27,128,128]{2,1,0:T(8,128)(2,1)}, u32[]{:S(2)}) copy-start(bf16[27,128,128]{2,1,0:T(8,128)(2,1)} %conv_hbm.1) | copy-start | bytes 2654212
  0.6 7.9 %collective-permute-start.2 = (bf16[512,128]{1,0:T(8,128)(2,1)}, bf16[512,128]{1,0:T(8,128)(2,1)S(1)}, u32[]{:S(2)}, u32[]{:S(2)}) collective-permute-start(bf16[512,128]{1,0:T(8,128)(2,1)} %part0.3), channel_id=1, source_target_pairs={{0,3},{1,2},{2,1},{3,0},{4,7},{5,6},{6,5},{7,4},{8,11},{9,10},{10,... | collective-permute-start | bytes 393224 | tf_op jit(solution)/shard_map/ppermute | solution.py:31
  4.0 5.6 %collective-permute-start.1 = (bf16[512,128]{1,0:T(8,128)(2,1)}, bf16[512,128]{1,0:T(8,128)(2,1)S(1)}, u32[]{:S(2)}, u32[]{:S(2)}) collective-permute-start(bf16[512,128]{1,0:T(8,128)(2,1)} %part0.3), channel_id=1, source_target_pairs={{0,2},{1,3},{2,0},{3,1},{4,6},{5,7},{6,4},{7,5},{8,10},{9,11},{10,... | collective-permute-start | bytes 393224 | tf_op jit(solution)/shard_map/ppermute | solution.py:31
  4.6 5.1 %collective-permute-start = (bf16[512,128]{1,0:T(8,128)(2,1)}, bf16[512,128]{1,0:T(8,128)(2,1)S(1)}, u32[]{:S(2)}, u32[]{:S(2)}) collective-permute-start(bf16[512,128]{1,0:T(8,128)(2,1)} %part0.3), channel_id=1, source_target_pairs={{0,1},{1,0},{2,3},{3,2},{4,5},{5,4},{6,7},{7,6},{8,9},{9,8},{10,11... | collective-permute-start | bytes 393224 | tf_op jit(solution)/shard_map/ppermute | solution.py:31
  10.6 4.2 %copy-start.4 = (bf16[512,128]{1,0:T(8,128)(2,1)}, bf16[512,128]{1,0:T(8,128)(2,1)S(1)}, u32[]{:S(2)}) copy-start(bf16[512,128]{1,0:T(8,128)(2,1)S(1)} %collective-permute-done.part1) | copy-start | bytes 393220
  10.6 19.3 %copy-start.7 = (bf16[256,256]{1,0:T(8,128)(2,1)S(1)}, bf16[256,256]{1,0:T(8,128)(2,1)}, u32[]{:S(2)}) copy-start(bf16[256,256]{1,0:T(8,128)(2,1)} %grad0) | copy-start | bytes 393220
  10.6 22.6 %copy-start.15 = (s32[27,512]{1,0:T(8,128)S(1)}, s32[27,512]{1,0:T(8,128)}, u32[]{:S(2)}) copy-start(s32[27,512]{1,0:T(8,128)} %param.8) | copy-start | bytes 165892
  10.6 36.6 %copy-start.3 = (bf16[512,128]{1,0:T(8,128)(2,1)S(1)}, bf16[512,128]{1,0:T(8,128)(2,1)}, u32[]{:S(2)}) copy-start(bf16[512,128]{1,0:T(8,128)(2,1)} %part0.3) | copy-start | bytes 393220
  14.8 32.4 %all-to-all-start = ((bf16[64,32,128]{2,1,0:T(8,128)(2,1)}), bf16[64,32,128]{2,1,0:T(8,128)(2,1)S(1)}, u32[]{:S(2)}, u32[]{:S(2)}) async-start(bf16[64,32,128]{2,1,0:T(8,128)(2,1)} %bitcast), calls=%async_computation | async-start | bytes 1048576 | tf_op jit(solution)/shard_map/all_to_all | solution.py:281
  29.9 5.9 %collective-permute-start.5 = (bf16[256,256]{1,0:T(8,128)(2,1)S(1)}, bf16[256,256]{1,0:T(8,128)(2,1)S(1)}, u32[]{:S(2)}, u32[]{:S(2)}) collective-permute-start(bf16[256,256]{1,0:T(8,128)(2,1)S(1)} %copy-done.7), channel_id=1, source_target_pairs={{0,3},{1,2},{2,1},{3,0},{4,7},{5,6},{6,5},{7,4},{8,11},{9,10},{10,... | collective-permute-start | bytes 393224 | tf_op jit(solution)/shard_map/ppermute | solution.py:31
  31.6 5.9 %collective-permute-start.4 = (bf16[256,256]{1,0:T(8,128)(2,1)S(1)}, bf16[256,256]{1,0:T(8,128)(2,1)S(1)}, u32[]{:S(2)}, u32[]{:S(2)}) collective-permute-start(bf16[256,256]{1,0:T(8,128)(2,1)S(1)} %copy-done.7), channel_id=1, source_target_pairs={{0,2},{1,3},{2,0},{3,1},{4,6},{5,7},{6,4},{7,5},{8,10},{9,11},{10,... | collective-permute-start | bytes 393224 | tf_op jit(solution)/shard_map/ppermute | solution.py:31
  32.2 6.7 %collective-permute-start.3 = (bf16[256,256]{1,0:T(8,128)(2,1)S(1)}, bf16[256,256]{1,0:T(8,128)(2,1)S(1)}, u32[]{:S(2)}, u32[]{:S(2)}) collective-permute-start(bf16[256,256]{1,0:T(8,128)(2,1)S(1)} %copy-done.7), channel_id=1, source_target_pairs={{0,1},{1,0},{2,3},{3,2},{4,5},{5,4},{6,7},{7,6},{8,9},{9,8},{10,11... | collective-permute-start | bytes 393224 | tf_op jit(solution)/shard_map/ppermute | solution.py:31
  75.7 2.3 %collective-permute-start.6 = (bf16[2816,128]{1,0:T(8,128)(2,1)S(1)}, bf16[2816,128]{1,0:T(8,128)(2,1)S(1)}, u32[]{:S(2)}, u32[]{:S(2)}) collective-permute-start(bf16[2816,128]{1,0:T(8,128)(2,1)S(1)} %dynamic-slice_bitcast_fusion), channel_id=1, source_target_pairs={{0,4},{1,5},{2,6},{3,7},{4,0},{5,1},{6,2},{7,3},{8,12},{9,13},{10,... | collective-permute-start | bytes 2162696 | tf_op jit(solution)/shard_map/ppermute | solution.py:31
  78.3 4.7 %collective-permute-start.7 = (bf16[704,128]{1,0:T(8,128)(2,1)S(1)}, bf16[704,128]{1,0:T(8,128)(2,1)S(1)}, u32[]{:S(2)}, u32[]{:S(2)}) collective-permute-start(bf16[704,128]{1,0:T(8,128)(2,1)S(1)} %get-tuple-element.27), channel_id=1, source_target_pairs={{0,1},{1,0},{2,3},{3,2},{4,68},{5,69},{6,70},{7,71},{8,9},{9,8},{1... | collective-permute-start | bytes 540680 | tf_op jit(solution)/shard_map/ppermute | solution.py:31
  79.6 6.3 %collective-permute-start.9 = (bf16[704,128]{1,0:T(8,128)(2,1)S(1)}, bf16[704,128]{1,0:T(8,128)(2,1)S(1)}, u32[]{:S(2)}, u32[]{:S(2)}) collective-permute-start(bf16[704,128]{1,0:T(8,128)(2,1)S(1)} %get-tuple-element.28), channel_id=1, source_target_pairs={{0,3},{1,2},{2,1},{3,0},{4,196},{5,197},{6,198},{7,199},{8,11},{9,... | collective-permute-start | bytes 540680 | tf_op jit(solution)/shard_map/ppermute | solution.py:31
  81.5 6.1 %collective-permute-start.8 = (bf16[704,128]{1,0:T(8,128)(2,1)S(1)}, bf16[704,128]{1,0:T(8,128)(2,1)S(1)}, u32[]{:S(2)}, u32[]{:S(2)}) collective-permute-start(bf16[704,128]{1,0:T(8,128)(2,1)S(1)} %get-tuple-element.29), channel_id=1, source_target_pairs={{0,2},{1,3},{2,0},{3,1},{4,132},{5,133},{6,134},{7,135},{8,10},{9,... | collective-permute-start | bytes 540680 | tf_op jit(solution)/shard_map/ppermute | solution.py:31
  87.7 7.0 %collective-permute-start.10 = (bf16[176,128]{1,0:T(8,128)(2,1)S(1)}, bf16[176,128]{1,0:T(8,128)(2,1)S(1)}, u32[]{:S(2)}, u32[]{:S(2)}) collective-permute-start(bf16[176,128]{1,0:T(8,128)(2,1)S(1)} %get-tuple-element.34), channel_id=1, source_target_pairs={{0,64},{1,65},{2,66},{3,67},{4,5},{5,4},{6,7},{7,6},{8,72},{9,73},... | collective-permute-start | bytes 135176 | tf_op jit(solution)/shard_map/ppermute | solution.py:31
  88.2 6.6 %collective-permute-start.12 = (bf16[176,128]{1,0:T(8,128)(2,1)S(1)}, bf16[176,128]{1,0:T(8,128)(2,1)S(1)}, u32[]{:S(2)}, u32[]{:S(2)}) collective-permute-start(bf16[176,128]{1,0:T(8,128)(2,1)S(1)} %get-tuple-element.35), channel_id=1, source_target_pairs={{0,192},{1,193},{2,194},{3,195},{4,7},{5,6},{6,5},{7,4},{8,200},{9... | collective-permute-start | bytes 135176 | tf_op jit(solution)/shard_map/ppermute | solution.py:31
  90.0 4.8 %collective-permute-start.11 = (bf16[176,128]{1,0:T(8,128)(2,1)S(1)}, bf16[176,128]{1,0:T(8,128)(2,1)S(1)}, u32[]{:S(2)}, u32[]{:S(2)}) collective-permute-start(bf16[176,128]{1,0:T(8,128)(2,1)S(1)} %get-tuple-element.36), channel_id=1, source_target_pairs={{0,128},{1,129},{2,130},{3,131},{4,6},{5,7},{6,4},{7,5},{8,136},{9... | collective-permute-start | bytes 135176 | tf_op jit(solution)/shard_map/ppermute | solution.py:31
  91.3 10.8 %all-to-all-start.1 = ((bf16[4,256,256]{2,1,0:T(8,128)(2,1)}), bf16[4,256,256]{2,1,0:T(8,128)(2,1)S(1)}, u32[]{:S(2)}, u32[]{:S(2)}) async-start(bf16[4,256,256]{2,1,0:T(8,128)(2,1)} %bitcast.20), calls=%async_computation.1 | async-start | bytes 1048576 | tf_op jit(solution)/shard_map/all_to_all | solution.py:105
  94.8 2.7 %collective-permute-start.13 = (bf16[88,128]{1,0:T(8,128)(2,1)S(1)}, bf16[88,128]{1,0:T(8,128)(2,1)S(1)}, u32[]{:S(2)}, u32[]{:S(2)}) collective-permute-start(bf16[88,128]{1,0:T(8,128)(2,1)S(1)} %dynamic-slice_bitcast_fusion.7), channel_id=1, source_target_pairs={{0,8},{1,9},{2,10},{3,11},{4,12},{5,13},{6,14},{7,15},{8,0},{9,1},... | collective-permute-start | bytes 67592 | tf_op jit(solution)/shard_map/ppermute | solution.py:31
  102.8 5.7 %collective-permute-start.16 = (bf16[88,128]{1,0:T(8,128)(2,1)S(1)}, bf16[88,128]{1,0:T(8,128)(2,1)S(1)}, u32[]{:S(2)}, u32[]{:S(2)}) collective-permute-start(bf16[88,128]{1,0:T(8,128)(2,1)S(1)} %fusion.7), channel_id=1, source_target_pairs={{0,48},{1,49},{2,50},{3,51},{4,52},{5,53},{6,54},{7,55},{8,56},{9,... | collective-permute-start | bytes 67592 | tf_op jit(solution)/shard_map/ppermute | solution.py:31
  103.3 6.6 %collective-permute-start.15 = (bf16[88,128]{1,0:T(8,128)(2,1)S(1)}, bf16[88,128]{1,0:T(8,128)(2,1)S(1)}, u32[]{:S(2)}, u32[]{:S(2)}) collective-permute-start(bf16[88,128]{1,0:T(8,128)(2,1)S(1)} %fusion.7), channel_id=1, source_target_pairs={{0,32},{1,33},{2,34},{3,35},{4,36},{5,37},{6,38},{7,39},{8,40},{9,... | collective-permute-start | bytes 67592 | tf_op jit(solution)/shard_map/ppermute | solution.py:31
  107.1 4.1 %collective-permute-start.14 = (bf16[88,128]{1,0:T(8,128)(2,1)S(1)}, bf16[88,128]{1,0:T(8,128)(2,1)S(1)}, u32[]{:S(2)}, u32[]{:S(2)}) collective-permute-start(bf16[88,128]{1,0:T(8,128)(2,1)S(1)} %fusion.7), channel_id=1, source_target_pairs={{0,16},{1,17},{2,18},{3,19},{4,20},{5,21},{6,22},{7,23},{8,24},{9,... | collective-permute-start | bytes 67592 | tf_op jit(solution)/shard_map/ppermute | solution.py:31
  111.2 3.1 %collective-permute-start.17 = (bf16[88,128]{1,0:T(8,128)(2,1)S(1)}, bf16[88,128]{1,0:T(8,128)(2,1)S(1)}, u32[]{:S(2)}, u32[]{:S(2)}) collective-permute-start(bf16[88,128]{1,0:T(8,128)(2,1)S(1)} %add_convert_fusion), channel_id=1, source_target_pairs={{0,8},{1,9},{2,10},{3,11},{4,12},{5,13},{6,14},{7,15},{8,0},{9,1},... | collective-permute-start | bytes 67592 | tf_op jit(solution)/shard_map/ppermute | solution.py:31
  114.3 3.9 %collective-permute-start.20 = (bf16[176,128]{1,0:T(8,128)(2,1)S(1)}, bf16[176,128]{1,0:T(8,128)(2,1)S(1)}, u32[]{:S(2)}, u32[]{:S(2)}) collective-permute-start(bf16[176,128]{1,0:T(8,128)(2,1)S(1)} %bitcast.98), channel_id=1, source_target_pairs={{0,64},{1,65},{2,66},{3,67},{4,5},{5,4},{6,7},{7,6},{8,72},{9,73},... | collective-permute-start | bytes 135176 | tf_op jit(solution)/shard_map/ppermute | solution.py:31
  114.7 4.4 %collective-permute-start.19 = (bf16[176,128]{1,0:T(8,128)(2,1)S(1)}, bf16[176,128]{1,0:T(8,128)(2,1)S(1)}, u32[]{:S(2)}, u32[]{:S(2)}) collective-permute-start(bf16[176,128]{1,0:T(8,128)(2,1)S(1)} %bitcast.99), channel_id=1, source_target_pairs={{0,128},{1,129},{2,130},{3,131},{4,6},{5,7},{6,4},{7,5},{8,136},{9... | collective-permute-start | bytes 135176 | tf_op jit(solution)/shard_map/ppermute | solution.py:31
  116.5 4.1 %collective-permute-start.18 = (bf16[176,128]{1,0:T(8,128)(2,1)S(1)}, bf16[176,128]{1,0:T(8,128)(2,1)S(1)}, u32[]{:S(2)}, u32[]{:S(2)}) collective-permute-start(bf16[176,128]{1,0:T(8,128)(2,1)S(1)} %bitcast.100), channel_id=1, source_target_pairs={{0,192},{1,193},{2,194},{3,195},{4,7},{5,6},{6,5},{7,4},{8,200},{9... | collective-permute-start | bytes 135176 | tf_op jit(solution)/shard_map/ppermute | solution.py:31
  120.7 5.1 %collective-permute-start.23 = (bf16[704,128]{1,0:T(8,128)(2,1)S(1)}, bf16[704,128]{1,0:T(8,128)(2,1)S(1)}, u32[]{:S(2)}, u32[]{:S(2)}) collective-permute-start(bf16[704,128]{1,0:T(8,128)(2,1)S(1)} %bitcast.91), channel_id=1, source_target_pairs={{0,1},{1,0},{2,3},{3,2},{4,68},{5,69},{6,70},{7,71},{8,9},{9,8},{1... | collective-permute-start | bytes 540680 | tf_op jit(solution)/shard_map/ppermute | solution.py:31
  120.8 8.4 %collective-permute-start.22 = (bf16[704,128]{1,0:T(8,128)(2,1)S(1)}, bf16[704,128]{1,0:T(8,128)(2,1)S(1)}, u32[]{:S(2)}, u32[]{:S(2)}) collective-permute-start(bf16[704,128]{1,0:T(8,128)(2,1)S(1)} %bitcast.92), channel_id=1, source_target_pairs={{0,2},{1,3},{2,0},{3,1},{4,132},{5,133},{6,134},{7,135},{8,10},{9,... | collective-permute-start | bytes 540680 | tf_op jit(solution)/shard_map/ppermute | solution.py:31
  123.7 7.8 %collective-permute-start.21 = (bf16[704,128]{1,0:T(8,128)(2,1)S(1)}, bf16[704,128]{1,0:T(8,128)(2,1)S(1)}, u32[]{:S(2)}, u32[]{:S(2)}) collective-permute-start(bf16[704,128]{1,0:T(8,128)(2,1)S(1)} %bitcast.93), channel_id=1, source_target_pairs={{0,3},{1,2},{2,1},{3,0},{4,196},{5,197},{6,198},{7,199},{8,11},{9,... | collective-permute-start | bytes 540680 | tf_op jit(solution)/shard_map/ppermute | solution.py:31
  131.7 10.7 %collective-permute-start.24 = (bf16[2816,128]{1,0:T(8,128)(2,1)S(1)}, bf16[2816,128]{1,0:T(8,128)(2,1)S(1)}, u32[]{:S(2)}, u32[]{:S(2)}) collective-permute-start(bf16[2816,128]{1,0:T(8,128)(2,1)S(1)} %bitcast.88), channel_id=1, source_target_pairs={{0,4},{1,5},{2,6},{3,7},{4,0},{5,1},{6,2},{7,3},{8,12},{9,13},{10,... | collective-permute-start | bytes 2162696 | tf_op jit(solution)/shard_map/ppermute | solution.py:31
  (11 other events, 9.3 us)

commit v4 on v3

--- a/solution.py
+++ b/solution.py
@@ -35,12 +35,19 @@
     return (y, z, 1 - core, x)
 
 
+def square(step, hop):
+    def partner(y, z, core, x):
+        return (y ^ (hop if step & 2 else 0), z, core, x ^ (hop if step & 1 else 0))
+
+    return partner
+
+
 def first_ring(step):
-    return lambda y, z, core, x: (y, z, core, x ^ step) if core == 0 else (y ^ step, z, core, x)
+    return lambda y, z, core, x: square(step, 3 if core else 1)(y, z, core, x)
 
 
 def second_ring(step):
-    return lambda y, z, core, x: (y ^ step, z, core, x) if core == 0 else (y, z, core, x ^ step)
+    return lambda y, z, core, x: square(step, 1 if core else 3)(y, z, core, x)
 
 
 def along_z(step):
@@ -93,25 +100,25 @@
 
 def sum_over_devices(partial_sums, coarse):
     y, z, core, x = (lax.axis_index(name) for name in AXES)
-    ring_one = jnp.where(core == 0, x, y)
-    ring_two = jnp.where(core == 0, y, x)
-    rows = partial_sums.shape[0] // (CORES * RING_X * RING_Y * 2)
+    near_x, near_y = (x ^ (x >> 1)) & 1, (y ^ (y >> 1)) & 1
+    far_x, far_y = x >> 1, y >> 1
+    near, far = near_x + 2 * near_y, far_x + 2 * far_y
+    ring_one = jnp.where(core == 0, near, far)
+    ring_two = jnp.where(core == 0, far, near)
+    rows = partial_sums.shape[0] // (CORES * RING_X * RING_Y)
     lanes = partial_sums.shape[1]
-    parts = partial_sums.reshape(CORES, RING_X * RING_Y * 2 * rows, lanes)
+    parts = partial_sums.reshape(CORES, RING_X * RING_Y * rows, lanes)
     part = scatter_pair(parts, core, across_core)
-    part = scatter_ring(part.reshape(RING_X, RING_Y * 2 * rows, lanes), ring_one, first_ring)
+    part = scatter_ring(part.reshape(RING_X, RING_Y * rows, lanes), ring_one, first_ring)
     part, coarse = lax.optimization_barrier((part, coarse))
     shares = coarse.reshape(RING_X, coarse.shape[0] // RING_X, coarse.shape[1])
     shares = lax.all_to_all(shares, "x", split_axis=0, concat_axis=0, tiled=True)
     coarse_out = narrow(jnp.sum(wide(shares), axis=0))
-    part = scatter_ring(part.reshape(RING_Y, 2 * rows, lanes), ring_two, second_ring)
-    part = scatter_pair(part.reshape(2, rows, lanes), z % 2, along_z(1))
-    part, coarse_out = lax.optimization_barrier((part, coarse_out))
-    others = [send(part, along_z(step)) for step in (2, 4, 6)]
-    part = narrow((wide(part) + wide(others[0])) + (wide(others[1]) + wide(others[2])))
-    part = gather_pair(part, z % 2, along_z(1)).reshape(2 * rows, lanes)
-    part = gather_ring(part, ring_two, second_ring).reshape(RING_Y * 2 * rows, lanes)
-    part = gather_ring(part, ring_one, first_ring).reshape(RING_X * RING_Y * 2 * rows, lanes)
+    part = scatter_ring(part.reshape(RING_Y, rows, lanes), ring_two, second_ring)
+    for step in (1, 2, 7):
+        part = narrow(wide(part) + wide(send(part, along_z(step))))
+    part = gather_ring(part, ring_two, second_ring).reshape(RING_Y * rows, lanes)
+    part = gather_ring(part, ring_one, first_ring).reshape(RING_X * RING_Y * rows, lanes)
     return wide(gather_pair(part, core, across_core)).reshape(partial_sums.shape), coarse_out
 
 
@@ -261,7 +268,7 @@
     coarse_rows = coarse_grad.shape[0]
     coarse_tile = RING_X * coarse_rows
     smem, vmem = pl.BlockSpec(memory_space=pltpu.SMEM), pl.BlockSpec(memory_space=pltpu.VMEM)
-    anywhere = pl.BlockSpec(memory_space=pl.ANY)
+    anywhere = pl.BlockSpec(memory_space=pltpu.HBM)
     parts = share_over_x(features)
     outgoing = pl.pallas_call(
         pick_halo,
@@ -306,7 +313,7 @@
             pltpu.VMEM((coarse_tile, out_channels), jnp.bfloat16),
             pltpu.SemaphoreType.DMA((11,)),
         ],
-        compiler_params=pltpu.CompilerParams(vmem_limit_bytes=40 << 20),
+        compiler_params=pltpu.CompilerParams(vmem_limit_bytes=56 << 20),
         name="step",
     )(
         kernel_map.reshape(offsets * rows), *parts, incoming.reshape(halo_rows, channels),

time: 146 us -> 147 us (level)
  waiting for transfers between devices: 45.3 us -> 51.8 us
  local copies, waits for them, and re-layouts: 13.2 us -> 7.58 us
    unnamed x33 -> x25, local copies, waits for them, and re-layouts: 10.1 us -> 2.53 us
    all_to_all x1, waiting for transfers between devices: 4.48 us -> 9.3 us  [sum_over_devices(): lax.all_to_all(shares, 'x', split_axis=0, concat_axis=0, tiled=True)]
    ppermute x25 -> x23, starting transfers between devices: 38.2 us -> 37.2 us  [send(): return lax.ppermute(value, AXES, partner_pairs(partner))]
    ppermute x25 -> x23, waiting for transfers between devices: 33.3 us -> 34.3 us  [send(): return lax.ppermute(value, AXES, partner_pairs(partner))]
  transfers between devices with their start and end apart: 27 -> 25, of which waited for: 21 -> 23; matrix products, arithmetic and copies ran while one was open for 2% -> 3% of each run, Pallas kernels for 0% -> 0%
where the time goes in v4:
time: 147 us; the launch traced here: 146 us
  starting transfers between devices  56.2 us (38%)
  waiting for transfers between devices  51.8 us (35%)
  Pallas kernels  26.8 us (18%)
  local copies, waits for them, and re-layouts  7.58 us (5%)
  other arithmetic  2.92 us (2%)
    ppermute x23, starting transfers between devices, send(): return lax.ppermute(value, AXES, partner_pairs(partner))  37.2 us
    ppermute x23, waiting for transfers between devices, send(): return lax.ppermute(value, AXES, partner_pairs(partner))  34.3 us
    pallas_call x1, Pallas kernels, shards(): pl.pallas_call(step_kernel, out_shape=(jax.ShapeDtypeStruct((coarse_tile,...  22.6 us
    all_to_all x1, starting transfers between devices, shards(): lax.all_to_all(outgoing.reshape(tiles, slots, channels), TILE, split_axis...  15.1 us
    all_to_all x1, waiting for transfers between devices, sum_over_devices(): lax.all_to_all(shares, 'x', split_axis=0, concat_axis=0, tiled=True)  9.3 us
    all_to_all x1, waiting for transfers between devices, shards(): lax.all_to_all(outgoing.reshape(tiles, slots, channels), TILE, split_axis...  8.24 us
    pallas_call x1, Pallas kernels, shards(): pl.pallas_call(pick_halo, out_shape=jax.ShapeDtypeStruct((halo_rows, chan...  4.18 us
    all_to_all x1, starting transfers between devices, sum_over_devices(): lax.all_to_all(shares, 'x', split_axis=0, concat_axis=0, tiled=True)  3.96 us
  transfers between devices with their start and end apart: 25, of which 23 were waited for; matrix products, arithmetic and copies ran while one was open for 3% of the time, Pallas kernels for 0%

profile of v4, /device:TPU:1, one launch (start us, length us, event | category | flops | bytes accessed | tf_op | source)
XLA Modules:
  0.0 146.2 jit_solution(13167976461370919194)
XLA Ops:
  0.6 3.4 %collective-permute-start.2 = (bf16[512,128]{1,0:T(8,128)(2,1)}, bf16[512,128]{1,0:T(8,128)(2,1)S(1)}, u32[]{:S(2)}, u32[]{:S(2)}) collective-permute-start(bf16[512,128]{1,0:T(8,128)(2,1)} %part0.3), channel_id=1, source_target_pairs={{0,3},{1,2},{2,1},{3,0},{4,7},{5,6},{6,5},{7,4},{8,11},{9,10},{10,... | collective-permute-start | bytes 393224 | tf_op jit(solution)/shard_map/ppermute | solution.py:31
  5.6 3.0 %collective-permute-done.2.part3 = bf16[512,128]{1,0:T(8,128)(2,1)S(1)} collective-permute-done((bf16[512,128]{1,0:T(8,128)(2,1)}, bf16[512,128]{1,0:T(8,128)(2,1)S(1)}, u32[]{:S(2)}, u32[]{:S(2)}) %collective-permute-start.2) | collective-permute-done | bytes 131104 | tf_op jit(solution)/shard_map/ppermute | solution.py:31
  8.6 1.1 collective-permute-done.1.part2
  10.6 4.2 %pick_halo.1 = bf16[2048,128]{1,0:T(8,128)(2,1)} custom-call(s32[2048]{0:T(1024)S(1)} %reshape.59.lists, bf16[512,128]{1,0:T(8,128)(2,1)S(1)} %copy-done, bf16[512,128]{1,0:T(8,128)(2,1)S(1)} %collective-permute-done.part1, bf16[512,128]{1,0:T(8,128)(2,1)S(1)} %collective-permute-done.1.part2, bf16[512,128]{1,0:T(8,128)(2,1)S(1)} %collective-permute-done.2.part3), custom_call_target="tpu_custom_call" | custom-call | tf_op jit(solution)/shard_map/pick_halo/pallas_call | solution.py:273
  14.8 15.1 %all-to-all-start = ((bf16[64,32,128]{2,1,0:T(8,128)(2,1)}), bf16[64,32,128]{2,1,0:T(8,128)(2,1)S(1)}, u32[]{:S(2)}, u32[]{:S(2)}) async-start(bf16[64,32,128]{2,1,0:T(8,128)(2,1)} %bitcast), calls=%async_computation | async-start | bytes 1048576 | tf_op jit(solution)/shard_map/all_to_all | solution.py:288
  29.9 1.7 %collective-permute-start.5 = (bf16[256,256]{1,0:T(8,128)(2,1)S(1)}, bf16[256,256]{1,0:T(8,128)(2,1)S(1)}, u32[]{:S(2)}, u32[]{:S(2)}) collective-permute-start(bf16[256,256]{1,0:T(8,128)(2,1)S(1)} %copy-done.6), channel_id=1, source_target_pairs={{0,3},{1,2},{2,1},{3,0},{4,7},{5,6},{6,5},{7,4},{8,11},{9,10},{10,... | collective-permute-start | bytes 393224 | tf_op jit(solution)/shard_map/ppermute | solution.py:31
  32.2 1.1 collective-permute-start.3
  35.8 1.7 %collective-permute-done.4.grad2 = bf16[256,256]{1,0:T(8,128)(2,1)S(1)} collective-permute-done((bf16[256,256]{1,0:T(8,128)(2,1)S(1)}, bf16[256,256]{1,0:T(8,128)(2,1)S(1)}, u32[]{:S(2)}, u32[]{:S(2)}) %collective-permute-start.4) | collective-permute-done | bytes 131104 | tf_op jit(solution)/shard_map/ppermute | solution.py:31
  37.5 1.5 collective-permute-done.3.grad1
  39.0 8.2 %all-to-all-done = bf16[64,32,128]{2,1,0:T(8,128)(2,1)S(1)} async-done(((bf16[64,32,128]{2,1,0:T(8,128)(2,1)}), bf16[64,32,128]{2,1,0:T(8,128)(2,1)S(1)}, u32[]{:S(2)}, u32[]{:S(2)}) %all-to-all-start) | async-done | bytes 524320 | tf_op jit(solution)/shard_map/all_to_all | solution.py:288
  48.0 22.6 %step.1 = (bf16[1024,256]{1,0:T(8,128)(2,1)}, bf16[5632,128]{1,0:T(8,128)(2,1)}) custom-call(s32[13824]{0:T(1024)} %reshape.58.kernel_map, bf16[512,128]{1,0:T(8,128)(2,1)} %part0.3, bf16[512,128]{1,0:T(8,128)(2,1)} %copy-done.3, bf16[512,128]{1,0:T(8,128)(2,1)} %copy-done.2, bf16[512,128]{1,0:T(8,128)(2,1)} %copy-done.1, bf16[2048,128]{1,0:T(8,128)(2,1)} %bitcast.69, ...), custom_call_target="tpu_custom_call" | custom-call | tf_op jit(solution)/shard_map/step/pallas_call | solution.py:296
  70.6 1.3 dynamic-slice_bitcast_fusion
  72.3 1.9 %collective-permute-done.6 = bf16[2816,128]{1,0:T(8,128)(2,1)S(1)} collective-permute-done((bf16[2816,128]{1,0:T(8,128)(2,1)S(1)}, bf16[2816,128]{1,0:T(8,128)(2,1)S(1)}, u32[]{:S(2)}, u32[]{:S(2)}) %collective-permute-start.6) | collective-permute-done | bytes 720928 | tf_op jit(solution)/shard_map/ppermute | solution.py:31
  74.5 1.7 %collective-permute-start.7 = (bf16[704,128]{1,0:T(8,128)(2,1)S(1)}, bf16[704,128]{1,0:T(8,128)(2,1)S(1)}, u32[]{:S(2)}, u32[]{:S(2)}) collective-permute-start(bf16[704,128]{1,0:T(8,128)(2,1)S(1)} %get-tuple-element.23), channel_id=1, source_target_pairs={{0,1},{1,0},{2,3},{3,2},{4,7},{5,6},{6,5},{7,4},{8,9},{9,8},{10,11... | collective-permute-start | bytes 540680 | tf_op jit(solution)/shard_map/ppermute | solution.py:31
  76.2 3.4 %collective-permute-start.9 = (bf16[704,128]{1,0:T(8,128)(2,1)S(1)}, bf16[704,128]{1,0:T(8,128)(2,1)S(1)}, u32[]{:S(2)}, u32[]{:S(2)}) collective-permute-start(bf16[704,128]{1,0:T(8,128)(2,1)S(1)} %get-tuple-element.24), channel_id=1, source_target_pairs={{0,65},{1,64},{2,67},{3,66},{4,199},{5,198},{6,197},{7,196},{8,73}... | collective-permute-start | bytes 540680 | tf_op jit(solution)/shard_map/ppermute | solution.py:31
  80.1 4.4 %collective-permute-done.9 = bf16[704,128]{1,0:T(8,128)(2,1)S(1)} collective-permute-done((bf16[704,128]{1,0:T(8,128)(2,1)S(1)}, bf16[704,128]{1,0:T(8,128)(2,1)S(1)}, u32[]{:S(2)}, u32[]{:S(2)}) %collective-permute-start.9) | collective-permute-done | bytes 180256 | tf_op jit(solution)/shard_map/ppermute | solution.py:31
  84.5 1.8 %collective-permute-done.8 = bf16[704,128]{1,0:T(8,128)(2,1)S(1)} collective-permute-done((bf16[704,128]{1,0:T(8,128)(2,1)S(1)}, bf16[704,128]{1,0:T(8,128)(2,1)S(1)}, u32[]{:S(2)}, u32[]{:S(2)}) %collective-permute-start.8) | collective-permute-done | bytes 180256 | tf_op jit(solution)/shard_map/ppermute | solution.py:31
  87.3 2.1 %collective-permute-start.11 = (bf16[176,128]{1,0:T(8,128)(2,1)S(1)}, bf16[176,128]{1,0:T(8,128)(2,1)S(1)}, u32[]{:S(2)}, u32[]{:S(2)}) collective-permute-start(bf16[176,128]{1,0:T(8,128)(2,1)S(1)} %get-tuple-element.32), channel_id=1, source_target_pairs={{0,192},{1,193},{2,194},{3,195},{4,68},{5,69},{6,70},{7,71},{8,200... | collective-permute-start | bytes 135176 | tf_op jit(solution)/shard_map/ppermute | solution.py:31
  91.8 2.4 %collective-permute-done.13 = bf16[176,128]{1,0:T(8,128)(2,1)S(1)} collective-permute-done((bf16[176,128]{1,0:T(8,128)(2,1)S(1)}, bf16[176,128]{1,0:T(8,128)(2,1)S(1)}, u32[]{:S(2)}, u32[]{:S(2)}) %collective-permute-start.13) | collective-permute-done | bytes 45088 | tf_op jit(solution)/shard_map/ppermute | solution.py:31
  94.3 1.1 collective-permute-start.14
  95.3 3.4 %collective-permute-done.14 = bf16[176,128]{1,0:T(8,128)(2,1)S(1)} collective-permute-done((bf16[176,128]{1,0:T(8,128)(2,1)S(1)}, bf16[176,128]{1,0:T(8,128)(2,1)S(1)}, u32[]{:S(2)}, u32[]{:S(2)}) %collective-permute-start.14) | collective-permute-done | bytes 45088 | tf_op jit(solution)/shard_map/ppermute | solution.py:31
  99.7 3.3 %collective-permute-done.15 = bf16[176,128]{1,0:T(8,128)(2,1)S(1)} collective-permute-done((bf16[176,128]{1,0:T(8,128)(2,1)S(1)}, bf16[176,128]{1,0:T(8,128)(2,1)S(1)}, u32[]{:S(2)}, u32[]{:S(2)}) %collective-permute-start.15) | collective-permute-done | bytes 45088 | tf_op jit(solution)/shard_map/ppermute | solution.py:31
  104.4 1.3 collective-permute-start.16
  106.5 1.7 %collective-permute-done.16 = bf16[176,128]{1,0:T(8,128)(2,1)S(1)} collective-permute-done((bf16[176,128]{1,0:T(8,128)(2,1)S(1)}, bf16[176,128]{1,0:T(8,128)(2,1)S(1)}, u32[]{:S(2)}, u32[]{:S(2)}) %collective-permute-start.16) | collective-permute-done | bytes 45088 | tf_op jit(solution)/shard_map/ppermute | solution.py:31
  108.3 1.4 collective-permute-start.21
  110.2 3.2 %collective-permute-start.19 = (bf16[704,128]{1,0:T(8,128)(2,1)S(1)}, bf16[704,128]{1,0:T(8,128)(2,1)S(1)}, u32[]{:S(2)}, u32[]{:S(2)}) collective-permute-start(bf16[704,128]{1,0:T(8,128)(2,1)S(1)} %bitcast.76), channel_id=1, source_target_pairs={{0,65},{1,64},{2,67},{3,66},{4,199},{5,198},{6,197},{7,196},{8,73}... | collective-permute-start | bytes 540680 | tf_op jit(solution)/shard_map/ppermute | solution.py:31
  113.9 1.6 %collective-permute-done.20 = bf16[704,128]{1,0:T(8,128)(2,1)S(1)} collective-permute-done((bf16[704,128]{1,0:T(8,128)(2,1)S(1)}, bf16[704,128]{1,0:T(8,128)(2,1)S(1)}, u32[]{:S(2)}, u32[]{:S(2)}) %collective-permute-start.20) | collective-permute-done | bytes 180256 | tf_op jit(solution)/shard_map/ppermute | solution.py:31
  115.5 2.7 %collective-permute-done.19 = bf16[704,128]{1,0:T(8,128)(2,1)S(1)} collective-permute-done((bf16[704,128]{1,0:T(8,128)(2,1)S(1)}, bf16[704,128]{1,0:T(8,128)(2,1)S(1)}, u32[]{:S(2)}, u32[]{:S(2)}) %collective-permute-start.19) | collective-permute-done | bytes 180256 | tf_op jit(solution)/shard_map/ppermute | solution.py:31
  118.4 10.7 %collective-permute-start.22 = (bf16[2816,128]{1,0:T(8,128)(2,1)S(1)}, bf16[2816,128]{1,0:T(8,128)(2,1)S(1)}, u32[]{:S(2)}, u32[]{:S(2)}) collective-permute-start(bf16[2816,128]{1,0:T(8,128)(2,1)S(1)} %bitcast.68), channel_id=1, source_target_pairs={{0,4},{1,5},{2,6},{3,7},{4,0},{5,1},{6,2},{7,3},{8,12},{9,13},{10,... | collective-permute-start | bytes 2162696 | tf_op jit(solution)/shard_map/ppermute | solution.py:31
  129.1 4.0 %all-to-all-start.1 = ((bf16[4,256,256]{2,1,0:T(8,128)(2,1)}), bf16[4,256,256]{2,1,0:T(8,128)(2,1)S(1)}, u32[]{:S(2)}, u32[]{:S(2)}) async-start(bf16[4,256,256]{2,1,0:T(8,128)(2,1)} %bitcast.12), calls=%async_computation.1 | async-start | bytes 1048576 | tf_op jit(solution)/shard_map/all_to_all | solution.py:115
  133.1 9.3 %all-to-all-done.1 = bf16[4,256,256]{2,1,0:T(8,128)(2,1)S(1)} async-done(((bf16[4,256,256]{2,1,0:T(8,128)(2,1)}), bf16[4,256,256]{2,1,0:T(8,128)(2,1)S(1)}, u32[]{:S(2)}, u32[]{:S(2)}) %all-to-all-start.1) | async-done | bytes 524320 | tf_op jit(solution)/shard_map/all_to_all | solution.py:115
  143.8 1.3 slice.15
  (69 shorter events, 17.7 us)
Async XLA Ops:
  0.6 32.6 %copy-start.10 = (s32[27,512]{1,0:T(8,128)S(1)}, s32[27,512]{1,0:T(8,128)}, u32[]{:S(2)}) copy-start(s32[27,512]{1,0:T(8,128)} %param.8) | copy-start | bytes 165892
  0.6 7.9 %collective-permute-start.2 = (bf16[512,128]{1,0:T(8,128)(2,1)}, bf16[512,128]{1,0:T(8,128)(2,1)S(1)}, u32[]{:S(2)}, u32[]{:S(2)}) collective-permute-start(bf16[512,128]{1,0:T(8,128)(2,1)} %part0.3), channel_id=1, source_target_pairs={{0,3},{1,2},{2,1},{3,0},{4,7},{5,6},{6,5},{7,4},{8,11},{9,10},{10,... | collective-permute-start | bytes 393224 | tf_op jit(solution)/shard_map/ppermute | solution.py:31
  4.0 5.6 %collective-permute-start.1 = (bf16[512,128]{1,0:T(8,128)(2,1)}, bf16[512,128]{1,0:T(8,128)(2,1)S(1)}, u32[]{:S(2)}, u32[]{:S(2)}) collective-permute-start(bf16[512,128]{1,0:T(8,128)(2,1)} %part0.3), channel_id=1, source_target_pairs={{0,2},{1,3},{2,0},{3,1},{4,6},{5,7},{6,4},{7,5},{8,10},{9,11},{10,... | collective-permute-start | bytes 393224 | tf_op jit(solution)/shard_map/ppermute | solution.py:31
  4.6 5.1 %collective-permute-start = (bf16[512,128]{1,0:T(8,128)(2,1)}, bf16[512,128]{1,0:T(8,128)(2,1)S(1)}, u32[]{:S(2)}, u32[]{:S(2)}) collective-permute-start(bf16[512,128]{1,0:T(8,128)(2,1)} %part0.3), channel_id=1, source_target_pairs={{0,1},{1,0},{2,3},{3,2},{4,5},{5,4},{6,7},{7,6},{8,9},{9,8},{10,11... | collective-permute-start | bytes 393224 | tf_op jit(solution)/shard_map/ppermute | solution.py:31
  8.6 38.7 %copy-start.1 = (bf16[512,128]{1,0:T(8,128)(2,1)}, bf16[512,128]{1,0:T(8,128)(2,1)S(1)}, u32[]{:S(2)}) copy-start(bf16[512,128]{1,0:T(8,128)(2,1)S(1)} %collective-permute-done.2.part3) | copy-start | bytes 393220
  9.7 37.5 %copy-start.2 = (bf16[512,128]{1,0:T(8,128)(2,1)}, bf16[512,128]{1,0:T(8,128)(2,1)S(1)}, u32[]{:S(2)}) copy-start(bf16[512,128]{1,0:T(8,128)(2,1)S(1)} %collective-permute-done.1.part2) | copy-start | bytes 393220
  10.6 36.6 %copy-start.3 = (bf16[512,128]{1,0:T(8,128)(2,1)}, bf16[512,128]{1,0:T(8,128)(2,1)S(1)}, u32[]{:S(2)}) copy-start(bf16[512,128]{1,0:T(8,128)(2,1)S(1)} %collective-permute-done.part1) | copy-start | bytes 393220
  10.6 19.3 %copy-start.6 = (bf16[256,256]{1,0:T(8,128)(2,1)S(1)}, bf16[256,256]{1,0:T(8,128)(2,1)}, u32[]{:S(2)}) copy-start(bf16[256,256]{1,0:T(8,128)(2,1)} %grad0) | copy-start | bytes 393220
  14.8 32.4 %all-to-all-start = ((bf16[64,32,128]{2,1,0:T(8,128)(2,1)}), bf16[64,32,128]{2,1,0:T(8,128)(2,1)S(1)}, u32[]{:S(2)}, u32[]{:S(2)}) async-start(bf16[64,32,128]{2,1,0:T(8,128)(2,1)} %bitcast), calls=%async_computation | async-start | bytes 1048576 | tf_op jit(solution)/shard_map/all_to_all | solution.py:288
  29.9 5.9 %collective-permute-start.5 = (bf16[256,256]{1,0:T(8,128)(2,1)S(1)}, bf16[256,256]{1,0:T(8,128)(2,1)S(1)}, u32[]{:S(2)}, u32[]{:S(2)}) collective-permute-start(bf16[256,256]{1,0:T(8,128)(2,1)S(1)} %copy-done.6), channel_id=1, source_target_pairs={{0,3},{1,2},{2,1},{3,0},{4,7},{5,6},{6,5},{7,4},{8,11},{9,10},{10,... | collective-permute-start | bytes 393224 | tf_op jit(solution)/shard_map/ppermute | solution.py:31
  31.6 5.9 %collective-permute-start.4 = (bf16[256,256]{1,0:T(8,128)(2,1)S(1)}, bf16[256,256]{1,0:T(8,128)(2,1)S(1)}, u32[]{:S(2)}, u32[]{:S(2)}) collective-permute-start(bf16[256,256]{1,0:T(8,128)(2,1)S(1)} %copy-done.6), channel_id=1, source_target_pairs={{0,2},{1,3},{2,0},{3,1},{4,6},{5,7},{6,4},{7,5},{8,10},{9,11},{10,... | collective-permute-start | bytes 393224 | tf_op jit(solution)/shard_map/ppermute | solution.py:31
  32.2 6.8 %collective-permute-start.3 = (bf16[256,256]{1,0:T(8,128)(2,1)S(1)}, bf16[256,256]{1,0:T(8,128)(2,1)S(1)}, u32[]{:S(2)}, u32[]{:S(2)}) collective-permute-start(bf16[256,256]{1,0:T(8,128)(2,1)S(1)} %copy-done.6), channel_id=1, source_target_pairs={{0,1},{1,0},{2,3},{3,2},{4,5},{5,4},{6,7},{7,6},{8,9},{9,8},{10,11... | collective-permute-start | bytes 393224 | tf_op jit(solution)/shard_map/ppermute | solution.py:31
  34.6 12.6 %copy-start.11 = (s32[512]{0:T(512)}, s32[512]{0:T(512)S(1)}, u32[]{:S(2)}) copy-start(s32[512]{0:T(512)S(1)} %dynamic_slice.36) | copy-start | bytes 6148
  35.8 11.4 %copy-start.7 = (bf16[256,256]{1,0:T(8,128)(2,1)}, bf16[256,256]{1,0:T(8,128)(2,1)S(1)}, u32[]{:S(2)}) copy-start(bf16[256,256]{1,0:T(8,128)(2,1)S(1)} %collective-permute-done.5.grad3) | copy-start | bytes 393220
  71.9 2.3 %collective-permute-start.6 = (bf16[2816,128]{1,0:T(8,128)(2,1)S(1)}, bf16[2816,128]{1,0:T(8,128)(2,1)S(1)}, u32[]{:S(2)}, u32[]{:S(2)}) collective-permute-start(bf16[2816,128]{1,0:T(8,128)(2,1)S(1)} %dynamic-slice_bitcast_fusion), channel_id=1, source_target_pairs={{0,4},{1,5},{2,6},{3,7},{4,0},{5,1},{6,2},{7,3},{8,12},{9,13},{10,... | collective-permute-start | bytes 2162696 | tf_op jit(solution)/shard_map/ppermute | solution.py:31
  74.5 5.6 %collective-permute-start.7 = (bf16[704,128]{1,0:T(8,128)(2,1)S(1)}, bf16[704,128]{1,0:T(8,128)(2,1)S(1)}, u32[]{:S(2)}, u32[]{:S(2)}) collective-permute-start(bf16[704,128]{1,0:T(8,128)(2,1)S(1)} %get-tuple-element.23), channel_id=1, source_target_pairs={{0,1},{1,0},{2,3},{3,2},{4,7},{5,6},{6,5},{7,4},{8,9},{9,8},{10,11... | collective-permute-start | bytes 540680 | tf_op jit(solution)/shard_map/ppermute | solution.py:31
  76.2 8.3 %collective-permute-start.9 = (bf16[704,128]{1,0:T(8,128)(2,1)S(1)}, bf16[704,128]{1,0:T(8,128)(2,1)S(1)}, u32[]{:S(2)}, u32[]{:S(2)}) collective-permute-start(bf16[704,128]{1,0:T(8,128)(2,1)S(1)} %get-tuple-element.24), channel_id=1, source_target_pairs={{0,65},{1,64},{2,67},{3,66},{4,199},{5,198},{6,197},{7,196},{8,73}... | collective-permute-start | bytes 540680 | tf_op jit(solution)/shard_map/ppermute | solution.py:31
  79.6 6.7 %collective-permute-start.8 = (bf16[704,128]{1,0:T(8,128)(2,1)S(1)}, bf16[704,128]{1,0:T(8,128)(2,1)S(1)}, u32[]{:S(2)}, u32[]{:S(2)}) collective-permute-start(bf16[704,128]{1,0:T(8,128)(2,1)S(1)} %get-tuple-element.25), channel_id=1, source_target_pairs={{0,64},{1,65},{2,66},{3,67},{4,196},{5,197},{6,198},{7,199},{8,72}... | collective-permute-start | bytes 540680 | tf_op jit(solution)/shard_map/ppermute | solution.py:31
  86.5 3.5 %collective-permute-start.10 = (bf16[176,128]{1,0:T(8,128)(2,1)S(1)}, bf16[176,128]{1,0:T(8,128)(2,1)S(1)}, u32[]{:S(2)}, u32[]{:S(2)}) collective-permute-start(bf16[176,128]{1,0:T(8,128)(2,1)S(1)} %get-tuple-element.30), channel_id=1, source_target_pairs={{0,3},{1,2},{2,1},{3,0},{4,5},{5,4},{6,7},{7,6},{8,11},{9,10},{10,... | collective-permute-start | bytes 135176 | tf_op jit(solution)/shard_map/ppermute | solution.py:31
  86.7 3.9 %collective-permute-start.12 = (bf16[176,128]{1,0:T(8,128)(2,1)S(1)}, bf16[176,128]{1,0:T(8,128)(2,1)S(1)}, u32[]{:S(2)}, u32[]{:S(2)}) collective-permute-start(bf16[176,128]{1,0:T(8,128)(2,1)S(1)} %get-tuple-element.31), channel_id=1, source_target_pairs={{0,195},{1,194},{2,193},{3,192},{4,69},{5,68},{6,71},{7,70},{8,203... | collective-permute-start | bytes 135176 | tf_op jit(solution)/shard_map/ppermute | solution.py:31
  87.3 3.8 %collective-permute-start.11 = (bf16[176,128]{1,0:T(8,128)(2,1)S(1)}, bf16[176,128]{1,0:T(8,128)(2,1)S(1)}, u32[]{:S(2)}, u32[]{:S(2)}) collective-permute-start(bf16[176,128]{1,0:T(8,128)(2,1)S(1)} %get-tuple-element.32), channel_id=1, source_target_pairs={{0,192},{1,193},{2,194},{3,195},{4,68},{5,69},{6,70},{7,71},{8,200... | collective-permute-start | bytes 135176 | tf_op jit(solution)/shard_map/ppermute | solution.py:31
  91.1 3.1 %collective-permute-start.13 = (bf16[176,128]{1,0:T(8,128)(2,1)S(1)}, bf16[176,128]{1,0:T(8,128)(2,1)S(1)}, u32[]{:S(2)}, u32[]{:S(2)}) collective-permute-start(bf16[176,128]{1,0:T(8,128)(2,1)S(1)} %fusion.6), channel_id=1, source_target_pairs={{0,8},{1,9},{2,10},{3,11},{4,12},{5,13},{6,14},{7,15},{8,0},{9,1},... | collective-permute-start | bytes 135176 | tf_op jit(solution)/shard_map/ppermute | solution.py:31
  94.3 4.5 %collective-permute-start.14 = (bf16[176,128]{1,0:T(8,128)(2,1)S(1)}, bf16[176,128]{1,0:T(8,128)(2,1)S(1)}, u32[]{:S(2)}, u32[]{:S(2)}) collective-permute-start(bf16[176,128]{1,0:T(8,128)(2,1)S(1)} %add_convert_fusion.2), channel_id=1, source_target_pairs={{0,16},{1,17},{2,18},{3,19},{4,20},{5,21},{6,22},{7,23},{8,24},{9,... | collective-permute-start | bytes 135176 | tf_op jit(solution)/shard_map/ppermute | solution.py:31
  98.8 4.2 %collective-permute-start.15 = (bf16[176,128]{1,0:T(8,128)(2,1)S(1)}, bf16[176,128]{1,0:T(8,128)(2,1)S(1)}, u32[]{:S(2)}, u32[]{:S(2)}) collective-permute-start(bf16[176,128]{1,0:T(8,128)(2,1)S(1)} %add_convert_fusion.1), channel_id=1, source_target_pairs={{0,56},{1,57},{2,58},{3,59},{4,60},{5,61},{6,62},{7,63},{8,48},{9,... | collective-permute-start | bytes 135176 | tf_op jit(solution)/shard_map/ppermute | solution.py:31
  103.0 3.0 %collective-permute-start.18 = (bf16[176,128]{1,0:T(8,128)(2,1)S(1)}, bf16[176,128]{1,0:T(8,128)(2,1)S(1)}, u32[]{:S(2)}, u32[]{:S(2)}) collective-permute-start(bf16[176,128]{1,0:T(8,128)(2,1)S(1)} %add_convert_fusion), channel_id=1, source_target_pairs={{0,3},{1,2},{2,1},{3,0},{4,5},{5,4},{6,7},{7,6},{8,11},{9,10},{10,... | collective-permute-start | bytes 135176 | tf_op jit(solution)/shard_map/ppermute | solution.py:31
  103.6 2.9 %collective-permute-start.17 = (bf16[176,128]{1,0:T(8,128)(2,1)S(1)}, bf16[176,128]{1,0:T(8,128)(2,1)S(1)}, u32[]{:S(2)}, u32[]{:S(2)}) collective-permute-start(bf16[176,128]{1,0:T(8,128)(2,1)S(1)} %add_convert_fusion), channel_id=1, source_target_pairs={{0,192},{1,193},{2,194},{3,195},{4,68},{5,69},{6,70},{7,71},{8,200... | collective-permute-start | bytes 135176 | tf_op jit(solution)/shard_map/ppermute | solution.py:31
  104.4 3.8 %collective-permute-start.16 = (bf16[176,128]{1,0:T(8,128)(2,1)S(1)}, bf16[176,128]{1,0:T(8,128)(2,1)S(1)}, u32[]{:S(2)}, u32[]{:S(2)}) collective-permute-start(bf16[176,128]{1,0:T(8,128)(2,1)S(1)} %add_convert_fusion), channel_id=1, source_target_pairs={{0,195},{1,194},{2,193},{3,192},{4,69},{5,68},{6,71},{7,70},{8,203... | collective-permute-start | bytes 135176 | tf_op jit(solution)/shard_map/ppermute | solution.py:31
  108.3 5.6 %collective-permute-start.21 = (bf16[704,128]{1,0:T(8,128)(2,1)S(1)}, bf16[704,128]{1,0:T(8,128)(2,1)S(1)}, u32[]{:S(2)}, u32[]{:S(2)}) collective-permute-start(bf16[704,128]{1,0:T(8,128)(2,1)S(1)} %bitcast.74), channel_id=1, source_target_pairs={{0,1},{1,0},{2,3},{3,2},{4,7},{5,6},{6,5},{7,4},{8,9},{9,8},{10,11... | collective-permute-start | bytes 540680 | tf_op jit(solution)/shard_map/ppermute | solution.py:31
  109.7 5.8 %collective-permute-start.20 = (bf16[704,128]{1,0:T(8,128)(2,1)S(1)}, bf16[704,128]{1,0:T(8,128)(2,1)S(1)}, u32[]{:S(2)}, u32[]{:S(2)}) collective-permute-start(bf16[704,128]{1,0:T(8,128)(2,1)S(1)} %bitcast.75), channel_id=1, source_target_pairs={{0,64},{1,65},{2,66},{3,67},{4,196},{5,197},{6,198},{7,199},{8,72}... | collective-permute-start | bytes 540680 | tf_op jit(solution)/shard_map/ppermute | solution.py:31
  110.2 8.0 %collective-permute-start.19 = (bf16[704,128]{1,0:T(8,128)(2,1)S(1)}, bf16[704,128]{1,0:T(8,128)(2,1)S(1)}, u32[]{:S(2)}, u32[]{:S(2)}) collective-permute-start(bf16[704,128]{1,0:T(8,128)(2,1)S(1)} %bitcast.76), channel_id=1, source_target_pairs={{0,65},{1,64},{2,67},{3,66},{4,199},{5,198},{6,197},{7,196},{8,73}... | collective-permute-start | bytes 540680 | tf_op jit(solution)/shard_map/ppermute | solution.py:31
  118.4 24.7 %collective-permute-start.22 = (bf16[2816,128]{1,0:T(8,128)(2,1)S(1)}, bf16[2816,128]{1,0:T(8,128)(2,1)S(1)}, u32[]{:S(2)}, u32[]{:S(2)}) collective-permute-start(bf16[2816,128]{1,0:T(8,128)(2,1)S(1)} %bitcast.68), channel_id=1, source_target_pairs={{0,4},{1,5},{2,6},{3,7},{4,0},{5,1},{6,2},{7,3},{8,12},{9,13},{10,... | collective-permute-start | bytes 2162696 | tf_op jit(solution)/shard_map/ppermute | solution.py:31
  129.1 13.3 %all-to-all-start.1 = ((bf16[4,256,256]{2,1,0:T(8,128)(2,1)}), bf16[4,256,256]{2,1,0:T(8,128)(2,1)S(1)}, u32[]{:S(2)}, u32[]{:S(2)}) async-start(bf16[4,256,256]{2,1,0:T(8,128)(2,1)} %bitcast.12), calls=%async_computation.1 | async-start | bytes 1048576 | tf_op jit(solution)/shard_map/all_to_all | solution.py:115
  (5 other events, 23.3 us)

commit v5 on v4

--- a/solution.py
+++ b/solution.py
@@ -43,11 +43,11 @@
 
 
 def first_ring(step):
+    return lambda y, z, core, x: square(step, 1 if core else 3)(y, z, core, x)
+
+
+def second_ring(step):
     return lambda y, z, core, x: square(step, 3 if core else 1)(y, z, core, x)
-
-
-def second_ring(step):
-    return lambda y, z, core, x: square(step, 1 if core else 3)(y, z, core, x)
 
 
 def along_z(step):
@@ -103,8 +103,8 @@
     near_x, near_y = (x ^ (x >> 1)) & 1, (y ^ (y >> 1)) & 1
     far_x, far_y = x >> 1, y >> 1
     near, far = near_x + 2 * near_y, far_x + 2 * far_y
-    ring_one = jnp.where(core == 0, near, far)
-    ring_two = jnp.where(core == 0, far, near)
+    ring_one = jnp.where(core == 0, far, near)
+    ring_two = jnp.where(core == 0, near, far)
     rows = partial_sums.shape[0] // (CORES * RING_X * RING_Y)
     lanes = partial_sums.shape[1]
     parts = partial_sums.reshape(CORES, RING_X * RING_Y * rows, lanes)
@@ -117,6 +117,7 @@
     part = scatter_ring(part.reshape(RING_Y, rows, lanes), ring_two, second_ring)
     for step in (1, 2, 7):
         part = narrow(wide(part) + wide(send(part, along_z(step))))
+    part, coarse_out = lax.optimization_barrier((part, coarse_out))
     part = gather_ring(part, ring_two, second_ring).reshape(RING_Y * rows, lanes)
     part = gather_ring(part, ring_one, first_ring).reshape(RING_X * RING_Y * rows, lanes)
     return wide(gather_pair(part, core, across_core)).reshape(partial_sums.shape), coarse_out
@@ -178,19 +179,18 @@
     kernel_map, part0, part1, part2, part3, incoming, conv_hbm, down_hbm,
     grad0, grad1, grad2, grad3, link_column, link_row,
     coarse, sums,
-    tile_feats, halo_feats, table, stage, gathered, pre_act, conv_weight, down_weight, tile_grad, sems,
+    tile_feats, table, stage, gathered, pre_act, conv_weight, down_weight, tile_grad, sems,
 ):
     rows, channels = part0.shape
     offsets = conv_weight.shape[0]
     octants, _, out_channels = down_weight.shape
-    tile_rows, halo_rows = tile_feats.shape[0], halo_feats.shape[0]
+    tile_rows, halo_rows = tile_feats.shape[0], incoming.shape[0]
     coarse_tile = tile_grad.shape[0]
     feats = part_copies((part0, part1, part2, part3), tile_feats, sems, 0)
-    halo = pltpu.make_async_copy(incoming, halo_feats, sems.at[4])
-    conv = pltpu.make_async_copy(conv_hbm, conv_weight, sems.at[5])
-    down = pltpu.make_async_copy(down_hbm, down_weight, sems.at[6])
-    grads = part_copies((grad0, grad1, grad2, grad3), tile_grad, sems, 7)
-    for copy in feats + [halo, conv, down] + grads:
+    conv = pltpu.make_async_copy(conv_hbm, conv_weight, sems.at[4])
+    down = pltpu.make_async_copy(down_hbm, down_weight, sems.at[5])
+    grads = part_copies((grad0, grad1, grad2, grad3), tile_grad, sems, 6)
+    for copy in feats + [conv, down] + grads:
         copy.start()
     pre_act[...] = jnp.zeros_like(pre_act)
     table[pl.ds(tile_rows + halo_rows, 8), :] = jnp.zeros((8, channels), jnp.float32)
@@ -200,8 +200,7 @@
     middle = offsets // 2
     own = pl.multiple_of(lax.axis_index("x") * rows, rows)
     gathered[middle] = tile_feats[pl.ds(own, rows), :]
-    halo.wait()
-    table[pl.ds(tile_rows, halo_rows), :] = halo_feats[...].astype(jnp.float32)
+    table[pl.ds(tile_rows, halo_rows), :] = incoming[...].astype(jnp.float32)
     conv.wait()
 
     def forward(at, previous):
@@ -281,7 +280,7 @@
             pltpu.VMEM((128, channels), jnp.float32),
             pltpu.SemaphoreType.DMA((4,)),
         ],
-        compiler_params=pltpu.CompilerParams(vmem_limit_bytes=16 << 20),
+        compiler_params=pltpu.CompilerParams(vmem_limit_bytes=56 << 20),
         name="pick_halo",
     )(send_lists.reshape(halo_rows), *parts)
     later_grad, outgoing = lax.optimization_barrier((coarse_grad, outgoing))
@@ -299,11 +298,10 @@
             jax.ShapeDtypeStruct((coarse_tile, out_channels), jnp.bfloat16),
             jax.ShapeDtypeStruct((total, channels), jnp.bfloat16),
         ),
-        in_specs=[smem] + [anywhere] * 11 + [vmem] * 2,
+        in_specs=[smem] + [anywhere] * 4 + [vmem] + [anywhere] * 6 + [vmem] * 2,
         out_specs=(vmem, vmem),
         scratch_shapes=[
             pltpu.VMEM((tile_rows, channels), jnp.bfloat16),
-            pltpu.VMEM((halo_rows, channels), jnp.bfloat16),
             pltpu.VMEM((tile_rows + halo_rows + 8, channels), jnp.float32),
             pltpu.VMEM((rows, channels), jnp.float32),
             pltpu.VMEM((offsets, rows, channels), jnp.bfloat16),
@@ -311,7 +309,7 @@
             pltpu.VMEM(conv_weight.shape, jnp.bfloat16),
             pltpu.VMEM(down_weight.shape, jnp.bfloat16),
             pltpu.VMEM((coarse_tile, out_channels), jnp.bfloat16),
-            pltpu.SemaphoreType.DMA((11,)),
+            pltpu.SemaphoreType.DMA((10,)),
         ],
         compiler_params=pltpu.CompilerParams(vmem_limit_bytes=56 << 20),
         name="step",

time: 147 us -> 137 us (0.932)
  waiting for transfers between devices: 51.8 us -> 45.6 us
  starting transfers between devices: 56.2 us -> 51.6 us
    all_to_all x1, waiting for transfers between devices: 9.3 us -> 2.65 us  [sum_over_devices(): lax.all_to_all(shares, 'x', split_axis=0, concat_axis=0, tiled=True)]
    ppermute x23, starting transfers between devices: 37.2 us -> 33.1 us  [send(): return lax.ppermute(value, AXES, partner_pairs(partner))]
  transfers between devices with their start and end apart: 25 -> 25, of which waited for: 23 -> 18; matrix products, arithmetic and copies ran while one was open for 3% -> 3% of each run, Pallas kernels for 0% -> 0%
where the time goes in v5:
time: 137 us
  starting transfers between devices  51.6 us (38%)
  waiting for transfers between devices  45.6 us (33%)
  Pallas kernels  27.3 us (20%)
  local copies, waits for them, and re-layouts  8.55 us (6%)
  other arithmetic  2.92 us (2%)
    ppermute x23, waiting for transfers between devices, send(): return lax.ppermute(value, AXES, partner_pairs(partner))  34.7 us
    ppermute x23, starting transfers between devices, send(): return lax.ppermute(value, AXES, partner_pairs(partner))  33.1 us
    pallas_call x1, Pallas kernels, shards(): pl.pallas_call(step_kernel, out_shape=(jax.ShapeDtypeStruct((coarse_tile,...  22.6 us
    all_to_all x1, starting transfers between devices, shards(): lax.all_to_all(outgoing.reshape(tiles, slots, channels), TILE, split_axis...  15.1 us
    all_to_all x1, waiting for transfers between devices, shards(): lax.all_to_all(outgoing.reshape(tiles, slots, channels), TILE, split_axis...  8.24 us
    pallas_call x1, Pallas kernels, shards(): pl.pallas_call(pick_halo, out_shape=jax.ShapeDtypeStruct((halo_rows, chan...  4.71 us
    all_to_all x1, starting transfers between devices, sum_over_devices(): lax.all_to_all(shares, 'x', split_axis=0, concat_axis=0, tiled=True)  3.47 us
    unnamed x23, local copies, waits for them, and re-layouts  2.89 us
  transfers between devices with their start and end apart: 25, of which 18 were waited for; matrix products, arithmetic and copies ran while one was open for 3% of the time, Pallas kernels for 0%

profile of v5, /device:TPU:1, one launch (start us, length us, event | category | flops | bytes accessed | tf_op | source)
XLA Modules:
  0.0 136.9 jit_solution(9697000724685843975)
XLA Ops:
  0.7 3.4 %collective-permute-start.2 = (bf16[512,128]{1,0:T(8,128)(2,1)}, bf16[512,128]{1,0:T(8,128)(2,1)S(1)}, u32[]{:S(2)}, u32[]{:S(2)}) collective-permute-start(bf16[512,128]{1,0:T(8,128)(2,1)} %part0.3), channel_id=1, source_target_pairs={{0,3},{1,2},{2,1},{3,0},{4,7},{5,6},{6,5},{7,4},{8,11},{9,10},{10,... | collective-permute-start | bytes 393224 | tf_op jit(solution)/shard_map/ppermute | solution.py:31
  6.2 2.4 %collective-permute-done.2.part3 = bf16[512,128]{1,0:T(8,128)(2,1)S(1)} collective-permute-done((bf16[512,128]{1,0:T(8,128)(2,1)}, bf16[512,128]{1,0:T(8,128)(2,1)S(1)}, u32[]{:S(2)}, u32[]{:S(2)}) %collective-permute-start.2) | collective-permute-done | bytes 131104 | tf_op jit(solution)/shard_map/ppermute | solution.py:31
  11.0 4.7 %pick_halo.1 = bf16[2048,128]{1,0:T(8,128)(2,1)} custom-call(s32[2048]{0:T(1024)} %reshape.59.lists, bf16[512,128]{1,0:T(8,128)(2,1)} %part0.3, bf16[512,128]{1,0:T(8,128)(2,1)} %copy-done.4, bf16[512,128]{1,0:T(8,128)(2,1)} %copy-done.3, bf16[512,128]{1,0:T(8,128)(2,1)} %copy-done.2), custom_call_target="tpu_custom_call" | custom-call | tf_op jit(solution)/shard_map/pick_halo/pallas_call | solution.py:272
  15.7 15.1 %all-to-all-start = ((bf16[64,32,128]{2,1,0:T(8,128)(2,1)}), bf16[64,32,128]{2,1,0:T(8,128)(2,1)S(1)}, u32[]{:S(2)}, u32[]{:S(2)}) async-start(bf16[64,32,128]{2,1,0:T(8,128)(2,1)} %bitcast.69), calls=%async_computation | async-start | bytes 1048576 | tf_op jit(solution)/shard_map/all_to_all | solution.py:287
  30.8 1.3 collective-permute-start.5
  32.6 1.5 %collective-permute-start.3 = (bf16[256,256]{1,0:T(8,128)(2,1)S(1)}, bf16[256,256]{1,0:T(8,128)(2,1)S(1)}, u32[]{:S(2)}, u32[]{:S(2)}) collective-permute-start(bf16[256,256]{1,0:T(8,128)(2,1)S(1)} %copy-done.5), channel_id=1, source_target_pairs={{0,1},{1,0},{2,3},{3,2},{4,5},{5,4},{6,7},{7,6},{8,9},{9,8},{10,11... | collective-permute-start | bytes 393224 | tf_op jit(solution)/shard_map/ppermute | solution.py:31
  36.4 2.3 %collective-permute-done.5.grad3 = bf16[256,256]{1,0:T(8,128)(2,1)S(1)} collective-permute-done((bf16[256,256]{1,0:T(8,128)(2,1)S(1)}, bf16[256,256]{1,0:T(8,128)(2,1)S(1)}, u32[]{:S(2)}, u32[]{:S(2)}) %collective-permute-start.5) | collective-permute-done | bytes 131104 | tf_op jit(solution)/shard_map/ppermute | solution.py:31
  39.8 8.2 %all-to-all-done = bf16[64,32,128]{2,1,0:T(8,128)(2,1)S(1)} async-done(((bf16[64,32,128]{2,1,0:T(8,128)(2,1)}), bf16[64,32,128]{2,1,0:T(8,128)(2,1)S(1)}, u32[]{:S(2)}, u32[]{:S(2)}) %all-to-all-start) | async-done | bytes 524320 | tf_op jit(solution)/shard_map/all_to_all | solution.py:287
  48.9 22.6 %step.1 = (bf16[1024,256]{1,0:T(8,128)(2,1)}, bf16[5632,128]{1,0:T(8,128)(2,1)}) custom-call(s32[13824]{0:T(1024)} %reshape.58.kernel_map, bf16[512,128]{1,0:T(8,128)(2,1)} %part0.3, bf16[512,128]{1,0:T(8,128)(2,1)} %copy-done.4, bf16[512,128]{1,0:T(8,128)(2,1)} %copy-done.3, bf16[512,128]{1,0:T(8,128)(2,1)} %copy-done.2, bf16[2048,128]{1,0:T(8,128)(2,1)} %bitcast.70, ...), custom_call_target="tpu_custom_call" | custom-call | tf_op jit(solution)/shard_map/step/pallas_call | solution.py:295
  71.5 1.3 dynamic-slice_bitcast_fusion
  73.2 1.9 %collective-permute-done.6 = bf16[2816,128]{1,0:T(8,128)(2,1)S(1)} collective-permute-done((bf16[2816,128]{1,0:T(8,128)(2,1)S(1)}, bf16[2816,128]{1,0:T(8,128)(2,1)S(1)}, u32[]{:S(2)}, u32[]{:S(2)}) %collective-permute-start.6) | collective-permute-done | bytes 720928 | tf_op jit(solution)/shard_map/ppermute | solution.py:31
  75.4 2.4 %collective-permute-start.9 = (bf16[704,128]{1,0:T(8,128)(2,1)S(1)}, bf16[704,128]{1,0:T(8,128)(2,1)S(1)}, u32[]{:S(2)}, u32[]{:S(2)}) collective-permute-start(bf16[704,128]{1,0:T(8,128)(2,1)S(1)} %get-tuple-element.28), channel_id=1, source_target_pairs={{0,195},{1,194},{2,193},{3,192},{4,69},{5,68},{6,71},{7,70},{8,203... | collective-permute-start | bytes 540680 | tf_op jit(solution)/shard_map/ppermute | solution.py:31
  78.0 1.7 %collective-permute-done.7 = bf16[704,128]{1,0:T(8,128)(2,1)S(1)} collective-permute-done((bf16[704,128]{1,0:T(8,128)(2,1)S(1)}, bf16[704,128]{1,0:T(8,128)(2,1)S(1)}, u32[]{:S(2)}, u32[]{:S(2)}) %collective-permute-start.7) | collective-permute-done | bytes 180256 | tf_op jit(solution)/shard_map/ppermute | solution.py:31
  79.7 3.0 %collective-permute-done.9 = bf16[704,128]{1,0:T(8,128)(2,1)S(1)} collective-permute-done((bf16[704,128]{1,0:T(8,128)(2,1)S(1)}, bf16[704,128]{1,0:T(8,128)(2,1)S(1)}, u32[]{:S(2)}, u32[]{:S(2)}) %collective-permute-start.9) | collective-permute-done | bytes 180256 | tf_op jit(solution)/shard_map/ppermute | solution.py:31
  82.7 1.7 %collective-permute-done.8 = bf16[704,128]{1,0:T(8,128)(2,1)S(1)} collective-permute-done((bf16[704,128]{1,0:T(8,128)(2,1)S(1)}, bf16[704,128]{1,0:T(8,128)(2,1)S(1)}, u32[]{:S(2)}, u32[]{:S(2)}) %collective-permute-start.8) | collective-permute-done | bytes 180256 | tf_op jit(solution)/shard_map/ppermute | solution.py:31
  84.5 1.4 %collective-permute-start.10 = (bf16[176,128]{1,0:T(8,128)(2,1)S(1)}, bf16[176,128]{1,0:T(8,128)(2,1)S(1)}, u32[]{:S(2)}, u32[]{:S(2)}) collective-permute-start(bf16[176,128]{1,0:T(8,128)(2,1)S(1)} %get-tuple-element.34), channel_id=1, source_target_pairs={{0,1},{1,0},{2,3},{3,2},{4,7},{5,6},{6,5},{7,4},{8,9},{9,8},{10,11... | collective-permute-start | bytes 135176 | tf_op jit(solution)/shard_map/ppermute | solution.py:31
  85.9 3.1 %collective-permute-start.12 = (bf16[176,128]{1,0:T(8,128)(2,1)S(1)}, bf16[176,128]{1,0:T(8,128)(2,1)S(1)}, u32[]{:S(2)}, u32[]{:S(2)}) collective-permute-start(bf16[176,128]{1,0:T(8,128)(2,1)S(1)} %get-tuple-element.35), channel_id=1, source_target_pairs={{0,65},{1,64},{2,67},{3,66},{4,199},{5,198},{6,197},{7,196},{8,73}... | collective-permute-start | bytes 135176 | tf_op jit(solution)/shard_map/ppermute | solution.py:31
  89.8 2.3 %collective-permute-done.12 = bf16[176,128]{1,0:T(8,128)(2,1)S(1)} collective-permute-done((bf16[176,128]{1,0:T(8,128)(2,1)S(1)}, bf16[176,128]{1,0:T(8,128)(2,1)S(1)}, u32[]{:S(2)}, u32[]{:S(2)}) %collective-permute-start.12) | collective-permute-done | bytes 45088 | tf_op jit(solution)/shard_map/ppermute | solution.py:31
  93.4 2.9 %collective-permute-done.13 = bf16[176,128]{1,0:T(8,128)(2,1)S(1)} collective-permute-done((bf16[176,128]{1,0:T(8,128)(2,1)S(1)}, bf16[176,128]{1,0:T(8,128)(2,1)S(1)}, u32[]{:S(2)}, u32[]{:S(2)}) %collective-permute-start.13) | collective-permute-done | bytes 45088 | tf_op jit(solution)/shard_map/ppermute | solution.py:31
  96.3 1.2 collective-permute-start.14
  97.5 3.5 %all-to-all-start.1 = ((bf16[4,256,256]{2,1,0:T(8,128)(2,1)}), bf16[4,256,256]{2,1,0:T(8,128)(2,1)S(1)}, u32[]{:S(2)}, u32[]{:S(2)}) async-start(bf16[4,256,256]{2,1,0:T(8,128)(2,1)} %bitcast.17), calls=%async_computation.1 | async-start | bytes 1048576 | tf_op jit(solution)/shard_map/all_to_all | solution.py:115
  101.1 4.1 %collective-permute-done.15 = bf16[176,128]{1,0:T(8,128)(2,1)S(1)} collective-permute-done((bf16[176,128]{1,0:T(8,128)(2,1)S(1)}, bf16[176,128]{1,0:T(8,128)(2,1)S(1)}, u32[]{:S(2)}, u32[]{:S(2)}) %collective-permute-start.15) | collective-permute-done | bytes 45088 | tf_op jit(solution)/shard_map/ppermute | solution.py:31
  105.2 2.6 %all-to-all-done.1 = bf16[4,256,256]{2,1,0:T(8,128)(2,1)S(1)} async-done(((bf16[4,256,256]{2,1,0:T(8,128)(2,1)}), bf16[4,256,256]{2,1,0:T(8,128)(2,1)S(1)}, u32[]{:S(2)}, u32[]{:S(2)}) %all-to-all-start.1) | async-done | bytes 524320 | tf_op jit(solution)/shard_map/all_to_all | solution.py:115
  109.6 1.5 %collective-permute-start.17 = (bf16[176,128]{1,0:T(8,128)(2,1)S(1)}, bf16[176,128]{1,0:T(8,128)(2,1)S(1)}, u32[]{:S(2)}, u32[]{:S(2)}) collective-permute-start(bf16[176,128]{1,0:T(8,128)(2,1)S(1)} %add_convert_fusion), channel_id=1, source_target_pairs={{0,64},{1,65},{2,66},{3,67},{4,196},{5,197},{6,198},{7,199},{8,72}... | collective-permute-start | bytes 135176 | tf_op jit(solution)/shard_map/ppermute | solution.py:31
  111.1 2.6 %collective-permute-start.16 = (bf16[176,128]{1,0:T(8,128)(2,1)S(1)}, bf16[176,128]{1,0:T(8,128)(2,1)S(1)}, u32[]{:S(2)}, u32[]{:S(2)}) collective-permute-start(bf16[176,128]{1,0:T(8,128)(2,1)S(1)} %add_convert_fusion), channel_id=1, source_target_pairs={{0,65},{1,64},{2,67},{3,66},{4,199},{5,198},{6,197},{7,196},{8,73}... | collective-permute-start | bytes 135176 | tf_op jit(solution)/shard_map/ppermute | solution.py:31
  113.7 3.6 %collective-permute-done.16 = bf16[176,128]{1,0:T(8,128)(2,1)S(1)} collective-permute-done((bf16[176,128]{1,0:T(8,128)(2,1)S(1)}, bf16[176,128]{1,0:T(8,128)(2,1)S(1)}, u32[]{:S(2)}, u32[]{:S(2)}) %collective-permute-start.16) | collective-permute-done | bytes 45088 | tf_op jit(solution)/shard_map/ppermute | solution.py:31
  117.5 2.5 %collective-permute-start.19 = (bf16[704,128]{1,0:T(8,128)(2,1)S(1)}, bf16[704,128]{1,0:T(8,128)(2,1)S(1)}, u32[]{:S(2)}, u32[]{:S(2)}) collective-permute-start(bf16[704,128]{1,0:T(8,128)(2,1)S(1)} %bitcast.77), channel_id=1, source_target_pairs={{0,195},{1,194},{2,193},{3,192},{4,69},{5,68},{6,71},{7,70},{8,203... | collective-permute-start | bytes 540680 | tf_op jit(solution)/shard_map/ppermute | solution.py:31
  120.1 1.7 %collective-permute-done.21 = bf16[704,128]{1,0:T(8,128)(2,1)S(1)} collective-permute-done((bf16[704,128]{1,0:T(8,128)(2,1)S(1)}, bf16[704,128]{1,0:T(8,128)(2,1)S(1)}, u32[]{:S(2)}, u32[]{:S(2)}) %collective-permute-start.21) | collective-permute-done | bytes 180256 | tf_op jit(solution)/shard_map/ppermute | solution.py:31
  121.8 2.0 %collective-permute-done.20 = bf16[704,128]{1,0:T(8,128)(2,1)S(1)} collective-permute-done((bf16[704,128]{1,0:T(8,128)(2,1)S(1)}, bf16[704,128]{1,0:T(8,128)(2,1)S(1)}, u32[]{:S(2)}, u32[]{:S(2)}) %collective-permute-start.20) | collective-permute-done | bytes 180256 | tf_op jit(solution)/shard_map/ppermute | solution.py:31
  124.0 8.1 %collective-permute-start.22 = (bf16[2816,128]{1,0:T(8,128)(2,1)S(1)}, bf16[2816,128]{1,0:T(8,128)(2,1)S(1)}, u32[]{:S(2)}, u32[]{:S(2)}) collective-permute-start(bf16[2816,128]{1,0:T(8,128)(2,1)S(1)} %bitcast.68), channel_id=1, source_target_pairs={{0,4},{1,5},{2,6},{3,7},{4,0},{5,1},{6,2},{7,3},{8,12},{9,13},{10,... | collective-permute-start | bytes 2162696 | tf_op jit(solution)/shard_map/ppermute | solution.py:31
  132.0 1.8 %collective-permute-done.22 = bf16[2816,128]{1,0:T(8,128)(2,1)S(1)} collective-permute-done((bf16[2816,128]{1,0:T(8,128)(2,1)S(1)}, bf16[2816,128]{1,0:T(8,128)(2,1)S(1)}, u32[]{:S(2)}, u32[]{:S(2)}) %collective-permute-start.22) | collective-permute-done | bytes 720928 | tf_op jit(solution)/shard_map/ppermute | solution.py:31
  134.5 1.3 slice.15
  (67 shorter events, 16.4 us)
Async XLA Ops:
  0.6 30.1 %copy-start.5 = (bf16[256,256]{1,0:T(8,128)(2,1)S(1)}, bf16[256,256]{1,0:T(8,128)(2,1)}, u32[]{:S(2)}) copy-start(bf16[256,256]{1,0:T(8,128)(2,1)} %grad0) | copy-start | bytes 393220
  0.6 33.5 %copy-start.9 = (s32[27,512]{1,0:T(8,128)S(1)}, s32[27,512]{1,0:T(8,128)}, u32[]{:S(2)}) copy-start(s32[27,512]{1,0:T(8,128)} %param.8) | copy-start | bytes 165892
  0.7 7.9 %collective-permute-start.2 = (bf16[512,128]{1,0:T(8,128)(2,1)}, bf16[512,128]{1,0:T(8,128)(2,1)S(1)}, u32[]{:S(2)}, u32[]{:S(2)}) collective-permute-start(bf16[512,128]{1,0:T(8,128)(2,1)} %part0.3), channel_id=1, source_target_pairs={{0,3},{1,2},{2,1},{3,0},{4,7},{5,6},{6,5},{7,4},{8,11},{9,10},{10,... | collective-permute-start | bytes 393224 | tf_op jit(solution)/shard_map/ppermute | solution.py:31
  4.0 5.6 %collective-permute-start.1 = (bf16[512,128]{1,0:T(8,128)(2,1)}, bf16[512,128]{1,0:T(8,128)(2,1)S(1)}, u32[]{:S(2)}, u32[]{:S(2)}) collective-permute-start(bf16[512,128]{1,0:T(8,128)(2,1)} %part0.3), channel_id=1, source_target_pairs={{0,2},{1,3},{2,0},{3,1},{4,6},{5,7},{6,4},{7,5},{8,10},{9,11},{10,... | collective-permute-start | bytes 393224 | tf_op jit(solution)/shard_map/ppermute | solution.py:31
  4.6 5.1 %collective-permute-start = (bf16[512,128]{1,0:T(8,128)(2,1)}, bf16[512,128]{1,0:T(8,128)(2,1)S(1)}, u32[]{:S(2)}, u32[]{:S(2)}) collective-permute-start(bf16[512,128]{1,0:T(8,128)(2,1)} %part0.3), channel_id=1, source_target_pairs={{0,1},{1,0},{2,3},{3,2},{4,5},{5,4},{6,7},{7,6},{8,9},{9,8},{10,11... | collective-permute-start | bytes 393224 | tf_op jit(solution)/shard_map/ppermute | solution.py:31
  15.7 32.4 %all-to-all-start = ((bf16[64,32,128]{2,1,0:T(8,128)(2,1)}), bf16[64,32,128]{2,1,0:T(8,128)(2,1)S(1)}, u32[]{:S(2)}, u32[]{:S(2)}) async-start(bf16[64,32,128]{2,1,0:T(8,128)(2,1)} %bitcast.69), calls=%async_computation | async-start | bytes 1048576 | tf_op jit(solution)/shard_map/all_to_all | solution.py:287
  30.8 7.9 %collective-permute-start.5 = (bf16[256,256]{1,0:T(8,128)(2,1)S(1)}, bf16[256,256]{1,0:T(8,128)(2,1)S(1)}, u32[]{:S(2)}, u32[]{:S(2)}) collective-permute-start(bf16[256,256]{1,0:T(8,128)(2,1)S(1)} %copy-done.5), channel_id=1, source_target_pairs={{0,3},{1,2},{2,1},{3,0},{4,7},{5,6},{6,5},{7,4},{8,11},{9,10},{10,... | collective-permute-start | bytes 393224 | tf_op jit(solution)/shard_map/ppermute | solution.py:31
  32.0 6.7 %collective-permute-start.4 = (bf16[256,256]{1,0:T(8,128)(2,1)S(1)}, bf16[256,256]{1,0:T(8,128)(2,1)S(1)}, u32[]{:S(2)}, u32[]{:S(2)}) collective-permute-start(bf16[256,256]{1,0:T(8,128)(2,1)S(1)} %copy-done.5), channel_id=1, source_target_pairs={{0,2},{1,3},{2,0},{3,1},{4,6},{5,7},{6,4},{7,5},{8,10},{9,11},{10,... | collective-permute-start | bytes 393224 | tf_op jit(solution)/shard_map/ppermute | solution.py:31
  32.6 7.2 %collective-permute-start.3 = (bf16[256,256]{1,0:T(8,128)(2,1)S(1)}, bf16[256,256]{1,0:T(8,128)(2,1)S(1)}, u32[]{:S(2)}, u32[]{:S(2)}) collective-permute-start(bf16[256,256]{1,0:T(8,128)(2,1)S(1)} %copy-done.5), channel_id=1, source_target_pairs={{0,1},{1,0},{2,3},{3,2},{4,5},{5,4},{6,7},{7,6},{8,9},{9,8},{10,11... | collective-permute-start | bytes 393224 | tf_op jit(solution)/shard_map/ppermute | solution.py:31
  35.5 12.6 %copy-start.10 = (s32[512]{0:T(512)}, s32[512]{0:T(512)S(1)}, u32[]{:S(2)}) copy-start(s32[512]{0:T(512)S(1)} %dynamic_slice.36) | copy-start | bytes 6148
  38.7 9.4 %copy-start.6 = (bf16[256,256]{1,0:T(8,128)(2,1)}, bf16[256,256]{1,0:T(8,128)(2,1)S(1)}, u32[]{:S(2)}) copy-start(bf16[256,256]{1,0:T(8,128)(2,1)S(1)} %collective-permute-done.5.grad3) | copy-start | bytes 393220
  38.7 9.4 %copy-start.7 = (bf16[256,256]{1,0:T(8,128)(2,1)}, bf16[256,256]{1,0:T(8,128)(2,1)S(1)}, u32[]{:S(2)}) copy-start(bf16[256,256]{1,0:T(8,128)(2,1)S(1)} %collective-permute-done.4.grad2) | copy-start | bytes 393220
  39.8 8.3 %copy-start.8 = (bf16[256,256]{1,0:T(8,128)(2,1)}, bf16[256,256]{1,0:T(8,128)(2,1)S(1)}, u32[]{:S(2)}) copy-start(bf16[256,256]{1,0:T(8,128)(2,1)S(1)} %collective-permute-done.3.grad1) | copy-start | bytes 393220
  71.5 3.6 %copy-start.1 = (bf16[5632,128]{1,0:T(8,128)(2,1)S(1)}, bf16[5632,128]{1,0:T(8,128)(2,1)}, u32[]{:S(2)}) copy-start(bf16[5632,128]{1,0:T(8,128)(2,1)} %get-tuple-element.13) | copy-start | bytes 4325380
  72.8 2.3 %collective-permute-start.6 = (bf16[2816,128]{1,0:T(8,128)(2,1)S(1)}, bf16[2816,128]{1,0:T(8,128)(2,1)S(1)}, u32[]{:S(2)}, u32[]{:S(2)}) collective-permute-start(bf16[2816,128]{1,0:T(8,128)(2,1)S(1)} %dynamic-slice_bitcast_fusion), channel_id=1, source_target_pairs={{0,4},{1,5},{2,6},{3,7},{4,0},{5,1},{6,2},{7,3},{8,12},{9,13},{10,... | collective-permute-start | bytes 2162696 | tf_op jit(solution)/shard_map/ppermute | solution.py:31
  75.3 4.4 %collective-permute-start.7 = (bf16[704,128]{1,0:T(8,128)(2,1)S(1)}, bf16[704,128]{1,0:T(8,128)(2,1)S(1)}, u32[]{:S(2)}, u32[]{:S(2)}) collective-permute-start(bf16[704,128]{1,0:T(8,128)(2,1)S(1)} %get-tuple-element.27), channel_id=1, source_target_pairs={{0,3},{1,2},{2,1},{3,0},{4,5},{5,4},{6,7},{7,6},{8,11},{9,10},{10,... | collective-permute-start | bytes 540680 | tf_op jit(solution)/shard_map/ppermute | solution.py:31
  75.4 7.3 %collective-permute-start.9 = (bf16[704,128]{1,0:T(8,128)(2,1)S(1)}, bf16[704,128]{1,0:T(8,128)(2,1)S(1)}, u32[]{:S(2)}, u32[]{:S(2)}) collective-permute-start(bf16[704,128]{1,0:T(8,128)(2,1)S(1)} %get-tuple-element.28), channel_id=1, source_target_pairs={{0,195},{1,194},{2,193},{3,192},{4,69},{5,68},{6,71},{7,70},{8,203... | collective-permute-start | bytes 540680 | tf_op jit(solution)/shard_map/ppermute | solution.py:31
  77.8 6.6 %collective-permute-start.8 = (bf16[704,128]{1,0:T(8,128)(2,1)S(1)}, bf16[704,128]{1,0:T(8,128)(2,1)S(1)}, u32[]{:S(2)}, u32[]{:S(2)}) collective-permute-start(bf16[704,128]{1,0:T(8,128)(2,1)S(1)} %get-tuple-element.29), channel_id=1, source_target_pairs={{0,192},{1,193},{2,194},{3,195},{4,68},{5,69},{6,70},{7,71},{8,200... | collective-permute-start | bytes 540680 | tf_op jit(solution)/shard_map/ppermute | solution.py:31
  84.5 5.3 %collective-permute-start.10 = (bf16[176,128]{1,0:T(8,128)(2,1)S(1)}, bf16[176,128]{1,0:T(8,128)(2,1)S(1)}, u32[]{:S(2)}, u32[]{:S(2)}) collective-permute-start(bf16[176,128]{1,0:T(8,128)(2,1)S(1)} %get-tuple-element.34), channel_id=1, source_target_pairs={{0,1},{1,0},{2,3},{3,2},{4,7},{5,6},{6,5},{7,4},{8,9},{9,8},{10,11... | collective-permute-start | bytes 135176 | tf_op jit(solution)/shard_map/ppermute | solution.py:31
  85.9 6.2 %collective-permute-start.12 = (bf16[176,128]{1,0:T(8,128)(2,1)S(1)}, bf16[176,128]{1,0:T(8,128)(2,1)S(1)}, u32[]{:S(2)}, u32[]{:S(2)}) collective-permute-start(bf16[176,128]{1,0:T(8,128)(2,1)S(1)} %get-tuple-element.35), channel_id=1, source_target_pairs={{0,65},{1,64},{2,67},{3,66},{4,199},{5,198},{6,197},{7,196},{8,73}... | collective-permute-start | bytes 135176 | tf_op jit(solution)/shard_map/ppermute | solution.py:31
  89.1 4.2 %collective-permute-start.11 = (bf16[176,128]{1,0:T(8,128)(2,1)S(1)}, bf16[176,128]{1,0:T(8,128)(2,1)S(1)}, u32[]{:S(2)}, u32[]{:S(2)}) collective-permute-start(bf16[176,128]{1,0:T(8,128)(2,1)S(1)} %get-tuple-element.36), channel_id=1, source_target_pairs={{0,64},{1,65},{2,66},{3,67},{4,196},{5,197},{6,198},{7,199},{8,72}... | collective-permute-start | bytes 135176 | tf_op jit(solution)/shard_map/ppermute | solution.py:31
  93.3 3.0 %collective-permute-start.13 = (bf16[176,128]{1,0:T(8,128)(2,1)S(1)}, bf16[176,128]{1,0:T(8,128)(2,1)S(1)}, u32[]{:S(2)}, u32[]{:S(2)}) collective-permute-start(bf16[176,128]{1,0:T(8,128)(2,1)S(1)} %fusion.6), channel_id=1, source_target_pairs={{0,8},{1,9},{2,10},{3,11},{4,12},{5,13},{6,14},{7,15},{8,0},{9,1},... | collective-permute-start | bytes 135176 | tf_op jit(solution)/shard_map/ppermute | solution.py:31
  96.3 4.7 %collective-permute-start.14 = (bf16[176,128]{1,0:T(8,128)(2,1)S(1)}, bf16[176,128]{1,0:T(8,128)(2,1)S(1)}, u32[]{:S(2)}, u32[]{:S(2)}) collective-permute-start(bf16[176,128]{1,0:T(8,128)(2,1)S(1)} %add_convert_fusion.2), channel_id=1, source_target_pairs={{0,16},{1,17},{2,18},{3,19},{4,20},{5,21},{6,22},{7,23},{8,24},{9,... | collective-permute-start | bytes 135176 | tf_op jit(solution)/shard_map/ppermute | solution.py:31
  97.5 10.4 %all-to-all-start.1 = ((bf16[4,256,256]{2,1,0:T(8,128)(2,1)}), bf16[4,256,256]{2,1,0:T(8,128)(2,1)S(1)}, u32[]{:S(2)}, u32[]{:S(2)}) async-start(bf16[4,256,256]{2,1,0:T(8,128)(2,1)} %bitcast.17), calls=%async_computation.1 | async-start | bytes 1048576 | tf_op jit(solution)/shard_map/all_to_all | solution.py:115
  101.0 4.2 %collective-permute-start.15 = (bf16[176,128]{1,0:T(8,128)(2,1)S(1)}, bf16[176,128]{1,0:T(8,128)(2,1)S(1)}, u32[]{:S(2)}, u32[]{:S(2)}) collective-permute-start(bf16[176,128]{1,0:T(8,128)(2,1)S(1)} %add_convert_fusion.1), channel_id=1, source_target_pairs={{0,56},{1,57},{2,58},{3,59},{4,60},{5,61},{6,62},{7,63},{8,48},{9,... | collective-permute-start | bytes 135176 | tf_op jit(solution)/shard_map/ppermute | solution.py:31
  108.6 5.1 %collective-permute-start.18 = (bf16[176,128]{1,0:T(8,128)(2,1)S(1)}, bf16[176,128]{1,0:T(8,128)(2,1)S(1)}, u32[]{:S(2)}, u32[]{:S(2)}) collective-permute-start(bf16[176,128]{1,0:T(8,128)(2,1)S(1)} %add_convert_fusion), channel_id=1, source_target_pairs={{0,1},{1,0},{2,3},{3,2},{4,7},{5,6},{6,5},{7,4},{8,9},{9,8},{10,11... | collective-permute-start | bytes 135176 | tf_op jit(solution)/shard_map/ppermute | solution.py:31
  109.6 4.1 %collective-permute-start.17 = (bf16[176,128]{1,0:T(8,128)(2,1)S(1)}, bf16[176,128]{1,0:T(8,128)(2,1)S(1)}, u32[]{:S(2)}, u32[]{:S(2)}) collective-permute-start(bf16[176,128]{1,0:T(8,128)(2,1)S(1)} %add_convert_fusion), channel_id=1, source_target_pairs={{0,64},{1,65},{2,66},{3,67},{4,196},{5,197},{6,198},{7,199},{8,72}... | collective-permute-start | bytes 135176 | tf_op jit(solution)/shard_map/ppermute | solution.py:31
  111.1 6.2 %collective-permute-start.16 = (bf16[176,128]{1,0:T(8,128)(2,1)S(1)}, bf16[176,128]{1,0:T(8,128)(2,1)S(1)}, u32[]{:S(2)}, u32[]{:S(2)}) collective-permute-start(bf16[176,128]{1,0:T(8,128)(2,1)S(1)} %add_convert_fusion), channel_id=1, source_target_pairs={{0,65},{1,64},{2,67},{3,66},{4,199},{5,198},{6,197},{7,196},{8,73}... | collective-permute-start | bytes 135176 | tf_op jit(solution)/shard_map/ppermute | solution.py:31
  117.3 4.4 %collective-permute-start.21 = (bf16[704,128]{1,0:T(8,128)(2,1)S(1)}, bf16[704,128]{1,0:T(8,128)(2,1)S(1)}, u32[]{:S(2)}, u32[]{:S(2)}) collective-permute-start(bf16[704,128]{1,0:T(8,128)(2,1)S(1)} %bitcast.75), channel_id=1, source_target_pairs={{0,3},{1,2},{2,1},{3,0},{4,5},{5,4},{6,7},{7,6},{8,11},{9,10},{10,... | collective-permute-start | bytes 540680 | tf_op jit(solution)/shard_map/ppermute | solution.py:31
  117.4 6.4 %collective-permute-start.20 = (bf16[704,128]{1,0:T(8,128)(2,1)S(1)}, bf16[704,128]{1,0:T(8,128)(2,1)S(1)}, u32[]{:S(2)}, u32[]{:S(2)}) collective-permute-start(bf16[704,128]{1,0:T(8,128)(2,1)S(1)} %bitcast.76), channel_id=1, source_target_pairs={{0,192},{1,193},{2,194},{3,195},{4,68},{5,69},{6,70},{7,71},{8,200... | collective-permute-start | bytes 540680 | tf_op jit(solution)/shard_map/ppermute | solution.py:31
  117.5 6.3 %collective-permute-start.19 = (bf16[704,128]{1,0:T(8,128)(2,1)S(1)}, bf16[704,128]{1,0:T(8,128)(2,1)S(1)}, u32[]{:S(2)}, u32[]{:S(2)}) collective-permute-start(bf16[704,128]{1,0:T(8,128)(2,1)S(1)} %bitcast.77), channel_id=1, source_target_pairs={{0,195},{1,194},{2,193},{3,192},{4,69},{5,68},{6,71},{7,70},{8,203... | collective-permute-start | bytes 540680 | tf_op jit(solution)/shard_map/ppermute | solution.py:31
  124.0 9.9 %collective-permute-start.22 = (bf16[2816,128]{1,0:T(8,128)(2,1)S(1)}, bf16[2816,128]{1,0:T(8,128)(2,1)S(1)}, u32[]{:S(2)}, u32[]{:S(2)}) collective-permute-start(bf16[2816,128]{1,0:T(8,128)(2,1)S(1)} %bitcast.68), channel_id=1, source_target_pairs={{0,4},{1,5},{2,6},{3,7},{4,0},{5,1},{6,2},{7,3},{8,12},{9,13},{10,... | collective-permute-start | bytes 2162696 | tf_op jit(solution)/shard_map/ppermute | solution.py:31
  (4 other events, 3.2 us)

commit v6 on v5

--- a/solution.py
+++ b/solution.py
@@ -9,6 +9,7 @@
 AXES = ("y", "z", "core", "x")
 TILE = ("y", "z", "core")
 UNROLL = 32
+GRID_W, GRID_H = 8, 4
 
 
 def device_index(place):
@@ -66,11 +67,6 @@
     return lax.dynamic_index_in_dim(parts, digit, 0, keepdims=False)
 
 
-def scatter_pair(parts, digit, partner):
-    other = send(pick(parts, 1 - digit), partner)
-    return narrow(wide(pick(parts, digit)) + wide(other))
-
-
 def scatter_ring(parts, digit, ring):
     received = [send(pick(parts, digit ^ step), ring(step)) for step in (1, 2, 3)]
     total = wide(pick(parts, digit))
@@ -98,17 +94,15 @@
     return jnp.stack([first, second, third, fourth])
 
 
-def sum_over_devices(partial_sums, coarse):
+def sum_over_devices(mine, other, coarse):
     y, z, core, x = (lax.axis_index(name) for name in AXES)
     near_x, near_y = (x ^ (x >> 1)) & 1, (y ^ (y >> 1)) & 1
     far_x, far_y = x >> 1, y >> 1
     near, far = near_x + 2 * near_y, far_x + 2 * far_y
     ring_one = jnp.where(core == 0, far, near)
     ring_two = jnp.where(core == 0, near, far)
-    rows = partial_sums.shape[0] // (CORES * RING_X * RING_Y)
-    lanes = partial_sums.shape[1]
-    parts = partial_sums.reshape(CORES, RING_X * RING_Y * rows, lanes)
-    part = scatter_pair(parts, core, across_core)
+    rows, lanes = mine.shape[0] // (RING_X * RING_Y), mine.shape[1]
+    part = narrow(wide(mine) + wide(send(other, across_core)))
     part = scatter_ring(part.reshape(RING_X, RING_Y * rows, lanes), ring_one, first_ring)
     part, coarse = lax.optimization_barrier((part, coarse))
     shares = coarse.reshape(RING_X, coarse.shape[0] // RING_X, coarse.shape[1])
@@ -120,7 +114,7 @@
     part, coarse_out = lax.optimization_barrier((part, coarse_out))
     part = gather_ring(part, ring_two, second_ring).reshape(RING_Y * rows, lanes)
     part = gather_ring(part, ring_one, first_ring).reshape(RING_X * RING_Y * rows, lanes)
-    return wide(gather_pair(part, core, across_core)).reshape(partial_sums.shape), coarse_out
+    return wide(gather_pair(part, core, across_core)).reshape(-1, lanes), coarse_out
 
 
 def ring_x(step):
@@ -157,50 +151,85 @@
 
 def pick_halo(lists, part0, part1, part2, part3, out, tile_feats, table, stage, sems):
     tile_rows, channels = tile_feats.shape
-    block = stage.shape[0]
+    slots = stage.shape[0]
     copies = part_copies((part0, part1, part2, part3), tile_feats, sems, 0)
     for copy in copies:
         copy.start()
     table[pl.ds(tile_rows, 8), :] = jnp.zeros((8, channels), jnp.float32)
+    out[...] = jnp.zeros_like(out)
+    y, z, core = (lax.axis_index(name) for name in TILE)
+    own = (y * DEPTH_Z + z) * CORES + core
     for copy in copies:
         copy.wait()
     table[pl.ds(0, tile_rows), :] = tile_feats[...].astype(jnp.float32)
-
-    def body(block_id, carry):
-        first = pl.multiple_of(block_id * block, block)
-        copy_rows(table, stage, lists, first, block)
-        out[pl.ds(first, block), :] = stage[...].astype(jnp.bfloat16)
+    planes, lines = RING_X * RING_Y * DEPTH_Z * CORES // (RING_X * GRID_W * GRID_H), GRID_H
+
+    def body(at, carry):
+        line = own % (GRID_W * GRID_H) // GRID_W + at // 3 % 3 - 1
+        column = own % GRID_W + at % 3 - 1
+        inside = (line >= 0) & (line < lines) & (column >= 0) & (column < GRID_W)
+        tile = (at // 9 % planes * GRID_H + line) * GRID_W + column
+        tile = jnp.where(inside, tile, own)
+        first = pl.multiple_of(tile * slots, slots)
+        copy_rows(table, stage, lists, first, slots)
+        out[pl.ds(first, slots), :] = stage[...].astype(jnp.bfloat16)
         return carry
 
-    lax.fori_loop(0, out.shape[0] // block, body, 0)
+    lax.fori_loop(0, 9 * planes, body, 0)
+
+
+def grad_kernel(
+    grad0, grad1, grad2, grad3, down_weight, link_column, parent_out, hidden_out, tile_grad, sems
+):
+    copies = part_copies((grad0, grad1, grad2, grad3), tile_grad, sems, 0)
+    for copy in copies:
+        copy.start()
+    octants = down_weight.shape[0]
+    rows, channels = hidden_out.shape
+    link = link_column[...]
+    octant = link % octants
+    columns = lax.broadcasted_iota(jnp.int32, (rows, tile_grad.shape[0]), 1)
+    at_parent = ((link // octants) == columns).astype(jnp.bfloat16)
+    for copy in copies:
+        copy.wait()
+    parent_grad = matmul(at_parent, tile_grad[...]).astype(jnp.bfloat16)
+    hidden_grad = jnp.zeros((rows, channels), jnp.float32)
+    for o in range(octants):
+        back = matmul(parent_grad, down_weight[o], 1, 1)
+        hidden_grad += jnp.where(octant == o, back, 0.0)
+    parent_out[...] = parent_grad
+    hidden_out[...] = hidden_grad
 
 
 def step_kernel(
-    kernel_map, part0, part1, part2, part3, incoming, conv_hbm, down_hbm,
-    grad0, grad1, grad2, grad3, link_column, link_row,
-    coarse, sums,
-    tile_feats, table, stage, gathered, pre_act, conv_weight, down_weight, tile_grad, sems,
+    kernel_map, part0, part1, part2, part3, incoming, conv_hbm, down_hbm, parent_hbm, back_hbm,
+    link_column, link_row,
+    coarse, mine, other,
+    tile_feats, table, stage, gathered, pre_act, conv_weight, down_weight, parent_grad, back_grad, sems,
 ):
     rows, channels = part0.shape
     offsets = conv_weight.shape[0]
     octants, _, out_channels = down_weight.shape
     tile_rows, halo_rows = tile_feats.shape[0], incoming.shape[0]
-    coarse_tile = tile_grad.shape[0]
+    coarse_tile = coarse.shape[0]
     feats = part_copies((part0, part1, part2, part3), tile_feats, sems, 0)
     conv = pltpu.make_async_copy(conv_hbm, conv_weight, sems.at[4])
-    down = pltpu.make_async_copy(down_hbm, down_weight, sems.at[5])
-    grads = part_copies((grad0, grad1, grad2, grad3), tile_grad, sems, 6)
-    for copy in feats + [conv, down] + grads:
+    late = [
+        pltpu.make_async_copy(down_hbm, down_weight, sems.at[5]),
+        pltpu.make_async_copy(parent_hbm, parent_grad, sems.at[6]),
+        pltpu.make_async_copy(back_hbm, back_grad, sems.at[7]),
+    ]
+    for copy in feats + [conv] + late:
         copy.start()
     pre_act[...] = jnp.zeros_like(pre_act)
     table[pl.ds(tile_rows + halo_rows, 8), :] = jnp.zeros((8, channels), jnp.float32)
+    table[pl.ds(tile_rows, halo_rows), :] = incoming[...].astype(jnp.float32)
     for copy in feats:
         copy.wait()
     table[pl.ds(0, tile_rows), :] = tile_feats[...].astype(jnp.float32)
     middle = offsets // 2
     own = pl.multiple_of(lax.axis_index("x") * rows, rows)
     gathered[middle] = tile_feats[pl.ds(own, rows), :]
-    table[pl.ds(tile_rows, halo_rows), :] = incoming[...].astype(jnp.float32)
     conv.wait()
 
     def forward(at, previous):
@@ -211,51 +240,63 @@
         return offset
 
     last = lax.fori_loop(0, offsets - 1, forward, jnp.int32(middle))
-    pre_act[...] += matmul(gathered[last], conv_weight[last])
-
-    act = pre_act[...]
+    for copy in late:
+        copy.wait()
+    act = pre_act[...] + matmul(gathered[last], conv_weight[last])
     gate = 1.0 / (1.0 + jnp.exp(-act))
     hidden_wide = act * gate
     hidden = hidden_wide.astype(jnp.bfloat16)
     hidden_turned = hidden_wide.T.astype(jnp.bfloat16)
-    link = link_column[...]
-    octant = link % octants
+    pre_grad = back_grad[...] * gate * (1.0 + act * (1.0 - gate))
+    pre_grad_turned = pre_grad.T.astype(jnp.bfloat16)
+    octant = link_column[...] % octants
     link_turned = link_row[...]
     octant_turned = link_turned % octants
-    at_parent = (link // octants) == lax.broadcasted_iota(jnp.int32, (rows, coarse_tile), 1)
-    for copy in [down] + grads:
-        copy.wait()
-    parent_grad = matmul(at_parent.astype(jnp.bfloat16), tile_grad[...]).astype(jnp.bfloat16)
     own_term = jnp.zeros((rows, out_channels), jnp.float32)
-    hidden_grad = jnp.zeros((rows, channels), jnp.float32)
-    conv_rows = offsets * channels
     for o in range(octants):
-        hit = octant == o
-        weight = down_weight[o]
-        own_term += matmul(jnp.where(hit, hidden, jnp.zeros_like(hidden)), weight)
-        hidden_grad += jnp.where(hit, matmul(parent_grad, weight, 1, 1), 0.0)
-        only = jnp.where(octant_turned == o, hidden_turned, jnp.zeros_like(hidden_turned))
-        product = matmul(only, parent_grad).astype(jnp.bfloat16)
-        sums[pl.ds(conv_rows + o * channels, channels), :] = product[:, :channels]
-        sums[pl.ds(conv_rows + (octants + o) * channels, channels), :] = product[:, channels:]
-    pre_grad = hidden_grad * gate * (1.0 + act * (1.0 - gate))
-    pre_grad_turned = pre_grad.T.astype(jnp.bfloat16)
-
+        only = jnp.where(octant == o, hidden, jnp.zeros_like(hidden))
+        own_term += matmul(only, down_weight[o])
     from_row = (link_turned // octants) == lax.broadcasted_iota(jnp.int32, (coarse_tile, rows), 0)
     from_row = from_row.astype(jnp.bfloat16)
     high = own_term.astype(jnp.bfloat16)
     low = (own_term - high.astype(jnp.float32)).astype(jnp.bfloat16)
     coarse[...] = (matmul(from_row, high) + matmul(from_row, low)).astype(jnp.bfloat16)
 
-    def backward(offset, carry):
-        start = pl.multiple_of(offset * channels, channels)
-        turned = matmul(pre_grad_turned, gathered[offset])
-        sums[pl.ds(start, channels), :] = turned.T.astype(jnp.bfloat16)
-        return carry
-
-    lax.fori_loop(0, offsets, backward, 0, unroll=3)
-    used = conv_rows + 2 * octants * channels
-    sums[pl.ds(used, sums.shape[0] - used), :] = jnp.zeros((sums.shape[0] - used, channels), jnp.bfloat16)
+    half_blocks = mine.shape[0] // channels
+    down_first = offsets - half_blocks
+
+    def fill(first, second):
+        def backward(target, start):
+            def body(at, carry):
+                turned = matmul(pre_grad_turned, gathered[start + at])
+                place = pl.ds(pl.multiple_of(at * channels, channels), channels)
+                target[place, :] = turned.T.astype(jnp.bfloat16)
+                return carry
+
+            return body
+
+        lax.fori_loop(0, half_blocks, backward(first, 0), 0, unroll=2)
+        lax.fori_loop(0, down_first, backward(second, half_blocks), 0, unroll=True)
+        for o in range(octants):
+            only = jnp.where(octant_turned == o, hidden_turned, jnp.zeros_like(hidden_turned))
+            product = matmul(only, parent_grad[...]).astype(jnp.bfloat16)
+            left, right = (down_first + o) * channels, (down_first + octants + o) * channels
+            second[pl.ds(left, channels), :] = product[:, :channels]
+            second[pl.ds(right, channels), :] = product[:, channels:]
+        used = (down_first + 2 * octants) * channels
+        second[pl.ds(used, second.shape[0] - used), :] = jnp.zeros(
+            (second.shape[0] - used, channels), jnp.bfloat16
+        )
+
+    core = lax.axis_index("core")
+
+    @pl.when(core == 0)
+    def _():
+        fill(mine, other)
+
+    @pl.when(core == 1)
+    def _():
+        fill(other, mine)
 
 
 def shards(features, kernel_map, send_lists, fine_to_coarse, conv_weight, down_weight, coarse_grad):
@@ -277,7 +318,7 @@
         scratch_shapes=[
             pltpu.VMEM((tile_rows, channels), jnp.bfloat16),
             pltpu.VMEM((tile_rows + 8, channels), jnp.float32),
-            pltpu.VMEM((128, channels), jnp.float32),
+            pltpu.VMEM((slots, channels), jnp.float32),
             pltpu.SemaphoreType.DMA((4,)),
         ],
         compiler_params=pltpu.CompilerParams(vmem_limit_bytes=56 << 20),
@@ -292,14 +333,32 @@
     link = lax.dynamic_slice_in_dim(fine_to_coarse, x * rows, rows)
     used = offsets * channels + 2 * octants * channels
     total = used + (-used % 512)
-    coarse, sums = pl.pallas_call(
+    link_column, link_row = link.reshape(rows, 1), link.reshape(1, rows)
+    parent_grad, back_grad = pl.pallas_call(
+        grad_kernel,
+        out_shape=(
+            jax.ShapeDtypeStruct((rows, out_channels), jnp.bfloat16),
+            jax.ShapeDtypeStruct((rows, channels), jnp.float32),
+        ),
+        in_specs=[anywhere] * 4 + [vmem] * 2,
+        out_specs=(vmem, vmem),
+        scratch_shapes=[
+            pltpu.VMEM((coarse_tile, out_channels), jnp.bfloat16),
+            pltpu.SemaphoreType.DMA((4,)),
+        ],
+        compiler_params=pltpu.CompilerParams(vmem_limit_bytes=56 << 20),
+        name="coarse_back",
+    )(*grads, down_weight, link_column)
+    half = total // CORES
+    coarse, mine, other = pl.pallas_call(
         step_kernel,
         out_shape=(
             jax.ShapeDtypeStruct((coarse_tile, out_channels), jnp.bfloat16),
-            jax.ShapeDtypeStruct((total, channels), jnp.bfloat16),
+            jax.ShapeDtypeStruct((half, channels), jnp.bfloat16),
+            jax.ShapeDtypeStruct((half, channels), jnp.bfloat16),
         ),
-        in_specs=[smem] + [anywhere] * 4 + [vmem] + [anywhere] * 6 + [vmem] * 2,
-        out_specs=(vmem, vmem),
+        in_specs=[smem] + [anywhere] * 4 + [vmem] + [anywhere] * 4 + [vmem] * 2,
+        out_specs=(vmem, vmem, vmem),
         scratch_shapes=[
             pltpu.VMEM((tile_rows, channels), jnp.bfloat16),
             pltpu.VMEM((tile_rows + halo_rows + 8, channels), jnp.float32),
@@ -308,16 +367,17 @@
             pltpu.VMEM((rows, channels), jnp.float32),
             pltpu.VMEM(conv_weight.shape, jnp.bfloat16),
             pltpu.VMEM(down_weight.shape, jnp.bfloat16),
-            pltpu.VMEM((coarse_tile, out_channels), jnp.bfloat16),
-            pltpu.SemaphoreType.DMA((10,)),
+            pltpu.VMEM((rows, out_channels), jnp.bfloat16),
+            pltpu.VMEM((rows, channels), jnp.float32),
+            pltpu.SemaphoreType.DMA((8,)),
         ],
         compiler_params=pltpu.CompilerParams(vmem_limit_bytes=56 << 20),
         name="step",
     )(
         kernel_map.reshape(offsets * rows), *parts, incoming.reshape(halo_rows, channels),
-        conv_weight, down_weight, *grads, link.reshape(rows, 1), link.reshape(1, rows),
+        conv_weight, down_weight, parent_grad, back_grad, link_column, link_row,
     )
-    sums, coarse_out = sum_over_devices(sums, coarse)
+    sums, coarse_out = sum_over_devices(mine, other, coarse)
     conv_grad = sums[: offsets * channels].reshape(offsets, channels, channels)
     down_sums = sums[offsets * channels : used]
     half = octants * channels

time: 137 us -> 137 us (level)
  waiting for transfers between devices: 45.6 us -> 39 us
  Pallas kernels: 27.3 us -> 31 us
  starting transfers between devices: 51.6 us -> 54.1 us
    all_to_all x1, waiting for transfers between devices: 8.24 us -> 3.14 us  [shards(): lax.all_to_all(outgoing.reshape(tiles, slots, channels), TILE, split_axis...]
    pallas_call x0 -> x1, Pallas kernels: none -> 4.44 us  [shards(): pl.pallas_call(grad_kernel, out_shape=(jax.ShapeDtypeStruct((rows, out_ch...]
    ppermute x23, starting transfers between devices: 33.1 us -> 35.6 us  [send(): return lax.ppermute(value, AXES, partner_pairs(partner))]
    ppermute x23, waiting for transfers between devices: 34.7 us -> 33.2 us  [send(): return lax.ppermute(value, AXES, partner_pairs(partner))]
    unnamed x23 -> x21, local copies, waits for them, and re-layouts: 2.89 us -> 3.55 us
  transfers between devices with their start and end apart: 25 -> 25, of which waited for: 18 -> 18; matrix products, arithmetic and copies ran while one was open for 3% -> 3% of each run, Pallas kernels for 0% -> 3%
where the time goes in v6:
time: 137 us
  starting transfers between devices  54.1 us (39%)
  waiting for transfers between devices  39 us (28%)
  Pallas kernels  31 us (23%)
  local copies, waits for them, and re-layouts  7.94 us (6%)
  other arithmetic  4.03 us (3%)
    ppermute x23, starting transfers between devices, send(): return lax.ppermute(value, AXES, partner_pairs(partner))  35.6 us
    ppermute x23, waiting for transfers between devices, send(): return lax.ppermute(value, AXES, partner_pairs(partner))  33.2 us
    pallas_call x1, Pallas kernels, shards(): pl.pallas_call(step_kernel, out_shape=(jax.ShapeDtypeStruct((coarse_tile,...  22.6 us
    all_to_all x1, starting transfers between devices, shards(): lax.all_to_all(outgoing.reshape(tiles, slots, channels), TILE, split_axis...  15.1 us
    pallas_call x1, Pallas kernels, shards(): pl.pallas_call(grad_kernel, out_shape=(jax.ShapeDtypeStruct((rows, out_ch...  4.44 us
    pallas_call x1, Pallas kernels, shards(): pl.pallas_call(pick_halo, out_shape=jax.ShapeDtypeStruct((halo_rows, chan...  3.94 us
    unnamed x21, local copies, waits for them, and re-layouts  3.55 us
    all_to_all x1, starting transfers between devices, sum_over_devices(): lax.all_to_all(shares, 'x', split_axis=0, concat_axis=0, tiled=True)  3.47 us
  transfers between devices with their start and end apart: 25, of which 18 were waited for; matrix products, arithmetic and copies ran while one was open for 3% of the time, Pallas kernels for 3%

profile of v6, /device:TPU:1, one launch (start us, length us, event | category | flops | bytes accessed | tf_op | source)
XLA Modules:
  0.0 136.9 jit_solution(2232417074127523062)
XLA Ops:
  0.7 3.4 %collective-permute-start.2 = (bf16[512,128]{1,0:T(8,128)(2,1)}, bf16[512,128]{1,0:T(8,128)(2,1)S(1)}, u32[]{:S(2)}, u32[]{:S(2)}) collective-permute-start(bf16[512,128]{1,0:T(8,128)(2,1)} %part0.3), channel_id=1, source_target_pairs={{0,3},{1,2},{2,1},{3,0},{4,7},{5,6},{6,5},{7,4},{8,11},{9,10},{10,... | collective-permute-start | bytes 393224 | tf_op jit(solution)/shard_map/ppermute | solution.py:32
  6.2 2.4 %collective-permute-done.2.part3 = bf16[512,128]{1,0:T(8,128)(2,1)S(1)} collective-permute-done((bf16[512,128]{1,0:T(8,128)(2,1)}, bf16[512,128]{1,0:T(8,128)(2,1)S(1)}, u32[]{:S(2)}, u32[]{:S(2)}) %collective-permute-start.2) | collective-permute-done | bytes 131104 | tf_op jit(solution)/shard_map/ppermute | solution.py:32
  11.0 3.9 %pick_halo.1 = bf16[2048,128]{1,0:T(8,128)(2,1)} custom-call(s32[2048]{0:T(1024)} %reshape.54.lists, bf16[512,128]{1,0:T(8,128)(2,1)} %part0.3, bf16[512,128]{1,0:T(8,128)(2,1)} %copy-done.3, bf16[512,128]{1,0:T(8,128)(2,1)} %copy-done.2, bf16[512,128]{1,0:T(8,128)(2,1)} %copy-done.1), custom_call_target="tpu_custom_call" | custom-call | tf_op jit(solution)/shard_map/pick_halo/pallas_call | solution.py:313
  14.9 15.1 %all-to-all-start = ((bf16[64,32,128]{2,1,0:T(8,128)(2,1)}), bf16[64,32,128]{2,1,0:T(8,128)(2,1)S(1)}, u32[]{:S(2)}, u32[]{:S(2)}) async-start(bf16[64,32,128]{2,1,0:T(8,128)(2,1)} %bitcast.63), calls=%async_computation | async-start | bytes 1048576 | tf_op jit(solution)/shard_map/all_to_all | solution.py:328
  30.0 1.3 collective-permute-start.5
  31.9 1.5 %collective-permute-start.3 = (bf16[256,256]{1,0:T(8,128)(2,1)S(1)}, bf16[256,256]{1,0:T(8,128)(2,1)S(1)}, u32[]{:S(2)}, u32[]{:S(2)}) collective-permute-start(bf16[256,256]{1,0:T(8,128)(2,1)S(1)} %copy-done.4), channel_id=1, source_target_pairs={{0,1},{1,0},{2,3},{3,2},{4,5},{5,4},{6,7},{7,6},{8,9},{9,8},{10,11... | collective-permute-start | bytes 393224 | tf_op jit(solution)/shard_map/ppermute | solution.py:32
  35.6 2.3 %collective-permute-done.5.grad3 = bf16[256,256]{1,0:T(8,128)(2,1)S(1)} collective-permute-done((bf16[256,256]{1,0:T(8,128)(2,1)S(1)}, bf16[256,256]{1,0:T(8,128)(2,1)S(1)}, u32[]{:S(2)}, u32[]{:S(2)}) %collective-permute-start.5) | collective-permute-done | bytes 131104 | tf_op jit(solution)/shard_map/ppermute | solution.py:32
  39.7 4.4 %coarse_back.1 = (bf16[512,256]{1,0:T(8,128)(2,1)}, f32[512,128]{1,0:T(8,128)}) custom-call(bf16[256,256]{1,0:T(8,128)(2,1)} %grad0, bf16[256,256]{1,0:T(8,128)(2,1)} %copy-done.7, bf16[256,256]{1,0:T(8,128)(2,1)} %copy-done.6, bf16[256,256]{1,0:T(8,128)(2,1)} %copy-done.5, bf16[8,128,256]{2,1,0:T(8,128)(2,1)} %down_hbm.1, s32[512,1]{1,0:T(8,128)} %copy.11.link_column), custom_call_target="tpu_custom_call" | custom-call | tf_op jit(solution)/shard_map/coarse_back/pallas_call | solution.py:337
  44.2 3.1 %all-to-all-done = bf16[64,32,128]{2,1,0:T(8,128)(2,1)S(1)} async-done(((bf16[64,32,128]{2,1,0:T(8,128)(2,1)}), bf16[64,32,128]{2,1,0:T(8,128)(2,1)S(1)}, u32[]{:S(2)}, u32[]{:S(2)}) %all-to-all-start) | async-done | bytes 524320 | tf_op jit(solution)/shard_map/all_to_all | solution.py:328
  48.1 22.6 %step.1 = (bf16[1024,256]{1,0:T(8,128)(2,1)}, bf16[2816,128]{1,0:T(8,128)(2,1)}, bf16[2816,128]{1,0:T(8,128)(2,1)}) custom-call(s32[13824]{0:T(1024)} %reshape.53.kernel_map, bf16[512,128]{1,0:T(8,128)(2,1)} %part0.3, bf16[512,128]{1,0:T(8,128)(2,1)} %copy-done.3, bf16[512,128]{1,0:T(8,128)(2,1)} %copy-done.2, bf16[512,128]{1,0:T(8,128)(2,1)} %copy-done.1, ...), custom_call_target="tpu_custom_call" | custom-call | tf_op jit(solution)/shard_map/step/pallas_call | solution.py:353
  71.1 2.1 %collective-permute-done.6 = bf16[2816,128]{1,0:T(8,128)(2,1)S(1)} collective-permute-done((bf16[2816,128]{1,0:T(8,128)(2,1)}, bf16[2816,128]{1,0:T(8,128)(2,1)S(1)}, u32[]{:S(2)}, u32[]{:S(2)}) %collective-permute-start.6) | collective-permute-done | bytes 720928 | tf_op jit(solution)/shard_map/ppermute | solution.py:32
  73.2 1.3 add_convert_fusion
  74.9 2.4 %collective-permute-start.9 = (bf16[704,128]{1,0:T(8,128)(2,1)S(1)}, bf16[704,128]{1,0:T(8,128)(2,1)S(1)}, u32[]{:S(2)}, u32[]{:S(2)}) collective-permute-start(bf16[704,128]{1,0:T(8,128)(2,1)S(1)} %get-tuple-element.34), channel_id=1, source_target_pairs={{0,195},{1,194},{2,193},{3,192},{4,69},{5,68},{6,71},{7,70},{8,203... | collective-permute-start | bytes 540680 | tf_op jit(solution)/shard_map/ppermute | solution.py:32
  77.5 1.7 %collective-permute-done.7 = bf16[704,128]{1,0:T(8,128)(2,1)S(1)} collective-permute-done((bf16[704,128]{1,0:T(8,128)(2,1)S(1)}, bf16[704,128]{1,0:T(8,128)(2,1)S(1)}, u32[]{:S(2)}, u32[]{:S(2)}) %collective-permute-start.7) | collective-permute-done | bytes 180256 | tf_op jit(solution)/shard_map/ppermute | solution.py:32
  79.2 3.0 %collective-permute-done.9 = bf16[704,128]{1,0:T(8,128)(2,1)S(1)} collective-permute-done((bf16[704,128]{1,0:T(8,128)(2,1)S(1)}, bf16[704,128]{1,0:T(8,128)(2,1)S(1)}, u32[]{:S(2)}, u32[]{:S(2)}) %collective-permute-start.9) | collective-permute-done | bytes 180256 | tf_op jit(solution)/shard_map/ppermute | solution.py:32
  82.2 1.7 %collective-permute-done.8 = bf16[704,128]{1,0:T(8,128)(2,1)S(1)} collective-permute-done((bf16[704,128]{1,0:T(8,128)(2,1)S(1)}, bf16[704,128]{1,0:T(8,128)(2,1)S(1)}, u32[]{:S(2)}, u32[]{:S(2)}) %collective-permute-start.8) | collective-permute-done | bytes 180256 | tf_op jit(solution)/shard_map/ppermute | solution.py:32
  85.2 3.1 %collective-permute-start.12 = (bf16[176,128]{1,0:T(8,128)(2,1)S(1)}, bf16[176,128]{1,0:T(8,128)(2,1)S(1)}, u32[]{:S(2)}, u32[]{:S(2)}) collective-permute-start(bf16[176,128]{1,0:T(8,128)(2,1)S(1)} %get-tuple-element.41), channel_id=1, source_target_pairs={{0,65},{1,64},{2,67},{3,66},{4,199},{5,198},{6,197},{7,196},{8,73}... | collective-permute-start | bytes 135176 | tf_op jit(solution)/shard_map/ppermute | solution.py:32
  89.1 2.3 %collective-permute-done.12 = bf16[176,128]{1,0:T(8,128)(2,1)S(1)} collective-permute-done((bf16[176,128]{1,0:T(8,128)(2,1)S(1)}, bf16[176,128]{1,0:T(8,128)(2,1)S(1)}, u32[]{:S(2)}, u32[]{:S(2)}) %collective-permute-start.12) | collective-permute-done | bytes 45088 | tf_op jit(solution)/shard_map/ppermute | solution.py:32
  92.7 2.9 %collective-permute-done.13 = bf16[176,128]{1,0:T(8,128)(2,1)S(1)} collective-permute-done((bf16[176,128]{1,0:T(8,128)(2,1)S(1)}, bf16[176,128]{1,0:T(8,128)(2,1)S(1)}, u32[]{:S(2)}, u32[]{:S(2)}) %collective-permute-start.13) | collective-permute-done | bytes 45088 | tf_op jit(solution)/shard_map/ppermute | solution.py:32
  96.8 3.5 %all-to-all-start.1 = ((bf16[4,256,256]{2,1,0:T(8,128)(2,1)}), bf16[4,256,256]{2,1,0:T(8,128)(2,1)S(1)}, u32[]{:S(2)}, u32[]{:S(2)}) async-start(bf16[4,256,256]{2,1,0:T(8,128)(2,1)} %bitcast.14), calls=%async_computation.1 | async-start | bytes 1048576 | tf_op jit(solution)/shard_map/all_to_all | solution.py:109
  100.3 1.8 %collective-permute-start.15 = (bf16[176,128]{1,0:T(8,128)(2,1)S(1)}, bf16[176,128]{1,0:T(8,128)(2,1)S(1)}, u32[]{:S(2)}, u32[]{:S(2)}) collective-permute-start(bf16[176,128]{1,0:T(8,128)(2,1)S(1)} %add_convert_fusion.2), channel_id=1, source_target_pairs={{0,56},{1,57},{2,58},{3,59},{4,60},{5,61},{6,62},{7,63},{8,48},{9,... | collective-permute-start | bytes 135176 | tf_op jit(solution)/shard_map/ppermute | solution.py:32
  102.1 2.4 %collective-permute-done.15 = bf16[176,128]{1,0:T(8,128)(2,1)S(1)} collective-permute-done((bf16[176,128]{1,0:T(8,128)(2,1)S(1)}, bf16[176,128]{1,0:T(8,128)(2,1)S(1)}, u32[]{:S(2)}, u32[]{:S(2)}) %collective-permute-start.15) | collective-permute-done | bytes 45088 | tf_op jit(solution)/shard_map/ppermute | solution.py:32
  104.5 2.6 %all-to-all-done.1 = bf16[4,256,256]{2,1,0:T(8,128)(2,1)S(1)} async-done(((bf16[4,256,256]{2,1,0:T(8,128)(2,1)}), bf16[4,256,256]{2,1,0:T(8,128)(2,1)S(1)}, u32[]{:S(2)}, u32[]{:S(2)}) %all-to-all-start.1) | async-done | bytes 524320 | tf_op jit(solution)/shard_map/all_to_all | solution.py:109
  108.9 1.4 %collective-permute-start.17 = (bf16[176,128]{1,0:T(8,128)(2,1)S(1)}, bf16[176,128]{1,0:T(8,128)(2,1)S(1)}, u32[]{:S(2)}, u32[]{:S(2)}) collective-permute-start(bf16[176,128]{1,0:T(8,128)(2,1)S(1)} %add_convert_fusion.1), channel_id=1, source_target_pairs={{0,64},{1,65},{2,66},{3,67},{4,196},{5,197},{6,198},{7,199},{8,72}... | collective-permute-start | bytes 135176 | tf_op jit(solution)/shard_map/ppermute | solution.py:32
  110.3 2.7 %collective-permute-start.16 = (bf16[176,128]{1,0:T(8,128)(2,1)S(1)}, bf16[176,128]{1,0:T(8,128)(2,1)S(1)}, u32[]{:S(2)}, u32[]{:S(2)}) collective-permute-start(bf16[176,128]{1,0:T(8,128)(2,1)S(1)} %add_convert_fusion.1), channel_id=1, source_target_pairs={{0,65},{1,64},{2,67},{3,66},{4,199},{5,198},{6,197},{7,196},{8,73}... | collective-permute-start | bytes 135176 | tf_op jit(solution)/shard_map/ppermute | solution.py:32
  113.0 3.5 %collective-permute-done.16 = bf16[176,128]{1,0:T(8,128)(2,1)S(1)} collective-permute-done((bf16[176,128]{1,0:T(8,128)(2,1)S(1)}, bf16[176,128]{1,0:T(8,128)(2,1)S(1)}, u32[]{:S(2)}, u32[]{:S(2)}) %collective-permute-start.16) | collective-permute-done | bytes 45088 | tf_op jit(solution)/shard_map/ppermute | solution.py:32
  116.8 2.5 %collective-permute-start.19 = (bf16[704,128]{1,0:T(8,128)(2,1)S(1)}, bf16[704,128]{1,0:T(8,128)(2,1)S(1)}, u32[]{:S(2)}, u32[]{:S(2)}) collective-permute-start(bf16[704,128]{1,0:T(8,128)(2,1)S(1)} %bitcast.69), channel_id=1, source_target_pairs={{0,195},{1,194},{2,193},{3,192},{4,69},{5,68},{6,71},{7,70},{8,203... | collective-permute-start | bytes 540680 | tf_op jit(solution)/shard_map/ppermute | solution.py:32
  119.3 1.7 %collective-permute-done.21 = bf16[704,128]{1,0:T(8,128)(2,1)S(1)} collective-permute-done((bf16[704,128]{1,0:T(8,128)(2,1)S(1)}, bf16[704,128]{1,0:T(8,128)(2,1)S(1)}, u32[]{:S(2)}, u32[]{:S(2)}) %collective-permute-start.21) | collective-permute-done | bytes 180256 | tf_op jit(solution)/shard_map/ppermute | solution.py:32
  121.0 2.0 %collective-permute-done.20 = bf16[704,128]{1,0:T(8,128)(2,1)S(1)} collective-permute-done((bf16[704,128]{1,0:T(8,128)(2,1)S(1)}, bf16[704,128]{1,0:T(8,128)(2,1)S(1)}, u32[]{:S(2)}, u32[]{:S(2)}) %collective-permute-start.20) | collective-permute-done | bytes 180256 | tf_op jit(solution)/shard_map/ppermute | solution.py:32
  123.2 8.8 %collective-permute-start.22 = (bf16[2816,128]{1,0:T(8,128)(2,1)S(1)}, bf16[2816,128]{1,0:T(8,128)(2,1)S(1)}, u32[]{:S(2)}, u32[]{:S(2)}) collective-permute-start(bf16[2816,128]{1,0:T(8,128)(2,1)S(1)} %bitcast.62), channel_id=1, source_target_pairs={{0,4},{1,5},{2,6},{3,7},{4,0},{5,1},{6,2},{7,3},{8,12},{9,13},{10,... | collective-permute-start | bytes 2162696 | tf_op jit(solution)/shard_map/ppermute | solution.py:32
  132.0 1.8 %collective-permute-done.22 = bf16[2816,128]{1,0:T(8,128)(2,1)S(1)} collective-permute-done((bf16[2816,128]{1,0:T(8,128)(2,1)S(1)}, bf16[2816,128]{1,0:T(8,128)(2,1)S(1)}, u32[]{:S(2)}, u32[]{:S(2)}) %collective-permute-start.22) | collective-permute-done | bytes 720928 | tf_op jit(solution)/shard_map/ppermute | solution.py:32
  134.5 1.3 slice.15
  (65 shorter events, 19.4 us)
Async XLA Ops:
  0.6 29.4 %copy-start.4 = (bf16[256,256]{1,0:T(8,128)(2,1)S(1)}, bf16[256,256]{1,0:T(8,128)(2,1)}, u32[]{:S(2)}) copy-start(bf16[256,256]{1,0:T(8,128)(2,1)} %grad0) | copy-start | bytes 393220
  0.6 32.7 %copy-start.8 = (s32[27,512]{1,0:T(8,128)S(1)}, s32[27,512]{1,0:T(8,128)}, u32[]{:S(2)}) copy-start(s32[27,512]{1,0:T(8,128)} %param.8) | copy-start | bytes 165892
  0.7 7.9 %collective-permute-start.2 = (bf16[512,128]{1,0:T(8,128)(2,1)}, bf16[512,128]{1,0:T(8,128)(2,1)S(1)}, u32[]{:S(2)}, u32[]{:S(2)}) collective-permute-start(bf16[512,128]{1,0:T(8,128)(2,1)} %part0.3), channel_id=1, source_target_pairs={{0,3},{1,2},{2,1},{3,0},{4,7},{5,6},{6,5},{7,4},{8,11},{9,10},{10,... | collective-permute-start | bytes 393224 | tf_op jit(solution)/shard_map/ppermute | solution.py:32
  4.0 5.6 %collective-permute-start.1 = (bf16[512,128]{1,0:T(8,128)(2,1)}, bf16[512,128]{1,0:T(8,128)(2,1)S(1)}, u32[]{:S(2)}, u32[]{:S(2)}) collective-permute-start(bf16[512,128]{1,0:T(8,128)(2,1)} %part0.3), channel_id=1, source_target_pairs={{0,2},{1,3},{2,0},{3,1},{4,6},{5,7},{6,4},{7,5},{8,10},{9,11},{10,... | collective-permute-start | bytes 393224 | tf_op jit(solution)/shard_map/ppermute | solution.py:32
  4.6 5.1 %collective-permute-start = (bf16[512,128]{1,0:T(8,128)(2,1)}, bf16[512,128]{1,0:T(8,128)(2,1)S(1)}, u32[]{:S(2)}, u32[]{:S(2)}) collective-permute-start(bf16[512,128]{1,0:T(8,128)(2,1)} %part0.3), channel_id=1, source_target_pairs={{0,1},{1,0},{2,3},{3,2},{4,5},{5,4},{6,7},{7,6},{8,9},{9,8},{10,11... | collective-permute-start | bytes 393224 | tf_op jit(solution)/shard_map/ppermute | solution.py:32
  8.6 1.1 copy-start.1
  14.9 32.4 %all-to-all-start = ((bf16[64,32,128]{2,1,0:T(8,128)(2,1)}), bf16[64,32,128]{2,1,0:T(8,128)(2,1)S(1)}, u32[]{:S(2)}, u32[]{:S(2)}) async-start(bf16[64,32,128]{2,1,0:T(8,128)(2,1)} %bitcast.63), calls=%async_computation | async-start | bytes 1048576 | tf_op jit(solution)/shard_map/all_to_all | solution.py:328
  30.0 7.9 %collective-permute-start.5 = (bf16[256,256]{1,0:T(8,128)(2,1)S(1)}, bf16[256,256]{1,0:T(8,128)(2,1)S(1)}, u32[]{:S(2)}, u32[]{:S(2)}) collective-permute-start(bf16[256,256]{1,0:T(8,128)(2,1)S(1)} %copy-done.4), channel_id=1, source_target_pairs={{0,3},{1,2},{2,1},{3,0},{4,7},{5,6},{6,5},{7,4},{8,11},{9,10},{10,... | collective-permute-start | bytes 393224 | tf_op jit(solution)/shard_map/ppermute | solution.py:32
  31.3 6.7 %collective-permute-start.4 = (bf16[256,256]{1,0:T(8,128)(2,1)S(1)}, bf16[256,256]{1,0:T(8,128)(2,1)S(1)}, u32[]{:S(2)}, u32[]{:S(2)}) collective-permute-start(bf16[256,256]{1,0:T(8,128)(2,1)S(1)} %copy-done.4), channel_id=1, source_target_pairs={{0,2},{1,3},{2,0},{3,1},{4,6},{5,7},{6,4},{7,5},{8,10},{9,11},{10,... | collective-permute-start | bytes 393224 | tf_op jit(solution)/shard_map/ppermute | solution.py:32
  31.9 7.2 %collective-permute-start.3 = (bf16[256,256]{1,0:T(8,128)(2,1)S(1)}, bf16[256,256]{1,0:T(8,128)(2,1)S(1)}, u32[]{:S(2)}, u32[]{:S(2)}) collective-permute-start(bf16[256,256]{1,0:T(8,128)(2,1)S(1)} %copy-done.4), channel_id=1, source_target_pairs={{0,1},{1,0},{2,3},{3,2},{4,5},{5,4},{6,7},{7,6},{8,9},{9,8},{10,11... | collective-permute-start | bytes 393224 | tf_op jit(solution)/shard_map/ppermute | solution.py:32
  34.8 12.6 %copy-start.9 = (s32[512]{0:T(512)}, s32[512]{0:T(512)S(1)}, u32[]{:S(2)}) copy-start(s32[512]{0:T(512)S(1)} %dynamic_slice.29) | copy-start | bytes 6148
  37.9 1.1 copy-start.5
  38.0 1.1 copy-start.6
  47.3 0.8 copy-start
  70.7 2.5 %collective-permute-start.6 = (bf16[2816,128]{1,0:T(8,128)(2,1)}, bf16[2816,128]{1,0:T(8,128)(2,1)S(1)}, u32[]{:S(2)}, u32[]{:S(2)}) collective-permute-start(bf16[2816,128]{1,0:T(8,128)(2,1)} %get-tuple-element.19), channel_id=1, source_target_pairs={{0,4},{1,5},{2,6},{3,7},{4,0},{5,1},{6,2},{7,3},{8,12},{9,13},{10,... | collective-permute-start | bytes 2162696 | tf_op jit(solution)/shard_map/ppermute | solution.py:32
  74.6 4.6 %collective-permute-start.7 = (bf16[704,128]{1,0:T(8,128)(2,1)S(1)}, bf16[704,128]{1,0:T(8,128)(2,1)S(1)}, u32[]{:S(2)}, u32[]{:S(2)}) collective-permute-start(bf16[704,128]{1,0:T(8,128)(2,1)S(1)} %get-tuple-element.33), channel_id=1, source_target_pairs={{0,3},{1,2},{2,1},{3,0},{4,5},{5,4},{6,7},{7,6},{8,11},{9,10},{10,... | collective-permute-start | bytes 540680 | tf_op jit(solution)/shard_map/ppermute | solution.py:32
  74.9 7.3 %collective-permute-start.9 = (bf16[704,128]{1,0:T(8,128)(2,1)S(1)}, bf16[704,128]{1,0:T(8,128)(2,1)S(1)}, u32[]{:S(2)}, u32[]{:S(2)}) collective-permute-start(bf16[704,128]{1,0:T(8,128)(2,1)S(1)} %get-tuple-element.34), channel_id=1, source_target_pairs={{0,195},{1,194},{2,193},{3,192},{4,69},{5,68},{6,71},{7,70},{8,203... | collective-permute-start | bytes 540680 | tf_op jit(solution)/shard_map/ppermute | solution.py:32
  77.3 6.6 %collective-permute-start.8 = (bf16[704,128]{1,0:T(8,128)(2,1)S(1)}, bf16[704,128]{1,0:T(8,128)(2,1)S(1)}, u32[]{:S(2)}, u32[]{:S(2)}) collective-permute-start(bf16[704,128]{1,0:T(8,128)(2,1)S(1)} %get-tuple-element.35), channel_id=1, source_target_pairs={{0,192},{1,193},{2,194},{3,195},{4,68},{5,69},{6,70},{7,71},{8,200... | collective-permute-start | bytes 540680 | tf_op jit(solution)/shard_map/ppermute | solution.py:32
  84.0 5.2 %collective-permute-start.10 = (bf16[176,128]{1,0:T(8,128)(2,1)S(1)}, bf16[176,128]{1,0:T(8,128)(2,1)S(1)}, u32[]{:S(2)}, u32[]{:S(2)}) collective-permute-start(bf16[176,128]{1,0:T(8,128)(2,1)S(1)} %get-tuple-element.40), channel_id=1, source_target_pairs={{0,1},{1,0},{2,3},{3,2},{4,7},{5,6},{6,5},{7,4},{8,9},{9,8},{10,11... | collective-permute-start | bytes 135176 | tf_op jit(solution)/shard_map/ppermute | solution.py:32
  85.2 6.2 %collective-permute-start.12 = (bf16[176,128]{1,0:T(8,128)(2,1)S(1)}, bf16[176,128]{1,0:T(8,128)(2,1)S(1)}, u32[]{:S(2)}, u32[]{:S(2)}) collective-permute-start(bf16[176,128]{1,0:T(8,128)(2,1)S(1)} %get-tuple-element.41), channel_id=1, source_target_pairs={{0,65},{1,64},{2,67},{3,66},{4,199},{5,198},{6,197},{7,196},{8,73}... | collective-permute-start | bytes 135176 | tf_op jit(solution)/shard_map/ppermute | solution.py:32
  88.3 4.2 %collective-permute-start.11 = (bf16[176,128]{1,0:T(8,128)(2,1)S(1)}, bf16[176,128]{1,0:T(8,128)(2,1)S(1)}, u32[]{:S(2)}, u32[]{:S(2)}) collective-permute-start(bf16[176,128]{1,0:T(8,128)(2,1)S(1)} %get-tuple-element.42), channel_id=1, source_target_pairs={{0,64},{1,65},{2,66},{3,67},{4,196},{5,197},{6,198},{7,199},{8,72}... | collective-permute-start | bytes 135176 | tf_op jit(solution)/shard_map/ppermute | solution.py:32
  92.6 3.0 %collective-permute-start.13 = (bf16[176,128]{1,0:T(8,128)(2,1)S(1)}, bf16[176,128]{1,0:T(8,128)(2,1)S(1)}, u32[]{:S(2)}, u32[]{:S(2)}) collective-permute-start(bf16[176,128]{1,0:T(8,128)(2,1)S(1)} %fusion.5), channel_id=1, source_target_pairs={{0,8},{1,9},{2,10},{3,11},{4,12},{5,13},{6,14},{7,15},{8,0},{9,1},... | collective-permute-start | bytes 135176 | tf_op jit(solution)/shard_map/ppermute | solution.py:32
  95.6 4.7 %collective-permute-start.14 = (bf16[176,128]{1,0:T(8,128)(2,1)S(1)}, bf16[176,128]{1,0:T(8,128)(2,1)S(1)}, u32[]{:S(2)}, u32[]{:S(2)}) collective-permute-start(bf16[176,128]{1,0:T(8,128)(2,1)S(1)} %add_convert_fusion.3), channel_id=1, source_target_pairs={{0,16},{1,17},{2,18},{3,19},{4,20},{5,21},{6,22},{7,23},{8,24},{9,... | collective-permute-start | bytes 135176 | tf_op jit(solution)/shard_map/ppermute | solution.py:32
  96.8 10.4 %all-to-all-start.1 = ((bf16[4,256,256]{2,1,0:T(8,128)(2,1)}), bf16[4,256,256]{2,1,0:T(8,128)(2,1)S(1)}, u32[]{:S(2)}, u32[]{:S(2)}) async-start(bf16[4,256,256]{2,1,0:T(8,128)(2,1)} %bitcast.14), calls=%async_computation.1 | async-start | bytes 1048576 | tf_op jit(solution)/shard_map/all_to_all | solution.py:109
  100.3 4.2 %collective-permute-start.15 = (bf16[176,128]{1,0:T(8,128)(2,1)S(1)}, bf16[176,128]{1,0:T(8,128)(2,1)S(1)}, u32[]{:S(2)}, u32[]{:S(2)}) collective-permute-start(bf16[176,128]{1,0:T(8,128)(2,1)S(1)} %add_convert_fusion.2), channel_id=1, source_target_pairs={{0,56},{1,57},{2,58},{3,59},{4,60},{5,61},{6,62},{7,63},{8,48},{9,... | collective-permute-start | bytes 135176 | tf_op jit(solution)/shard_map/ppermute | solution.py:32
  107.9 5.1 %collective-permute-start.18 = (bf16[176,128]{1,0:T(8,128)(2,1)S(1)}, bf16[176,128]{1,0:T(8,128)(2,1)S(1)}, u32[]{:S(2)}, u32[]{:S(2)}) collective-permute-start(bf16[176,128]{1,0:T(8,128)(2,1)S(1)} %add_convert_fusion.1), channel_id=1, source_target_pairs={{0,1},{1,0},{2,3},{3,2},{4,7},{5,6},{6,5},{7,4},{8,9},{9,8},{10,11... | collective-permute-start | bytes 135176 | tf_op jit(solution)/shard_map/ppermute | solution.py:32
  108.9 4.1 %collective-permute-start.17 = (bf16[176,128]{1,0:T(8,128)(2,1)S(1)}, bf16[176,128]{1,0:T(8,128)(2,1)S(1)}, u32[]{:S(2)}, u32[]{:S(2)}) collective-permute-start(bf16[176,128]{1,0:T(8,128)(2,1)S(1)} %add_convert_fusion.1), channel_id=1, source_target_pairs={{0,64},{1,65},{2,66},{3,67},{4,196},{5,197},{6,198},{7,199},{8,72}... | collective-permute-start | bytes 135176 | tf_op jit(solution)/shard_map/ppermute | solution.py:32
  110.3 6.2 %collective-permute-start.16 = (bf16[176,128]{1,0:T(8,128)(2,1)S(1)}, bf16[176,128]{1,0:T(8,128)(2,1)S(1)}, u32[]{:S(2)}, u32[]{:S(2)}) collective-permute-start(bf16[176,128]{1,0:T(8,128)(2,1)S(1)} %add_convert_fusion.1), channel_id=1, source_target_pairs={{0,65},{1,64},{2,67},{3,66},{4,199},{5,198},{6,197},{7,196},{8,73}... | collective-permute-start | bytes 135176 | tf_op jit(solution)/shard_map/ppermute | solution.py:32
  116.6 4.4 %collective-permute-start.21 = (bf16[704,128]{1,0:T(8,128)(2,1)S(1)}, bf16[704,128]{1,0:T(8,128)(2,1)S(1)}, u32[]{:S(2)}, u32[]{:S(2)}) collective-permute-start(bf16[704,128]{1,0:T(8,128)(2,1)S(1)} %bitcast.67), channel_id=1, source_target_pairs={{0,3},{1,2},{2,1},{3,0},{4,5},{5,4},{6,7},{7,6},{8,11},{9,10},{10,... | collective-permute-start | bytes 540680 | tf_op jit(solution)/shard_map/ppermute | solution.py:32
  116.7 6.4 %collective-permute-start.20 = (bf16[704,128]{1,0:T(8,128)(2,1)S(1)}, bf16[704,128]{1,0:T(8,128)(2,1)S(1)}, u32[]{:S(2)}, u32[]{:S(2)}) collective-permute-start(bf16[704,128]{1,0:T(8,128)(2,1)S(1)} %bitcast.68), channel_id=1, source_target_pairs={{0,192},{1,193},{2,194},{3,195},{4,68},{5,69},{6,70},{7,71},{8,200... | collective-permute-start | bytes 540680 | tf_op jit(solution)/shard_map/ppermute | solution.py:32
  116.8 6.3 %collective-permute-start.19 = (bf16[704,128]{1,0:T(8,128)(2,1)S(1)}, bf16[704,128]{1,0:T(8,128)(2,1)S(1)}, u32[]{:S(2)}, u32[]{:S(2)}) collective-permute-start(bf16[704,128]{1,0:T(8,128)(2,1)S(1)} %bitcast.69), channel_id=1, source_target_pairs={{0,195},{1,194},{2,193},{3,192},{4,69},{5,68},{6,71},{7,70},{8,203... | collective-permute-start | bytes 540680 | tf_op jit(solution)/shard_map/ppermute | solution.py:32
  123.2 10.6 %collective-permute-start.22 = (bf16[2816,128]{1,0:T(8,128)(2,1)S(1)}, bf16[2816,128]{1,0:T(8,128)(2,1)S(1)}, u32[]{:S(2)}, u32[]{:S(2)}) collective-permute-start(bf16[2816,128]{1,0:T(8,128)(2,1)S(1)} %bitcast.62), channel_id=1, source_target_pairs={{0,4},{1,5},{2,6},{3,7},{4,0},{5,1},{6,2},{7,3},{8,12},{9,13},{10,... | collective-permute-start | bytes 2162696 | tf_op jit(solution)/shard_map/ppermute | solution.py:32
  (3 other events, 2.0 us)

commit v7 on v6

--- a/solution.py
+++ b/solution.py
@@ -43,8 +43,28 @@
     return partner
 
 
-def first_ring(step):
-    return lambda y, z, core, x: square(step, 1 if core else 3)(y, z, core, x)
+def ring_digits(y, z, core, x):
+    near = ((x ^ (x >> 1)) & 1) + 2 * ((y ^ (y >> 1)) & 1)
+    far = (x >> 1) + 2 * (y >> 1)
+    return (far, near) if core == 0 else (near, far)
+
+
+def square_groups():
+    groups = {}
+    for y in range(RING_Y):
+        for z in range(DEPTH_Z):
+            for core in range(CORES):
+                for x in range(RING_X):
+                    digit, rest = ring_digits(y, z, core, x)
+                    members = groups.setdefault((z, core, rest), [0] * 4)
+                    members[digit] = device_index((y, z, core, x))
+    return [groups[key] for key in sorted(groups)]
+
+
+def exchange_first(parts):
+    return lax.all_to_all(
+        parts, AXES, split_axis=0, concat_axis=0, tiled=True, axis_index_groups=square_groups()
+    )
 
 
 def second_ring(step):
@@ -96,24 +116,26 @@
 
 def sum_over_devices(mine, other, coarse):
     y, z, core, x = (lax.axis_index(name) for name in AXES)
-    near_x, near_y = (x ^ (x >> 1)) & 1, (y ^ (y >> 1)) & 1
-    far_x, far_y = x >> 1, y >> 1
-    near, far = near_x + 2 * near_y, far_x + 2 * far_y
-    ring_one = jnp.where(core == 0, far, near)
+    near = ((x ^ (x >> 1)) & 1) + 2 * ((y ^ (y >> 1)) & 1)
+    far = (x >> 1) + 2 * (y >> 1)
     ring_two = jnp.where(core == 0, near, far)
     rows, lanes = mine.shape[0] // (RING_X * RING_Y), mine.shape[1]
     part = narrow(wide(mine) + wide(send(other, across_core)))
-    part = scatter_ring(part.reshape(RING_X, RING_Y * rows, lanes), ring_one, first_ring)
-    part, coarse = lax.optimization_barrier((part, coarse))
+    parts = exchange_first(part.reshape(4, 4 * rows, lanes))
+    part = narrow(jnp.sum(wide(parts), axis=0))
     shares = coarse.reshape(RING_X, coarse.shape[0] // RING_X, coarse.shape[1])
     shares = lax.all_to_all(shares, "x", split_axis=0, concat_axis=0, tiled=True)
-    coarse_out = narrow(jnp.sum(wide(shares), axis=0))
-    part = scatter_ring(part.reshape(RING_Y, rows, lanes), ring_two, second_ring)
+    part = scatter_ring(part.reshape(4, rows, lanes), ring_two, second_ring)
     for step in (1, 2, 7):
         part = narrow(wide(part) + wide(send(part, along_z(step))))
+    part, shares = lax.optimization_barrier((part, shares))
+    part = gather_ring(part, ring_two, second_ring).reshape(4 * rows, lanes)
+    spread, shares = lax.optimization_barrier(
+        (jnp.broadcast_to(part[None], (4, 4 * rows, lanes)), shares)
+    )
+    part = exchange_first(spread).reshape(16 * rows, lanes)
+    coarse_out = narrow(jnp.sum(wide(shares), axis=0))
     part, coarse_out = lax.optimization_barrier((part, coarse_out))
-    part = gather_ring(part, ring_two, second_ring).reshape(RING_Y * rows, lanes)
-    part = gather_ring(part, ring_one, first_ring).reshape(RING_X * RING_Y * rows, lanes)
     return wide(gather_pair(part, core, across_core)).reshape(-1, lanes), coarse_out
 
 

time: 137 us -> 140 us (1.022)
  waiting for transfers between devices: 39 us -> 41.6 us
    all_to_all x0 -> x2, waiting for transfers between devices: none -> 12.5 us  [exchange_first(): lax.all_to_all(parts, AXES, split_axis=0, concat_axis=0, tiled=True, axis...]
    ppermute x23 -> x17, waiting for transfers between devices: 33.2 us -> 23.7 us  [send(): return lax.ppermute(value, AXES, partner_pairs(partner))]
    ppermute x23 -> x17, starting transfers between devices: 35.6 us -> 27.2 us  [send(): return lax.ppermute(value, AXES, partner_pairs(partner))]
    all_to_all x0 -> x2, starting transfers between devices: none -> 6.98 us  [exchange_first(): lax.all_to_all(parts, AXES, split_axis=0, concat_axis=0, tiled=True, axis...]
  transfers between devices with their start and end apart: 25 -> 21, of which waited for: 18 -> 16; matrix products, arithmetic and copies ran while one was open for 3% -> 3% of each run, Pallas kernels for 3% -> 3%
where the time goes in v7:
time: 140 us
  starting transfers between devices  52.7 us (38%)
  waiting for transfers between devices  41.6 us (30%)
  Pallas kernels  31 us (22%)
  local copies, waits for them, and re-layouts  8.83 us (6%)
  other arithmetic  4.73 us (3%)
    ppermute x17, starting transfers between devices, send(): return lax.ppermute(value, AXES, partner_pairs(partner))  27.2 us
    ppermute x17, waiting for transfers between devices, send(): return lax.ppermute(value, AXES, partner_pairs(partner))  23.7 us
    pallas_call x1, Pallas kernels, shards(): pl.pallas_call(step_kernel, out_shape=(jax.ShapeDtypeStruct((coarse_tile,...  22.6 us
    all_to_all x1, starting transfers between devices, shards(): lax.all_to_all(outgoing.reshape(tiles, slots, channels), TILE, split_axis...  15.1 us
    all_to_all x2, waiting for transfers between devices, exchange_first(): lax.all_to_all(parts, AXES, split_axis=0, concat_axis=0, tiled=True, axis...  12.5 us
    all_to_all x2, starting transfers between devices, exchange_first(): lax.all_to_all(parts, AXES, split_axis=0, concat_axis=0, tiled=True, axis...  6.98 us
    pallas_call x1, Pallas kernels, shards(): pl.pallas_call(grad_kernel, out_shape=(jax.ShapeDtypeStruct((rows, out_ch...  4.46 us
    pallas_call x1, Pallas kernels, shards(): pl.pallas_call(pick_halo, out_shape=jax.ShapeDtypeStruct((halo_rows, chan...  3.94 us
  transfers between devices with their start and end apart: 21, of which 16 were waited for; matrix products, arithmetic and copies ran while one was open for 3% of the time, Pallas kernels for 3%

profile of v7, /device:TPU:1, one launch (start us, length us, event | category | flops | bytes accessed | tf_op | source)
XLA Modules:
  0.0 139.7 jit_solution(8994220853026157849)
XLA Ops:
  0.7 3.4 %collective-permute-start.2 = (bf16[512,128]{1,0:T(8,128)(2,1)}, bf16[512,128]{1,0:T(8,128)(2,1)S(1)}, u32[]{:S(2)}, u32[]{:S(2)}) collective-permute-start(bf16[512,128]{1,0:T(8,128)(2,1)} %part0.3), channel_id=1, source_target_pairs={{0,3},{1,2},{2,1},{3,0},{4,7},{5,6},{6,5},{7,4},{8,11},{9,10},{10,... | collective-permute-start | bytes 393224 | tf_op jit(solution)/shard_map/ppermute | solution.py:32
  6.2 2.4 %collective-permute-done.2.part3 = bf16[512,128]{1,0:T(8,128)(2,1)S(1)} collective-permute-done((bf16[512,128]{1,0:T(8,128)(2,1)}, bf16[512,128]{1,0:T(8,128)(2,1)S(1)}, u32[]{:S(2)}, u32[]{:S(2)}) %collective-permute-start.2) | collective-permute-done | bytes 131104 | tf_op jit(solution)/shard_map/ppermute | solution.py:32
  11.0 3.9 %pick_halo.1 = bf16[2048,128]{1,0:T(8,128)(2,1)} custom-call(s32[2048]{0:T(1024)} %reshape.50.lists, bf16[512,128]{1,0:T(8,128)(2,1)} %part0.3, bf16[512,128]{1,0:T(8,128)(2,1)} %copy-done.3, bf16[512,128]{1,0:T(8,128)(2,1)} %copy-done.2, bf16[512,128]{1,0:T(8,128)(2,1)} %copy-done.1), custom_call_target="tpu_custom_call" | custom-call | tf_op jit(solution)/shard_map/pick_halo/pallas_call | solution.py:335
  14.9 15.1 %all-to-all-start = ((bf16[64,32,128]{2,1,0:T(8,128)(2,1)}), bf16[64,32,128]{2,1,0:T(8,128)(2,1)S(1)}, u32[]{:S(2)}, u32[]{:S(2)}) async-start(bf16[64,32,128]{2,1,0:T(8,128)(2,1)} %bitcast.39), calls=%async_computation | async-start | bytes 1048576 | tf_op jit(solution)/shard_map/all_to_all | solution.py:350
  30.0 1.3 collective-permute-start.5
  31.9 1.5 %collective-permute-start.3 = (bf16[256,256]{1,0:T(8,128)(2,1)S(1)}, bf16[256,256]{1,0:T(8,128)(2,1)S(1)}, u32[]{:S(2)}, u32[]{:S(2)}) collective-permute-start(bf16[256,256]{1,0:T(8,128)(2,1)S(1)} %copy-done.4), channel_id=1, source_target_pairs={{0,1},{1,0},{2,3},{3,2},{4,5},{5,4},{6,7},{7,6},{8,9},{9,8},{10,11... | collective-permute-start | bytes 393224 | tf_op jit(solution)/shard_map/ppermute | solution.py:32
  35.6 2.4 %collective-permute-done.5.grad3 = bf16[256,256]{1,0:T(8,128)(2,1)S(1)} collective-permute-done((bf16[256,256]{1,0:T(8,128)(2,1)S(1)}, bf16[256,256]{1,0:T(8,128)(2,1)S(1)}, u32[]{:S(2)}, u32[]{:S(2)}) %collective-permute-start.5) | collective-permute-done | bytes 131104 | tf_op jit(solution)/shard_map/ppermute | solution.py:32
  38.0 1.1 collective-permute-done.3.grad1
  39.7 4.5 %coarse_back.1 = (bf16[512,256]{1,0:T(8,128)(2,1)}, f32[512,128]{1,0:T(8,128)}) custom-call(bf16[256,256]{1,0:T(8,128)(2,1)} %grad0, bf16[256,256]{1,0:T(8,128)(2,1)} %copy-done.7, bf16[256,256]{1,0:T(8,128)(2,1)} %copy-done.6, bf16[256,256]{1,0:T(8,128)(2,1)} %copy-done.5, bf16[8,128,256]{2,1,0:T(8,128)(2,1)} %down_hbm.1, s32[512,1]{1,0:T(8,128)} %copy.11.link_column), custom_call_target="tpu_custom_call" | custom-call | tf_op jit(solution)/shard_map/coarse_back/pallas_call | solution.py:359
  44.2 3.1 %all-to-all-done = bf16[64,32,128]{2,1,0:T(8,128)(2,1)S(1)} async-done(((bf16[64,32,128]{2,1,0:T(8,128)(2,1)}), bf16[64,32,128]{2,1,0:T(8,128)(2,1)S(1)}, u32[]{:S(2)}, u32[]{:S(2)}) %all-to-all-start) | async-done | bytes 524320 | tf_op jit(solution)/shard_map/all_to_all | solution.py:350
  48.1 22.6 %step.1 = (bf16[1024,256]{1,0:T(8,128)(2,1)}, bf16[2816,128]{1,0:T(8,128)(2,1)}, bf16[2816,128]{1,0:T(8,128)(2,1)}) custom-call(s32[13824]{0:T(1024)} %reshape.49.kernel_map, bf16[512,128]{1,0:T(8,128)(2,1)} %part0.3, bf16[512,128]{1,0:T(8,128)(2,1)} %copy-done.3, bf16[512,128]{1,0:T(8,128)(2,1)} %copy-done.2, bf16[512,128]{1,0:T(8,128)(2,1)} %copy-done.1, ...), custom_call_target="tpu_custom_call" | custom-call | tf_op jit(solution)/shard_map/step/pallas_call | solution.py:375
  71.1 2.1 %collective-permute-done.6 = bf16[2816,128]{1,0:T(8,128)(2,1)S(1)} collective-permute-done((bf16[2816,128]{1,0:T(8,128)(2,1)}, bf16[2816,128]{1,0:T(8,128)(2,1)S(1)}, u32[]{:S(2)}, u32[]{:S(2)}) %collective-permute-start.6) | collective-permute-done | bytes 720928 | tf_op jit(solution)/shard_map/ppermute | solution.py:32
  73.2 2.2 %add_convert_fusion = bf16[2816,128]{1,0:T(8,128)(2,1)} fusion(bf16[2816,128]{1,0:T(8,128)(2,1)S(1)} %collective-permute-done.6, bf16[2816,128]{1,0:T(8,128)(2,1)} %get-tuple-element.20), kind=kLoop, calls=%fused_computation.2 | loop fusion | flops 1441792 | bytes 2162688 | tf_op jit(solution)/shard_map/convert_element_type | solution.py:79
  75.4 3.5 %all-to-all-start.1 = ((bf16[4,704,128]{2,1,0:T(8,128)(2,1)}), bf16[4,704,128]{2,1,0:T(8,128)(2,1)S(1)}, u32[]{:S(2)}, u32[]{:S(2)}) async-start(bf16[4,704,128]{2,1,0:T(8,128)(2,1)} %bitcast.4), calls=%async_computation.1 | async-start | bytes 1441792 | tf_op jit(solution)/shard_map/all_to_all | solution.py:65
  78.9 6.8 %all-to-all-done.1 = bf16[4,704,128]{2,1,0:T(8,128)(2,1)S(1)} async-done(((bf16[4,704,128]{2,1,0:T(8,128)(2,1)}), bf16[4,704,128]{2,1,0:T(8,128)(2,1)S(1)}, u32[]{:S(2)}, u32[]{:S(2)}) %all-to-all-start.1) | async-done | bytes 720928 | tf_op jit(solution)/shard_map/all_to_all | solution.py:65
  85.8 1.4 %collective-permute-start.7 = (bf16[176,128]{1,0:T(8,128)(2,1)S(1)}, bf16[176,128]{1,0:T(8,128)(2,1)S(1)}, u32[]{:S(2)}, u32[]{:S(2)}) collective-permute-start(bf16[176,128]{1,0:T(8,128)(2,1)S(1)} %get-tuple-element.37), channel_id=1, source_target_pairs={{0,1},{1,0},{2,3},{3,2},{4,7},{5,6},{6,5},{7,4},{8,9},{9,8},{10,11... | collective-permute-start | bytes 135176 | tf_op jit(solution)/shard_map/ppermute | solution.py:32
  87.3 3.9 %collective-permute-start.9 = (bf16[176,128]{1,0:T(8,128)(2,1)S(1)}, bf16[176,128]{1,0:T(8,128)(2,1)S(1)}, u32[]{:S(2)}, u32[]{:S(2)}) collective-permute-start(bf16[176,128]{1,0:T(8,128)(2,1)S(1)} %get-tuple-element.38), channel_id=1, source_target_pairs={{0,65},{1,64},{2,67},{3,66},{4,199},{5,198},{6,197},{7,196},{8,73}... | collective-permute-start | bytes 135176 | tf_op jit(solution)/shard_map/ppermute | solution.py:32
  91.2 2.3 %collective-permute-done.9 = bf16[176,128]{1,0:T(8,128)(2,1)S(1)} collective-permute-done((bf16[176,128]{1,0:T(8,128)(2,1)S(1)}, bf16[176,128]{1,0:T(8,128)(2,1)S(1)}, u32[]{:S(2)}, u32[]{:S(2)}) %collective-permute-start.9) | collective-permute-done | bytes 45088 | tf_op jit(solution)/shard_map/ppermute | solution.py:32
  93.5 1.8 %collective-permute-done.8 = bf16[176,128]{1,0:T(8,128)(2,1)S(1)} collective-permute-done((bf16[176,128]{1,0:T(8,128)(2,1)S(1)}, bf16[176,128]{1,0:T(8,128)(2,1)S(1)}, u32[]{:S(2)}, u32[]{:S(2)}) %collective-permute-start.8) | collective-permute-done | bytes 45088 | tf_op jit(solution)/shard_map/ppermute | solution.py:32
  95.7 2.6 %collective-permute-done.10 = bf16[176,128]{1,0:T(8,128)(2,1)S(1)} collective-permute-done((bf16[176,128]{1,0:T(8,128)(2,1)S(1)}, bf16[176,128]{1,0:T(8,128)(2,1)S(1)}, u32[]{:S(2)}, u32[]{:S(2)}) %collective-permute-start.10) | collective-permute-done | bytes 45088 | tf_op jit(solution)/shard_map/ppermute | solution.py:32
  98.8 3.5 %all-to-all-start.2 = ((bf16[4,256,256]{2,1,0:T(8,128)(2,1)}), bf16[4,256,256]{2,1,0:T(8,128)(2,1)S(1)}, u32[]{:S(2)}, u32[]{:S(2)}) async-start(bf16[4,256,256]{2,1,0:T(8,128)(2,1)} %bitcast.10), calls=%async_computation.2 | async-start | bytes 1048576 | tf_op jit(solution)/shard_map/all_to_all | solution.py:127
  102.7 2.1 %collective-permute-start.12 = (bf16[176,128]{1,0:T(8,128)(2,1)S(1)}, bf16[176,128]{1,0:T(8,128)(2,1)S(1)}, u32[]{:S(2)}, u32[]{:S(2)}) collective-permute-start(bf16[176,128]{1,0:T(8,128)(2,1)S(1)} %add_convert_fusion.2), channel_id=1, source_target_pairs={{0,56},{1,57},{2,58},{3,59},{4,60},{5,61},{6,62},{7,63},{8,48},{9,... | collective-permute-start | bytes 135176 | tf_op jit(solution)/shard_map/ppermute | solution.py:32
  104.8 2.1 %collective-permute-done.12 = bf16[176,128]{1,0:T(8,128)(2,1)S(1)} collective-permute-done((bf16[176,128]{1,0:T(8,128)(2,1)S(1)}, bf16[176,128]{1,0:T(8,128)(2,1)S(1)}, u32[]{:S(2)}, u32[]{:S(2)}) %collective-permute-start.12) | collective-permute-done | bytes 45088 | tf_op jit(solution)/shard_map/ppermute | solution.py:32
  106.9 2.3 %all-to-all-done.2 = bf16[4,256,256]{2,1,0:T(8,128)(2,1)S(1)} async-done(((bf16[4,256,256]{2,1,0:T(8,128)(2,1)}), bf16[4,256,256]{2,1,0:T(8,128)(2,1)S(1)}, u32[]{:S(2)}, u32[]{:S(2)}) %all-to-all-start.2) | async-done | bytes 524320 | tf_op jit(solution)/shard_map/all_to_all | solution.py:127
  110.1 1.6 %collective-permute-start.14 = (bf16[176,128]{1,0:T(8,128)(2,1)S(1)}, bf16[176,128]{1,0:T(8,128)(2,1)S(1)}, u32[]{:S(2)}, u32[]{:S(2)}) collective-permute-start(bf16[176,128]{1,0:T(8,128)(2,1)S(1)} %add_convert_fusion.1), channel_id=1, source_target_pairs={{0,64},{1,65},{2,66},{3,67},{4,196},{5,197},{6,198},{7,199},{8,72}... | collective-permute-start | bytes 135176 | tf_op jit(solution)/shard_map/ppermute | solution.py:32
  111.7 2.5 %collective-permute-start.13 = (bf16[176,128]{1,0:T(8,128)(2,1)S(1)}, bf16[176,128]{1,0:T(8,128)(2,1)S(1)}, u32[]{:S(2)}, u32[]{:S(2)}) collective-permute-start(bf16[176,128]{1,0:T(8,128)(2,1)S(1)} %add_convert_fusion.1), channel_id=1, source_target_pairs={{0,65},{1,64},{2,67},{3,66},{4,199},{5,198},{6,197},{7,196},{8,73}... | collective-permute-start | bytes 135176 | tf_op jit(solution)/shard_map/ppermute | solution.py:32
  114.2 3.7 %collective-permute-done.13 = bf16[176,128]{1,0:T(8,128)(2,1)S(1)} collective-permute-done((bf16[176,128]{1,0:T(8,128)(2,1)S(1)}, bf16[176,128]{1,0:T(8,128)(2,1)S(1)}, u32[]{:S(2)}, u32[]{:S(2)}) %collective-permute-start.13) | collective-permute-done | bytes 45088 | tf_op jit(solution)/shard_map/ppermute | solution.py:32
  118.9 3.5 %all-to-all-start.3 = ((bf16[4,704,128]{2,1,0:T(8,128)(2,1)}), bf16[4,704,128]{2,1,0:T(8,128)(2,1)S(1)}, u32[]{:S(2)}, u32[]{:S(2)}) async-start(bf16[4,704,128]{2,1,0:T(8,128)(2,1)} %broadcast_in_dim.8), calls=%async_computation.3 | async-start | bytes 1441792 | tf_op jit(solution)/shard_map/all_to_all | solution.py:65
  123.2 5.7 %all-to-all-done.3 = bf16[4,704,128]{2,1,0:T(8,128)(2,1)S(1)} async-done(((bf16[4,704,128]{2,1,0:T(8,128)(2,1)}), bf16[4,704,128]{2,1,0:T(8,128)(2,1)S(1)}, u32[]{:S(2)}, u32[]{:S(2)}) %all-to-all-start.3) | async-done | bytes 720928 | tf_op jit(solution)/shard_map/all_to_all | solution.py:65
  128.9 6.0 %collective-permute-start.16 = (bf16[2816,128]{1,0:T(8,128)(2,1)S(1)}, bf16[2816,128]{1,0:T(8,128)(2,1)S(1)}, u32[]{:S(2)}, u32[]{:S(2)}) collective-permute-start(bf16[2816,128]{1,0:T(8,128)(2,1)S(1)} %bitcast.37), channel_id=1, source_target_pairs={{0,4},{1,5},{2,6},{3,7},{4,0},{5,1},{6,2},{7,3},{8,12},{9,13},{10,... | collective-permute-start | bytes 2162696 | tf_op jit(solution)/shard_map/ppermute | solution.py:32
  134.9 1.8 %collective-permute-done.16 = bf16[2816,128]{1,0:T(8,128)(2,1)S(1)} collective-permute-done((bf16[2816,128]{1,0:T(8,128)(2,1)S(1)}, bf16[2816,128]{1,0:T(8,128)(2,1)S(1)}, u32[]{:S(2)}, u32[]{:S(2)}) %collective-permute-start.16) | collective-permute-done | bytes 720928 | tf_op jit(solution)/shard_map/ppermute | solution.py:32
  137.3 1.3 slice.15
  (55 shorter events, 15.1 us)
Async XLA Ops:
  0.6 29.4 %copy-start.4 = (bf16[256,256]{1,0:T(8,128)(2,1)S(1)}, bf16[256,256]{1,0:T(8,128)(2,1)}, u32[]{:S(2)}) copy-start(bf16[256,256]{1,0:T(8,128)(2,1)} %grad0) | copy-start | bytes 393220
  0.6 32.7 %copy-start.8 = (s32[27,512]{1,0:T(8,128)S(1)}, s32[27,512]{1,0:T(8,128)}, u32[]{:S(2)}) copy-start(s32[27,512]{1,0:T(8,128)} %param.8) | copy-start | bytes 165892
  0.7 7.9 %collective-permute-start.2 = (bf16[512,128]{1,0:T(8,128)(2,1)}, bf16[512,128]{1,0:T(8,128)(2,1)S(1)}, u32[]{:S(2)}, u32[]{:S(2)}) collective-permute-start(bf16[512,128]{1,0:T(8,128)(2,1)} %part0.3), channel_id=1, source_target_pairs={{0,3},{1,2},{2,1},{3,0},{4,7},{5,6},{6,5},{7,4},{8,11},{9,10},{10,... | collective-permute-start | bytes 393224 | tf_op jit(solution)/shard_map/ppermute | solution.py:32
  4.0 5.6 %collective-permute-start.1 = (bf16[512,128]{1,0:T(8,128)(2,1)}, bf16[512,128]{1,0:T(8,128)(2,1)S(1)}, u32[]{:S(2)}, u32[]{:S(2)}) collective-permute-start(bf16[512,128]{1,0:T(8,128)(2,1)} %part0.3), channel_id=1, source_target_pairs={{0,2},{1,3},{2,0},{3,1},{4,6},{5,7},{6,4},{7,5},{8,10},{9,11},{10,... | collective-permute-start | bytes 393224 | tf_op jit(solution)/shard_map/ppermute | solution.py:32
  4.6 5.1 %collective-permute-start = (bf16[512,128]{1,0:T(8,128)(2,1)}, bf16[512,128]{1,0:T(8,128)(2,1)S(1)}, u32[]{:S(2)}, u32[]{:S(2)}) collective-permute-start(bf16[512,128]{1,0:T(8,128)(2,1)} %part0.3), channel_id=1, source_target_pairs={{0,1},{1,0},{2,3},{3,2},{4,5},{5,4},{6,7},{7,6},{8,9},{9,8},{10,11... | collective-permute-start | bytes 393224 | tf_op jit(solution)/shard_map/ppermute | solution.py:32
  8.6 1.1 copy-start.1
  9.7 0.6 copy-start.2
  10.3 0.7 copy-start.3
  14.9 32.4 %all-to-all-start = ((bf16[64,32,128]{2,1,0:T(8,128)(2,1)}), bf16[64,32,128]{2,1,0:T(8,128)(2,1)S(1)}, u32[]{:S(2)}, u32[]{:S(2)}) async-start(bf16[64,32,128]{2,1,0:T(8,128)(2,1)} %bitcast.39), calls=%async_computation | async-start | bytes 1048576 | tf_op jit(solution)/shard_map/all_to_all | solution.py:350
  30.0 7.9 %collective-permute-start.5 = (bf16[256,256]{1,0:T(8,128)(2,1)S(1)}, bf16[256,256]{1,0:T(8,128)(2,1)S(1)}, u32[]{:S(2)}, u32[]{:S(2)}) collective-permute-start(bf16[256,256]{1,0:T(8,128)(2,1)S(1)} %copy-done.4), channel_id=1, source_target_pairs={{0,3},{1,2},{2,1},{3,0},{4,7},{5,6},{6,5},{7,4},{8,11},{9,10},{10,... | collective-permute-start | bytes 393224 | tf_op jit(solution)/shard_map/ppermute | solution.py:32
  31.3 6.7 %collective-permute-start.4 = (bf16[256,256]{1,0:T(8,128)(2,1)S(1)}, bf16[256,256]{1,0:T(8,128)(2,1)S(1)}, u32[]{:S(2)}, u32[]{:S(2)}) collective-permute-start(bf16[256,256]{1,0:T(8,128)(2,1)S(1)} %copy-done.4), channel_id=1, source_target_pairs={{0,2},{1,3},{2,0},{3,1},{4,6},{5,7},{6,4},{7,5},{8,10},{9,11},{10,... | collective-permute-start | bytes 393224 | tf_op jit(solution)/shard_map/ppermute | solution.py:32
  31.9 7.2 %collective-permute-start.3 = (bf16[256,256]{1,0:T(8,128)(2,1)S(1)}, bf16[256,256]{1,0:T(8,128)(2,1)S(1)}, u32[]{:S(2)}, u32[]{:S(2)}) collective-permute-start(bf16[256,256]{1,0:T(8,128)(2,1)S(1)} %copy-done.4), channel_id=1, source_target_pairs={{0,1},{1,0},{2,3},{3,2},{4,5},{5,4},{6,7},{7,6},{8,9},{9,8},{10,11... | collective-permute-start | bytes 393224 | tf_op jit(solution)/shard_map/ppermute | solution.py:32
  34.7 12.6 %copy-start.9 = (s32[512]{0:T(512)}, s32[512]{0:T(512)S(1)}, u32[]{:S(2)}) copy-start(s32[512]{0:T(512)S(1)} %dynamic_slice.16) | copy-start | bytes 6148
  37.9 1.1 copy-start.5
  38.0 1.1 copy-start.6
  39.1 0.7 copy-start.7
  47.3 0.8 copy-start
  70.7 2.5 %collective-permute-start.6 = (bf16[2816,128]{1,0:T(8,128)(2,1)}, bf16[2816,128]{1,0:T(8,128)(2,1)S(1)}, u32[]{:S(2)}, u32[]{:S(2)}) collective-permute-start(bf16[2816,128]{1,0:T(8,128)(2,1)} %get-tuple-element.21), channel_id=1, source_target_pairs={{0,4},{1,5},{2,6},{3,7},{4,0},{5,1},{6,2},{7,3},{8,12},{9,13},{10,... | collective-permute-start | bytes 2162696 | tf_op jit(solution)/shard_map/ppermute | solution.py:32
  75.4 10.3 %all-to-all-start.1 = ((bf16[4,704,128]{2,1,0:T(8,128)(2,1)}), bf16[4,704,128]{2,1,0:T(8,128)(2,1)S(1)}, u32[]{:S(2)}, u32[]{:S(2)}) async-start(bf16[4,704,128]{2,1,0:T(8,128)(2,1)} %bitcast.4), calls=%async_computation.1 | async-start | bytes 1441792 | tf_op jit(solution)/shard_map/all_to_all | solution.py:65
  85.8 5.3 %collective-permute-start.7 = (bf16[176,128]{1,0:T(8,128)(2,1)S(1)}, bf16[176,128]{1,0:T(8,128)(2,1)S(1)}, u32[]{:S(2)}, u32[]{:S(2)}) collective-permute-start(bf16[176,128]{1,0:T(8,128)(2,1)S(1)} %get-tuple-element.37), channel_id=1, source_target_pairs={{0,1},{1,0},{2,3},{3,2},{4,7},{5,6},{6,5},{7,4},{8,9},{9,8},{10,11... | collective-permute-start | bytes 135176 | tf_op jit(solution)/shard_map/ppermute | solution.py:32
  87.3 6.2 %collective-permute-start.9 = (bf16[176,128]{1,0:T(8,128)(2,1)S(1)}, bf16[176,128]{1,0:T(8,128)(2,1)S(1)}, u32[]{:S(2)}, u32[]{:S(2)}) collective-permute-start(bf16[176,128]{1,0:T(8,128)(2,1)S(1)} %get-tuple-element.38), channel_id=1, source_target_pairs={{0,65},{1,64},{2,67},{3,66},{4,199},{5,198},{6,197},{7,196},{8,73}... | collective-permute-start | bytes 135176 | tf_op jit(solution)/shard_map/ppermute | solution.py:32
  91.2 4.1 %collective-permute-start.8 = (bf16[176,128]{1,0:T(8,128)(2,1)S(1)}, bf16[176,128]{1,0:T(8,128)(2,1)S(1)}, u32[]{:S(2)}, u32[]{:S(2)}) collective-permute-start(bf16[176,128]{1,0:T(8,128)(2,1)S(1)} %get-tuple-element.39), channel_id=1, source_target_pairs={{0,64},{1,65},{2,66},{3,67},{4,196},{5,197},{6,198},{7,199},{8,72}... | collective-permute-start | bytes 135176 | tf_op jit(solution)/shard_map/ppermute | solution.py:32
  95.3 3.0 %collective-permute-start.10 = (bf16[176,128]{1,0:T(8,128)(2,1)S(1)}, bf16[176,128]{1,0:T(8,128)(2,1)S(1)}, u32[]{:S(2)}, u32[]{:S(2)}) collective-permute-start(bf16[176,128]{1,0:T(8,128)(2,1)S(1)} %fusion.2), channel_id=1, source_target_pairs={{0,8},{1,9},{2,10},{3,11},{4,12},{5,13},{6,14},{7,15},{8,0},{9,1},... | collective-permute-start | bytes 135176 | tf_op jit(solution)/shard_map/ppermute | solution.py:32
  98.3 4.4 %collective-permute-start.11 = (bf16[176,128]{1,0:T(8,128)(2,1)S(1)}, bf16[176,128]{1,0:T(8,128)(2,1)S(1)}, u32[]{:S(2)}, u32[]{:S(2)}) collective-permute-start(bf16[176,128]{1,0:T(8,128)(2,1)S(1)} %add_convert_fusion.3), channel_id=1, source_target_pairs={{0,16},{1,17},{2,18},{3,19},{4,20},{5,21},{6,22},{7,23},{8,24},{9,... | collective-permute-start | bytes 135176 | tf_op jit(solution)/shard_map/ppermute | solution.py:32
  98.8 10.4 %all-to-all-start.2 = ((bf16[4,256,256]{2,1,0:T(8,128)(2,1)}), bf16[4,256,256]{2,1,0:T(8,128)(2,1)S(1)}, u32[]{:S(2)}, u32[]{:S(2)}) async-start(bf16[4,256,256]{2,1,0:T(8,128)(2,1)} %bitcast.10), calls=%async_computation.2 | async-start | bytes 1048576 | tf_op jit(solution)/shard_map/all_to_all | solution.py:127
  102.7 4.2 %collective-permute-start.12 = (bf16[176,128]{1,0:T(8,128)(2,1)S(1)}, bf16[176,128]{1,0:T(8,128)(2,1)S(1)}, u32[]{:S(2)}, u32[]{:S(2)}) collective-permute-start(bf16[176,128]{1,0:T(8,128)(2,1)S(1)} %add_convert_fusion.2), channel_id=1, source_target_pairs={{0,56},{1,57},{2,58},{3,59},{4,60},{5,61},{6,62},{7,63},{8,48},{9,... | collective-permute-start | bytes 135176 | tf_op jit(solution)/shard_map/ppermute | solution.py:32
  109.2 5.1 %collective-permute-start.15 = (bf16[176,128]{1,0:T(8,128)(2,1)S(1)}, bf16[176,128]{1,0:T(8,128)(2,1)S(1)}, u32[]{:S(2)}, u32[]{:S(2)}) collective-permute-start(bf16[176,128]{1,0:T(8,128)(2,1)S(1)} %add_convert_fusion.1), channel_id=1, source_target_pairs={{0,1},{1,0},{2,3},{3,2},{4,7},{5,6},{6,5},{7,4},{8,9},{9,8},{10,11... | collective-permute-start | bytes 135176 | tf_op jit(solution)/shard_map/ppermute | solution.py:32
  110.1 4.2 %collective-permute-start.14 = (bf16[176,128]{1,0:T(8,128)(2,1)S(1)}, bf16[176,128]{1,0:T(8,128)(2,1)S(1)}, u32[]{:S(2)}, u32[]{:S(2)}) collective-permute-start(bf16[176,128]{1,0:T(8,128)(2,1)S(1)} %add_convert_fusion.1), channel_id=1, source_target_pairs={{0,64},{1,65},{2,66},{3,67},{4,196},{5,197},{6,198},{7,199},{8,72}... | collective-permute-start | bytes 135176 | tf_op jit(solution)/shard_map/ppermute | solution.py:32
  111.7 6.2 %collective-permute-start.13 = (bf16[176,128]{1,0:T(8,128)(2,1)S(1)}, bf16[176,128]{1,0:T(8,128)(2,1)S(1)}, u32[]{:S(2)}, u32[]{:S(2)}) collective-permute-start(bf16[176,128]{1,0:T(8,128)(2,1)S(1)} %add_convert_fusion.1), channel_id=1, source_target_pairs={{0,65},{1,64},{2,67},{3,66},{4,199},{5,198},{6,197},{7,196},{8,73}... | collective-permute-start | bytes 135176 | tf_op jit(solution)/shard_map/ppermute | solution.py:32
  118.9 10.0 %all-to-all-start.3 = ((bf16[4,704,128]{2,1,0:T(8,128)(2,1)}), bf16[4,704,128]{2,1,0:T(8,128)(2,1)S(1)}, u32[]{:S(2)}, u32[]{:S(2)}) async-start(bf16[4,704,128]{2,1,0:T(8,128)(2,1)} %broadcast_in_dim.8), calls=%async_computation.3 | async-start | bytes 1441792 | tf_op jit(solution)/shard_map/all_to_all | solution.py:65
  128.9 7.8 %collective-permute-start.16 = (bf16[2816,128]{1,0:T(8,128)(2,1)S(1)}, bf16[2816,128]{1,0:T(8,128)(2,1)S(1)}, u32[]{:S(2)}, u32[]{:S(2)}) collective-permute-start(bf16[2816,128]{1,0:T(8,128)(2,1)S(1)} %bitcast.37), channel_id=1, source_target_pairs={{0,4},{1,5},{2,6},{3,7},{4,0},{5,1},{6,2},{7,3},{8,12},{9,13},{10,... | collective-permute-start | bytes 2162696 | tf_op jit(solution)/shard_map/ppermute | solution.py:32

commit v8 on v6

--- a/solution.py
+++ b/solution.py
@@ -67,12 +67,15 @@
     return lax.dynamic_index_in_dim(parts, digit, 0, keepdims=False)
 
 
-def scatter_ring(parts, digit, ring):
-    received = [send(pick(parts, digit ^ step), ring(step)) for step in (1, 2, 3)]
+def scatter_ring(parts, digit, ring, extra):
+    rows = parts.shape[1]
+    first = jnp.concatenate([pick(parts, digit ^ 1), extra], axis=0)
+    first = send(first, ring(1))
+    received = [first[:rows]] + [send(pick(parts, digit ^ step), ring(step)) for step in (2, 3)]
     total = wide(pick(parts, digit))
     for part in received:
         total = total + wide(part)
-    return narrow(total)
+    return narrow(total), first[rows:]
 
 
 def swap(first, second, flip):
@@ -103,15 +106,18 @@
     ring_two = jnp.where(core == 0, near, far)
     rows, lanes = mine.shape[0] // (RING_X * RING_Y), mine.shape[1]
     part = narrow(wide(mine) + wide(send(other, across_core)))
-    part = scatter_ring(part.reshape(RING_X, RING_Y * rows, lanes), ring_one, first_ring)
-    part, coarse = lax.optimization_barrier((part, coarse))
-    shares = coarse.reshape(RING_X, coarse.shape[0] // RING_X, coarse.shape[1])
-    shares = lax.all_to_all(shares, "x", split_axis=0, concat_axis=0, tiled=True)
-    coarse_out = narrow(jnp.sum(wide(shares), axis=0))
-    part = scatter_ring(part.reshape(RING_Y, rows, lanes), ring_two, second_ring)
+    hop_one, hop_two = jnp.where(core == 0, 3, 1), jnp.where(core == 0, 1, 3)
+    quarters = coarse.reshape(RING_X, coarse.shape[0] // RING_X, lanes)
+    extra = jnp.concatenate([pick(quarters, x ^ hop_one), pick(quarters, x ^ 2)], axis=0)
+    part, extra = scatter_ring(part.reshape(4, 4 * rows, lanes), ring_one, first_ring, extra)
+    quarter = quarters.shape[1]
+    kept = wide(pick(quarters, x)) + wide(extra[:quarter])
+    passed = narrow(wide(pick(quarters, x ^ hop_two)) + wide(extra[quarter:]))
+    part, extra = scatter_ring(part.reshape(4, rows, lanes), ring_two, second_ring, passed)
+    halves = narrow(kept + wide(extra)).reshape(2, quarter // 2, lanes)
+    coarse_out = jnp.concatenate([halves[0], halves[1]], axis=1)
     for step in (1, 2, 7):
         part = narrow(wide(part) + wide(send(part, along_z(step))))
-    part, coarse_out = lax.optimization_barrier((part, coarse_out))
     part = gather_ring(part, ring_two, second_ring).reshape(RING_Y * rows, lanes)
     part = gather_ring(part, ring_one, first_ring).reshape(RING_X * RING_Y * rows, lanes)
     return wide(gather_pair(part, core, across_core)).reshape(-1, lanes), coarse_out
@@ -211,7 +217,7 @@
     offsets = conv_weight.shape[0]
     octants, _, out_channels = down_weight.shape
     tile_rows, halo_rows = tile_feats.shape[0], incoming.shape[0]
-    coarse_tile = coarse.shape[0]
+    coarse_tile = coarse.shape[0] * channels // out_channels
     feats = part_copies((part0, part1, part2, part3), tile_feats, sems, 0)
     conv = pltpu.make_async_copy(conv_hbm, conv_weight, sems.at[4])
     late = [
@@ -260,7 +266,12 @@
     from_row = from_row.astype(jnp.bfloat16)
     high = own_term.astype(jnp.bfloat16)
     low = (own_term - high.astype(jnp.float32)).astype(jnp.bfloat16)
-    coarse[...] = (matmul(from_row, high) + matmul(from_row, low)).astype(jnp.bfloat16)
+    coarse_sums = (matmul(from_row, high) + matmul(from_row, low)).astype(jnp.bfloat16)
+    quarter = coarse_tile // RING_X
+    for at in range(2 * RING_X):
+        block = coarse_sums[at // 2 * quarter : (at // 2 + 1) * quarter]
+        block = block[:, at % 2 * channels : (at % 2 + 1) * channels]
+        coarse[pl.ds(at * quarter, quarter), :] = block
 
     half_blocks = mine.shape[0] // channels
     down_first = offsets - half_blocks
@@ -353,7 +364,7 @@
     coarse, mine, other = pl.pallas_call(
         step_kernel,
         out_shape=(
-            jax.ShapeDtypeStruct((coarse_tile, out_channels), jnp.bfloat16),
+            jax.ShapeDtypeStruct((coarse_tile * out_channels // channels, channels), jnp.bfloat16),
             jax.ShapeDtypeStruct((half, channels), jnp.bfloat16),
             jax.ShapeDtypeStruct((half, channels), jnp.bfloat16),
         ),

time: 137 us -> 135 us (0.985)
  starting transfers between devices: 54.1 us -> 47.8 us
  waiting for transfers between devices: 39 us -> 41.5 us
    ppermute x23, waiting for transfers between devices: 33.2 us -> 38.4 us  [send(): return lax.ppermute(value, AXES, partner_pairs(partner))]
    all_to_all x1 -> x0, starting transfers between devices: 3.47 us -> none  [sum_over_devices(): lax.all_to_all(shares, 'x', split_axis=0, concat_axis=0, tiled=True)]
    ppermute x23, starting transfers between devices: 35.6 us -> 32.8 us  [send(): return lax.ppermute(value, AXES, partner_pairs(partner))]
    all_to_all x1 -> x0, waiting for transfers between devices: 2.65 us -> none  [sum_over_devices(): lax.all_to_all(shares, 'x', split_axis=0, concat_axis=0, tiled=True)]
    unnamed x21 -> x23, local copies, waits for them, and re-layouts: 3.55 us -> 3.55 us
  transfers between devices with their start and end apart: 25 -> 24, of which waited for: 18 -> 18; matrix products, arithmetic and copies ran while one was open for 3% -> 4% of each run, Pallas kernels for 3% -> 3%
where the time goes in v8:
time: 135 us; the launch traced here: 134 us
  starting transfers between devices  47.8 us (35%)
  waiting for transfers between devices  41.5 us (31%)
  Pallas kernels  31 us (23%)
  local copies, waits for them, and re-layouts  8.93 us (7%)
  other arithmetic  4.1 us (3%)
    ppermute x23, waiting for transfers between devices, send(): return lax.ppermute(value, AXES, partner_pairs(partner))  38.4 us
    ppermute x23, starting transfers between devices, send(): return lax.ppermute(value, AXES, partner_pairs(partner))  32.8 us
    pallas_call x1, Pallas kernels, shards(): pl.pallas_call(step_kernel, out_shape=(jax.ShapeDtypeStruct((coarse_tile...  22.6 us
    all_to_all x1, starting transfers between devices, shards(): lax.all_to_all(outgoing.reshape(tiles, slots, channels), TILE, split_axis...  15.1 us
    pallas_call x1, Pallas kernels, shards(): pl.pallas_call(grad_kernel, out_shape=(jax.ShapeDtypeStruct((rows, out_ch...  4.43 us
    pallas_call x1, Pallas kernels, shards(): pl.pallas_call(pick_halo, out_shape=jax.ShapeDtypeStruct((halo_rows, chan...  3.94 us
    unnamed x23, local copies, waits for them, and re-layouts  3.55 us
    all_to_all x1, waiting for transfers between devices, shards(): lax.all_to_all(outgoing.reshape(tiles, slots, channels), TILE, split_axis...  3.14 us
  transfers between devices with their start and end apart: 24, of which 18 were waited for; matrix products, arithmetic and copies ran while one was open for 4% of the time, Pallas kernels for 3%

profile of v8, /device:TPU:1, one launch (start us, length us, event | category | flops | bytes accessed | tf_op | source)
XLA Modules:
  0.0 134.3 jit_solution(13490795735519684889)
XLA Ops:
  0.7 3.4 %collective-permute-start.2 = (bf16[512,128]{1,0:T(8,128)(2,1)}, bf16[512,128]{1,0:T(8,128)(2,1)S(1)}, u32[]{:S(2)}, u32[]{:S(2)}) collective-permute-start(bf16[512,128]{1,0:T(8,128)(2,1)} %part0.3), channel_id=1, source_target_pairs={{0,3},{1,2},{2,1},{3,0},{4,7},{5,6},{6,5},{7,4},{8,11},{9,10},{10,... | collective-permute-start | bytes 393224 | tf_op jit(solution)/shard_map/ppermute | solution.py:32
  6.2 2.4 %collective-permute-done.2.part3 = bf16[512,128]{1,0:T(8,128)(2,1)S(1)} collective-permute-done((bf16[512,128]{1,0:T(8,128)(2,1)}, bf16[512,128]{1,0:T(8,128)(2,1)S(1)}, u32[]{:S(2)}, u32[]{:S(2)}) %collective-permute-start.2) | collective-permute-done | bytes 131104 | tf_op jit(solution)/shard_map/ppermute | solution.py:32
  8.6 1.1 collective-permute-done.1.part2
  11.0 3.9 %pick_halo.1 = bf16[2048,128]{1,0:T(8,128)(2,1)} custom-call(s32[2048]{0:T(1024)} %reshape.63.lists, bf16[512,128]{1,0:T(8,128)(2,1)} %part0.3, bf16[512,128]{1,0:T(8,128)(2,1)} %copy-done.4, bf16[512,128]{1,0:T(8,128)(2,1)} %copy-done.3, bf16[512,128]{1,0:T(8,128)(2,1)} %copy-done.2), custom_call_target="tpu_custom_call" | custom-call | tf_op jit(solution)/shard_map/pick_halo/pallas_call | solution.py:324
  14.9 15.1 %all-to-all-start = ((bf16[64,32,128]{2,1,0:T(8,128)(2,1)}), bf16[64,32,128]{2,1,0:T(8,128)(2,1)S(1)}, u32[]{:S(2)}, u32[]{:S(2)}) async-start(bf16[64,32,128]{2,1,0:T(8,128)(2,1)} %bitcast.73), calls=%async_computation | async-start | bytes 1048576 | tf_op jit(solution)/shard_map/all_to_all | solution.py:339
  30.0 1.2 collective-permute-start.5
  31.9 1.5 %collective-permute-start.3 = (bf16[256,256]{1,0:T(8,128)(2,1)S(1)}, bf16[256,256]{1,0:T(8,128)(2,1)S(1)}, u32[]{:S(2)}, u32[]{:S(2)}) collective-permute-start(bf16[256,256]{1,0:T(8,128)(2,1)S(1)} %copy-done.5), channel_id=1, source_target_pairs={{0,1},{1,0},{2,3},{3,2},{4,5},{5,4},{6,7},{7,6},{8,9},{9,8},{10,11... | collective-permute-start | bytes 393224 | tf_op jit(solution)/shard_map/ppermute | solution.py:32
  35.6 2.4 %collective-permute-done.5.grad3 = bf16[256,256]{1,0:T(8,128)(2,1)S(1)} collective-permute-done((bf16[256,256]{1,0:T(8,128)(2,1)S(1)}, bf16[256,256]{1,0:T(8,128)(2,1)S(1)}, u32[]{:S(2)}, u32[]{:S(2)}) %collective-permute-start.5) | collective-permute-done | bytes 131104 | tf_op jit(solution)/shard_map/ppermute | solution.py:32
  38.0 1.1 collective-permute-done.3.grad1
  39.7 4.4 %coarse_back.1 = (bf16[512,256]{1,0:T(8,128)(2,1)}, f32[512,128]{1,0:T(8,128)}) custom-call(bf16[256,256]{1,0:T(8,128)(2,1)} %grad0, bf16[256,256]{1,0:T(8,128)(2,1)} %copy-done.8, bf16[256,256]{1,0:T(8,128)(2,1)} %copy-done.7, bf16[256,256]{1,0:T(8,128)(2,1)} %copy-done.6, bf16[8,128,256]{2,1,0:T(8,128)(2,1)} %down_hbm.1, s32[512,1]{1,0:T(8,128)} %copy.11.link_column), custom_call_target="tpu_custom_call" | custom-call | tf_op jit(solution)/shard_map/coarse_back/pallas_call | solution.py:348
  44.2 3.1 %all-to-all-done = bf16[64,32,128]{2,1,0:T(8,128)(2,1)S(1)} async-done(((bf16[64,32,128]{2,1,0:T(8,128)(2,1)}), bf16[64,32,128]{2,1,0:T(8,128)(2,1)S(1)}, u32[]{:S(2)}, u32[]{:S(2)}) %all-to-all-start) | async-done | bytes 524320 | tf_op jit(solution)/shard_map/all_to_all | solution.py:339
  48.1 22.6 %step.1 = (bf16[2048,128]{1,0:T(8,128)(2,1)}, bf16[2816,128]{1,0:T(8,128)(2,1)}, bf16[2816,128]{1,0:T(8,128)(2,1)}) custom-call(s32[13824]{0:T(1024)} %reshape.62.kernel_map, bf16[512,128]{1,0:T(8,128)(2,1)} %part0.3, bf16[512,128]{1,0:T(8,128)(2,1)} %copy-done.4, bf16[512,128]{1,0:T(8,128)(2,1)} %copy-done.3, bf16[512,128]{1,0:T(8,128)(2,1)} %copy-done.2, ...), custom_call_target="tpu_custom_call" | custom-call | tf_op jit(solution)/shard_map/step/pallas_call | solution.py:364
  73.2 1.3 add_convert_fusion
  74.9 1.3 collective-permute-start.8
  76.2 1.3 collective-permute-start.9
  77.5 2.1 %collective-permute-done.8 = bf16[704,128]{1,0:T(8,128)(2,1)S(1)} collective-permute-done((bf16[704,128]{1,0:T(8,128)(2,1)S(1)}, bf16[704,128]{1,0:T(8,128)(2,1)S(1)}, u32[]{:S(2)}, u32[]{:S(2)}) %collective-permute-start.8) | collective-permute-done | bytes 180256 | tf_op jit(solution)/shard_map/ppermute | solution.py:32
  79.6 5.3 %collective-permute-done.9 = bf16[704,128]{1,0:T(8,128)(2,1)S(1)} collective-permute-done((bf16[704,128]{1,0:T(8,128)(2,1)S(1)}, bf16[704,128]{1,0:T(8,128)(2,1)S(1)}, u32[]{:S(2)}, u32[]{:S(2)}) %collective-permute-start.9) | collective-permute-done | bytes 180256 | tf_op jit(solution)/shard_map/ppermute | solution.py:32
  85.1 1.2 collective-permute-start.10
  86.4 2.2 %collective-permute-start.11 = (bf16[176,128]{1,0:T(8,128)(2,1)S(1)}, bf16[176,128]{1,0:T(8,128)(2,1)S(1)}, u32[]{:S(2)}, u32[]{:S(2)}) collective-permute-start(bf16[176,128]{1,0:T(8,128)(2,1)S(1)} %get-tuple-element.34), channel_id=1, source_target_pairs={{0,64},{1,65},{2,66},{3,67},{4,196},{5,197},{6,198},{7,199},{8,72}... | collective-permute-start | bytes 135176 | tf_op jit(solution)/shard_map/ppermute | solution.py:32
  88.6 1.7 %collective-permute-start.12 = (bf16[176,128]{1,0:T(8,128)(2,1)S(1)}, bf16[176,128]{1,0:T(8,128)(2,1)S(1)}, u32[]{:S(2)}, u32[]{:S(2)}) collective-permute-start(bf16[176,128]{1,0:T(8,128)(2,1)S(1)} %get-tuple-element.35), channel_id=1, source_target_pairs={{0,65},{1,64},{2,67},{3,66},{4,199},{5,198},{6,197},{7,196},{8,73}... | collective-permute-start | bytes 135176 | tf_op jit(solution)/shard_map/ppermute | solution.py:32
  90.5 4.3 %collective-permute-done.12 = bf16[176,128]{1,0:T(8,128)(2,1)S(1)} collective-permute-done((bf16[176,128]{1,0:T(8,128)(2,1)S(1)}, bf16[176,128]{1,0:T(8,128)(2,1)S(1)}, u32[]{:S(2)}, u32[]{:S(2)}) %collective-permute-start.12) | collective-permute-done | bytes 45088 | tf_op jit(solution)/shard_map/ppermute | solution.py:32
  95.1 3.1 %collective-permute-done.13 = bf16[176,128]{1,0:T(8,128)(2,1)S(1)} collective-permute-done((bf16[176,128]{1,0:T(8,128)(2,1)S(1)}, bf16[176,128]{1,0:T(8,128)(2,1)S(1)}, u32[]{:S(2)}, u32[]{:S(2)}) %collective-permute-start.13) | collective-permute-done | bytes 45088 | tf_op jit(solution)/shard_map/ppermute | solution.py:32
  99.1 3.1 %collective-permute-done.14 = bf16[176,128]{1,0:T(8,128)(2,1)S(1)} collective-permute-done((bf16[176,128]{1,0:T(8,128)(2,1)S(1)}, bf16[176,128]{1,0:T(8,128)(2,1)S(1)}, u32[]{:S(2)}, u32[]{:S(2)}) %collective-permute-start.14) | collective-permute-done | bytes 45088 | tf_op jit(solution)/shard_map/ppermute | solution.py:32
  102.6 3.8 %collective-permute-done.15 = bf16[176,128]{1,0:T(8,128)(2,1)S(1)} collective-permute-done((bf16[176,128]{1,0:T(8,128)(2,1)S(1)}, bf16[176,128]{1,0:T(8,128)(2,1)S(1)}, u32[]{:S(2)}, u32[]{:S(2)}) %collective-permute-start.15) | collective-permute-done | bytes 45088 | tf_op jit(solution)/shard_map/ppermute | solution.py:32
  106.4 2.1 %collective-permute-start.18 = (bf16[176,128]{1,0:T(8,128)(2,1)S(1)}, bf16[176,128]{1,0:T(8,128)(2,1)S(1)}, u32[]{:S(2)}, u32[]{:S(2)}) collective-permute-start(bf16[176,128]{1,0:T(8,128)(2,1)S(1)} %add_convert_fusion.1), channel_id=1, source_target_pairs={{0,1},{1,0},{2,3},{3,2},{4,7},{5,6},{6,5},{7,4},{8,9},{9,8},{10,11... | collective-permute-start | bytes 135176 | tf_op jit(solution)/shard_map/ppermute | solution.py:32
  109.0 2.5 %collective-permute-start.16 = (bf16[176,128]{1,0:T(8,128)(2,1)S(1)}, bf16[176,128]{1,0:T(8,128)(2,1)S(1)}, u32[]{:S(2)}, u32[]{:S(2)}) collective-permute-start(bf16[176,128]{1,0:T(8,128)(2,1)S(1)} %add_convert_fusion.1), channel_id=1, source_target_pairs={{0,65},{1,64},{2,67},{3,66},{4,199},{5,198},{6,197},{7,196},{8,73}... | collective-permute-start | bytes 135176 | tf_op jit(solution)/shard_map/ppermute | solution.py:32
  112.6 2.7 %collective-permute-done.16 = bf16[176,128]{1,0:T(8,128)(2,1)S(1)} collective-permute-done((bf16[176,128]{1,0:T(8,128)(2,1)S(1)}, bf16[176,128]{1,0:T(8,128)(2,1)S(1)}, u32[]{:S(2)}, u32[]{:S(2)}) %collective-permute-start.16) | collective-permute-done | bytes 45088 | tf_op jit(solution)/shard_map/ppermute | solution.py:32
  115.5 2.5 %collective-permute-start.19 = (bf16[704,128]{1,0:T(8,128)(2,1)S(1)}, bf16[704,128]{1,0:T(8,128)(2,1)S(1)}, u32[]{:S(2)}, u32[]{:S(2)}) collective-permute-start(bf16[704,128]{1,0:T(8,128)(2,1)S(1)} %bitcast.79), channel_id=1, source_target_pairs={{0,195},{1,194},{2,193},{3,192},{4,69},{5,68},{6,71},{7,70},{8,203... | collective-permute-start | bytes 540680 | tf_op jit(solution)/shard_map/ppermute | solution.py:32
  118.1 1.7 %collective-permute-done.21 = bf16[704,128]{1,0:T(8,128)(2,1)S(1)} collective-permute-done((bf16[704,128]{1,0:T(8,128)(2,1)S(1)}, bf16[704,128]{1,0:T(8,128)(2,1)S(1)}, u32[]{:S(2)}, u32[]{:S(2)}) %collective-permute-start.21) | collective-permute-done | bytes 180256 | tf_op jit(solution)/shard_map/ppermute | solution.py:32
  119.7 2.0 %collective-permute-done.20 = bf16[704,128]{1,0:T(8,128)(2,1)S(1)} collective-permute-done((bf16[704,128]{1,0:T(8,128)(2,1)S(1)}, bf16[704,128]{1,0:T(8,128)(2,1)S(1)}, u32[]{:S(2)}, u32[]{:S(2)}) %collective-permute-start.20) | collective-permute-done | bytes 180256 | tf_op jit(solution)/shard_map/ppermute | solution.py:32
  122.0 7.5 %collective-permute-start.22 = (bf16[2816,128]{1,0:T(8,128)(2,1)S(1)}, bf16[2816,128]{1,0:T(8,128)(2,1)S(1)}, u32[]{:S(2)}, u32[]{:S(2)}) collective-permute-start(bf16[2816,128]{1,0:T(8,128)(2,1)S(1)} %bitcast.72), channel_id=1, source_target_pairs={{0,4},{1,5},{2,6},{3,7},{4,0},{5,1},{6,2},{7,3},{8,12},{9,13},{10,... | collective-permute-start | bytes 2162696 | tf_op jit(solution)/shard_map/ppermute | solution.py:32
  131.9 1.3 slice.55
  (71 shorter events, 18.0 us)
Async XLA Ops:
  0.6 29.4 %copy-start.5 = (bf16[256,256]{1,0:T(8,128)(2,1)S(1)}, bf16[256,256]{1,0:T(8,128)(2,1)}, u32[]{:S(2)}) copy-start(bf16[256,256]{1,0:T(8,128)(2,1)} %grad0) | copy-start | bytes 393220
  0.6 32.7 %copy-start.9 = (s32[27,512]{1,0:T(8,128)S(1)}, s32[27,512]{1,0:T(8,128)}, u32[]{:S(2)}) copy-start(s32[27,512]{1,0:T(8,128)} %param.8) | copy-start | bytes 165892
  0.7 7.9 %collective-permute-start.2 = (bf16[512,128]{1,0:T(8,128)(2,1)}, bf16[512,128]{1,0:T(8,128)(2,1)S(1)}, u32[]{:S(2)}, u32[]{:S(2)}) collective-permute-start(bf16[512,128]{1,0:T(8,128)(2,1)} %part0.3), channel_id=1, source_target_pairs={{0,3},{1,2},{2,1},{3,0},{4,7},{5,6},{6,5},{7,4},{8,11},{9,10},{10,... | collective-permute-start | bytes 393224 | tf_op jit(solution)/shard_map/ppermute | solution.py:32
  4.0 5.6 %collective-permute-start.1 = (bf16[512,128]{1,0:T(8,128)(2,1)}, bf16[512,128]{1,0:T(8,128)(2,1)S(1)}, u32[]{:S(2)}, u32[]{:S(2)}) collective-permute-start(bf16[512,128]{1,0:T(8,128)(2,1)} %part0.3), channel_id=1, source_target_pairs={{0,2},{1,3},{2,0},{3,1},{4,6},{5,7},{6,4},{7,5},{8,10},{9,11},{10,... | collective-permute-start | bytes 393224 | tf_op jit(solution)/shard_map/ppermute | solution.py:32
  4.6 5.1 %collective-permute-start = (bf16[512,128]{1,0:T(8,128)(2,1)}, bf16[512,128]{1,0:T(8,128)(2,1)S(1)}, u32[]{:S(2)}, u32[]{:S(2)}) collective-permute-start(bf16[512,128]{1,0:T(8,128)(2,1)} %part0.3), channel_id=1, source_target_pairs={{0,1},{1,0},{2,3},{3,2},{4,5},{5,4},{6,7},{7,6},{8,9},{9,8},{10,11... | collective-permute-start | bytes 393224 | tf_op jit(solution)/shard_map/ppermute | solution.py:32
  8.6 1.1 copy-start.2
  14.9 32.4 %all-to-all-start = ((bf16[64,32,128]{2,1,0:T(8,128)(2,1)}), bf16[64,32,128]{2,1,0:T(8,128)(2,1)S(1)}, u32[]{:S(2)}, u32[]{:S(2)}) async-start(bf16[64,32,128]{2,1,0:T(8,128)(2,1)} %bitcast.73), calls=%async_computation | async-start | bytes 1048576 | tf_op jit(solution)/shard_map/all_to_all | solution.py:339
  30.0 8.0 %collective-permute-start.5 = (bf16[256,256]{1,0:T(8,128)(2,1)S(1)}, bf16[256,256]{1,0:T(8,128)(2,1)S(1)}, u32[]{:S(2)}, u32[]{:S(2)}) collective-permute-start(bf16[256,256]{1,0:T(8,128)(2,1)S(1)} %copy-done.5), channel_id=1, source_target_pairs={{0,3},{1,2},{2,1},{3,0},{4,7},{5,6},{6,5},{7,4},{8,11},{9,10},{10,... | collective-permute-start | bytes 393224 | tf_op jit(solution)/shard_map/ppermute | solution.py:32
  31.3 6.7 %collective-permute-start.4 = (bf16[256,256]{1,0:T(8,128)(2,1)S(1)}, bf16[256,256]{1,0:T(8,128)(2,1)S(1)}, u32[]{:S(2)}, u32[]{:S(2)}) collective-permute-start(bf16[256,256]{1,0:T(8,128)(2,1)S(1)} %copy-done.5), channel_id=1, source_target_pairs={{0,2},{1,3},{2,0},{3,1},{4,6},{5,7},{6,4},{7,5},{8,10},{9,11},{10,... | collective-permute-start | bytes 393224 | tf_op jit(solution)/shard_map/ppermute | solution.py:32
  31.9 7.2 %collective-permute-start.3 = (bf16[256,256]{1,0:T(8,128)(2,1)S(1)}, bf16[256,256]{1,0:T(8,128)(2,1)S(1)}, u32[]{:S(2)}, u32[]{:S(2)}) collective-permute-start(bf16[256,256]{1,0:T(8,128)(2,1)S(1)} %copy-done.5), channel_id=1, source_target_pairs={{0,1},{1,0},{2,3},{3,2},{4,5},{5,4},{6,7},{7,6},{8,9},{9,8},{10,11... | collective-permute-start | bytes 393224 | tf_op jit(solution)/shard_map/ppermute | solution.py:32
  34.7 12.6 %copy-start.10 = (s32[512]{0:T(512)}, s32[512]{0:T(512)S(1)}, u32[]{:S(2)}) copy-start(s32[512]{0:T(512)S(1)} %dynamic_slice.42) | copy-start | bytes 6148
  38.0 1.1 copy-start.6
  38.0 1.1 copy-start.7
  47.3 0.8 copy-start
  70.7 2.5 %collective-permute-start.6 = (bf16[2816,128]{1,0:T(8,128)(2,1)}, bf16[2816,128]{1,0:T(8,128)(2,1)S(1)}, u32[]{:S(2)}, u32[]{:S(2)}) collective-permute-start(bf16[2816,128]{1,0:T(8,128)(2,1)} %get-tuple-element.16), channel_id=1, source_target_pairs={{0,4},{1,5},{2,6},{3,7},{4,0},{5,1},{6,2},{7,3},{8,12},{9,13},{10,... | collective-permute-start | bytes 2162696 | tf_op jit(solution)/shard_map/ppermute | solution.py:32
  74.5 10.5 %copy-start.1 = (bf16[2048,128]{1,0:T(8,128)(2,1)S(1)}, bf16[2048,128]{1,0:T(8,128)(2,1)}, u32[]{:S(2)}) copy-start(bf16[2048,128]{1,0:T(8,128)(2,1)} %get-tuple-element.14) | copy-start | bytes 1572868
  74.6 10.3 %collective-permute-start.7 = (bf16[1728,128]{1,0:T(8,128)(2,1)S(1)}, bf16[1728,128]{1,0:T(8,128)(2,1)S(1)}, u32[]{:S(2)}, u32[]{:S(2)}) collective-permute-start(bf16[1728,128]{1,0:T(8,128)(2,1)S(1)} %pad_maximum_fusion.3), channel_id=1, source_target_pairs={{0,3},{1,2},{2,1},{3,0},{4,5},{5,4},{6,7},{7,6},{8,11},{9,10},{10,... | collective-permute-start | bytes 1327112 | tf_op jit(solution)/shard_map/ppermute | solution.py:32
  74.9 4.7 %collective-permute-start.8 = (bf16[704,128]{1,0:T(8,128)(2,1)S(1)}, bf16[704,128]{1,0:T(8,128)(2,1)S(1)}, u32[]{:S(2)}, u32[]{:S(2)}) collective-permute-start(bf16[704,128]{1,0:T(8,128)(2,1)S(1)} %get-tuple-element.25), channel_id=1, source_target_pairs={{0,192},{1,193},{2,194},{3,195},{4,68},{5,69},{6,70},{7,71},{8,200... | collective-permute-start | bytes 540680 | tf_op jit(solution)/shard_map/ppermute | solution.py:32
  76.2 8.7 %collective-permute-start.9 = (bf16[704,128]{1,0:T(8,128)(2,1)S(1)}, bf16[704,128]{1,0:T(8,128)(2,1)S(1)}, u32[]{:S(2)}, u32[]{:S(2)}) collective-permute-start(bf16[704,128]{1,0:T(8,128)(2,1)S(1)} %get-tuple-element.26), channel_id=1, source_target_pairs={{0,195},{1,194},{2,193},{3,192},{4,69},{5,68},{6,71},{7,70},{8,203... | collective-permute-start | bytes 540680 | tf_op jit(solution)/shard_map/ppermute | solution.py:32
  85.1 9.7 %collective-permute-start.10 = (bf16[688,128]{1,0:T(8,128)(2,1)S(1)}, bf16[688,128]{1,0:T(8,128)(2,1)S(1)}, u32[]{:S(2)}, u32[]{:S(2)}) collective-permute-start(bf16[688,128]{1,0:T(8,128)(2,1)S(1)} %pad_maximum_fusion.5), channel_id=1, source_target_pairs={{0,1},{1,0},{2,3},{3,2},{4,7},{5,6},{6,5},{7,4},{8,9},{9,8},{10,11... | collective-permute-start | bytes 528392 | tf_op jit(solution)/shard_map/ppermute | solution.py:32
  86.4 4.1 %collective-permute-start.11 = (bf16[176,128]{1,0:T(8,128)(2,1)S(1)}, bf16[176,128]{1,0:T(8,128)(2,1)S(1)}, u32[]{:S(2)}, u32[]{:S(2)}) collective-permute-start(bf16[176,128]{1,0:T(8,128)(2,1)S(1)} %get-tuple-element.34), channel_id=1, source_target_pairs={{0,64},{1,65},{2,66},{3,67},{4,196},{5,197},{6,198},{7,199},{8,72}... | collective-permute-start | bytes 135176 | tf_op jit(solution)/shard_map/ppermute | solution.py:32
  88.6 6.2 %collective-permute-start.12 = (bf16[176,128]{1,0:T(8,128)(2,1)S(1)}, bf16[176,128]{1,0:T(8,128)(2,1)S(1)}, u32[]{:S(2)}, u32[]{:S(2)}) collective-permute-start(bf16[176,128]{1,0:T(8,128)(2,1)S(1)} %get-tuple-element.35), channel_id=1, source_target_pairs={{0,65},{1,64},{2,67},{3,66},{4,199},{5,198},{6,197},{7,196},{8,73}... | collective-permute-start | bytes 135176 | tf_op jit(solution)/shard_map/ppermute | solution.py:32
  94.8 3.4 %collective-permute-start.13 = (bf16[176,128]{1,0:T(8,128)(2,1)S(1)}, bf16[176,128]{1,0:T(8,128)(2,1)S(1)}, u32[]{:S(2)}, u32[]{:S(2)}) collective-permute-start(bf16[176,128]{1,0:T(8,128)(2,1)S(1)} %fusion.8), channel_id=1, source_target_pairs={{0,8},{1,9},{2,10},{3,11},{4,12},{5,13},{6,14},{7,15},{8,0},{9,1},... | collective-permute-start | bytes 135176 | tf_op jit(solution)/shard_map/ppermute | solution.py:32
  98.3 3.9 %collective-permute-start.14 = (bf16[176,128]{1,0:T(8,128)(2,1)S(1)}, bf16[176,128]{1,0:T(8,128)(2,1)S(1)}, u32[]{:S(2)}, u32[]{:S(2)}) collective-permute-start(bf16[176,128]{1,0:T(8,128)(2,1)S(1)} %add_convert_fusion.3), channel_id=1, source_target_pairs={{0,16},{1,17},{2,18},{3,19},{4,20},{5,21},{6,22},{7,23},{8,24},{9,... | collective-permute-start | bytes 135176 | tf_op jit(solution)/shard_map/ppermute | solution.py:32
  102.2 4.2 %collective-permute-start.15 = (bf16[176,128]{1,0:T(8,128)(2,1)S(1)}, bf16[176,128]{1,0:T(8,128)(2,1)S(1)}, u32[]{:S(2)}, u32[]{:S(2)}) collective-permute-start(bf16[176,128]{1,0:T(8,128)(2,1)S(1)} %add_convert_fusion.2), channel_id=1, source_target_pairs={{0,56},{1,57},{2,58},{3,59},{4,60},{5,61},{6,62},{7,63},{8,48},{9,... | collective-permute-start | bytes 135176 | tf_op jit(solution)/shard_map/ppermute | solution.py:32
  106.4 5.2 %collective-permute-start.18 = (bf16[176,128]{1,0:T(8,128)(2,1)S(1)}, bf16[176,128]{1,0:T(8,128)(2,1)S(1)}, u32[]{:S(2)}, u32[]{:S(2)}) collective-permute-start(bf16[176,128]{1,0:T(8,128)(2,1)S(1)} %add_convert_fusion.1), channel_id=1, source_target_pairs={{0,1},{1,0},{2,3},{3,2},{4,7},{5,6},{6,5},{7,4},{8,9},{9,8},{10,11... | collective-permute-start | bytes 135176 | tf_op jit(solution)/shard_map/ppermute | solution.py:32
  108.5 4.1 %collective-permute-start.17 = (bf16[176,128]{1,0:T(8,128)(2,1)S(1)}, bf16[176,128]{1,0:T(8,128)(2,1)S(1)}, u32[]{:S(2)}, u32[]{:S(2)}) collective-permute-start(bf16[176,128]{1,0:T(8,128)(2,1)S(1)} %add_convert_fusion.1), channel_id=1, source_target_pairs={{0,64},{1,65},{2,66},{3,67},{4,196},{5,197},{6,198},{7,199},{8,72}... | collective-permute-start | bytes 135176 | tf_op jit(solution)/shard_map/ppermute | solution.py:32
  109.0 6.2 %collective-permute-start.16 = (bf16[176,128]{1,0:T(8,128)(2,1)S(1)}, bf16[176,128]{1,0:T(8,128)(2,1)S(1)}, u32[]{:S(2)}, u32[]{:S(2)}) collective-permute-start(bf16[176,128]{1,0:T(8,128)(2,1)S(1)} %add_convert_fusion.1), channel_id=1, source_target_pairs={{0,65},{1,64},{2,67},{3,66},{4,199},{5,198},{6,197},{7,196},{8,73}... | collective-permute-start | bytes 135176 | tf_op jit(solution)/shard_map/ppermute | solution.py:32
  115.3 4.4 %collective-permute-start.21 = (bf16[704,128]{1,0:T(8,128)(2,1)S(1)}, bf16[704,128]{1,0:T(8,128)(2,1)S(1)}, u32[]{:S(2)}, u32[]{:S(2)}) collective-permute-start(bf16[704,128]{1,0:T(8,128)(2,1)S(1)} %bitcast.77), channel_id=1, source_target_pairs={{0,3},{1,2},{2,1},{3,0},{4,5},{5,4},{6,7},{7,6},{8,11},{9,10},{10,... | collective-permute-start | bytes 540680 | tf_op jit(solution)/shard_map/ppermute | solution.py:32
  115.4 6.4 %collective-permute-start.20 = (bf16[704,128]{1,0:T(8,128)(2,1)S(1)}, bf16[704,128]{1,0:T(8,128)(2,1)S(1)}, u32[]{:S(2)}, u32[]{:S(2)}) collective-permute-start(bf16[704,128]{1,0:T(8,128)(2,1)S(1)} %bitcast.78), channel_id=1, source_target_pairs={{0,192},{1,193},{2,194},{3,195},{4,68},{5,69},{6,70},{7,71},{8,200... | collective-permute-start | bytes 540680 | tf_op jit(solution)/shard_map/ppermute | solution.py:32
  115.5 6.3 %collective-permute-start.19 = (bf16[704,128]{1,0:T(8,128)(2,1)S(1)}, bf16[704,128]{1,0:T(8,128)(2,1)S(1)}, u32[]{:S(2)}, u32[]{:S(2)}) collective-permute-start(bf16[704,128]{1,0:T(8,128)(2,1)S(1)} %bitcast.79), channel_id=1, source_target_pairs={{0,195},{1,194},{2,193},{3,192},{4,69},{5,68},{6,71},{7,70},{8,203... | collective-permute-start | bytes 540680 | tf_op jit(solution)/shard_map/ppermute | solution.py:32
  122.0 9.3 %collective-permute-start.22 = (bf16[2816,128]{1,0:T(8,128)(2,1)S(1)}, bf16[2816,128]{1,0:T(8,128)(2,1)S(1)}, u32[]{:S(2)}, u32[]{:S(2)}) collective-permute-start(bf16[2816,128]{1,0:T(8,128)(2,1)S(1)} %bitcast.72), channel_id=1, source_target_pairs={{0,4},{1,5},{2,6},{3,7},{4,0},{5,1},{6,2},{7,3},{8,12},{9,13},{10,... | collective-permute-start | bytes 2162696 | tf_op jit(solution)/shard_map/ppermute | solution.py:32
  (3 other events, 2.0 us)

commit v9 on v8

--- a/solution.py
+++ b/solution.py
@@ -146,6 +146,18 @@
         places = range(start, min(start + UNROLL, count))
         rows = [table[pl.ds(picks[first + at], 1), :] for at in places]
         for at, row in zip(places, rows):
+            target[at : at + 1, :] = row
+
+
+def copy_pairs(table, target, words, first, count):
+    half = count // 2
+    for start in range(0, half, UNROLL // 2):
+        rows = []
+        for at in range(start, start + UNROLL // 2):
+            word = words[first + at]
+            rows.append((at, table[pl.ds(word & 0xFFFF, 1), :]))
+            rows.append((half + at, table[pl.ds(lax.shift_right_logical(word, 16), 1), :]))
+        for at, row in rows:
             target[at : at + 1, :] = row
 
 
@@ -241,7 +253,7 @@
     def forward(at, previous):
         offset = at + (at >= middle).astype(jnp.int32)
         pre_act[...] += matmul(gathered[previous], conv_weight[previous])
-        copy_rows(table, stage, kernel_map, offset * rows, rows)
+        copy_pairs(table, stage, kernel_map, offset * (rows // 2), rows)
         gathered[offset] = stage[...].astype(jnp.bfloat16)
         return offset
 
@@ -286,7 +298,7 @@
 
             return body
 
-        lax.fori_loop(0, half_blocks, backward(first, 0), 0, unroll=2)
+        lax.fori_loop(0, half_blocks, backward(first, 0), 0, unroll=11)
         lax.fori_loop(0, down_first, backward(second, half_blocks), 0, unroll=True)
         for o in range(octants):
             only = jnp.where(octant_turned == o, hidden_turned, jnp.zeros_like(hidden_turned))
@@ -361,6 +373,8 @@
         name="coarse_back",
     )(*grads, down_weight, link_column)
     half = total // CORES
+    map_pairs = kernel_map[:, : rows // 2] | (kernel_map[:, rows // 2 :] << 16)
+    map_pairs = map_pairs.reshape(offsets * rows // 2)
     coarse, mine, other = pl.pallas_call(
         step_kernel,
         out_shape=(
@@ -385,7 +399,7 @@
         compiler_params=pltpu.CompilerParams(vmem_limit_bytes=56 << 20),
         name="step",
     )(
-        kernel_map.reshape(offsets * rows), *parts, incoming.reshape(halo_rows, channels),
+        map_pairs, *parts, incoming.reshape(halo_rows, channels),
         conv_weight, down_weight, parent_grad, back_grad, link_column, link_row,
     )
     sums, coarse_out = sum_over_devices(mine, other, coarse)

time: 135 us -> 132 us (0.978)
  Pallas kernels: 31 us -> 28 us
    pallas_call x1, Pallas kernels: 22.6 us -> 19.6 us  [shards(): pl.pallas_call(step_kernel, out_shape=(jax.ShapeDtypeStruct((coarse_tile...]
where the time goes in v9:
time: 132 us; the launch traced here: 131 us
  starting transfers between devices  47.8 us (36%)
  waiting for transfers between devices  41.6 us (32%)
  Pallas kernels  28 us (21%)
  local copies, waits for them, and re-layouts  8.91 us (7%)
  other arithmetic  4.11 us (3%)
    ppermute x23, waiting for transfers between devices, send(): return lax.ppermute(value, AXES, partner_pairs(partner))  38.4 us
    ppermute x23, starting transfers between devices, send(): return lax.ppermute(value, AXES, partner_pairs(partner))  32.7 us
    pallas_call x1, Pallas kernels, shards(): pl.pallas_call(step_kernel, out_shape=(jax.ShapeDtypeStruct((coarse_tile...  19.6 us
    all_to_all x1, starting transfers between devices, shards(): lax.all_to_all(outgoing.reshape(tiles, slots, channels), TILE, split_axis...  15.1 us
    pallas_call x1, Pallas kernels, shards(): pl.pallas_call(grad_kernel, out_shape=(jax.ShapeDtypeStruct((rows, out_ch...  4.43 us
    pallas_call x1, Pallas kernels, shards(): pl.pallas_call(pick_halo, out_shape=jax.ShapeDtypeStruct((halo_rows, chan...  3.94 us
    unnamed x23, local copies, waits for them, and re-layouts  3.55 us
    all_to_all x1, waiting for transfers between devices, shards(): lax.all_to_all(outgoing.reshape(tiles, slots, channels), TILE, split_axis...  3.14 us
  transfers between devices with their start and end apart: 24, of which 18 were waited for; matrix products, arithmetic and copies ran while one was open for 4% of the time, Pallas kernels for 3%

profile of v9, /device:TPU:1, one launch (start us, length us, event | category | flops | bytes accessed | tf_op | source)
XLA Modules:
  0.0 131.2 jit_solution(8500930349288676925)
XLA Ops:
  0.7 3.4 %collective-permute-start.2 = (bf16[512,128]{1,0:T(8,128)(2,1)}, bf16[512,128]{1,0:T(8,128)(2,1)S(1)}, u32[]{:S(2)}, u32[]{:S(2)}) collective-permute-start(bf16[512,128]{1,0:T(8,128)(2,1)} %part0.3), channel_id=1, source_target_pairs={{0,3},{1,2},{2,1},{3,0},{4,7},{5,6},{6,5},{7,4},{8,11},{9,10},{10,... | collective-permute-start | bytes 393224 | tf_op jit(solution)/shard_map/ppermute | solution.py:32
  6.2 2.4 %collective-permute-done.2.part3 = bf16[512,128]{1,0:T(8,128)(2,1)S(1)} collective-permute-done((bf16[512,128]{1,0:T(8,128)(2,1)}, bf16[512,128]{1,0:T(8,128)(2,1)S(1)}, u32[]{:S(2)}, u32[]{:S(2)}) %collective-permute-start.2) | collective-permute-done | bytes 131104 | tf_op jit(solution)/shard_map/ppermute | solution.py:32
  8.6 1.1 collective-permute-done.1.part2
  11.0 3.9 %pick_halo.1 = bf16[2048,128]{1,0:T(8,128)(2,1)} custom-call(s32[2048]{0:T(1024)} %reshape.63.lists, bf16[512,128]{1,0:T(8,128)(2,1)} %part0.3, bf16[512,128]{1,0:T(8,128)(2,1)} %copy-done.4, bf16[512,128]{1,0:T(8,128)(2,1)} %copy-done.3, bf16[512,128]{1,0:T(8,128)(2,1)} %copy-done.2), custom_call_target="tpu_custom_call" | custom-call | tf_op jit(solution)/shard_map/pick_halo/pallas_call | solution.py:336
  14.9 15.1 %all-to-all-start = ((bf16[64,32,128]{2,1,0:T(8,128)(2,1)}), bf16[64,32,128]{2,1,0:T(8,128)(2,1)S(1)}, u32[]{:S(2)}, u32[]{:S(2)}) async-start(bf16[64,32,128]{2,1,0:T(8,128)(2,1)} %bitcast.73), calls=%async_computation | async-start | bytes 1048576 | tf_op jit(solution)/shard_map/all_to_all | solution.py:351
  30.0 1.2 collective-permute-start.5
  31.9 1.5 %collective-permute-start.3 = (bf16[256,256]{1,0:T(8,128)(2,1)S(1)}, bf16[256,256]{1,0:T(8,128)(2,1)S(1)}, u32[]{:S(2)}, u32[]{:S(2)}) collective-permute-start(bf16[256,256]{1,0:T(8,128)(2,1)S(1)} %copy-done.5), channel_id=1, source_target_pairs={{0,1},{1,0},{2,3},{3,2},{4,5},{5,4},{6,7},{7,6},{8,9},{9,8},{10,11... | collective-permute-start | bytes 393224 | tf_op jit(solution)/shard_map/ppermute | solution.py:32
  35.6 2.4 %collective-permute-done.5.grad3 = bf16[256,256]{1,0:T(8,128)(2,1)S(1)} collective-permute-done((bf16[256,256]{1,0:T(8,128)(2,1)S(1)}, bf16[256,256]{1,0:T(8,128)(2,1)S(1)}, u32[]{:S(2)}, u32[]{:S(2)}) %collective-permute-start.5) | collective-permute-done | bytes 131104 | tf_op jit(solution)/shard_map/ppermute | solution.py:32
  38.0 1.1 collective-permute-done.3.grad1
  39.7 4.4 %coarse_back.1 = (bf16[512,256]{1,0:T(8,128)(2,1)}, f32[512,128]{1,0:T(8,128)}) custom-call(bf16[256,256]{1,0:T(8,128)(2,1)} %grad0, bf16[256,256]{1,0:T(8,128)(2,1)} %copy-done.8, bf16[256,256]{1,0:T(8,128)(2,1)} %copy-done.7, bf16[256,256]{1,0:T(8,128)(2,1)} %copy-done.6, bf16[8,128,256]{2,1,0:T(8,128)(2,1)} %down_hbm.1, s32[512,1]{1,0:T(8,128)} %copy.11.link_column), custom_call_target="tpu_custom_call" | custom-call | tf_op jit(solution)/shard_map/coarse_back/pallas_call | solution.py:360
  44.2 3.1 %all-to-all-done = bf16[64,32,128]{2,1,0:T(8,128)(2,1)S(1)} async-done(((bf16[64,32,128]{2,1,0:T(8,128)(2,1)}), bf16[64,32,128]{2,1,0:T(8,128)(2,1)S(1)}, u32[]{:S(2)}, u32[]{:S(2)}) %all-to-all-start) | async-done | bytes 524320 | tf_op jit(solution)/shard_map/all_to_all | solution.py:351
  48.1 19.6 %step.1 = (bf16[2048,128]{1,0:T(8,128)(2,1)}, bf16[2816,128]{1,0:T(8,128)(2,1)}, bf16[2816,128]{1,0:T(8,128)(2,1)}) custom-call(s32[6912]{0:T(1024)} %reshape.62.kernel_map, bf16[512,128]{1,0:T(8,128)(2,1)} %part0.3, bf16[512,128]{1,0:T(8,128)(2,1)} %copy-done.4, bf16[512,128]{1,0:T(8,128)(2,1)} %copy-done.3, bf16[512,128]{1,0:T(8,128)(2,1)} %copy-done.2, ...), custom_call_target="tpu_custom_call" | custom-call | tf_op jit(solution)/shard_map/step/pallas_call | solution.py:378
  70.4 1.3 add_convert_fusion
  71.9 1.3 %collective-permute-start.8 = (bf16[704,128]{1,0:T(8,128)(2,1)S(1)}, bf16[704,128]{1,0:T(8,128)(2,1)S(1)}, u32[]{:S(2)}, u32[]{:S(2)}) collective-permute-start(bf16[704,128]{1,0:T(8,128)(2,1)S(1)} %get-tuple-element.25), channel_id=1, source_target_pairs={{0,192},{1,193},{2,194},{3,195},{4,68},{5,69},{6,70},{7,71},{8,200... | collective-permute-start | bytes 540680 | tf_op jit(solution)/shard_map/ppermute | solution.py:32
  73.2 1.3 %collective-permute-start.9 = (bf16[704,128]{1,0:T(8,128)(2,1)S(1)}, bf16[704,128]{1,0:T(8,128)(2,1)S(1)}, u32[]{:S(2)}, u32[]{:S(2)}) collective-permute-start(bf16[704,128]{1,0:T(8,128)(2,1)S(1)} %get-tuple-element.26), channel_id=1, source_target_pairs={{0,195},{1,194},{2,193},{3,192},{4,69},{5,68},{6,71},{7,70},{8,203... | collective-permute-start | bytes 540680 | tf_op jit(solution)/shard_map/ppermute | solution.py:32
  74.5 2.1 %collective-permute-done.8 = bf16[704,128]{1,0:T(8,128)(2,1)S(1)} collective-permute-done((bf16[704,128]{1,0:T(8,128)(2,1)S(1)}, bf16[704,128]{1,0:T(8,128)(2,1)S(1)}, u32[]{:S(2)}, u32[]{:S(2)}) %collective-permute-start.8) | collective-permute-done | bytes 180256 | tf_op jit(solution)/shard_map/ppermute | solution.py:32
  76.6 5.3 %collective-permute-done.9 = bf16[704,128]{1,0:T(8,128)(2,1)S(1)} collective-permute-done((bf16[704,128]{1,0:T(8,128)(2,1)S(1)}, bf16[704,128]{1,0:T(8,128)(2,1)S(1)}, u32[]{:S(2)}, u32[]{:S(2)}) %collective-permute-start.9) | collective-permute-done | bytes 180256 | tf_op jit(solution)/shard_map/ppermute | solution.py:32
  82.1 1.2 collective-permute-start.10
  83.4 2.2 %collective-permute-start.11 = (bf16[176,128]{1,0:T(8,128)(2,1)S(1)}, bf16[176,128]{1,0:T(8,128)(2,1)S(1)}, u32[]{:S(2)}, u32[]{:S(2)}) collective-permute-start(bf16[176,128]{1,0:T(8,128)(2,1)S(1)} %get-tuple-element.34), channel_id=1, source_target_pairs={{0,64},{1,65},{2,66},{3,67},{4,196},{5,197},{6,198},{7,199},{8,72}... | collective-permute-start | bytes 135176 | tf_op jit(solution)/shard_map/ppermute | solution.py:32
  85.6 1.7 %collective-permute-start.12 = (bf16[176,128]{1,0:T(8,128)(2,1)S(1)}, bf16[176,128]{1,0:T(8,128)(2,1)S(1)}, u32[]{:S(2)}, u32[]{:S(2)}) collective-permute-start(bf16[176,128]{1,0:T(8,128)(2,1)S(1)} %get-tuple-element.35), channel_id=1, source_target_pairs={{0,65},{1,64},{2,67},{3,66},{4,199},{5,198},{6,197},{7,196},{8,73}... | collective-permute-start | bytes 135176 | tf_op jit(solution)/shard_map/ppermute | solution.py:32
  87.5 4.3 %collective-permute-done.12 = bf16[176,128]{1,0:T(8,128)(2,1)S(1)} collective-permute-done((bf16[176,128]{1,0:T(8,128)(2,1)S(1)}, bf16[176,128]{1,0:T(8,128)(2,1)S(1)}, u32[]{:S(2)}, u32[]{:S(2)}) %collective-permute-start.12) | collective-permute-done | bytes 45088 | tf_op jit(solution)/shard_map/ppermute | solution.py:32
  92.1 3.1 %collective-permute-done.13 = bf16[176,128]{1,0:T(8,128)(2,1)S(1)} collective-permute-done((bf16[176,128]{1,0:T(8,128)(2,1)S(1)}, bf16[176,128]{1,0:T(8,128)(2,1)S(1)}, u32[]{:S(2)}, u32[]{:S(2)}) %collective-permute-start.13) | collective-permute-done | bytes 45088 | tf_op jit(solution)/shard_map/ppermute | solution.py:32
  96.1 3.1 %collective-permute-done.14 = bf16[176,128]{1,0:T(8,128)(2,1)S(1)} collective-permute-done((bf16[176,128]{1,0:T(8,128)(2,1)S(1)}, bf16[176,128]{1,0:T(8,128)(2,1)S(1)}, u32[]{:S(2)}, u32[]{:S(2)}) %collective-permute-start.14) | collective-permute-done | bytes 45088 | tf_op jit(solution)/shard_map/ppermute | solution.py:32
  99.6 3.8 %collective-permute-done.15 = bf16[176,128]{1,0:T(8,128)(2,1)S(1)} collective-permute-done((bf16[176,128]{1,0:T(8,128)(2,1)S(1)}, bf16[176,128]{1,0:T(8,128)(2,1)S(1)}, u32[]{:S(2)}, u32[]{:S(2)}) %collective-permute-start.15) | collective-permute-done | bytes 45088 | tf_op jit(solution)/shard_map/ppermute | solution.py:32
  103.4 2.1 %collective-permute-start.18 = (bf16[176,128]{1,0:T(8,128)(2,1)S(1)}, bf16[176,128]{1,0:T(8,128)(2,1)S(1)}, u32[]{:S(2)}, u32[]{:S(2)}) collective-permute-start(bf16[176,128]{1,0:T(8,128)(2,1)S(1)} %add_convert_fusion.1), channel_id=1, source_target_pairs={{0,1},{1,0},{2,3},{3,2},{4,7},{5,6},{6,5},{7,4},{8,9},{9,8},{10,11... | collective-permute-start | bytes 135176 | tf_op jit(solution)/shard_map/ppermute | solution.py:32
  106.0 2.5 %collective-permute-start.16 = (bf16[176,128]{1,0:T(8,128)(2,1)S(1)}, bf16[176,128]{1,0:T(8,128)(2,1)S(1)}, u32[]{:S(2)}, u32[]{:S(2)}) collective-permute-start(bf16[176,128]{1,0:T(8,128)(2,1)S(1)} %add_convert_fusion.1), channel_id=1, source_target_pairs={{0,65},{1,64},{2,67},{3,66},{4,199},{5,198},{6,197},{7,196},{8,73}... | collective-permute-start | bytes 135176 | tf_op jit(solution)/shard_map/ppermute | solution.py:32
  109.6 2.6 %collective-permute-done.16 = bf16[176,128]{1,0:T(8,128)(2,1)S(1)} collective-permute-done((bf16[176,128]{1,0:T(8,128)(2,1)S(1)}, bf16[176,128]{1,0:T(8,128)(2,1)S(1)}, u32[]{:S(2)}, u32[]{:S(2)}) %collective-permute-start.16) | collective-permute-done | bytes 45088 | tf_op jit(solution)/shard_map/ppermute | solution.py:32
  112.5 2.5 %collective-permute-start.19 = (bf16[704,128]{1,0:T(8,128)(2,1)S(1)}, bf16[704,128]{1,0:T(8,128)(2,1)S(1)}, u32[]{:S(2)}, u32[]{:S(2)}) collective-permute-start(bf16[704,128]{1,0:T(8,128)(2,1)S(1)} %bitcast.79), channel_id=1, source_target_pairs={{0,195},{1,194},{2,193},{3,192},{4,69},{5,68},{6,71},{7,70},{8,203... | collective-permute-start | bytes 540680 | tf_op jit(solution)/shard_map/ppermute | solution.py:32
  115.0 1.7 %collective-permute-done.21 = bf16[704,128]{1,0:T(8,128)(2,1)S(1)} collective-permute-done((bf16[704,128]{1,0:T(8,128)(2,1)S(1)}, bf16[704,128]{1,0:T(8,128)(2,1)S(1)}, u32[]{:S(2)}, u32[]{:S(2)}) %collective-permute-start.21) | collective-permute-done | bytes 180256 | tf_op jit(solution)/shard_map/ppermute | solution.py:32
  116.7 2.0 %collective-permute-done.20 = bf16[704,128]{1,0:T(8,128)(2,1)S(1)} collective-permute-done((bf16[704,128]{1,0:T(8,128)(2,1)S(1)}, bf16[704,128]{1,0:T(8,128)(2,1)S(1)}, u32[]{:S(2)}, u32[]{:S(2)}) %collective-permute-start.20) | collective-permute-done | bytes 180256 | tf_op jit(solution)/shard_map/ppermute | solution.py:32
  118.9 7.5 %collective-permute-start.22 = (bf16[2816,128]{1,0:T(8,128)(2,1)S(1)}, bf16[2816,128]{1,0:T(8,128)(2,1)S(1)}, u32[]{:S(2)}, u32[]{:S(2)}) collective-permute-start(bf16[2816,128]{1,0:T(8,128)(2,1)S(1)} %bitcast.72), channel_id=1, source_target_pairs={{0,4},{1,5},{2,6},{3,7},{4,0},{5,1},{6,2},{7,3},{8,12},{9,13},{10,... | collective-permute-start | bytes 2162696 | tf_op jit(solution)/shard_map/ppermute | solution.py:32
  128.9 1.3 %slice.63 = f32[3456,128]{1,0:T(8,128)} slice(f32[5632,128]{1,0:T(8,128)S(1)} %bitcast_convert_fusion), slice={[0:3456], [0:128]} | slice | bytes 3538944 | tf_op jit(solution)/shard_map/slice | solution.py:406
  (72 shorter events, 18.0 us)
Async XLA Ops:
  0.6 29.4 %copy-start.5 = (bf16[256,256]{1,0:T(8,128)(2,1)S(1)}, bf16[256,256]{1,0:T(8,128)(2,1)}, u32[]{:S(2)}) copy-start(bf16[256,256]{1,0:T(8,128)(2,1)} %grad0) | copy-start | bytes 393220
  0.6 32.7 %copy-start.9 = (s32[27,512]{1,0:T(8,128)S(1)}, s32[27,512]{1,0:T(8,128)}, u32[]{:S(2)}) copy-start(s32[27,512]{1,0:T(8,128)} %param.8) | copy-start | bytes 165892
  0.7 7.9 %collective-permute-start.2 = (bf16[512,128]{1,0:T(8,128)(2,1)}, bf16[512,128]{1,0:T(8,128)(2,1)S(1)}, u32[]{:S(2)}, u32[]{:S(2)}) collective-permute-start(bf16[512,128]{1,0:T(8,128)(2,1)} %part0.3), channel_id=1, source_target_pairs={{0,3},{1,2},{2,1},{3,0},{4,7},{5,6},{6,5},{7,4},{8,11},{9,10},{10,... | collective-permute-start | bytes 393224 | tf_op jit(solution)/shard_map/ppermute | solution.py:32
  4.0 5.6 %collective-permute-start.1 = (bf16[512,128]{1,0:T(8,128)(2,1)}, bf16[512,128]{1,0:T(8,128)(2,1)S(1)}, u32[]{:S(2)}, u32[]{:S(2)}) collective-permute-start(bf16[512,128]{1,0:T(8,128)(2,1)} %part0.3), channel_id=1, source_target_pairs={{0,2},{1,3},{2,0},{3,1},{4,6},{5,7},{6,4},{7,5},{8,10},{9,11},{10,... | collective-permute-start | bytes 393224 | tf_op jit(solution)/shard_map/ppermute | solution.py:32
  4.6 5.1 %collective-permute-start = (bf16[512,128]{1,0:T(8,128)(2,1)}, bf16[512,128]{1,0:T(8,128)(2,1)S(1)}, u32[]{:S(2)}, u32[]{:S(2)}) collective-permute-start(bf16[512,128]{1,0:T(8,128)(2,1)} %part0.3), channel_id=1, source_target_pairs={{0,1},{1,0},{2,3},{3,2},{4,5},{5,4},{6,7},{7,6},{8,9},{9,8},{10,11... | collective-permute-start | bytes 393224 | tf_op jit(solution)/shard_map/ppermute | solution.py:32
  8.6 1.1 copy-start.2
  14.9 32.4 %all-to-all-start = ((bf16[64,32,128]{2,1,0:T(8,128)(2,1)}), bf16[64,32,128]{2,1,0:T(8,128)(2,1)S(1)}, u32[]{:S(2)}, u32[]{:S(2)}) async-start(bf16[64,32,128]{2,1,0:T(8,128)(2,1)} %bitcast.73), calls=%async_computation | async-start | bytes 1048576 | tf_op jit(solution)/shard_map/all_to_all | solution.py:351
  30.0 8.0 %collective-permute-start.5 = (bf16[256,256]{1,0:T(8,128)(2,1)S(1)}, bf16[256,256]{1,0:T(8,128)(2,1)S(1)}, u32[]{:S(2)}, u32[]{:S(2)}) collective-permute-start(bf16[256,256]{1,0:T(8,128)(2,1)S(1)} %copy-done.5), channel_id=1, source_target_pairs={{0,3},{1,2},{2,1},{3,0},{4,7},{5,6},{6,5},{7,4},{8,11},{9,10},{10,... | collective-permute-start | bytes 393224 | tf_op jit(solution)/shard_map/ppermute | solution.py:32
  31.3 6.7 %collective-permute-start.4 = (bf16[256,256]{1,0:T(8,128)(2,1)S(1)}, bf16[256,256]{1,0:T(8,128)(2,1)S(1)}, u32[]{:S(2)}, u32[]{:S(2)}) collective-permute-start(bf16[256,256]{1,0:T(8,128)(2,1)S(1)} %copy-done.5), channel_id=1, source_target_pairs={{0,2},{1,3},{2,0},{3,1},{4,6},{5,7},{6,4},{7,5},{8,10},{9,11},{10,... | collective-permute-start | bytes 393224 | tf_op jit(solution)/shard_map/ppermute | solution.py:32
  31.9 7.2 %collective-permute-start.3 = (bf16[256,256]{1,0:T(8,128)(2,1)S(1)}, bf16[256,256]{1,0:T(8,128)(2,1)S(1)}, u32[]{:S(2)}, u32[]{:S(2)}) collective-permute-start(bf16[256,256]{1,0:T(8,128)(2,1)S(1)} %copy-done.5), channel_id=1, source_target_pairs={{0,1},{1,0},{2,3},{3,2},{4,5},{5,4},{6,7},{7,6},{8,9},{9,8},{10,11... | collective-permute-start | bytes 393224 | tf_op jit(solution)/shard_map/ppermute | solution.py:32
  34.7 12.6 %copy-start.10 = (s32[512]{0:T(512)}, s32[512]{0:T(512)S(1)}, u32[]{:S(2)}) copy-start(s32[512]{0:T(512)S(1)} %dynamic_slice.42) | copy-start | bytes 6148
  38.0 1.1 copy-start.6
  38.0 1.1 copy-start.7
  47.3 0.8 copy-start
  67.7 2.7 %collective-permute-start.6 = (bf16[2816,128]{1,0:T(8,128)(2,1)}, bf16[2816,128]{1,0:T(8,128)(2,1)S(1)}, u32[]{:S(2)}, u32[]{:S(2)}) collective-permute-start(bf16[2816,128]{1,0:T(8,128)(2,1)} %get-tuple-element.16), channel_id=1, source_target_pairs={{0,4},{1,5},{2,6},{3,7},{4,0},{5,1},{6,2},{7,3},{8,12},{9,13},{10,... | collective-permute-start | bytes 2162696 | tf_op jit(solution)/shard_map/ppermute | solution.py:32
  71.7 10.4 %copy-start.1 = (bf16[2048,128]{1,0:T(8,128)(2,1)S(1)}, bf16[2048,128]{1,0:T(8,128)(2,1)}, u32[]{:S(2)}) copy-start(bf16[2048,128]{1,0:T(8,128)(2,1)} %get-tuple-element.14) | copy-start | bytes 1572868
  71.8 10.1 %collective-permute-start.7 = (bf16[1728,128]{1,0:T(8,128)(2,1)S(1)}, bf16[1728,128]{1,0:T(8,128)(2,1)S(1)}, u32[]{:S(2)}, u32[]{:S(2)}) collective-permute-start(bf16[1728,128]{1,0:T(8,128)(2,1)S(1)} %pad_maximum_fusion.3), channel_id=1, source_target_pairs={{0,3},{1,2},{2,1},{3,0},{4,5},{5,4},{6,7},{7,6},{8,11},{9,10},{10,... | collective-permute-start | bytes 1327112 | tf_op jit(solution)/shard_map/ppermute | solution.py:32
  71.9 4.7 %collective-permute-start.8 = (bf16[704,128]{1,0:T(8,128)(2,1)S(1)}, bf16[704,128]{1,0:T(8,128)(2,1)S(1)}, u32[]{:S(2)}, u32[]{:S(2)}) collective-permute-start(bf16[704,128]{1,0:T(8,128)(2,1)S(1)} %get-tuple-element.25), channel_id=1, source_target_pairs={{0,192},{1,193},{2,194},{3,195},{4,68},{5,69},{6,70},{7,71},{8,200... | collective-permute-start | bytes 540680 | tf_op jit(solution)/shard_map/ppermute | solution.py:32
  73.2 8.7 %collective-permute-start.9 = (bf16[704,128]{1,0:T(8,128)(2,1)S(1)}, bf16[704,128]{1,0:T(8,128)(2,1)S(1)}, u32[]{:S(2)}, u32[]{:S(2)}) collective-permute-start(bf16[704,128]{1,0:T(8,128)(2,1)S(1)} %get-tuple-element.26), channel_id=1, source_target_pairs={{0,195},{1,194},{2,193},{3,192},{4,69},{5,68},{6,71},{7,70},{8,203... | collective-permute-start | bytes 540680 | tf_op jit(solution)/shard_map/ppermute | solution.py:32
  82.1 9.7 %collective-permute-start.10 = (bf16[688,128]{1,0:T(8,128)(2,1)S(1)}, bf16[688,128]{1,0:T(8,128)(2,1)S(1)}, u32[]{:S(2)}, u32[]{:S(2)}) collective-permute-start(bf16[688,128]{1,0:T(8,128)(2,1)S(1)} %pad_maximum_fusion.5), channel_id=1, source_target_pairs={{0,1},{1,0},{2,3},{3,2},{4,7},{5,6},{6,5},{7,4},{8,9},{9,8},{10,11... | collective-permute-start | bytes 528392 | tf_op jit(solution)/shard_map/ppermute | solution.py:32
  83.4 4.1 %collective-permute-start.11 = (bf16[176,128]{1,0:T(8,128)(2,1)S(1)}, bf16[176,128]{1,0:T(8,128)(2,1)S(1)}, u32[]{:S(2)}, u32[]{:S(2)}) collective-permute-start(bf16[176,128]{1,0:T(8,128)(2,1)S(1)} %get-tuple-element.34), channel_id=1, source_target_pairs={{0,64},{1,65},{2,66},{3,67},{4,196},{5,197},{6,198},{7,199},{8,72}... | collective-permute-start | bytes 135176 | tf_op jit(solution)/shard_map/ppermute | solution.py:32
  85.6 6.2 %collective-permute-start.12 = (bf16[176,128]{1,0:T(8,128)(2,1)S(1)}, bf16[176,128]{1,0:T(8,128)(2,1)S(1)}, u32[]{:S(2)}, u32[]{:S(2)}) collective-permute-start(bf16[176,128]{1,0:T(8,128)(2,1)S(1)} %get-tuple-element.35), channel_id=1, source_target_pairs={{0,65},{1,64},{2,67},{3,66},{4,199},{5,198},{6,197},{7,196},{8,73}... | collective-permute-start | bytes 135176 | tf_op jit(solution)/shard_map/ppermute | solution.py:32
  91.8 3.4 %collective-permute-start.13 = (bf16[176,128]{1,0:T(8,128)(2,1)S(1)}, bf16[176,128]{1,0:T(8,128)(2,1)S(1)}, u32[]{:S(2)}, u32[]{:S(2)}) collective-permute-start(bf16[176,128]{1,0:T(8,128)(2,1)S(1)} %fusion.8), channel_id=1, source_target_pairs={{0,8},{1,9},{2,10},{3,11},{4,12},{5,13},{6,14},{7,15},{8,0},{9,1},... | collective-permute-start | bytes 135176 | tf_op jit(solution)/shard_map/ppermute | solution.py:32
  95.3 3.9 %collective-permute-start.14 = (bf16[176,128]{1,0:T(8,128)(2,1)S(1)}, bf16[176,128]{1,0:T(8,128)(2,1)S(1)}, u32[]{:S(2)}, u32[]{:S(2)}) collective-permute-start(bf16[176,128]{1,0:T(8,128)(2,1)S(1)} %add_convert_fusion.3), channel_id=1, source_target_pairs={{0,16},{1,17},{2,18},{3,19},{4,20},{5,21},{6,22},{7,23},{8,24},{9,... | collective-permute-start | bytes 135176 | tf_op jit(solution)/shard_map/ppermute | solution.py:32
  99.2 4.2 %collective-permute-start.15 = (bf16[176,128]{1,0:T(8,128)(2,1)S(1)}, bf16[176,128]{1,0:T(8,128)(2,1)S(1)}, u32[]{:S(2)}, u32[]{:S(2)}) collective-permute-start(bf16[176,128]{1,0:T(8,128)(2,1)S(1)} %add_convert_fusion.2), channel_id=1, source_target_pairs={{0,56},{1,57},{2,58},{3,59},{4,60},{5,61},{6,62},{7,63},{8,48},{9,... | collective-permute-start | bytes 135176 | tf_op jit(solution)/shard_map/ppermute | solution.py:32
  103.4 5.2 %collective-permute-start.18 = (bf16[176,128]{1,0:T(8,128)(2,1)S(1)}, bf16[176,128]{1,0:T(8,128)(2,1)S(1)}, u32[]{:S(2)}, u32[]{:S(2)}) collective-permute-start(bf16[176,128]{1,0:T(8,128)(2,1)S(1)} %add_convert_fusion.1), channel_id=1, source_target_pairs={{0,1},{1,0},{2,3},{3,2},{4,7},{5,6},{6,5},{7,4},{8,9},{9,8},{10,11... | collective-permute-start | bytes 135176 | tf_op jit(solution)/shard_map/ppermute | solution.py:32
  105.5 4.1 %collective-permute-start.17 = (bf16[176,128]{1,0:T(8,128)(2,1)S(1)}, bf16[176,128]{1,0:T(8,128)(2,1)S(1)}, u32[]{:S(2)}, u32[]{:S(2)}) collective-permute-start(bf16[176,128]{1,0:T(8,128)(2,1)S(1)} %add_convert_fusion.1), channel_id=1, source_target_pairs={{0,64},{1,65},{2,66},{3,67},{4,196},{5,197},{6,198},{7,199},{8,72}... | collective-permute-start | bytes 135176 | tf_op jit(solution)/shard_map/ppermute | solution.py:32
  106.0 6.2 %collective-permute-start.16 = (bf16[176,128]{1,0:T(8,128)(2,1)S(1)}, bf16[176,128]{1,0:T(8,128)(2,1)S(1)}, u32[]{:S(2)}, u32[]{:S(2)}) collective-permute-start(bf16[176,128]{1,0:T(8,128)(2,1)S(1)} %add_convert_fusion.1), channel_id=1, source_target_pairs={{0,65},{1,64},{2,67},{3,66},{4,199},{5,198},{6,197},{7,196},{8,73}... | collective-permute-start | bytes 135176 | tf_op jit(solution)/shard_map/ppermute | solution.py:32
  112.3 4.4 %collective-permute-start.21 = (bf16[704,128]{1,0:T(8,128)(2,1)S(1)}, bf16[704,128]{1,0:T(8,128)(2,1)S(1)}, u32[]{:S(2)}, u32[]{:S(2)}) collective-permute-start(bf16[704,128]{1,0:T(8,128)(2,1)S(1)} %bitcast.77), channel_id=1, source_target_pairs={{0,3},{1,2},{2,1},{3,0},{4,5},{5,4},{6,7},{7,6},{8,11},{9,10},{10,... | collective-permute-start | bytes 540680 | tf_op jit(solution)/shard_map/ppermute | solution.py:32
  112.4 6.4 %collective-permute-start.20 = (bf16[704,128]{1,0:T(8,128)(2,1)S(1)}, bf16[704,128]{1,0:T(8,128)(2,1)S(1)}, u32[]{:S(2)}, u32[]{:S(2)}) collective-permute-start(bf16[704,128]{1,0:T(8,128)(2,1)S(1)} %bitcast.78), channel_id=1, source_target_pairs={{0,192},{1,193},{2,194},{3,195},{4,68},{5,69},{6,70},{7,71},{8,200... | collective-permute-start | bytes 540680 | tf_op jit(solution)/shard_map/ppermute | solution.py:32
  112.5 6.3 %collective-permute-start.19 = (bf16[704,128]{1,0:T(8,128)(2,1)S(1)}, bf16[704,128]{1,0:T(8,128)(2,1)S(1)}, u32[]{:S(2)}, u32[]{:S(2)}) collective-permute-start(bf16[704,128]{1,0:T(8,128)(2,1)S(1)} %bitcast.79), channel_id=1, source_target_pairs={{0,195},{1,194},{2,193},{3,192},{4,69},{5,68},{6,71},{7,70},{8,203... | collective-permute-start | bytes 540680 | tf_op jit(solution)/shard_map/ppermute | solution.py:32
  118.9 9.3 %collective-permute-start.22 = (bf16[2816,128]{1,0:T(8,128)(2,1)S(1)}, bf16[2816,128]{1,0:T(8,128)(2,1)S(1)}, u32[]{:S(2)}, u32[]{:S(2)}) collective-permute-start(bf16[2816,128]{1,0:T(8,128)(2,1)S(1)} %bitcast.72), channel_id=1, source_target_pairs={{0,4},{1,5},{2,6},{3,7},{4,0},{5,1},{6,2},{7,3},{8,12},{9,13},{10,... | collective-permute-start | bytes 2162696 | tf_op jit(solution)/shard_map/ppermute | solution.py:32
  (3 other events, 2.0 us)

commit v10 on v9

--- a/solution.py
+++ b/solution.py
@@ -298,7 +298,7 @@
 
             return body
 
-        lax.fori_loop(0, half_blocks, backward(first, 0), 0, unroll=11)
+        lax.fori_loop(0, half_blocks, backward(first, 0), 0, unroll=True)
         lax.fori_loop(0, down_first, backward(second, half_blocks), 0, unroll=True)
         for o in range(octants):
             only = jnp.where(octant_turned == o, hidden_turned, jnp.zeros_like(hidden_turned))

time: 132 us -> 132 us (level)
  no operation moved by 1% of the time
where the time goes in v10:
time: 132 us; the launch traced here: 131 us
  starting transfers between devices  47.7 us (36%)
  waiting for transfers between devices  41.5 us (31%)
  Pallas kernels  27.7 us (21%)
  local copies, waits for them, and re-layouts  8.91 us (7%)
  other arithmetic  4.11 us (3%)
    ppermute x23, waiting for transfers between devices, send(): return lax.ppermute(value, AXES, partner_pairs(partner))  38.4 us
    ppermute x23, starting transfers between devices, send(): return lax.ppermute(value, AXES, partner_pairs(partner))  32.6 us
    pallas_call x1, Pallas kernels, shards(): pl.pallas_call(step_kernel, out_shape=(jax.ShapeDtypeStruct((coarse_tile...  19.4 us
    all_to_all x1, starting transfers between devices, shards(): lax.all_to_all(outgoing.reshape(tiles, slots, channels), TILE, split_axis...  15.1 us
    pallas_call x1, Pallas kernels, shards(): pl.pallas_call(grad_kernel, out_shape=(jax.ShapeDtypeStruct((rows, out_ch...  4.43 us
    pallas_call x1, Pallas kernels, shards(): pl.pallas_call(pick_halo, out_shape=jax.ShapeDtypeStruct((halo_rows, chan...  3.94 us
    unnamed x23, local copies, waits for them, and re-layouts  3.55 us
    all_to_all x1, waiting for transfers between devices, shards(): lax.all_to_all(outgoing.reshape(tiles, slots, channels), TILE, split_axis...  3.14 us
  transfers between devices with their start and end apart: 24, of which 18 were waited for; matrix products, arithmetic and copies ran while one was open for 4% of the time, Pallas kernels for 3%

profile of v10, /device:TPU:1, one launch (start us, length us, event | category | flops | bytes accessed | tf_op | source)
XLA Modules:
  0.0 130.8 jit_solution(2565936237038966276)
XLA Ops:
  0.7 3.4 %collective-permute-start.2 = (bf16[512,128]{1,0:T(8,128)(2,1)}, bf16[512,128]{1,0:T(8,128)(2,1)S(1)}, u32[]{:S(2)}, u32[]{:S(2)}) collective-permute-start(bf16[512,128]{1,0:T(8,128)(2,1)} %part0.3), channel_id=1, source_target_pairs={{0,3},{1,2},{2,1},{3,0},{4,7},{5,6},{6,5},{7,4},{8,11},{9,10},{10,... | collective-permute-start | bytes 393224 | tf_op jit(solution)/shard_map/ppermute | solution.py:32
  6.2 2.4 %collective-permute-done.2.part3 = bf16[512,128]{1,0:T(8,128)(2,1)S(1)} collective-permute-done((bf16[512,128]{1,0:T(8,128)(2,1)}, bf16[512,128]{1,0:T(8,128)(2,1)S(1)}, u32[]{:S(2)}, u32[]{:S(2)}) %collective-permute-start.2) | collective-permute-done | bytes 131104 | tf_op jit(solution)/shard_map/ppermute | solution.py:32
  8.6 1.1 collective-permute-done.1.part2
  11.0 3.9 %pick_halo.1 = bf16[2048,128]{1,0:T(8,128)(2,1)} custom-call(s32[2048]{0:T(1024)} %reshape.63.lists, bf16[512,128]{1,0:T(8,128)(2,1)} %part0.3, bf16[512,128]{1,0:T(8,128)(2,1)} %copy-done.4, bf16[512,128]{1,0:T(8,128)(2,1)} %copy-done.3, bf16[512,128]{1,0:T(8,128)(2,1)} %copy-done.2), custom_call_target="tpu_custom_call" | custom-call | tf_op jit(solution)/shard_map/pick_halo/pallas_call | solution.py:336
  14.9 15.1 %all-to-all-start = ((bf16[64,32,128]{2,1,0:T(8,128)(2,1)}), bf16[64,32,128]{2,1,0:T(8,128)(2,1)S(1)}, u32[]{:S(2)}, u32[]{:S(2)}) async-start(bf16[64,32,128]{2,1,0:T(8,128)(2,1)} %bitcast.73), calls=%async_computation | async-start | bytes 1048576 | tf_op jit(solution)/shard_map/all_to_all | solution.py:351
  30.0 1.2 collective-permute-start.5
  31.9 1.5 %collective-permute-start.3 = (bf16[256,256]{1,0:T(8,128)(2,1)S(1)}, bf16[256,256]{1,0:T(8,128)(2,1)S(1)}, u32[]{:S(2)}, u32[]{:S(2)}) collective-permute-start(bf16[256,256]{1,0:T(8,128)(2,1)S(1)} %copy-done.5), channel_id=1, source_target_pairs={{0,1},{1,0},{2,3},{3,2},{4,5},{5,4},{6,7},{7,6},{8,9},{9,8},{10,11... | collective-permute-start | bytes 393224 | tf_op jit(solution)/shard_map/ppermute | solution.py:32
  35.6 2.4 %collective-permute-done.5.grad3 = bf16[256,256]{1,0:T(8,128)(2,1)S(1)} collective-permute-done((bf16[256,256]{1,0:T(8,128)(2,1)S(1)}, bf16[256,256]{1,0:T(8,128)(2,1)S(1)}, u32[]{:S(2)}, u32[]{:S(2)}) %collective-permute-start.5) | collective-permute-done | bytes 131104 | tf_op jit(solution)/shard_map/ppermute | solution.py:32
  38.0 1.1 collective-permute-done.3.grad1
  39.7 4.4 %coarse_back.1 = (bf16[512,256]{1,0:T(8,128)(2,1)}, f32[512,128]{1,0:T(8,128)}) custom-call(bf16[256,256]{1,0:T(8,128)(2,1)} %grad0, bf16[256,256]{1,0:T(8,128)(2,1)} %copy-done.8, bf16[256,256]{1,0:T(8,128)(2,1)} %copy-done.7, bf16[256,256]{1,0:T(8,128)(2,1)} %copy-done.6, bf16[8,128,256]{2,1,0:T(8,128)(2,1)} %down_hbm.1, s32[512,1]{1,0:T(8,128)} %copy.11.link_column), custom_call_target="tpu_custom_call" | custom-call | tf_op jit(solution)/shard_map/coarse_back/pallas_call | solution.py:360
  44.2 3.1 %all-to-all-done = bf16[64,32,128]{2,1,0:T(8,128)(2,1)S(1)} async-done(((bf16[64,32,128]{2,1,0:T(8,128)(2,1)}), bf16[64,32,128]{2,1,0:T(8,128)(2,1)S(1)}, u32[]{:S(2)}, u32[]{:S(2)}) %all-to-all-start) | async-done | bytes 524320 | tf_op jit(solution)/shard_map/all_to_all | solution.py:351
  48.1 19.4 %step.1 = (bf16[2048,128]{1,0:T(8,128)(2,1)}, bf16[2816,128]{1,0:T(8,128)(2,1)}, bf16[2816,128]{1,0:T(8,128)(2,1)}) custom-call(s32[6912]{0:T(1024)} %reshape.62.kernel_map, bf16[512,128]{1,0:T(8,128)(2,1)} %part0.3, bf16[512,128]{1,0:T(8,128)(2,1)} %copy-done.4, bf16[512,128]{1,0:T(8,128)(2,1)} %copy-done.3, bf16[512,128]{1,0:T(8,128)(2,1)} %copy-done.2, ...), custom_call_target="tpu_custom_call" | custom-call | tf_op jit(solution)/shard_map/step/pallas_call | solution.py:378
  70.0 1.3 add_convert_fusion
  71.5 1.3 %collective-permute-start.8 = (bf16[704,128]{1,0:T(8,128)(2,1)S(1)}, bf16[704,128]{1,0:T(8,128)(2,1)S(1)}, u32[]{:S(2)}, u32[]{:S(2)}) collective-permute-start(bf16[704,128]{1,0:T(8,128)(2,1)S(1)} %get-tuple-element.25), channel_id=1, source_target_pairs={{0,192},{1,193},{2,194},{3,195},{4,68},{5,69},{6,70},{7,71},{8,200... | collective-permute-start | bytes 540680 | tf_op jit(solution)/shard_map/ppermute | solution.py:32
  72.8 1.3 %collective-permute-start.9 = (bf16[704,128]{1,0:T(8,128)(2,1)S(1)}, bf16[704,128]{1,0:T(8,128)(2,1)S(1)}, u32[]{:S(2)}, u32[]{:S(2)}) collective-permute-start(bf16[704,128]{1,0:T(8,128)(2,1)S(1)} %get-tuple-element.26), channel_id=1, source_target_pairs={{0,195},{1,194},{2,193},{3,192},{4,69},{5,68},{6,71},{7,70},{8,203... | collective-permute-start | bytes 540680 | tf_op jit(solution)/shard_map/ppermute | solution.py:32
  74.1 2.1 %collective-permute-done.8 = bf16[704,128]{1,0:T(8,128)(2,1)S(1)} collective-permute-done((bf16[704,128]{1,0:T(8,128)(2,1)S(1)}, bf16[704,128]{1,0:T(8,128)(2,1)S(1)}, u32[]{:S(2)}, u32[]{:S(2)}) %collective-permute-start.8) | collective-permute-done | bytes 180256 | tf_op jit(solution)/shard_map/ppermute | solution.py:32
  76.2 5.3 %collective-permute-done.9 = bf16[704,128]{1,0:T(8,128)(2,1)S(1)} collective-permute-done((bf16[704,128]{1,0:T(8,128)(2,1)S(1)}, bf16[704,128]{1,0:T(8,128)(2,1)S(1)}, u32[]{:S(2)}, u32[]{:S(2)}) %collective-permute-start.9) | collective-permute-done | bytes 180256 | tf_op jit(solution)/shard_map/ppermute | solution.py:32
  81.7 1.2 collective-permute-start.10
  82.9 2.2 %collective-permute-start.11 = (bf16[176,128]{1,0:T(8,128)(2,1)S(1)}, bf16[176,128]{1,0:T(8,128)(2,1)S(1)}, u32[]{:S(2)}, u32[]{:S(2)}) collective-permute-start(bf16[176,128]{1,0:T(8,128)(2,1)S(1)} %get-tuple-element.34), channel_id=1, source_target_pairs={{0,64},{1,65},{2,66},{3,67},{4,196},{5,197},{6,198},{7,199},{8,72}... | collective-permute-start | bytes 135176 | tf_op jit(solution)/shard_map/ppermute | solution.py:32
  85.1 1.7 %collective-permute-start.12 = (bf16[176,128]{1,0:T(8,128)(2,1)S(1)}, bf16[176,128]{1,0:T(8,128)(2,1)S(1)}, u32[]{:S(2)}, u32[]{:S(2)}) collective-permute-start(bf16[176,128]{1,0:T(8,128)(2,1)S(1)} %get-tuple-element.35), channel_id=1, source_target_pairs={{0,65},{1,64},{2,67},{3,66},{4,199},{5,198},{6,197},{7,196},{8,73}... | collective-permute-start | bytes 135176 | tf_op jit(solution)/shard_map/ppermute | solution.py:32
  87.0 4.3 %collective-permute-done.12 = bf16[176,128]{1,0:T(8,128)(2,1)S(1)} collective-permute-done((bf16[176,128]{1,0:T(8,128)(2,1)S(1)}, bf16[176,128]{1,0:T(8,128)(2,1)S(1)}, u32[]{:S(2)}, u32[]{:S(2)}) %collective-permute-start.12) | collective-permute-done | bytes 45088 | tf_op jit(solution)/shard_map/ppermute | solution.py:32
  91.7 3.1 %collective-permute-done.13 = bf16[176,128]{1,0:T(8,128)(2,1)S(1)} collective-permute-done((bf16[176,128]{1,0:T(8,128)(2,1)S(1)}, bf16[176,128]{1,0:T(8,128)(2,1)S(1)}, u32[]{:S(2)}, u32[]{:S(2)}) %collective-permute-start.13) | collective-permute-done | bytes 45088 | tf_op jit(solution)/shard_map/ppermute | solution.py:32
  95.7 3.1 %collective-permute-done.14 = bf16[176,128]{1,0:T(8,128)(2,1)S(1)} collective-permute-done((bf16[176,128]{1,0:T(8,128)(2,1)S(1)}, bf16[176,128]{1,0:T(8,128)(2,1)S(1)}, u32[]{:S(2)}, u32[]{:S(2)}) %collective-permute-start.14) | collective-permute-done | bytes 45088 | tf_op jit(solution)/shard_map/ppermute | solution.py:32
  99.1 3.8 %collective-permute-done.15 = bf16[176,128]{1,0:T(8,128)(2,1)S(1)} collective-permute-done((bf16[176,128]{1,0:T(8,128)(2,1)S(1)}, bf16[176,128]{1,0:T(8,128)(2,1)S(1)}, u32[]{:S(2)}, u32[]{:S(2)}) %collective-permute-start.15) | collective-permute-done | bytes 45088 | tf_op jit(solution)/shard_map/ppermute | solution.py:32
  103.0 2.1 %collective-permute-start.18 = (bf16[176,128]{1,0:T(8,128)(2,1)S(1)}, bf16[176,128]{1,0:T(8,128)(2,1)S(1)}, u32[]{:S(2)}, u32[]{:S(2)}) collective-permute-start(bf16[176,128]{1,0:T(8,128)(2,1)S(1)} %add_convert_fusion.1), channel_id=1, source_target_pairs={{0,1},{1,0},{2,3},{3,2},{4,7},{5,6},{6,5},{7,4},{8,9},{9,8},{10,11... | collective-permute-start | bytes 135176 | tf_op jit(solution)/shard_map/ppermute | solution.py:32
  105.6 2.5 %collective-permute-start.16 = (bf16[176,128]{1,0:T(8,128)(2,1)S(1)}, bf16[176,128]{1,0:T(8,128)(2,1)S(1)}, u32[]{:S(2)}, u32[]{:S(2)}) collective-permute-start(bf16[176,128]{1,0:T(8,128)(2,1)S(1)} %add_convert_fusion.1), channel_id=1, source_target_pairs={{0,65},{1,64},{2,67},{3,66},{4,199},{5,198},{6,197},{7,196},{8,73}... | collective-permute-start | bytes 135176 | tf_op jit(solution)/shard_map/ppermute | solution.py:32
  109.2 2.6 %collective-permute-done.16 = bf16[176,128]{1,0:T(8,128)(2,1)S(1)} collective-permute-done((bf16[176,128]{1,0:T(8,128)(2,1)S(1)}, bf16[176,128]{1,0:T(8,128)(2,1)S(1)}, u32[]{:S(2)}, u32[]{:S(2)}) %collective-permute-start.16) | collective-permute-done | bytes 45088 | tf_op jit(solution)/shard_map/ppermute | solution.py:32
  112.1 2.5 %collective-permute-start.19 = (bf16[704,128]{1,0:T(8,128)(2,1)S(1)}, bf16[704,128]{1,0:T(8,128)(2,1)S(1)}, u32[]{:S(2)}, u32[]{:S(2)}) collective-permute-start(bf16[704,128]{1,0:T(8,128)(2,1)S(1)} %bitcast.79), channel_id=1, source_target_pairs={{0,195},{1,194},{2,193},{3,192},{4,69},{5,68},{6,71},{7,70},{8,203... | collective-permute-start | bytes 540680 | tf_op jit(solution)/shard_map/ppermute | solution.py:32
  114.6 1.7 %collective-permute-done.21 = bf16[704,128]{1,0:T(8,128)(2,1)S(1)} collective-permute-done((bf16[704,128]{1,0:T(8,128)(2,1)S(1)}, bf16[704,128]{1,0:T(8,128)(2,1)S(1)}, u32[]{:S(2)}, u32[]{:S(2)}) %collective-permute-start.21) | collective-permute-done | bytes 180256 | tf_op jit(solution)/shard_map/ppermute | solution.py:32
  116.3 2.0 %collective-permute-done.20 = bf16[704,128]{1,0:T(8,128)(2,1)S(1)} collective-permute-done((bf16[704,128]{1,0:T(8,128)(2,1)S(1)}, bf16[704,128]{1,0:T(8,128)(2,1)S(1)}, u32[]{:S(2)}, u32[]{:S(2)}) %collective-permute-start.20) | collective-permute-done | bytes 180256 | tf_op jit(solution)/shard_map/ppermute | solution.py:32
  118.5 7.5 %collective-permute-start.22 = (bf16[2816,128]{1,0:T(8,128)(2,1)S(1)}, bf16[2816,128]{1,0:T(8,128)(2,1)S(1)}, u32[]{:S(2)}, u32[]{:S(2)}) collective-permute-start(bf16[2816,128]{1,0:T(8,128)(2,1)S(1)} %bitcast.72), channel_id=1, source_target_pairs={{0,4},{1,5},{2,6},{3,7},{4,0},{5,1},{6,2},{7,3},{8,12},{9,13},{10,... | collective-permute-start | bytes 2162696 | tf_op jit(solution)/shard_map/ppermute | solution.py:32
  128.5 1.3 %slice.63 = f32[3456,128]{1,0:T(8,128)} slice(f32[5632,128]{1,0:T(8,128)S(1)} %bitcast_convert_fusion), slice={[0:3456], [0:128]} | slice | bytes 3538944 | tf_op jit(solution)/shard_map/slice | solution.py:406
  (72 shorter events, 17.9 us)
Async XLA Ops:
  0.6 29.4 %copy-start.5 = (bf16[256,256]{1,0:T(8,128)(2,1)S(1)}, bf16[256,256]{1,0:T(8,128)(2,1)}, u32[]{:S(2)}) copy-start(bf16[256,256]{1,0:T(8,128)(2,1)} %grad0) | copy-start | bytes 393220
  0.6 32.7 %copy-start.9 = (s32[27,512]{1,0:T(8,128)S(1)}, s32[27,512]{1,0:T(8,128)}, u32[]{:S(2)}) copy-start(s32[27,512]{1,0:T(8,128)} %param.8) | copy-start | bytes 165892
  0.7 7.9 %collective-permute-start.2 = (bf16[512,128]{1,0:T(8,128)(2,1)}, bf16[512,128]{1,0:T(8,128)(2,1)S(1)}, u32[]{:S(2)}, u32[]{:S(2)}) collective-permute-start(bf16[512,128]{1,0:T(8,128)(2,1)} %part0.3), channel_id=1, source_target_pairs={{0,3},{1,2},{2,1},{3,0},{4,7},{5,6},{6,5},{7,4},{8,11},{9,10},{10,... | collective-permute-start | bytes 393224 | tf_op jit(solution)/shard_map/ppermute | solution.py:32
  4.0 5.6 %collective-permute-start.1 = (bf16[512,128]{1,0:T(8,128)(2,1)}, bf16[512,128]{1,0:T(8,128)(2,1)S(1)}, u32[]{:S(2)}, u32[]{:S(2)}) collective-permute-start(bf16[512,128]{1,0:T(8,128)(2,1)} %part0.3), channel_id=1, source_target_pairs={{0,2},{1,3},{2,0},{3,1},{4,6},{5,7},{6,4},{7,5},{8,10},{9,11},{10,... | collective-permute-start | bytes 393224 | tf_op jit(solution)/shard_map/ppermute | solution.py:32
  4.6 5.1 %collective-permute-start = (bf16[512,128]{1,0:T(8,128)(2,1)}, bf16[512,128]{1,0:T(8,128)(2,1)S(1)}, u32[]{:S(2)}, u32[]{:S(2)}) collective-permute-start(bf16[512,128]{1,0:T(8,128)(2,1)} %part0.3), channel_id=1, source_target_pairs={{0,1},{1,0},{2,3},{3,2},{4,5},{5,4},{6,7},{7,6},{8,9},{9,8},{10,11... | collective-permute-start | bytes 393224 | tf_op jit(solution)/shard_map/ppermute | solution.py:32
  8.6 1.1 copy-start.2
  14.9 32.4 %all-to-all-start = ((bf16[64,32,128]{2,1,0:T(8,128)(2,1)}), bf16[64,32,128]{2,1,0:T(8,128)(2,1)S(1)}, u32[]{:S(2)}, u32[]{:S(2)}) async-start(bf16[64,32,128]{2,1,0:T(8,128)(2,1)} %bitcast.73), calls=%async_computation | async-start | bytes 1048576 | tf_op jit(solution)/shard_map/all_to_all | solution.py:351
  30.0 8.0 %collective-permute-start.5 = (bf16[256,256]{1,0:T(8,128)(2,1)S(1)}, bf16[256,256]{1,0:T(8,128)(2,1)S(1)}, u32[]{:S(2)}, u32[]{:S(2)}) collective-permute-start(bf16[256,256]{1,0:T(8,128)(2,1)S(1)} %copy-done.5), channel_id=1, source_target_pairs={{0,3},{1,2},{2,1},{3,0},{4,7},{5,6},{6,5},{7,4},{8,11},{9,10},{10,... | collective-permute-start | bytes 393224 | tf_op jit(solution)/shard_map/ppermute | solution.py:32
  31.3 6.7 %collective-permute-start.4 = (bf16[256,256]{1,0:T(8,128)(2,1)S(1)}, bf16[256,256]{1,0:T(8,128)(2,1)S(1)}, u32[]{:S(2)}, u32[]{:S(2)}) collective-permute-start(bf16[256,256]{1,0:T(8,128)(2,1)S(1)} %copy-done.5), channel_id=1, source_target_pairs={{0,2},{1,3},{2,0},{3,1},{4,6},{5,7},{6,4},{7,5},{8,10},{9,11},{10,... | collective-permute-start | bytes 393224 | tf_op jit(solution)/shard_map/ppermute | solution.py:32
  31.9 7.2 %collective-permute-start.3 = (bf16[256,256]{1,0:T(8,128)(2,1)S(1)}, bf16[256,256]{1,0:T(8,128)(2,1)S(1)}, u32[]{:S(2)}, u32[]{:S(2)}) collective-permute-start(bf16[256,256]{1,0:T(8,128)(2,1)S(1)} %copy-done.5), channel_id=1, source_target_pairs={{0,1},{1,0},{2,3},{3,2},{4,5},{5,4},{6,7},{7,6},{8,9},{9,8},{10,11... | collective-permute-start | bytes 393224 | tf_op jit(solution)/shard_map/ppermute | solution.py:32
  34.7 12.6 %copy-start.10 = (s32[512]{0:T(512)}, s32[512]{0:T(512)S(1)}, u32[]{:S(2)}) copy-start(s32[512]{0:T(512)S(1)} %dynamic_slice.42) | copy-start | bytes 6148
  38.0 1.1 copy-start.6
  38.0 1.1 copy-start.7
  47.3 0.8 copy-start
  67.5 2.5 %collective-permute-start.6 = (bf16[2816,128]{1,0:T(8,128)(2,1)}, bf16[2816,128]{1,0:T(8,128)(2,1)S(1)}, u32[]{:S(2)}, u32[]{:S(2)}) collective-permute-start(bf16[2816,128]{1,0:T(8,128)(2,1)} %get-tuple-element.16), channel_id=1, source_target_pairs={{0,4},{1,5},{2,6},{3,7},{4,0},{5,1},{6,2},{7,3},{8,12},{9,13},{10,... | collective-permute-start | bytes 2162696 | tf_op jit(solution)/shard_map/ppermute | solution.py:32
  71.3 10.4 %copy-start.1 = (bf16[2048,128]{1,0:T(8,128)(2,1)S(1)}, bf16[2048,128]{1,0:T(8,128)(2,1)}, u32[]{:S(2)}) copy-start(bf16[2048,128]{1,0:T(8,128)(2,1)} %get-tuple-element.14) | copy-start | bytes 1572868
  71.4 10.1 %collective-permute-start.7 = (bf16[1728,128]{1,0:T(8,128)(2,1)S(1)}, bf16[1728,128]{1,0:T(8,128)(2,1)S(1)}, u32[]{:S(2)}, u32[]{:S(2)}) collective-permute-start(bf16[1728,128]{1,0:T(8,128)(2,1)S(1)} %pad_maximum_fusion.3), channel_id=1, source_target_pairs={{0,3},{1,2},{2,1},{3,0},{4,5},{5,4},{6,7},{7,6},{8,11},{9,10},{10,... | collective-permute-start | bytes 1327112 | tf_op jit(solution)/shard_map/ppermute | solution.py:32
  71.5 4.7 %collective-permute-start.8 = (bf16[704,128]{1,0:T(8,128)(2,1)S(1)}, bf16[704,128]{1,0:T(8,128)(2,1)S(1)}, u32[]{:S(2)}, u32[]{:S(2)}) collective-permute-start(bf16[704,128]{1,0:T(8,128)(2,1)S(1)} %get-tuple-element.25), channel_id=1, source_target_pairs={{0,192},{1,193},{2,194},{3,195},{4,68},{5,69},{6,70},{7,71},{8,200... | collective-permute-start | bytes 540680 | tf_op jit(solution)/shard_map/ppermute | solution.py:32
  72.8 8.7 %collective-permute-start.9 = (bf16[704,128]{1,0:T(8,128)(2,1)S(1)}, bf16[704,128]{1,0:T(8,128)(2,1)S(1)}, u32[]{:S(2)}, u32[]{:S(2)}) collective-permute-start(bf16[704,128]{1,0:T(8,128)(2,1)S(1)} %get-tuple-element.26), channel_id=1, source_target_pairs={{0,195},{1,194},{2,193},{3,192},{4,69},{5,68},{6,71},{7,70},{8,203... | collective-permute-start | bytes 540680 | tf_op jit(solution)/shard_map/ppermute | solution.py:32
  81.7 9.7 %collective-permute-start.10 = (bf16[688,128]{1,0:T(8,128)(2,1)S(1)}, bf16[688,128]{1,0:T(8,128)(2,1)S(1)}, u32[]{:S(2)}, u32[]{:S(2)}) collective-permute-start(bf16[688,128]{1,0:T(8,128)(2,1)S(1)} %pad_maximum_fusion.5), channel_id=1, source_target_pairs={{0,1},{1,0},{2,3},{3,2},{4,7},{5,6},{6,5},{7,4},{8,9},{9,8},{10,11... | collective-permute-start | bytes 528392 | tf_op jit(solution)/shard_map/ppermute | solution.py:32
  82.9 4.1 %collective-permute-start.11 = (bf16[176,128]{1,0:T(8,128)(2,1)S(1)}, bf16[176,128]{1,0:T(8,128)(2,1)S(1)}, u32[]{:S(2)}, u32[]{:S(2)}) collective-permute-start(bf16[176,128]{1,0:T(8,128)(2,1)S(1)} %get-tuple-element.34), channel_id=1, source_target_pairs={{0,64},{1,65},{2,66},{3,67},{4,196},{5,197},{6,198},{7,199},{8,72}... | collective-permute-start | bytes 135176 | tf_op jit(solution)/shard_map/ppermute | solution.py:32
  85.1 6.2 %collective-permute-start.12 = (bf16[176,128]{1,0:T(8,128)(2,1)S(1)}, bf16[176,128]{1,0:T(8,128)(2,1)S(1)}, u32[]{:S(2)}, u32[]{:S(2)}) collective-permute-start(bf16[176,128]{1,0:T(8,128)(2,1)S(1)} %get-tuple-element.35), channel_id=1, source_target_pairs={{0,65},{1,64},{2,67},{3,66},{4,199},{5,198},{6,197},{7,196},{8,73}... | collective-permute-start | bytes 135176 | tf_op jit(solution)/shard_map/ppermute | solution.py:32
  91.4 3.4 %collective-permute-start.13 = (bf16[176,128]{1,0:T(8,128)(2,1)S(1)}, bf16[176,128]{1,0:T(8,128)(2,1)S(1)}, u32[]{:S(2)}, u32[]{:S(2)}) collective-permute-start(bf16[176,128]{1,0:T(8,128)(2,1)S(1)} %fusion.8), channel_id=1, source_target_pairs={{0,8},{1,9},{2,10},{3,11},{4,12},{5,13},{6,14},{7,15},{8,0},{9,1},... | collective-permute-start | bytes 135176 | tf_op jit(solution)/shard_map/ppermute | solution.py:32
  94.8 3.9 %collective-permute-start.14 = (bf16[176,128]{1,0:T(8,128)(2,1)S(1)}, bf16[176,128]{1,0:T(8,128)(2,1)S(1)}, u32[]{:S(2)}, u32[]{:S(2)}) collective-permute-start(bf16[176,128]{1,0:T(8,128)(2,1)S(1)} %add_convert_fusion.3), channel_id=1, source_target_pairs={{0,16},{1,17},{2,18},{3,19},{4,20},{5,21},{6,22},{7,23},{8,24},{9,... | collective-permute-start | bytes 135176 | tf_op jit(solution)/shard_map/ppermute | solution.py:32
  98.7 4.2 %collective-permute-start.15 = (bf16[176,128]{1,0:T(8,128)(2,1)S(1)}, bf16[176,128]{1,0:T(8,128)(2,1)S(1)}, u32[]{:S(2)}, u32[]{:S(2)}) collective-permute-start(bf16[176,128]{1,0:T(8,128)(2,1)S(1)} %add_convert_fusion.2), channel_id=1, source_target_pairs={{0,56},{1,57},{2,58},{3,59},{4,60},{5,61},{6,62},{7,63},{8,48},{9,... | collective-permute-start | bytes 135176 | tf_op jit(solution)/shard_map/ppermute | solution.py:32
  103.0 5.2 %collective-permute-start.18 = (bf16[176,128]{1,0:T(8,128)(2,1)S(1)}, bf16[176,128]{1,0:T(8,128)(2,1)S(1)}, u32[]{:S(2)}, u32[]{:S(2)}) collective-permute-start(bf16[176,128]{1,0:T(8,128)(2,1)S(1)} %add_convert_fusion.1), channel_id=1, source_target_pairs={{0,1},{1,0},{2,3},{3,2},{4,7},{5,6},{6,5},{7,4},{8,9},{9,8},{10,11... | collective-permute-start | bytes 135176 | tf_op jit(solution)/shard_map/ppermute | solution.py:32
  105.1 4.1 %collective-permute-start.17 = (bf16[176,128]{1,0:T(8,128)(2,1)S(1)}, bf16[176,128]{1,0:T(8,128)(2,1)S(1)}, u32[]{:S(2)}, u32[]{:S(2)}) collective-permute-start(bf16[176,128]{1,0:T(8,128)(2,1)S(1)} %add_convert_fusion.1), channel_id=1, source_target_pairs={{0,64},{1,65},{2,66},{3,67},{4,196},{5,197},{6,198},{7,199},{8,72}... | collective-permute-start | bytes 135176 | tf_op jit(solution)/shard_map/ppermute | solution.py:32
  105.6 6.2 %collective-permute-start.16 = (bf16[176,128]{1,0:T(8,128)(2,1)S(1)}, bf16[176,128]{1,0:T(8,128)(2,1)S(1)}, u32[]{:S(2)}, u32[]{:S(2)}) collective-permute-start(bf16[176,128]{1,0:T(8,128)(2,1)S(1)} %add_convert_fusion.1), channel_id=1, source_target_pairs={{0,65},{1,64},{2,67},{3,66},{4,199},{5,198},{6,197},{7,196},{8,73}... | collective-permute-start | bytes 135176 | tf_op jit(solution)/shard_map/ppermute | solution.py:32
  111.9 4.4 %collective-permute-start.21 = (bf16[704,128]{1,0:T(8,128)(2,1)S(1)}, bf16[704,128]{1,0:T(8,128)(2,1)S(1)}, u32[]{:S(2)}, u32[]{:S(2)}) collective-permute-start(bf16[704,128]{1,0:T(8,128)(2,1)S(1)} %bitcast.77), channel_id=1, source_target_pairs={{0,3},{1,2},{2,1},{3,0},{4,5},{5,4},{6,7},{7,6},{8,11},{9,10},{10,... | collective-permute-start | bytes 540680 | tf_op jit(solution)/shard_map/ppermute | solution.py:32
  112.0 6.4 %collective-permute-start.20 = (bf16[704,128]{1,0:T(8,128)(2,1)S(1)}, bf16[704,128]{1,0:T(8,128)(2,1)S(1)}, u32[]{:S(2)}, u32[]{:S(2)}) collective-permute-start(bf16[704,128]{1,0:T(8,128)(2,1)S(1)} %bitcast.78), channel_id=1, source_target_pairs={{0,192},{1,193},{2,194},{3,195},{4,68},{5,69},{6,70},{7,71},{8,200... | collective-permute-start | bytes 540680 | tf_op jit(solution)/shard_map/ppermute | solution.py:32
  112.1 6.3 %collective-permute-start.19 = (bf16[704,128]{1,0:T(8,128)(2,1)S(1)}, bf16[704,128]{1,0:T(8,128)(2,1)S(1)}, u32[]{:S(2)}, u32[]{:S(2)}) collective-permute-start(bf16[704,128]{1,0:T(8,128)(2,1)S(1)} %bitcast.79), channel_id=1, source_target_pairs={{0,195},{1,194},{2,193},{3,192},{4,69},{5,68},{6,71},{7,70},{8,203... | collective-permute-start | bytes 540680 | tf_op jit(solution)/shard_map/ppermute | solution.py:32
  118.5 9.3 %collective-permute-start.22 = (bf16[2816,128]{1,0:T(8,128)(2,1)S(1)}, bf16[2816,128]{1,0:T(8,128)(2,1)S(1)}, u32[]{:S(2)}, u32[]{:S(2)}) collective-permute-start(bf16[2816,128]{1,0:T(8,128)(2,1)S(1)} %bitcast.72), channel_id=1, source_target_pairs={{0,4},{1,5},{2,6},{3,7},{4,0},{5,1},{6,2},{7,3},{8,12},{9,13},{10,... | collective-permute-start | bytes 2162696 | tf_op jit(solution)/shard_map/ppermute | solution.py:32
  (3 other events, 2.0 us)
